TPU v7x, 32 devices: a whole 2x2x4 slice. The times are simulated.
32 devices in a mesh: parts: 2 (over y), wide: 4 (over z), narrow: 4 (over x, core).
Axes of the slice: x: 2, y: 2, z: 4, core: 2. Of those that a mesh axis runs over, the one named last changes fastest.
Arguments:
- teacher: bfloat16 [4096, 4096], P(('parts', 'wide', 'narrow')), parts along dimension 0, may hold values from -6 to 6
- weight: float32 [4096, 256], replicated, may hold values from -0.09375 to 0.09375
- block_mask: int32 [8, 4], P('parts'), parts along dimension 0, may hold values 0 or 1
- item_group: int32 [4096], P(('parts', 'wide', 'narrow')), parts along dimension 0, may hold values from 0 to 7
Outputs:
- grad_weight: float32 [8192, 256], P(('parts', 'wide', 'narrow')), parts along dimension 0
There are 2 independent parts, one for each index of `parts`. A program takes and returns all parts, laid end to end along the dimension named above; an argument that names none is the same for every part. Nothing has to cross between parts.
Inputs may be any that keep to these rules, and one draw needn't show every extreme that they name: `block_mask`: 0 or 1 for each ordered pair of blocks.
All inputs are finite; a program needn't handle non-finite values.
Results may differ from a plain program's by a relative error of at most 0.0083.
Values may be sent and summed in bfloat16 or wider, within the bound.
No kernel may reach another device: no remote copies, remote signals or barrier semaphores. Data moves between devices by JAX's collectives and lax.ppermute only.
A program may use at most 64 MiB of HBM per device.

v0:
```python
import jax
import jax.numpy as jnp
from jax import lax
from jax.sharding import PartitionSpec as P


def shifted(value, axis, steps):
    count = lax.axis_size(axis)
    pairs = [(source, (source + steps) % count) for source in range(count)]
    return lax.ppermute(value, axis, pairs)


def tile_terms(panel, piece, factor):
    panel_t, panel_s, panel_g = panel
    piece_t, piece_s, piece_g = piece
    teach = (
        lax.dot_general(
            panel_t, piece_t, (((1,), (1,)), ((), ())), preferred_element_type=jnp.float32
        )
        / panel_t.shape[1]
    )
    stud = (
        lax.dot_general(
            panel_s, piece_s, (((1,), (1,)), ((), ())), preferred_element_type=jnp.float32
        )
        / panel_s.shape[1]
    )
    same = (panel_g[:, None] == piece_g[None, :]).astype(jnp.float32)
    pair_term = (factor * (1.0 + same) * (stud - teach)).astype(jnp.bfloat16)
    to_panel = jnp.dot(pair_term, piece_s, preferred_element_type=jnp.float32)
    to_piece = lax.dot_general(
        pair_term, panel_s, (((0,), (0,)), ((), ())), preferred_element_type=jnp.float32
    )
    return (to_panel, to_piece)


def per_device(teacher, weight, block_mask, item_group):
    rows_here = teacher.shape[0]
    width_out = weight.shape[1]
    low_weight = weight.astype(jnp.bfloat16)
    own_student = jnp.dot(teacher, low_weight, preferred_element_type=jnp.float32).astype(
        jnp.bfloat16
    )
    own_group = item_group.astype(jnp.bfloat16)
    panel = (
        lax.all_gather(teacher, "narrow", axis=0, tiled=True),
        lax.all_gather(own_student, "narrow", axis=0, tiled=True),
        lax.all_gather(own_group, "narrow", axis=0, tiled=True),
    )
    wide_count = lax.axis_size("wide")
    narrow_count = lax.axis_size("narrow")
    half_loop = wide_count // 2
    here = lax.axis_index("wide")
    mask_float = block_mask.astype(jnp.float32)
    row_ids = lax.broadcasted_iota(jnp.int32, mask_float.shape, 0)
    col_ids = lax.broadcasted_iota(jnp.int32, mask_float.shape, 1)

    def pick_mask(first, second):
        return jnp.sum(jnp.where((row_ids == first) & (col_ids == second), mask_float, 0.0))

    def tile_factor(step):
        other = (here - step) % wide_count
        forward = pick_mask(here, other)
        backward = pick_mask(other, here)
        both_ways = (step > 0) & (step < half_loop)
        return forward + jnp.where(both_ways, backward, 0.0)

    moving = (teacher, own_student, own_group)

    def advance(carried):
        return shifted((carried[0], carried[1], carried[2]), "wide", 1)

    def run_tile(carried, step):
        factor = tile_factor(step)
        return tile_terms(panel, carried, factor)

    panel_sum, accum = run_tile(moving, jnp.int32(0))

    def step_body(step, carry):
        carried, accum, panel_sum = carry
        carried = advance(carried)
        accum = shifted(accum, "wide", 1)
        to_panel, to_piece = run_tile(carried, step)
        return (carried, accum + to_piece, panel_sum + to_panel)

    moving, accum, panel_sum = lax.fori_loop(
        1, half_loop + 1, step_body, (moving, accum, panel_sum)
    )
    returned = shifted(accum, "wide", -half_loop)
    owned = lax.psum_scatter(panel_sum, "narrow", scatter_dimension=0, tiled=True)
    total_items = rows_here * wide_count * narrow_count
    coef = 2.0 * teacher.shape[1] / (total_items * width_out)
    grad_student = ((owned + returned) * coef).astype(jnp.bfloat16)
    return lax.psum_scatter(
        lax.dot_general(
            teacher, grad_student, (((0,), (0,)), ((), ())), preferred_element_type=jnp.float32
        ),
        ("wide", "narrow"),
        scatter_dimension=0,
        tiled=True,
    )


def solution(mesh):
    in_specs = (
        P(("parts", "wide", "narrow"), None),
        P(),
        P("parts", None),
        P(("parts", "wide", "narrow")),
    )
    out_specs = P(("parts", "wide", "narrow"), None)
    return jax.shard_map(
        per_device, mesh=mesh, in_specs=in_specs, out_specs=out_specs, check_vma=False
    )
```

profile of v0, /device:TPU:0, one launch (start us, length us, event | category | flops | bytes accessed | tf_op | source)
XLA Modules:
  0.0 225.8 jit_solution(6743651973957401759)
XLA Ops:
  6.5 0.7 all-gather.3.cloned.1.call-update
  7.3 2.3 %copy.9 = bf16[128,4096]{1,0:T(8,128)(2,1)} copy(bf16[128,4096]{1,0:T(8,128)(2,1)} %param.6) | data formatting | bytes 2097152
  9.6 0.7 convert_element_type.44
  10.3 0.7 convert_bitcast_fusion
  10.9 5.9 %all-gather = bf16[4,1,128]{2,1,0:T(2,128)(2,1)S(1)} all-gather(bf16[1,1,128]{2,1,0:T(2,128)(2,1)S(1)} %get-tuple-element.405), channel_id=1, replica_groups=mesh['parts'=2,'wide'=4,'narrow'=4] {'narrow'}, dimensions={0}, use_global_device_ids=true | all-gather | bytes 1280 | tf_op jit(solution)/shard_map/all_gather | solution.py:48
  16.9 3.5 %fusion.12 = bf16[128,256]{1,0:T(8,128)(2,1)S(1)} fusion(bf16[128,4096]{1,0:T(8,128)(2,1)} %param.6, f32[4096,256]{1,0:T(8,128)} %param.7), kind=kOutput, calls=%fused_computation.24 | convolution fusion | flops 269516800 | bytes 5308416 | tf_op jit(solution)/shard_map/dot_general | solution.py:41
  20.4 7.9 %all_gather.10 = bf16[512,256]{1,0:T(8,128)(2,1)S(1)} all-gather(bf16[128,256]{1,0:T(8,128)(2,1)S(1)} %fusion.12), channel_id=1, replica_groups=mesh['parts'=2,'wide'=4,'narrow'=4] {'narrow'}, dimensions={0}, use_global_device_ids=true | all-gather | bytes 327680 | tf_op jit(solution)/shard_map/all_gather | solution.py:47
  28.3 0.7 select_reduce_fusion.2
  29.0 18.5 %all-gather.3.cloned.1.call-done = bf16[512,4096]{1,0:T(8,128)(2,1)} async-done(((bf16[128,4096]{1,0:T(8,128)(2,1)}), bf16[512,4096]{1,0:T(8,128)(2,1)}) %all-gather.3.cloned.1.call-update) | async-done | bytes 4194320 | tf_op jit(solution)/shard_map/all_gather | solution.py:46
  47.5 3.4 %convolution_multiply_fusion.3 = f32[512,128]{1,0:T(8,128)S(1)} fusion(bf16[512,4096]{1,0:T(8,128)(2,1)} %all-gather.3.cloned.1.call-done, bf16[128,4096]{1,0:T(8,128)(2,1)S(1)} %copy-done), kind=kOutput, calls=%fused_computation.22 | convolution fusion | flops 536936448 | bytes 5505024 | tf_op jit(solution)/shard_map/dot_general | solution.py:17
  51.0 0.9 fusion.11
  52.3 68.4 %while.25 = (s32[]{:T(128)}, bf16[128,4096]{1,0:T(8,128)(2,1)}, bf16[128,256]{1,0:T(8,128)(2,1)S(1)}, bf16[128]{0:T(256)(128)(2,1)S(1)}, f32[128,256]{1,0:T(8,12...) while((s32[]{:T(128)}, bf16[128,4096]{1,0:T(8,128)(2,1)}, ...), condition=%wide.region_4.5_spmd.clone.clone, body=%wide.region_1.4_spmd.clone.clone.sunk | while | flops 638288000 | bytes 15338808 | solution.py:86
  52.3 1.5 collective-permute-start
  53.8 1.5 collective-permute-start.2
  55.3 1.5 collective-permute-start.1
  59.1 21.3 %collective-permute-done.2 = bf16[128]{0:T(256)(128)(2,1)S(1)} collective-permute-done((bf16[128]{0:T(256)(128)(2,1)S(1)}, bf16[128]{0:T(256)(128)(2,1)S(1)}, u32[]{:S(2)}, u32[]{:S(2)}) %collective-permute-start.2) | collective-permute-done | bytes 288 | tf_op jit(solution)/shard_map/while/body/eval_jaxpr/ppermute | solution.py:10
  80.4 1.3 collective-permute-done.1
  81.8 1.0 copy.21
  82.8 3.4 %convolution_multiply_fusion.5 = f32[512,128]{1,0:T(8,128)S(1)} fusion(bf16[512,4096]{1,0:T(8,128)(2,1)} %get-tuple-element.524, bf16[128,4096]{1,0:T(8,128)(2,1)S(1)} %collective-permute-done), kind=kOutput, calls=%fused_computation.5.clone.1 | convolution fusion | flops 536936448 | bytes 5505024 | tf_op jit(solution)/shard_map/while/body/eval_jaxpr/dot_general | solution.py:17
  87.0 1.1 collective-permute-start.2
  88.1 1.5 collective-permute-start.1
  89.6 2.3 %collective-permute-start.3 = (f32[128,256]{1,0:T(8,128)S(1)}, f32[128,256]{1,0:T(8,128)S(1)}, u32[]{:S(2)}, u32[]{:S(2)}) collective-permute-start(f32[128,256]{1,0:T(8,128)S(1)} %get-tuple-element.501), channel_id=1, source_target_pairs={{0,4},{4,8},{8,12},{12,0},{1,5},{5,9},{9,13},{13,1},{2,6},{6,10},{... | collective-permute-start | bytes 393224 | tf_op jit(solution)/shard_map/while/body/eval_jaxpr/ppermute | solution.py:10
  93.7 21.2 %collective-permute-done.2 = bf16[128]{0:T(256)(128)(2,1)S(1)} collective-permute-done((bf16[128]{0:T(256)(128)(2,1)S(1)}, bf16[128]{0:T(256)(128)(2,1)S(1)}, u32[]{:S(2)}, u32[]{:S(2)}) %collective-permute-start.2) | collective-permute-done | bytes 288 | tf_op jit(solution)/shard_map/while/body/eval_jaxpr/ppermute | solution.py:10
  114.9 0.6 collective-permute-done.1
  115.6 1.0 copy.21
  116.6 3.4 %convolution_multiply_fusion.5 = f32[512,128]{1,0:T(8,128)S(1)} fusion(bf16[512,4096]{1,0:T(8,128)(2,1)} %get-tuple-element.524, bf16[128,4096]{1,0:T(8,128)(2,1)S(1)} %collective-permute-done), kind=kOutput, calls=%fused_computation.5.clone.1 | convolution fusion | flops 536936448 | bytes 5505024 | tf_op jit(solution)/shard_map/while/body/eval_jaxpr/dot_general | solution.py:17
  120.7 0.8 copy-done.1
  121.7 5.9 %collective-permute-done.4 = f32[128,256]{1,0:T(8,128)S(1)} collective-permute-done((f32[128,256]{1,0:T(8,128)S(1)}, f32[128,256]{1,0:T(8,128)S(1)}, u32[]{:S(2)}, u32[]{:S(2)}) %collective-permute-start.4) | collective-permute-done | bytes 131104 | tf_op jit(solution)/shard_map/ppermute | solution.py:10
  127.5 13.1 %reduce-scatter.3.cloned.1.call-done = f32[128,256]{1,0:T(8,128)} async-done(((f32[512,256]{1,0:T(8,128)}), f32[128,256]{1,0:T(8,128)}) %reduce-scatter.3.cloned.1.call-update) | async-done | bytes 131088 | tf_op jit(solution)/shard_map/reduce_scatter | solution.py:90
  140.6 3.6 %convolution_bitcast_fusion = f32[4096,256]{0,1:T(8,128)} fusion(bf16[128,4096]{1,0:T(8,128)(2,1)S(1)} %copy-done, f32[128,256]{1,0:T(8,128)} %reduce-scatter.3.cloned.1.call-done, f32[128,256]{1,0:T(8,128)S(1)} %collective-permute-done.4), kind=kOutput, calls=%fused_computation.16 | convolution fusion | flops 268533760 | bytes 5505024 | tf_op jit(solution)/shard_map/dot_general | solution.py:95
  144.2 73.2 %reduce-scatter.5.cloned.1.call-done = f32[256,256]{0,1:T(8,128)} async-done(((f32[4096,256]{0,1:T(8,128)}), f32[256,256]{0,1:T(8,128)}) %reduce-scatter.5.cloned.1.call-update) | async-done | bytes 262160 | tf_op jit(solution)/shard_map/reduce_scatter | solution.py:94
  217.5 1.8 copy.7
  (33 shorter events, 3.8 us)
Async XLA Ops:
  6.5 41.0 %copy-start = (bf16[128,4096]{1,0:T(8,128)(2,1)S(1)}, bf16[128,4096]{1,0:T(8,128)(2,1)}, u32[]{:S(2)}) copy-start(bf16[128,4096]{1,0:T(8,128)(2,1)} %param.6) | copy-start | bytes 3145732
  6.5 21.8 %copy-start.2 = (s32[4,4]{1,0:T(4,128)S(1)}, s32[4,4]{1,0:T(4,128)}, u32[]{:S(2)}) copy-start(s32[4,4]{1,0:T(4,128)} %param.8) | copy-start | bytes 196
  6.5 41.0 %all-gather.3.cloned.1.call-start = ((), (), s32[]{:S(2)}) async-start(), calls=%async_computation.2 | async-start | bytes 5242880 | tf_op jit(solution)/shard_map/all_gather | solution.py:46
  7.3 133.4 %reduce-scatter.3.cloned.1.call-start = ((), (), s32[]{:S(2)}) async-start(), calls=%async_computation.3 | async-start | bytes 655360 | tf_op jit(solution)/shard_map/reduce_scatter | solution.py:90
  52.3 29.5 %collective-permute-start = (bf16[128,4096]{1,0:T(8,128)(2,1)}, bf16[128,4096]{1,0:T(8,128)(2,1)S(1)}, u32[]{:S(2)}, u32[]{:S(2)}) collective-permute-start(bf16[128,4096]{1,0:T(8,128)(2,1)} %get-tuple-element.498), channel_id=1, source_target_pairs={{0,4},{4,8},{8,12},{12,0},{1,5},{5,9},{9,13},{13,1},{2,6},{6,10},{... | collective-permute-start | bytes 3145736 | tf_op jit(solution)/shard_map/while/body/eval_jaxpr/ppermute | solution.py:10
  53.8 26.6 %collective-permute-start.2 = (bf16[128]{0:T(256)(128)(2,1)S(1)}, bf16[128]{0:T(256)(128)(2,1)S(1)}, u32[]{:S(2)}, u32[]{:S(2)}) collective-permute-start(bf16[128]{0:T(256)(128)(2,1)S(1)} %get-tuple-element.500), channel_id=1, source_target_pairs={{0,4},{4,8},{8,12},{12,0},{1,5},{5,9},{9,13},{13,1},{2,6},{6,10},{... | collective-permute-start | bytes 776 | tf_op jit(solution)/shard_map/while/body/eval_jaxpr/ppermute | solution.py:10
  55.3 26.5 %collective-permute-start.1 = (bf16[128,256]{1,0:T(8,128)(2,1)S(1)}, bf16[128,256]{1,0:T(8,128)(2,1)S(1)}, u32[]{:S(2)}, u32[]{:S(2)}) collective-permute-start(bf16[128,256]{1,0:T(8,128)(2,1)S(1)} %get-tuple-element.499), channel_id=1, source_target_pairs={{0,4},{4,8},{8,12},{12,0},{1,5},{5,9},{9,13},{13,1},{2,6},{6,10},{... | collective-permute-start | bytes 196616 | tf_op jit(solution)/shard_map/while/body/eval_jaxpr/ppermute | solution.py:10
  56.8 29.6 %collective-permute-start.3 = (f32[128,256]{1,0:T(8,128)S(1)}, f32[128,256]{1,0:T(8,128)S(1)}, u32[]{:S(2)}, u32[]{:S(2)}) collective-permute-start(f32[128,256]{1,0:T(8,128)S(1)} %get-tuple-element.501), channel_id=1, source_target_pairs={{0,4},{4,8},{8,12},{12,0},{1,5},{5,9},{9,13},{13,1},{2,6},{6,10},{... | collective-permute-start | bytes 393224 | tf_op jit(solution)/shard_map/while/body/eval_jaxpr/ppermute | solution.py:10
  86.9 28.7 %collective-permute-start = (bf16[128,4096]{1,0:T(8,128)(2,1)}, bf16[128,4096]{1,0:T(8,128)(2,1)S(1)}, u32[]{:S(2)}, u32[]{:S(2)}) collective-permute-start(bf16[128,4096]{1,0:T(8,128)(2,1)} %get-tuple-element.498), channel_id=1, source_target_pairs={{0,4},{4,8},{8,12},{12,0},{1,5},{5,9},{9,13},{13,1},{2,6},{6,10},{... | collective-permute-start | bytes 3145736 | tf_op jit(solution)/shard_map/while/body/eval_jaxpr/ppermute | solution.py:10
  87.0 27.9 %collective-permute-start.2 = (bf16[128]{0:T(256)(128)(2,1)S(1)}, bf16[128]{0:T(256)(128)(2,1)S(1)}, u32[]{:S(2)}, u32[]{:S(2)}) collective-permute-start(bf16[128]{0:T(256)(128)(2,1)S(1)} %get-tuple-element.500), channel_id=1, source_target_pairs={{0,4},{4,8},{8,12},{12,0},{1,5},{5,9},{9,13},{13,1},{2,6},{6,10},{... | collective-permute-start | bytes 776 | tf_op jit(solution)/shard_map/while/body/eval_jaxpr/ppermute | solution.py:10
  88.1 27.4 %collective-permute-start.1 = (bf16[128,256]{1,0:T(8,128)(2,1)S(1)}, bf16[128,256]{1,0:T(8,128)(2,1)S(1)}, u32[]{:S(2)}, u32[]{:S(2)}) collective-permute-start(bf16[128,256]{1,0:T(8,128)(2,1)S(1)} %get-tuple-element.499), channel_id=1, source_target_pairs={{0,4},{4,8},{8,12},{12,0},{1,5},{5,9},{9,13},{13,1},{2,6},{6,10},{... | collective-permute-start | bytes 196616 | tf_op jit(solution)/shard_map/while/body/eval_jaxpr/ppermute | solution.py:10
  89.6 30.6 %collective-permute-start.3 = (f32[128,256]{1,0:T(8,128)S(1)}, f32[128,256]{1,0:T(8,128)S(1)}, u32[]{:S(2)}, u32[]{:S(2)}) collective-permute-start(f32[128,256]{1,0:T(8,128)S(1)} %get-tuple-element.501), channel_id=1, source_target_pairs={{0,4},{4,8},{8,12},{12,0},{1,5},{5,9},{9,13},{13,1},{2,6},{6,10},{... | collective-permute-start | bytes 393224 | tf_op jit(solution)/shard_map/while/body/eval_jaxpr/ppermute | solution.py:10
  120.7 0.8 copy-start.1
  121.5 95.9 %reduce-scatter.5.cloned.1.call-start = ((), (), s32[]{:S(2)}) async-start(), calls=%async_computation.4 | async-start | bytes 4456448 | tf_op jit(solution)/shard_map/reduce_scatter | solution.py:94
  121.6 5.9 %collective-permute-start.4 = (f32[128,256]{1,0:T(8,128)S(1)}, f32[128,256]{1,0:T(8,128)S(1)}, u32[]{:S(2)}, u32[]{:S(2)}) collective-permute-start(f32[128,256]{1,0:T(8,128)S(1)} %get-tuple-element.322), channel_id=1, source_target_pairs={{0,8},{4,12},{8,0},{12,4},{1,9},{5,13},{9,1},{13,5},{2,10},{6,14},... | collective-permute-start | bytes 393224 | tf_op jit(solution)/shard_map/ppermute | solution.py:10
Sparse Core Ops, SparseCore 0:
  8.9 38.5 all-gather.2
  121.7 18.9 reduce-scatter.2
  145.0 72.4 reduce-scatter.4
where the time goes:
time: 226 us
  waiting for transfers between devices  156 us (69%)
  matrix products  20 us (9%)
  blocking collectives  13.9 us (6%)
  between operations  13.2 us (6%)
  starting transfers between devices  10.2 us (5%)
  local copies, waits for them, and re-layouts  6.83 us (3%)
  other arithmetic  3.27 us (1%)
  loops' own time  2.5 us (1%)
    reduce_scatter x1, waiting for transfers between devices, per_device(): lax.psum_scatter(lax.dot_general(teacher, grad_student, (((0,), (0,)), ((...  73.2 us
    ppermute x9, waiting for transfers between devices, shifted(): return lax.ppermute(value, axis, pairs)  50.3 us
    all_gather x1, waiting for transfers between devices, per_device(): lax.all_gather(teacher, 'narrow', axis=0, tiled=True)  18.5 us
    reduce_scatter x1, waiting for transfers between devices, per_device(): lax.psum_scatter(panel_sum, 'narrow', scatter_dimension=0, tiled=True)  13.1 us
    dot_general x3, matrix products, tile_terms(): lax.dot_general(panel_t, piece_t, (((1,), (1,)), ((), ())), preferred_ele...  10.3 us
    ppermute x9, starting transfers between devices, shifted(): return lax.ppermute(value, axis, pairs)  10.1 us
    all_gather x1, blocking collectives, per_device(): lax.all_gather(own_student, 'narrow', axis=0, tiled=True)  7.95 us
    all_gather x1, blocking collectives, per_device(): lax.all_gather(own_group, 'narrow', axis=0, tiled=True)  5.94 us
  transfers between devices with their start and end apart: 12, of which 8 were waited for; matrix products, arithmetic and copies ran while one was open for 8% of the time, Pallas kernels for 0%

commit v1 on v0

v1 whole, which is shorter than its diff:
```python
import functools

import jax
import jax.numpy as jnp
from jax import lax
from jax.experimental import pallas as pl
from jax.experimental.pallas import tpu as pltpu
from jax.sharding import PartitionSpec as P

ANY = pl.BlockSpec(memory_space=pl.ANY)
VMEM = pl.BlockSpec(memory_space=pltpu.VMEM)
SMEM = pl.BlockSpec(memory_space=pltpu.SMEM)
MIB = 1024 * 1024
EXTRA = 16


def swapped(value, axis, bit):
    count = lax.axis_size(axis)
    return lax.ppermute(value, axis, [(source, source ^ bit) for source in range(count)])


def in_plane(value, axis):
    found = {0: value}
    bit = lax.axis_size(axis) // 2
    while bit:
        for k in sorted(found):
            found[k ^ bit] = swapped(found[k], axis, bit)
        bit //= 2
    return [found[k] for k in sorted(found)]


def nt(a, b):
    return lax.dot_general(a, b, (((1,), (1,)), ((), ())), preferred_element_type=jnp.float32)


def loop(count, body):
    if count <= 4:
        for step in range(count):
            body(step)
    else:
        lax.fori_loop(0, count, lambda step, carry: (body(step), carry)[1], 0)


def pair_kernel(planes, lanes, rows, cols, out, width, *refs):
    pieces = planes * lanes
    panel = planes * rows
    pw = refs[0]
    t_in = refs[1 : 1 + pieces]
    s_in = refs[1 + pieces : 1 + pieces + lanes]
    outs = refs[1 + pieces + lanes : 1 + pieces + lanes + planes]
    t_all, s_all, g_raw, g_row, g_col, total, t_sem, s_sem = refs[1 + pieces + lanes + planes :]
    prow = rows + EXTRA

    def t_copy(m, k):
        at = m * planes + k
        return pltpu.make_async_copy(
            t_in[at], t_all.at[pl.ds(at * rows, rows)], t_sem.at[at]
        )

    def s_copy(m, k):
        at = m * planes + k
        return pltpu.make_async_copy(
            s_in[m].at[pl.ds(k * prow, rows)], s_all.at[pl.ds(at * rows, rows)], s_sem.at[0, at]
        )

    def g_copy(m, k):
        at = m * planes + k
        return pltpu.make_async_copy(
            s_in[m].at[pl.ds(k * prow + rows, EXTRA)],
            g_raw.at[pl.ds(at * EXTRA, EXTRA)],
            s_sem.at[1, at],
        )

    for m in range(lanes):
        for k in range(planes):
            g_copy(m, k).start()
            t_copy(m, k).start()
            s_copy(m, k).start()
    for m in range(lanes):
        for k in range(planes):
            at = m * planes + k
            g_copy(m, k).wait()
            line = g_raw[at * EXTRA : (at + 1) * EXTRA, :rows].astype(jnp.float32)[:1]
            g_row[:, at * rows : (at + 1) * rows] = jnp.broadcast_to(line, (8, rows))
            if m == 0:
                g_col[k * rows : (k + 1) * rows, :] = jnp.broadcast_to(line, (128, rows)).T
    total[...] = jnp.zeros_like(total)
    side = min(panel, 512)
    steps = panel // side
    group = side // rows

    for m in range(lanes):
        for k in range(planes):
            t_copy(m, k).wait()
            s_copy(m, k).wait()

        def one_row(it, m=m):
            at_i = pl.multiple_of(it * side, side)
            rows_t = t_all[pl.ds(at_i, side), :]
            col = g_col[pl.ds(at_i, side), :]

            def one_tile(jt):
                in_panel = pl.multiple_of(jt * side, side)
                at_j = pl.multiple_of(m * panel + jt * side, side)
                teach = nt(rows_t, t_all[pl.ds(at_j, side), :]) * (-1.0 / width)
                students = s_all[pl.ds(at_j, side), :]
                line = g_row[:1, pl.ds(at_j, side)]
                same = jnp.concatenate([col] * (side // 128), 1) == line
                terms = []
                for k in range(group):
                    weight = pw[pl.ds(it * group + k, 1), pl.ds(in_panel, side)]
                    factor = jnp.where(same[k * rows : (k + 1) * rows], 2.0 * weight, weight)
                    error = teach[k * rows : (k + 1) * rows]
                    if k == 0:
                        stud = nt(s_all[:rows, :], students) * (1.0 / out)
                        if steps > 1:
                            stud = jnp.where(it == 0, stud, 0.0)
                        error = error + stud
                    terms.append((factor * error).astype(jnp.bfloat16))
                term = jnp.concatenate(terms, 0)
                total[pl.ds(at_i, side), :] += jnp.dot(
                    term, students, preferred_element_type=jnp.float32
                )

            loop(steps, one_tile)

        loop(steps, one_row)
    for k in range(planes):
        outs[k][...] = total[k * rows : (k + 1) * rows, :].astype(outs[k].dtype)


def keep_kernel(pieces, rows, cols, lanes, lane, *refs):
    t_in, result, t_all, sem = refs[:pieces], refs[pieces], refs[pieces + 1], refs[pieces + 2]

    def copy(at):
        return pltpu.make_async_copy(t_in[at], t_all.at[pl.ds(at * rows, rows)], sem.at[at])

    for at in range(pieces):
        copy(at).start()
    for at in range(pieces):
        copy(at).wait()
    keep = cols // lanes
    for m in range(lanes):

        @pl.when(lane[0] == m)
        def _(m=m):
            result[...] = t_all[:, m * keep : (m + 1) * keep].T


def last_kernel(pieces, rows, *refs):
    t_keep, g_in, result, g_all, sem = refs[0], refs[1 : 1 + pieces], *refs[1 + pieces :]

    def copy(at):
        return pltpu.make_async_copy(g_in[at], g_all.at[pl.ds(at * rows, rows)], sem.at[at])

    for at in range(pieces):
        copy(at).start()
    for at in range(pieces):
        copy(at).wait()
    result[...] = jnp.dot(t_keep[...], g_all[...], preferred_element_type=jnp.float32)


def per_device(teacher, weight, block_mask, item_group):
    rows, width = teacher.shape
    out = weight.shape[1]
    planes = lax.axis_size("wide")
    lanes = lax.axis_size("narrow")
    plane = lax.axis_index("wide")
    lane = lax.axis_index("narrow")
    cols = width // planes
    items = rows * planes * lanes
    panel = rows * planes
    pieces = planes * lanes

    def cut(k):
        return lax.dynamic_slice_in_dim(teacher, (plane ^ k) * cols, cols, 1)

    t_parts = [cut(0)] + [swapped(cut(k), "wide", k) for k in range(1, planes)]
    low_weight = weight.astype(jnp.bfloat16)
    student = jnp.dot(teacher, low_weight, preferred_element_type=jnp.float32).astype(jnp.bfloat16)
    extra = jnp.zeros((EXTRA, out), jnp.bfloat16).at[0, :rows].set(item_group.astype(jnp.bfloat16))
    packed = jnp.concatenate([student, extra], 0)
    s_parts = [packed] + [swapped(packed, "wide", k) for k in range(1, planes)]

    t_all = [in_plane(t, "narrow") for t in t_parts]
    t_all = [t_all[k][m] for m in range(lanes) for k in range(planes)]
    s_all = in_plane(jnp.concatenate(s_parts, 0), "narrow")

    sym = (block_mask + block_mask.T).astype(jnp.float32)
    order = plane ^ jnp.arange(planes)
    sym = jnp.take(jnp.take(sym, order, 0), order, 1)
    pair_weight = jnp.repeat(sym, rows, 1)
    parts = pl.pallas_call(
        functools.partial(pair_kernel, planes, lanes, rows, cols, out, width),
        out_shape=[jax.ShapeDtypeStruct((rows, out), jnp.float32)]
        + [jax.ShapeDtypeStruct((rows, out), jnp.bfloat16)] * (planes - 1),
        in_specs=[VMEM] + [ANY] * (pieces + lanes),
        out_specs=[VMEM] * planes,
        scratch_shapes=[
            pltpu.VMEM((items, cols), jnp.bfloat16),
            pltpu.VMEM((items, out), jnp.bfloat16),
            pltpu.VMEM((pieces * EXTRA, out), jnp.bfloat16),
            pltpu.VMEM((8, items), jnp.float32),
            pltpu.VMEM((panel, 128), jnp.float32),
            pltpu.VMEM((panel, out), jnp.float32),
            pltpu.SemaphoreType.DMA((pieces,)),
            pltpu.SemaphoreType.DMA((2, pieces)),
        ],
        compiler_params=pltpu.CompilerParams(vmem_limit_bytes=44 * MIB),
        cost_estimate=pl.CostEstimate(
            flops=2 * panel * items * (cols + out),
            bytes_accessed=2 * items * (cols + out),
            transcendentals=0,
        ),
        name="pairs",
    )(pair_weight, *t_all, *s_all)

    keep = cols // lanes
    t_keep = pl.pallas_call(
        functools.partial(keep_kernel, pieces, rows, cols, lanes),
        out_shape=jax.ShapeDtypeStruct((keep, items), jnp.bfloat16),
        in_specs=[SMEM] + [ANY] * pieces,
        out_specs=VMEM,
        scratch_shapes=[
            pltpu.VMEM((items, cols), jnp.bfloat16),
            pltpu.SemaphoreType.DMA((pieces,)),
        ],
        compiler_params=pltpu.CompilerParams(vmem_limit_bytes=32 * MIB),
        cost_estimate=pl.CostEstimate(
            flops=0, bytes_accessed=2 * items * (cols + keep), transcendentals=0
        ),
        name="keep",
    )(lane.astype(jnp.int32).reshape(1), *t_all)

    mine = parts[0]
    for k in range(1, planes):
        mine = mine + swapped(parts[k], "wide", k).astype(jnp.float32)
    coef = 2.0 * width / (items * out)
    grad = (mine * coef).astype(jnp.bfloat16)
    g_parts = [grad] + [swapped(grad, "wide", k) for k in range(1, planes)]
    first = in_plane(grad, "narrow")
    rest = in_plane(jnp.concatenate(g_parts[1:], 0), "narrow")
    g_all = []
    for m in range(lanes):
        g_all.append(first[m])
        for k in range(planes - 1):
            g_all.append(rest[m][k * rows : (k + 1) * rows])
    return pl.pallas_call(
        functools.partial(last_kernel, pieces, rows),
        out_shape=jax.ShapeDtypeStruct((keep, out), jnp.float32),
        in_specs=[VMEM] + [ANY] * pieces,
        out_specs=VMEM,
        scratch_shapes=[
            pltpu.VMEM((items, out), jnp.bfloat16),
            pltpu.SemaphoreType.DMA((pieces,)),
        ],
        compiler_params=pltpu.CompilerParams(vmem_limit_bytes=24 * MIB),
        cost_estimate=pl.CostEstimate(
            flops=2 * items * keep * out, bytes_accessed=2 * items * (keep + out), transcendentals=0
        ),
        name="last",
    )(t_keep, *g_all)


def solution(mesh):
    in_specs = (
        P(("parts", "wide", "narrow"), None),
        P(),
        P("parts", None),
        P(("parts", "wide", "narrow")),
    )
    out_specs = P(("parts", "wide", "narrow"), None)
    return jax.shard_map(
        per_device, mesh=mesh, in_specs=in_specs, out_specs=out_specs, check_vma=False
    )
```

time: 226 us -> 102 us (0.45)
  waiting for transfers between devices: 156 us -> 46.3 us
  starting transfers between devices: 10.2 us -> 30.7 us
  matrix products: 20 us -> 2.95 us
  blocking collectives: 13.9 us -> 0 us
  between operations: 13.2 us -> 0.22 us
  Pallas kernels: 0 us -> 11.6 us
  loops' own time: 2.5 us -> 0 us
  other arithmetic: 3.27 us -> 0.96 us
    reduce_scatter x2 -> x0, waiting for transfers between devices: 86.3 us -> none  [the longest x1 73.2 us: per_device(): lax.psum_scatter(lax.dot_general(teacher, grad_student, (((0,), (0,)), ((...]
    ppermute x9 -> x33, starting transfers between devices: 10.1 us -> 30.7 us  [swapped(): lax.ppermute(value, axis, [(source, source ^ bit) for source in range(cou...]
    all_gather x1 -> x0, waiting for transfers between devices: 18.5 us -> none  [per_device(): lax.all_gather(teacher, 'narrow', axis=0, tiled=True)]
    dot_general x13 -> x0, matrix products: 16.5 us -> none  [the longest x3 10.3 us: tile_terms(): lax.dot_general(panel_t, piece_t, (((1,), (1,)), ((), ())), preferred_ele...]
    all_gather x2 -> x0, blocking collectives: 13.9 us -> none  [the longest x1 7.95 us: per_device(): lax.all_gather(own_student, 'narrow', axis=0, tiled=True)]
    pallas_call x0 -> x3, Pallas kernels: none -> 11.6 us  [the longest x1 7.03 us: per_device(): pl.pallas_call(functools.partial(pair_kernel, planes, lanes, rows, cols,...]
    ppermute x9 -> x33, waiting for transfers between devices: 50.3 us -> 46.3 us  [swapped(): lax.ppermute(value, axis, [(source, source ^ bit) for source in range(cou...]
    unnamed x7 -> x23, local copies, waits for them, and re-layouts: 3.08 us -> 5.74 us
  transfers between devices with their start and end apart: 12 -> 33, of which waited for: 8 -> 15; matrix products, arithmetic and copies ran while one was open for 8% -> 4% of each run, Pallas kernels for 0% -> 2%
where the time goes in v1:
time: 102 us; the launch traced here: 101 us
  waiting for transfers between devices  46.3 us (45%)
  starting transfers between devices  30.7 us (30%)
  Pallas kernels  11.6 us (11%)
  local copies, waits for them, and re-layouts  8.71 us (9%)
  matrix products  2.95 us (3%)
    ppermute x33, waiting for transfers between devices, swapped(): lax.ppermute(value, axis, [(source, source ^ bit) for source in range(cou...  46.3 us
    ppermute x33, starting transfers between devices, swapped(): lax.ppermute(value, axis, [(source, source ^ bit) for source in range(cou...  30.7 us
    pallas_call x1, Pallas kernels, per_device(): pl.pallas_call(functools.partial(pair_kernel, planes, lanes, rows, cols,...  7.03 us
    unnamed x23, local copies, waits for them, and re-layouts  5.74 us
    dot_general x1, matrix products, per_device(): jnp.dot(teacher, low_weight, preferred_element_type=jnp.float32)  2.95 us
    pallas_call x1, Pallas kernels, per_device(): pl.pallas_call(functools.partial(last_kernel, pieces, rows), out_shape=ja...  2.7 us
  transfers between devices with their start and end apart: 33, of which 15 were waited for; matrix products, arithmetic and copies ran while one was open for 4% of the time, Pallas kernels for 2%

profile of v1, /device:TPU:0, one launch (start us, length us, event | category | flops | bytes accessed | tf_op | source)
XLA Modules:
  0.0 101.4 jit_solution(17843558318225492935)
XLA Ops:
  0.8 3.0 %constant_dynamic-update-slice_fusion.4 = (bf16[576,256]{1,0:T(8,128)(2,1)S(1)}, bf16[128,256]{1,0:T(8,128)(2,1)S(1)}) fusion(bf16[128,4096]{1,0:T(8,128)(2,1)} %param.6, f32[4096,256]{1,0:T(8,128)} %param.7), kind=kOutput, calls=%fused_computation.11 | convolution fusion | flops 269516800 | bytes 5373952 | tf_op jit(solution)/shard_map/dot_general | solution.py:180
  3.7 5.1 %collective-permute-start.17 = (bf16[144,256]{1,0:T(8,128)(2,1)S(1)}, bf16[144,256]{1,0:T(8,128)(2,1)S(1)}, u32[]{:S(2)}, u32[]{:S(2)}) collective-permute-start(bf16[144,256]{1,0:T(8,128)(2,1)S(1)} %pad_maximum_fusion), channel_id=1, source_target_pairs={{0,12},{4,8},{8,4},{12,0},{1,13},{5,9},{9,5},{13,1},{2,14},{6,10},... | collective-permute-start | bytes 221192 | tf_op jit(solution)/shard_map/ppermute | solution.py:19
  9.6 3.8 %collective-permute-start.2 = (bf16[128,1024]{1,0:T(8,128)(2,1)S(1)}, bf16[128,1024]{1,0:T(8,128)(2,1)S(1)}, u32[]{:S(2)}, u32[]{:S(2)}) collective-permute-start(bf16[128,1024]{1,0:T(8,128)(2,1)S(1)} %get-tuple-element.25), channel_id=1, source_target_pairs={{0,12},{4,8},{8,4},{12,0},{1,13},{5,9},{9,5},{13,1},{2,14},{6,10},... | collective-permute-start | bytes 786440 | tf_op jit(solution)/shard_map/ppermute | solution.py:19
  13.4 1.2 %collective-permute-done.15 = bf16[144,256]{1,0:T(8,128)(2,1)S(1)} collective-permute-done((bf16[144,256]{1,0:T(8,128)(2,1)S(1)}, bf16[144,256]{1,0:T(8,128)(2,1)S(1)}, u32[]{:S(2)}, u32[]{:S(2)}) %collective-permute-start.15) | collective-permute-done | bytes 73760 | tf_op jit(solution)/shard_map/ppermute | solution.py:19
  14.6 2.5 %collective-permute-start = (bf16[128,1024]{1,0:T(8,128)(2,1)S(1)}, bf16[128,1024]{1,0:T(8,128)(2,1)S(1)}, u32[]{:S(2)}, u32[]{:S(2)}) collective-permute-start(bf16[128,1024]{1,0:T(8,128)(2,1)S(1)} %get-tuple-element.27), channel_id=1, source_target_pairs={{0,4},{4,0},{8,12},{12,8},{1,5},{5,1},{9,13},{13,9},{2,6},{6,2},{1... | collective-permute-start | bytes 786440 | tf_op jit(solution)/shard_map/ppermute | solution.py:19
  17.1 9.2 %collective-permute-done.16 = bf16[144,256]{1,0:T(8,128)(2,1)S(1)} collective-permute-done((bf16[144,256]{1,0:T(8,128)(2,1)S(1)}, bf16[144,256]{1,0:T(8,128)(2,1)S(1)}, u32[]{:S(2)}, u32[]{:S(2)}) %collective-permute-start.16) | collective-permute-done | bytes 73760 | tf_op jit(solution)/shard_map/ppermute | solution.py:19
  26.3 1.1 %collective-permute-start.7 = (bf16[128,1024]{1,0:T(8,128)(2,1)S(1)}, bf16[128,1024]{1,0:T(8,128)(2,1)S(1)}, u32[]{:S(2)}, u32[]{:S(2)}) collective-permute-start(bf16[128,1024]{1,0:T(8,128)(2,1)S(1)} %get-tuple-element.28.refs_0_.refs_1_), channel_id=1, source_target_pairs={{0,2},{1,3},{2,0},{3,1},{4,6},{5,7},{6,4},{7,5},{8,10},{9,11},{10,... | collective-permute-start | bytes 786440 | tf_op jit(solution)/shard_map/ppermute | solution.py:19
  27.4 1.0 %collective-permute-start.19 = (bf16[576,256]{1,0:T(8,128)(2,1)S(1)}, bf16[576,256]{1,0:T(8,128)(2,1)}, u32[]{:S(2)}, u32[]{:S(2)}) collective-permute-start(bf16[576,256]{1,0:T(8,128)(2,1)S(1)} %constant_dynamic-update-slice_fusion.refs_17_), channel_id=1, source_target_pairs={{0,2},{1,3},{2,0},{3,1},{4,6},{5,7},{6,4},{7,5},{8,10},{9,11},{10,... | collective-permute-start | bytes 884744 | tf_op jit(solution)/shard_map/ppermute | solution.py:19
  28.5 9.1 %collective-permute-done.1.refs_2_.refs_3_ = bf16[128,1024]{1,0:T(8,128)(2,1)S(1)} collective-permute-done((bf16[128,1024]{1,0:T(8,128)(2,1)S(1)}, bf16[128,1024]{1,0:T(8,128)(2,1)S(1)}, u32[]{:S(2)}, u32[]{:S(2)}) %collective-permute-start.1) | collective-permute-done | bytes 262176 | tf_op jit(solution)/shard_map/ppermute | solution.py:19
  38.3 1.5 %collective-permute-start.10 = (bf16[128,1024]{1,0:T(8,128)(2,1)S(1)}, bf16[128,1024]{1,0:T(8,128)(2,1)S(1)}, u32[]{:S(2)}, u32[]{:S(2)}) collective-permute-start(bf16[128,1024]{1,0:T(8,128)(2,1)S(1)} %collective-permute-done.2.refs_3_.refs_4_), channel_id=1, source_target_pairs={{0,2},{1,3},{2,0},{3,1},{4,6},{5,7},{6,4},{7,5},{8,10},{9,11},{10,... | collective-permute-start | bytes 786440 | tf_op jit(solution)/shard_map/ppermute | solution.py:19
  41.4 1.5 %collective-permute-start.8 = (bf16[128,1024]{1,0:T(8,128)(2,1)S(1)}, bf16[128,1024]{1,0:T(8,128)(2,1)S(1)}, u32[]{:S(2)}, u32[]{:S(2)}) collective-permute-start(bf16[128,1024]{1,0:T(8,128)(2,1)S(1)} %collective-permute-done.refs_1_.refs_2_), channel_id=1, source_target_pairs={{0,2},{1,3},{2,0},{3,1},{4,6},{5,7},{6,4},{7,5},{8,10},{9,11},{10,... | collective-permute-start | bytes 786440 | tf_op jit(solution)/shard_map/ppermute | solution.py:19
  42.9 4.5 %collective-permute-done.10.refs_11_.refs_12_ = bf16[128,1024]{1,0:T(8,128)(2,1)S(1)} collective-permute-done((bf16[128,1024]{1,0:T(8,128)(2,1)S(1)}, bf16[128,1024]{1,0:T(8,128)(2,1)S(1)}, u32[]{:S(2)}, u32[]{:S(2)}) %collective-permute-start.10) | collective-permute-done | bytes 262176 | tf_op jit(solution)/shard_map/ppermute | solution.py:19
  49.3 3.7 %collective-permute-done.9.refs_10_.refs_11_ = bf16[128,1024]{1,0:T(8,128)(2,1)S(1)} collective-permute-done((bf16[128,1024]{1,0:T(8,128)(2,1)S(1)}, bf16[128,1024]{1,0:T(8,128)(2,1)S(1)}, u32[]{:S(2)}, u32[]{:S(2)}) %collective-permute-start.9) | collective-permute-done | bytes 262176 | tf_op jit(solution)/shard_map/ppermute | solution.py:19
  53.5 4.7 %collective-permute-done.8.refs_9_.refs_10_ = bf16[128,1024]{1,0:T(8,128)(2,1)S(1)} collective-permute-done((bf16[128,1024]{1,0:T(8,128)(2,1)S(1)}, bf16[128,1024]{1,0:T(8,128)(2,1)S(1)}, u32[]{:S(2)}, u32[]{:S(2)}) %collective-permute-start.8) | collective-permute-done | bytes 262176 | tf_op jit(solution)/shard_map/ppermute | solution.py:19
  59.0 0.9 collective-permute-done.13.refs_14_.refs_15_
  60.3 1.0 copy-done.3
  61.2 1.0 copy-done.5
  62.2 7.0 %pairs.1 = (f32[128,256]{1,0:T(8,128)S(1)}, bf16[128,256]{1,0:T(8,128)(2,1)S(1)}, bf16[128,256]{1,0:T(8,128)(2,1)S(1)}, bf16[128,256]{1,0:T(8,128)(2,1)S(1)}) custom-call(f32[4,512]{1,0:T(4,128)S(1)} %bitcast.17, bf16[128,1024]{1,0:T(8,128)(2,1)S(1)} %get-tuple-element.28.refs_0_.refs_1_, bf16[128,1024]{1,0:T(8,128)(2,1)S(1)} %collective-permute-done.refs_1_.refs_2_, ...), custom_call_target="tpu_custom_call" | custom-call | flops 2684354560 | bytes 5242880 | tf_op jit(solution)/shard_map/pairs/pallas_call | solution.py:193
  69.3 3.3 %collective-permute-start.22 = (bf16[128,256]{1,0:T(8,128)(2,1)S(1)}, bf16[128,256]{1,0:T(8,128)(2,1)S(1)}, u32[]{:S(2)}, u32[]{:S(2)}) collective-permute-start(bf16[128,256]{1,0:T(8,128)(2,1)S(1)} %get-tuple-element.23), channel_id=1, source_target_pairs={{0,8},{4,12},{8,0},{12,4},{1,9},{5,13},{9,1},{13,5},{2,10},{6,14},... | collective-permute-start | bytes 196616 | tf_op jit(solution)/shard_map/ppermute | solution.py:19
  72.6 1.1 %collective-permute-start.23 = (bf16[128,256]{1,0:T(8,128)(2,1)S(1)}, bf16[128,256]{1,0:T(8,128)(2,1)S(1)}, u32[]{:S(2)}, u32[]{:S(2)}) collective-permute-start(bf16[128,256]{1,0:T(8,128)(2,1)S(1)} %get-tuple-element.24), channel_id=1, source_target_pairs={{0,12},{4,8},{8,4},{12,0},{1,13},{5,9},{9,5},{13,1},{2,14},{6,10},... | collective-permute-start | bytes 196616 | tf_op jit(solution)/shard_map/ppermute | solution.py:19
  74.4 3.1 %collective-permute-done.22 = bf16[128,256]{1,0:T(8,128)(2,1)S(1)} collective-permute-done((bf16[128,256]{1,0:T(8,128)(2,1)S(1)}, bf16[128,256]{1,0:T(8,128)(2,1)S(1)}, u32[]{:S(2)}, u32[]{:S(2)}) %collective-permute-start.22) | collective-permute-done | bytes 65568 | tf_op jit(solution)/shard_map/ppermute | solution.py:19
  77.5 1.3 %collective-permute-done.23 = bf16[128,256]{1,0:T(8,128)(2,1)S(1)} collective-permute-done((bf16[128,256]{1,0:T(8,128)(2,1)S(1)}, bf16[128,256]{1,0:T(8,128)(2,1)S(1)}, u32[]{:S(2)}, u32[]{:S(2)}) %collective-permute-start.23) | collective-permute-done | bytes 65568 | tf_op jit(solution)/shard_map/ppermute | solution.py:19
  78.8 0.9 collective-permute-start.24
  79.7 2.3 %collective-permute-start.26 = (bf16[128,256]{1,0:T(8,128)(2,1)S(1)}, bf16[128,256]{1,0:T(8,128)(2,1)S(1)}, u32[]{:S(2)}, u32[]{:S(2)}) collective-permute-start(bf16[128,256]{1,0:T(8,128)(2,1)S(1)} %multiply_convert_fusion.refs_1_), channel_id=1, source_target_pairs={{0,12},{4,8},{8,4},{12,0},{1,13},{5,9},{9,5},{13,1},{2,14},{6,10},... | collective-permute-start | bytes 196616 | tf_op jit(solution)/shard_map/ppermute | solution.py:19
  82.3 1.5 %collective-permute-done.24.refs_2_ = bf16[128,256]{1,0:T(8,128)(2,1)S(1)} collective-permute-done((bf16[128,256]{1,0:T(8,128)(2,1)S(1)}, bf16[128,256]{1,0:T(8,128)(2,1)S(1)}, u32[]{:S(2)}, u32[]{:S(2)}) %collective-permute-start.24) | collective-permute-done | bytes 65568 | tf_op jit(solution)/shard_map/ppermute | solution.py:19
  84.5 3.3 %collective-permute-done.25.refs_3_ = bf16[128,256]{1,0:T(8,128)(2,1)S(1)} collective-permute-done((bf16[128,256]{1,0:T(8,128)(2,1)S(1)}, bf16[128,256]{1,0:T(8,128)(2,1)S(1)}, u32[]{:S(2)}, u32[]{:S(2)}) %collective-permute-start.25) | collective-permute-done | bytes 65568 | tf_op jit(solution)/shard_map/ppermute | solution.py:19
  89.0 1.5 %collective-permute-start.30 = (bf16[384,256]{1,0:T(8,128)(2,1)}, bf16[384,256]{1,0:T(8,128)(2,1)}, u32[]{:S(2)}, u32[]{:S(2)}) collective-permute-start(bf16[384,256]{1,0:T(8,128)(2,1)} %constant_dynamic-update-slice_fusion.5), channel_id=1, source_target_pairs={{0,2},{1,3},{2,0},{3,1},{4,6},{5,7},{6,4},{7,5},{8,10},{9,11},{10,... | collective-permute-start | bytes 589832 | tf_op jit(solution)/shard_map/ppermute | solution.py:19
  91.1 0.9 copy-done.1
  92.0 1.8 %keep.1.refs_0_ = bf16[256,2048]{1,0:T(8,128)(2,1)S(1)} custom-call(s32[1]{0:T(128)} %bitcast.lane, bf16[128,1024]{1,0:T(8,128)(2,1)S(1)} %get-tuple-element.28.refs_0_.refs_1_, bf16[128,1024]{1,0:T(8,128)(2,1)S(1)} %collective-permute-done.refs_1_.refs_2_, bf16[128,1024]{1,0:T(8,128)(2,1)S(1)} %collective-permute-done.1.refs_2_.refs_3_, ...), custom_call_target="tpu_custom_call" | custom-call | bytes 5242880 | tf_op jit(solution)/shard_map/keep/pallas_call | solution.py:219
  94.5 2.5 %collective-permute-done.29.refs_9_ = bf16[128,256]{1,0:T(8,128)(2,1)S(1)} collective-permute-done((bf16[128,256]{1,0:T(8,128)(2,1)S(1)}, bf16[128,256]{1,0:T(8,128)(2,1)S(1)}, u32[]{:S(2)}, u32[]{:S(2)}) %collective-permute-start.29) | collective-permute-done | bytes 65568 | tf_op jit(solution)/shard_map/ppermute | solution.py:19
  97.4 0.9 fusion.8
  98.7 2.7 %last.1 = f32[256,256]{1,0:T(8,128)} custom-call(bf16[256,2048]{1,0:T(8,128)(2,1)S(1)} %keep.1.refs_0_, bf16[128,256]{1,0:T(8,128)(2,1)S(1)} %multiply_convert_fusion.refs_1_, bf16[128,256]{1,0:T(8,128)(2,1)S(1)} %collective-permute-done.24.refs_2_, bf16[128,256]{1,0:T(8,128)(2,1)S(1)} %collective-permute-done.25.refs_3_, ...), custom_call_target="tpu_custom_call" | custom-call | flops 268435456 | bytes 2097152 | tf_op jit(solution)/shard_map/last/pallas_call | solution.py:248
  (81 shorter events, 12.5 us)
Async XLA Ops:
  3.7 23.6 %collective-permute-start.17 = (bf16[144,256]{1,0:T(8,128)(2,1)S(1)}, bf16[144,256]{1,0:T(8,128)(2,1)S(1)}, u32[]{:S(2)}, u32[]{:S(2)}) collective-permute-start(bf16[144,256]{1,0:T(8,128)(2,1)S(1)} %pad_maximum_fusion), channel_id=1, source_target_pairs={{0,12},{4,8},{8,4},{12,0},{1,13},{5,9},{9,5},{13,1},{2,14},{6,10},... | collective-permute-start | bytes 221192 | tf_op jit(solution)/shard_map/ppermute | solution.py:19
  8.9 17.4 %collective-permute-start.16 = (bf16[144,256]{1,0:T(8,128)(2,1)S(1)}, bf16[144,256]{1,0:T(8,128)(2,1)S(1)}, u32[]{:S(2)}, u32[]{:S(2)}) collective-permute-start(bf16[144,256]{1,0:T(8,128)(2,1)S(1)} %pad_maximum_fusion), channel_id=1, source_target_pairs={{0,8},{4,12},{8,0},{12,4},{1,9},{5,13},{9,1},{13,5},{2,10},{6,14},... | collective-permute-start | bytes 221192 | tf_op jit(solution)/shard_map/ppermute | solution.py:19
  8.9 5.7 %collective-permute-start.15 = (bf16[144,256]{1,0:T(8,128)(2,1)S(1)}, bf16[144,256]{1,0:T(8,128)(2,1)S(1)}, u32[]{:S(2)}, u32[]{:S(2)}) collective-permute-start(bf16[144,256]{1,0:T(8,128)(2,1)S(1)} %pad_maximum_fusion), channel_id=1, source_target_pairs={{0,4},{4,0},{8,12},{12,8},{1,5},{5,1},{9,13},{13,9},{2,6},{6,2},{1... | collective-permute-start | bytes 221192 | tf_op jit(solution)/shard_map/ppermute | solution.py:19
  9.6 17.8 %collective-permute-start.2 = (bf16[128,1024]{1,0:T(8,128)(2,1)S(1)}, bf16[128,1024]{1,0:T(8,128)(2,1)S(1)}, u32[]{:S(2)}, u32[]{:S(2)}) collective-permute-start(bf16[128,1024]{1,0:T(8,128)(2,1)S(1)} %get-tuple-element.25), channel_id=1, source_target_pairs={{0,12},{4,8},{8,4},{12,0},{1,13},{5,9},{9,5},{13,1},{2,14},{6,10},... | collective-permute-start | bytes 786440 | tf_op jit(solution)/shard_map/ppermute | solution.py:19
  13.4 24.1 %collective-permute-start.1 = (bf16[128,1024]{1,0:T(8,128)(2,1)S(1)}, bf16[128,1024]{1,0:T(8,128)(2,1)S(1)}, u32[]{:S(2)}, u32[]{:S(2)}) collective-permute-start(bf16[128,1024]{1,0:T(8,128)(2,1)S(1)} %get-tuple-element.26), channel_id=1, source_target_pairs={{0,8},{4,12},{8,0},{12,4},{1,9},{5,13},{9,1},{13,5},{2,10},{6,14},... | collective-permute-start | bytes 786440 | tf_op jit(solution)/shard_map/ppermute | solution.py:19
  14.6 23.7 %collective-permute-start = (bf16[128,1024]{1,0:T(8,128)(2,1)S(1)}, bf16[128,1024]{1,0:T(8,128)(2,1)S(1)}, u32[]{:S(2)}, u32[]{:S(2)}) collective-permute-start(bf16[128,1024]{1,0:T(8,128)(2,1)S(1)} %get-tuple-element.27), channel_id=1, source_target_pairs={{0,4},{4,0},{8,12},{12,8},{1,5},{5,1},{9,13},{13,9},{2,6},{6,2},{1... | collective-permute-start | bytes 786440 | tf_op jit(solution)/shard_map/ppermute | solution.py:19
  26.3 13.6 %collective-permute-start.7 = (bf16[128,1024]{1,0:T(8,128)(2,1)S(1)}, bf16[128,1024]{1,0:T(8,128)(2,1)S(1)}, u32[]{:S(2)}, u32[]{:S(2)}) collective-permute-start(bf16[128,1024]{1,0:T(8,128)(2,1)S(1)} %get-tuple-element.28.refs_0_.refs_1_), channel_id=1, source_target_pairs={{0,2},{1,3},{2,0},{3,1},{4,6},{5,7},{6,4},{7,5},{8,10},{9,11},{10,... | collective-permute-start | bytes 786440 | tf_op jit(solution)/shard_map/ppermute | solution.py:19
  27.3 12.8 %collective-permute-start.3 = (bf16[128,1024]{1,0:T(8,128)(2,1)S(1)}, bf16[128,1024]{1,0:T(8,128)(2,1)S(1)}, u32[]{:S(2)}, u32[]{:S(2)}) collective-permute-start(bf16[128,1024]{1,0:T(8,128)(2,1)S(1)} %get-tuple-element.28.refs_0_.refs_1_), channel_id=1, source_target_pairs={{0,1},{1,0},{2,3},{3,2},{4,5},{5,4},{6,7},{7,6},{8,9},{9,8},{10,11... | collective-permute-start | bytes 786440 | tf_op jit(solution)/shard_map/ppermute | solution.py:19
  27.4 13.3 %collective-permute-start.19 = (bf16[576,256]{1,0:T(8,128)(2,1)S(1)}, bf16[576,256]{1,0:T(8,128)(2,1)}, u32[]{:S(2)}, u32[]{:S(2)}) collective-permute-start(bf16[576,256]{1,0:T(8,128)(2,1)S(1)} %constant_dynamic-update-slice_fusion.refs_17_), channel_id=1, source_target_pairs={{0,2},{1,3},{2,0},{3,1},{4,6},{5,7},{6,4},{7,5},{8,10},{9,11},{10,... | collective-permute-start | bytes 884744 | tf_op jit(solution)/shard_map/ppermute | solution.py:19
  37.5 3.2 %collective-permute-start.18 = (bf16[576,256]{1,0:T(8,128)(2,1)S(1)}, bf16[576,256]{1,0:T(8,128)(2,1)S(1)}, u32[]{:S(2)}, u32[]{:S(2)}) collective-permute-start(bf16[576,256]{1,0:T(8,128)(2,1)S(1)} %constant_dynamic-update-slice_fusion.refs_17_), channel_id=1, source_target_pairs={{0,1},{1,0},{2,3},{3,2},{4,5},{5,4},{6,7},{7,6},{8,9},{9,8},{10,11... | collective-permute-start | bytes 884744 | tf_op jit(solution)/shard_map/ppermute | solution.py:19
  38.3 9.1 %collective-permute-start.10 = (bf16[128,1024]{1,0:T(8,128)(2,1)S(1)}, bf16[128,1024]{1,0:T(8,128)(2,1)S(1)}, u32[]{:S(2)}, u32[]{:S(2)}) collective-permute-start(bf16[128,1024]{1,0:T(8,128)(2,1)S(1)} %collective-permute-done.2.refs_3_.refs_4_), channel_id=1, source_target_pairs={{0,2},{1,3},{2,0},{3,1},{4,6},{5,7},{6,4},{7,5},{8,10},{9,11},{10,... | collective-permute-start | bytes 786440 | tf_op jit(solution)/shard_map/ppermute | solution.py:19
  39.9 8.8 %collective-permute-start.6 = (bf16[128,1024]{1,0:T(8,128)(2,1)S(1)}, bf16[128,1024]{1,0:T(8,128)(2,1)S(1)}, u32[]{:S(2)}, u32[]{:S(2)}) collective-permute-start(bf16[128,1024]{1,0:T(8,128)(2,1)S(1)} %collective-permute-done.2.refs_3_.refs_4_), channel_id=1, source_target_pairs={{0,1},{1,0},{2,3},{3,2},{4,5},{5,4},{6,7},{7,6},{8,9},{9,8},{10,11... | collective-permute-start | bytes 786440 | tf_op jit(solution)/shard_map/ppermute | solution.py:19
  40.2 12.8 %collective-permute-start.9 = (bf16[128,1024]{1,0:T(8,128)(2,1)S(1)}, bf16[128,1024]{1,0:T(8,128)(2,1)S(1)}, u32[]{:S(2)}, u32[]{:S(2)}) collective-permute-start(bf16[128,1024]{1,0:T(8,128)(2,1)S(1)} %collective-permute-done.1.refs_2_.refs_3_), channel_id=1, source_target_pairs={{0,2},{1,3},{2,0},{3,1},{4,6},{5,7},{6,4},{7,5},{8,10},{9,11},{10,... | collective-permute-start | bytes 786440 | tf_op jit(solution)/shard_map/ppermute | solution.py:19
  40.7 12.3 %collective-permute-start.5 = (bf16[128,1024]{1,0:T(8,128)(2,1)S(1)}, bf16[128,1024]{1,0:T(8,128)(2,1)S(1)}, u32[]{:S(2)}, u32[]{:S(2)}) collective-permute-start(bf16[128,1024]{1,0:T(8,128)(2,1)S(1)} %collective-permute-done.1.refs_2_.refs_3_), channel_id=1, source_target_pairs={{0,1},{1,0},{2,3},{3,2},{4,5},{5,4},{6,7},{7,6},{8,9},{9,8},{10,11... | collective-permute-start | bytes 786440 | tf_op jit(solution)/shard_map/ppermute | solution.py:19
  41.4 16.8 %collective-permute-start.8 = (bf16[128,1024]{1,0:T(8,128)(2,1)S(1)}, bf16[128,1024]{1,0:T(8,128)(2,1)S(1)}, u32[]{:S(2)}, u32[]{:S(2)}) collective-permute-start(bf16[128,1024]{1,0:T(8,128)(2,1)S(1)} %collective-permute-done.refs_1_.refs_2_), channel_id=1, source_target_pairs={{0,2},{1,3},{2,0},{3,1},{4,6},{5,7},{6,4},{7,5},{8,10},{9,11},{10,... | collective-permute-start | bytes 786440 | tf_op jit(solution)/shard_map/ppermute | solution.py:19
  47.4 10.9 %collective-permute-start.4 = (bf16[128,1024]{1,0:T(8,128)(2,1)S(1)}, bf16[128,1024]{1,0:T(8,128)(2,1)S(1)}, u32[]{:S(2)}, u32[]{:S(2)}) collective-permute-start(bf16[128,1024]{1,0:T(8,128)(2,1)S(1)} %collective-permute-done.refs_1_.refs_2_), channel_id=1, source_target_pairs={{0,1},{1,0},{2,3},{3,2},{4,5},{5,4},{6,7},{7,6},{8,9},{9,8},{10,11... | collective-permute-start | bytes 786440 | tf_op jit(solution)/shard_map/ppermute | solution.py:19
  48.7 10.3 %collective-permute-start.11 = (bf16[128,1024]{1,0:T(8,128)(2,1)S(1)}, bf16[128,1024]{1,0:T(8,128)(2,1)S(1)}, u32[]{:S(2)}, u32[]{:S(2)}) collective-permute-start(bf16[128,1024]{1,0:T(8,128)(2,1)S(1)} %collective-permute-done.7.refs_8_.refs_9_), channel_id=1, source_target_pairs={{0,1},{1,0},{2,3},{3,2},{4,5},{5,4},{6,7},{7,6},{8,9},{9,8},{10,11... | collective-permute-start | bytes 786440 | tf_op jit(solution)/shard_map/ppermute | solution.py:19
  53.0 6.0 %collective-permute-start.20 = (bf16[576,256]{1,0:T(8,128)(2,1)}, bf16[576,256]{1,0:T(8,128)(2,1)}, u32[]{:S(2)}, u32[]{:S(2)}) collective-permute-start(bf16[576,256]{1,0:T(8,128)(2,1)} %collective-permute-done.19.refs_19_), channel_id=1, source_target_pairs={{0,1},{1,0},{2,3},{3,2},{4,5},{5,4},{6,7},{7,6},{8,9},{9,8},{10,11... | collective-permute-start | bytes 884744 | tf_op jit(solution)/shard_map/ppermute | solution.py:19
  53.0 6.0 %collective-permute-start.14 = (bf16[128,1024]{1,0:T(8,128)(2,1)S(1)}, bf16[128,1024]{1,0:T(8,128)(2,1)}, u32[]{:S(2)}, u32[]{:S(2)}) collective-permute-start(bf16[128,1024]{1,0:T(8,128)(2,1)S(1)} %collective-permute-done.10.refs_11_.refs_12_), channel_id=1, source_target_pairs={{0,1},{1,0},{2,3},{3,2},{4,5},{5,4},{6,7},{7,6},{8,9},{9,8},{10,11... | collective-permute-start | bytes 786440 | tf_op jit(solution)/shard_map/ppermute | solution.py:19
  58.2 2.0 %collective-permute-start.12 = (bf16[128,1024]{1,0:T(8,128)(2,1)S(1)}, bf16[128,1024]{1,0:T(8,128)(2,1)}, u32[]{:S(2)}, u32[]{:S(2)}) collective-permute-start(bf16[128,1024]{1,0:T(8,128)(2,1)S(1)} %collective-permute-done.8.refs_9_.refs_10_), channel_id=1, source_target_pairs={{0,1},{1,0},{2,3},{3,2},{4,5},{5,4},{6,7},{7,6},{8,9},{9,8},{10,11... | collective-permute-start | bytes 786440 | tf_op jit(solution)/shard_map/ppermute | solution.py:19
  69.2 5.1 %collective-permute-start.21 = (bf16[128,256]{1,0:T(8,128)(2,1)S(1)}, bf16[128,256]{1,0:T(8,128)(2,1)S(1)}, u32[]{:S(2)}, u32[]{:S(2)}) collective-permute-start(bf16[128,256]{1,0:T(8,128)(2,1)S(1)} %get-tuple-element.22), channel_id=1, source_target_pairs={{0,4},{4,0},{8,12},{12,8},{1,5},{5,1},{9,13},{13,9},{2,6},{6,2},{1... | collective-permute-start | bytes 196616 | tf_op jit(solution)/shard_map/ppermute | solution.py:19
  69.3 8.1 %collective-permute-start.22 = (bf16[128,256]{1,0:T(8,128)(2,1)S(1)}, bf16[128,256]{1,0:T(8,128)(2,1)S(1)}, u32[]{:S(2)}, u32[]{:S(2)}) collective-permute-start(bf16[128,256]{1,0:T(8,128)(2,1)S(1)} %get-tuple-element.23), channel_id=1, source_target_pairs={{0,8},{4,12},{8,0},{12,4},{1,9},{5,13},{9,1},{13,5},{2,10},{6,14},... | collective-permute-start | bytes 196616 | tf_op jit(solution)/shard_map/ppermute | solution.py:19
  72.6 6.2 %collective-permute-start.23 = (bf16[128,256]{1,0:T(8,128)(2,1)S(1)}, bf16[128,256]{1,0:T(8,128)(2,1)S(1)}, u32[]{:S(2)}, u32[]{:S(2)}) collective-permute-start(bf16[128,256]{1,0:T(8,128)(2,1)S(1)} %get-tuple-element.24), channel_id=1, source_target_pairs={{0,12},{4,8},{8,4},{12,0},{1,13},{5,9},{9,5},{13,1},{2,14},{6,10},... | collective-permute-start | bytes 196616 | tf_op jit(solution)/shard_map/ppermute | solution.py:19
  78.8 5.0 %collective-permute-start.24 = (bf16[128,256]{1,0:T(8,128)(2,1)S(1)}, bf16[128,256]{1,0:T(8,128)(2,1)S(1)}, u32[]{:S(2)}, u32[]{:S(2)}) collective-permute-start(bf16[128,256]{1,0:T(8,128)(2,1)S(1)} %multiply_convert_fusion.refs_1_), channel_id=1, source_target_pairs={{0,4},{4,0},{8,12},{12,8},{1,5},{5,1},{9,13},{13,9},{2,6},{6,2},{1... | collective-permute-start | bytes 196616 | tf_op jit(solution)/shard_map/ppermute | solution.py:19
  79.7 8.7 %collective-permute-start.26 = (bf16[128,256]{1,0:T(8,128)(2,1)S(1)}, bf16[128,256]{1,0:T(8,128)(2,1)S(1)}, u32[]{:S(2)}, u32[]{:S(2)}) collective-permute-start(bf16[128,256]{1,0:T(8,128)(2,1)S(1)} %multiply_convert_fusion.refs_1_), channel_id=1, source_target_pairs={{0,12},{4,8},{8,4},{12,0},{1,13},{5,9},{9,5},{13,1},{2,14},{6,10},... | collective-permute-start | bytes 196616 | tf_op jit(solution)/shard_map/ppermute | solution.py:19
  82.0 5.8 %collective-permute-start.25 = (bf16[128,256]{1,0:T(8,128)(2,1)S(1)}, bf16[128,256]{1,0:T(8,128)(2,1)S(1)}, u32[]{:S(2)}, u32[]{:S(2)}) collective-permute-start(bf16[128,256]{1,0:T(8,128)(2,1)S(1)} %multiply_convert_fusion.refs_1_), channel_id=1, source_target_pairs={{0,8},{4,12},{8,0},{12,4},{1,9},{5,13},{9,1},{13,5},{2,10},{6,14},... | collective-permute-start | bytes 196616 | tf_op jit(solution)/shard_map/ppermute | solution.py:19
  89.0 7.9 %collective-permute-start.30 = (bf16[384,256]{1,0:T(8,128)(2,1)}, bf16[384,256]{1,0:T(8,128)(2,1)}, u32[]{:S(2)}, u32[]{:S(2)}) collective-permute-start(bf16[384,256]{1,0:T(8,128)(2,1)} %constant_dynamic-update-slice_fusion.5), channel_id=1, source_target_pairs={{0,2},{1,3},{2,0},{3,1},{4,6},{5,7},{6,4},{7,5},{8,10},{9,11},{10,... | collective-permute-start | bytes 589832 | tf_op jit(solution)/shard_map/ppermute | solution.py:19
  90.5 6.4 %collective-permute-start.29 = (bf16[128,256]{1,0:T(8,128)(2,1)S(1)}, bf16[128,256]{1,0:T(8,128)(2,1)S(1)}, u32[]{:S(2)}, u32[]{:S(2)}) collective-permute-start(bf16[128,256]{1,0:T(8,128)(2,1)S(1)} %multiply_convert_fusion.refs_1_), channel_id=1, source_target_pairs={{0,2},{1,3},{2,0},{3,1},{4,6},{5,7},{6,4},{7,5},{8,10},{9,11},{10,... | collective-permute-start | bytes 196616 | tf_op jit(solution)/shard_map/ppermute | solution.py:19
  93.9 4.9 %collective-permute-start.27 = (bf16[128,256]{1,0:T(8,128)(2,1)S(1)}, bf16[128,256]{1,0:T(8,128)(2,1)S(1)}, u32[]{:S(2)}, u32[]{:S(2)}) collective-permute-start(bf16[128,256]{1,0:T(8,128)(2,1)S(1)} %multiply_convert_fusion.refs_1_), channel_id=1, source_target_pairs={{0,1},{1,0},{2,3},{3,2},{4,5},{5,4},{6,7},{7,6},{8,9},{9,8},{10,11... | collective-permute-start | bytes 196616 | tf_op jit(solution)/shard_map/ppermute | solution.py:19
  94.0 4.4 %collective-permute-start.28 = (bf16[384,256]{1,0:T(8,128)(2,1)}, bf16[384,256]{1,0:T(8,128)(2,1)S(1)}, u32[]{:S(2)}, u32[]{:S(2)}) collective-permute-start(bf16[384,256]{1,0:T(8,128)(2,1)} %constant_dynamic-update-slice_fusion.5), channel_id=1, source_target_pairs={{0,1},{1,0},{2,3},{3,2},{4,5},{5,4},{6,7},{7,6},{8,9},{9,8},{10,11... | collective-permute-start | bytes 589832 | tf_op jit(solution)/shard_map/ppermute | solution.py:19
  96.9 1.8 %collective-permute-start.31 = (bf16[128,256]{1,0:T(8,128)(2,1)S(1)}, bf16[128,256]{1,0:T(8,128)(2,1)S(1)}, u32[]{:S(2)}, u32[]{:S(2)}) collective-permute-start(bf16[128,256]{1,0:T(8,128)(2,1)S(1)} %collective-permute-done.29.refs_9_), channel_id=1, source_target_pairs={{0,1},{1,0},{2,3},{3,2},{4,5},{5,4},{6,7},{7,6},{8,9},{9,8},{10,11... | collective-permute-start | bytes 196616 | tf_op jit(solution)/shard_map/ppermute | solution.py:19
  96.9 1.8 %collective-permute-start.32 = (bf16[384,256]{1,0:T(8,128)(2,1)}, bf16[384,256]{1,0:T(8,128)(2,1)S(1)}, u32[]{:S(2)}, u32[]{:S(2)}) collective-permute-start(bf16[384,256]{1,0:T(8,128)(2,1)} %collective-permute-done.30), channel_id=1, source_target_pairs={{0,1},{1,0},{2,3},{3,2},{4,5},{5,4},{6,7},{7,6},{8,9},{9,8},{10,11... | collective-permute-start | bytes 589832 | tf_op jit(solution)/shard_map/ppermute | solution.py:19
  (9 other events, 65.5 us)

commit v2 on v1

v2 whole, which is shorter than its diff:
```python
import functools

import jax
import jax.numpy as jnp
from jax import lax
from jax.experimental import pallas as pl
from jax.experimental.pallas import tpu as pltpu
from jax.sharding import PartitionSpec as P

ANY = pl.BlockSpec(memory_space=pl.ANY)
VMEM = pl.BlockSpec(memory_space=pltpu.VMEM)
SMEM = pl.BlockSpec(memory_space=pltpu.SMEM)
MIB = 1024 * 1024
EXTRA = 16
FAR, CORE = 2, 1


def swapped(value, axis, bit):
    count = lax.axis_size(axis)
    return lax.ppermute(value, axis, [(source, source ^ bit) for source in range(count)])


def after(value, *others):
    return lax.optimization_barrier((value, *others))[0]


def vmem_room(held):
    return held + 14 * MIB


def cost(flops, moved):
    return pl.CostEstimate(flops=flops, bytes_accessed=moved, transcendentals=0)


def nt(a, b):
    return lax.dot_general(a, b, (((1,), (1,)), ((), ())), preferred_element_type=jnp.float32)


def loop(count, body):
    if count <= 4:
        for step in range(count):
            body(step)
    else:
        lax.fori_loop(0, count, lambda step, carry: (body(step), carry)[1], 0)


def student_kernel(steps, teacher, weight, group, packed, t_all, w_all, t_sem, w_sem):
    rows, width = teacher.shape
    out = weight.shape[1]
    depth = width // steps

    def w_copy(step):
        part = pl.ds(step * depth, depth)
        return pltpu.make_async_copy(weight.at[part], w_all.at[part], w_sem.at[step])

    def t_copy(step):
        part = pl.ds(step * depth, depth)
        return pltpu.make_async_copy(teacher.at[:, part], t_all.at[:, part], t_sem.at[step])

    for step in range(steps):
        t_copy(step).start()
        w_copy(step).start()
    line = jnp.broadcast_to(group[...].astype(jnp.float32), (EXTRA, rows))
    packed[rows:, :rows] = line.astype(jnp.bfloat16)
    total = jnp.zeros((rows, out), jnp.float32)
    for step in range(steps):
        t_copy(step).wait()
        w_copy(step).wait()
        total += jnp.dot(
            t_all[:, step * depth : (step + 1) * depth],
            w_all[step * depth : (step + 1) * depth, :].astype(jnp.bfloat16),
            preferred_element_type=jnp.float32,
        )
    packed[:rows, :] = total.astype(jnp.bfloat16)


def pair_kernel(planes, lanes, rows, out, width, own, mask, place, *refs):
    pieces = planes * lanes
    panel = planes * rows
    prow = rows + EXTRA
    t_in, s_in = refs[:pieces], refs[pieces : pieces + lanes]
    result = refs[pieces + lanes]
    rest = list(refs[pieces + lanes + 1 :])
    t_keep = rest.pop(0) if own else None
    t_all, s_all, g_raw, g_row, g_col, total, t_sem, s_sem, g_sem = rest
    here = place[0]
    lead = 0 if own else FAR

    def t_copy(m, k):
        at = m * planes + k
        return pltpu.make_async_copy(t_in[at], t_all.at[pl.ds(at * rows, rows)], t_sem.at[at])

    def s_copy(m, k):
        at = m * planes + k
        return pltpu.make_async_copy(
            s_in[m].at[pl.ds(k * prow, rows)], s_all.at[pl.ds(at * rows, rows)], s_sem.at[at]
        )

    def g_copy(m, k):
        at = m * planes + k
        return pltpu.make_async_copy(
            s_in[m].at[pl.ds(k * prow + rows, EXTRA)],
            g_raw.at[pl.ds(at * EXTRA, EXTRA)],
            g_sem.at[at],
        )

    order = [lead] + [m for m in range(lanes) if m != lead]
    for m in order:
        for k in range(planes):
            for copy in (g_copy(m, k), t_copy(m, k), s_copy(m, k)):
                copy.start()
    for m in order:
        for k in range(planes):
            at = m * planes + k
            g_copy(m, k).wait()
            line = g_raw[at * EXTRA : (at + 1) * EXTRA, :rows].astype(jnp.float32)[:1]
            g_row[:, at * rows : (at + 1) * rows] = jnp.broadcast_to(line, (8, rows))
            if m == lead:
                g_col[k * rows : (k + 1) * rows, :] = jnp.broadcast_to(line, (128, rows)).T
    total[...] = jnp.zeros_like(total)
    side = min(panel, 512)
    steps = panel // side
    group = side // rows

    for m in order:
        for k in range(planes):
            t_copy(m, k).wait()
            s_copy(m, k).wait()

        def one_row(it, m=m):
            at_i = pl.multiple_of(it * side, side)
            rows_t = t_all[pl.ds(lead * panel + at_i, side), :]
            col = g_col[pl.ds(at_i, side), :]

            def one_tile(jt):
                at_j = pl.multiple_of(m * panel + jt * side, side)
                teach = nt(rows_t, t_all[pl.ds(at_j, side), :]) * (-1.0 / width)
                students = s_all[pl.ds(at_j, side), :]
                line = g_row[:1, pl.ds(at_j, side)]
                same = jnp.concatenate([col] * (side // 128), 1) == line
                terms = []
                for k in range(group):
                    mine = here ^ (it * group + k)
                    weights = []
                    for other in range(group):
                        theirs = here ^ (jt * group + other)
                        both = mask[mine, theirs] + mask[theirs, mine]
                        weights.append(jnp.full((1, rows), both.astype(jnp.float32)))
                    weight = jnp.concatenate(weights, 1)
                    factor = jnp.where(same[k * rows : (k + 1) * rows], 2.0 * weight, weight)
                    error = teach[k * rows : (k + 1) * rows]
                    if own and k == 0:
                        stud = nt(s_all[:rows, :], students) * (1.0 / out)
                        if steps > 1:
                            stud = jnp.where(it == 0, stud, 0.0)
                        error = error + stud
                    terms.append((factor * error).astype(jnp.bfloat16))
                term = jnp.concatenate(terms, 0)
                total[pl.ds(at_i, side), :] += jnp.dot(
                    term, students, preferred_element_type=jnp.float32
                )

            loop(steps, one_tile)

        loop(steps, one_row)
    result[...] = total[...].astype(result.dtype)
    if own:
        keep = t_keep.shape[1]
        for c in range(2):

            @pl.when(place[1] % 2 == c)
            def _(c=c):
                t_keep[...] = t_all[:, c * keep : (c + 1) * keep]


def pair_values_kernel(planes, lanes, rows, out, width, own, mask, place, *refs):
    pieces = planes * lanes
    prow = rows + EXTRA
    t_in, s_in = refs[:pieces], refs[pieces : pieces + lanes]
    result = refs[pieces + lanes]
    here = place[0]
    lead = 0 if own else FAR

    def joined(parts, axis=0):
        return jnp.concatenate(list(parts), axis)

    def panel_of(m):
        return joined(t_in[m * planes + k][...] for k in range(planes))

    def students_of(m):
        return joined(s_in[m][k * prow : k * prow + rows, :] for k in range(planes))

    def groups_of(m, k):
        at = k * prow + rows
        return s_in[m][at : at + EXTRA, :rows].astype(jnp.float32)[:1]

    weights = []
    for k in range(planes):
        scalars = [mask[here ^ k, here ^ j] + mask[here ^ j, here ^ k] for j in range(planes)]
        line = [jnp.full((1, rows), one.astype(jnp.float32) * (-1.0 / width)) for one in scalars]
        weights.append(joined(line, 1))
    column = joined(jnp.broadcast_to(groups_of(lead, k), (128, rows)).T for k in range(planes))
    column = joined([column] * (planes * rows // 128), 1)
    lead_t = panel_of(lead)
    total = jnp.zeros((planes * rows, out), jnp.float32)
    for m in [lead] + [m for m in range(lanes) if m != lead]:
        students = students_of(m)
        teach = nt(lead_t, panel_of(m))
        same = column == joined((groups_of(m, k) for k in range(planes)), 1)
        terms = []
        for k in range(planes):
            error = teach[k * rows : (k + 1) * rows]
            if own and k == 0:
                error = error - nt(s_in[0][:rows, :], students) * (width / out)
            factor = jnp.where(same[k * rows : (k + 1) * rows], 2.0 * weights[k], weights[k])
            terms.append((factor * error).astype(jnp.bfloat16))
        total = total + jnp.dot(joined(terms), students, preferred_element_type=jnp.float32)
    result[...] = total.astype(result.dtype)
    if own:
        t_keep = refs[pieces + lanes + 1]
        keep = t_keep.shape[1]
        for c in range(2):

            @pl.when(place[1] % 2 == c)
            def _(c=c):
                for at in range(pieces):
                    t_keep[at * rows : (at + 1) * rows, :] = t_in[at][:, c * keep : (c + 1) * keep]


def flip_kernel(value, result):
    result[...] = value[...].T


def last_kernel(planes, lanes, rows, t_keep, *refs):
    g_in, result = refs[:4], refs[4]
    total = None
    for at in range(4):
        count = 1 if at < 2 else planes - 1
        for far in range(lanes // 2):
            first = (2 * far + at % 2) * planes + (at >= 2)
            one = jnp.dot(
                t_keep[:, first * rows : (first + count) * rows],
                g_in[at][far * count * rows : (far + 1) * count * rows, :],
                preferred_element_type=jnp.float32,
            )
            total = one if total is None else total + one
    result[...] = total


def per_device(teacher, weight, block_mask, item_group):
    rows, width = teacher.shape
    out = weight.shape[1]
    planes = lax.axis_size("wide")
    lanes = lax.axis_size("narrow")
    plane = lax.axis_index("wide")
    lane = lax.axis_index("narrow")
    cols = width // planes
    part = cols // 2
    keep = cols // lanes
    items = rows * planes * lanes
    panel = rows * planes
    pieces = planes * lanes
    here = jnp.stack([plane, lane]).astype(jnp.int32)
    half = planes // 2

    def cut(k, side):
        start = (plane ^ k) * cols + (lane // 2 ^ side) * part
        return lax.dynamic_slice_in_dim(teacher, start, part, 1)

    mine = [cut(k, 0) for k in range(planes)]
    theirs_far = jnp.concatenate([cut(k, 1) for k in range(half, planes)], 0)
    theirs_near = jnp.concatenate([cut(k, 1) for k in range(half)], 0)
    got_far = swapped(theirs_far, "narrow", FAR)
    got_near = swapped(after(theirs_near, got_far), "narrow", FAR)
    got = [
        (got_near, got_far)[k >= half][k % half * rows : (k % half + 1) * rows] for k in range(planes)
    ]
    first = [mine[0]] + [swapped(mine[k], "wide", k) for k in range(1, planes)]
    second = [got[0]] + [swapped(got[k], "wide", k) for k in range(1, planes)]

    steps = 8
    packed = pl.pallas_call(
        functools.partial(student_kernel, steps),
        out_shape=jax.ShapeDtypeStruct((rows + EXTRA, out), jnp.bfloat16),
        in_specs=[ANY, ANY, VMEM],
        out_specs=VMEM,
        scratch_shapes=[
            pltpu.VMEM((rows, width), jnp.bfloat16),
            pltpu.VMEM((width, out), jnp.float32),
            pltpu.SemaphoreType.DMA((steps,)),
            pltpu.SemaphoreType.DMA((steps,)),
        ],
        compiler_params=pltpu.CompilerParams(vmem_limit_bytes=56 * MIB),
        cost_estimate=cost(2 * rows * width * out, width * (2 * rows + 4 * out)),
        name="student",
    )(after(teacher, theirs_far), weight, item_group.reshape(1, rows))
    s_own = [packed] + [swapped(packed, "wide", k) for k in range(1, planes)]
    s_own = jnp.concatenate(s_own, 0)
    s_far = swapped(s_own, "narrow", FAR)
    s_all = [s_own, swapped(s_own, "narrow", CORE), s_far, swapped(s_far, "narrow", CORE)]

    t_all = [*first, *(swapped(t, "narrow", CORE) for t in first)]
    t_all += [*second, *(swapped(t, "narrow", CORE) for t in second)]

    def pairs(own):
        shapes = [jax.ShapeDtypeStruct((panel, out), jnp.float32 if own else jnp.bfloat16)]
        if own:
            shapes.append(jax.ShapeDtypeStruct((items, keep), jnp.bfloat16))
        held = items * (2 * part + 2 * out) + 4 * panel * out
        if pieces <= 16 and panel <= 512:
            return pl.pallas_call(
                functools.partial(pair_values_kernel, planes, lanes, rows, out, width, own),
                out_shape=shapes,
                in_specs=[SMEM, SMEM] + [VMEM] * (pieces + lanes),
                out_specs=[VMEM] * len(shapes),
                compiler_params=pltpu.CompilerParams(vmem_limit_bytes=vmem_room(held)),
                cost_estimate=cost(2 * panel * items * (part + out), 2 * items * (part + out)),
                name="pairs_own" if own else "pairs_far",
            )(block_mask, here, *t_all, *s_all)
        return pl.pallas_call(
            functools.partial(pair_kernel, planes, lanes, rows, out, width, own),
            out_shape=shapes,
            in_specs=[SMEM, SMEM] + [ANY] * (pieces + lanes),
            out_specs=[VMEM] * len(shapes),
            scratch_shapes=[
                pltpu.VMEM((items, part), jnp.bfloat16),
                pltpu.VMEM((items, out), jnp.bfloat16),
                pltpu.VMEM((pieces * EXTRA, out), jnp.bfloat16),
                pltpu.VMEM((8, items), jnp.float32),
                pltpu.VMEM((panel, 128), jnp.float32),
                pltpu.VMEM((panel, out), jnp.float32),
                pltpu.SemaphoreType.DMA((pieces,)),
                pltpu.SemaphoreType.DMA((pieces,)),
                pltpu.SemaphoreType.DMA((pieces,)),
            ],
            compiler_params=pltpu.CompilerParams(vmem_limit_bytes=vmem_room(held)),
            cost_estimate=cost(2 * panel * items * (part + out), 2 * items * (part + out)),
            name="pairs_own" if own else "pairs_far",
        )(block_mask, here, *t_all, *s_all)

    (far_sum,) = pairs(False)
    far_sum = swapped(far_sum, "narrow", FAR)
    own_sum, t_keep = pairs(True)
    sums = own_sum + far_sum.astype(jnp.float32)
    t_keep = pl.pallas_call(
        flip_kernel,
        out_shape=jax.ShapeDtypeStruct((keep, items), jnp.bfloat16),
        in_specs=[VMEM],
        out_specs=VMEM,
        compiler_params=pltpu.CompilerParams(vmem_limit_bytes=vmem_room(4 * items * keep)),
        cost_estimate=cost(0, 4 * items * keep),
        name="flip",
    )(t_keep)

    grad = after(sums[:rows], t_keep)
    for k in range(1, planes):
        piece = sums[k * rows : (k + 1) * rows].astype(jnp.bfloat16)
        grad = grad + swapped(piece, "wide", k).astype(jnp.float32)
    coef = 2.0 * width / (items * out)
    grad = (grad * coef).astype(jnp.bfloat16)
    g_parts = [swapped(grad, "wide", k) for k in range(1, planes)]
    g_near = jnp.concatenate([grad, swapped(grad, "narrow", FAR)], 0)
    g_rest = after(jnp.concatenate(g_parts, 0), g_near)
    g_rest = jnp.concatenate([g_rest, swapped(g_rest, "narrow", FAR)], 0)
    g_all = [g_near, swapped(g_near, "narrow", CORE), g_rest, swapped(g_rest, "narrow", CORE)]
    return pl.pallas_call(
        functools.partial(last_kernel, planes, lanes, rows),
        out_shape=jax.ShapeDtypeStruct((keep, out), jnp.float32),
        in_specs=[VMEM] * 5,
        out_specs=VMEM,
        compiler_params=pltpu.CompilerParams(vmem_limit_bytes=vmem_room(4 * items * (out + keep))),
        cost_estimate=cost(2 * items * keep * out, 2 * items * (keep + out)),
        name="last",
    )(t_keep, *g_all)


def solution(mesh):
    in_specs = (
        P(("parts", "wide", "narrow"), None),
        P(),
        P("parts", None),
        P(("parts", "wide", "narrow")),
    )
    out_specs = P(("parts", "wide", "narrow"), None)
    return jax.shard_map(
        per_device, mesh=mesh, in_specs=in_specs, out_specs=out_specs, check_vma=False
    )
```

time: 102 us -> 85.5 us (0.84)
  waiting for transfers between devices: 46.3 us -> 38.6 us
  local copies, waits for them, and re-layouts: 8.71 us -> 1.45 us
  matrix products: 2.95 us -> 0 us
  starting transfers between devices: 30.7 us -> 32.3 us
    ppermute x33, waiting for transfers between devices: 46.3 us -> 38.6 us  [swapped(): lax.ppermute(value, axis, [(source, source ^ bit) for source in range(cou...]
    unnamed x23 -> x3, local copies, waits for them, and re-layouts: 5.74 us -> 0.02 us
    dot_general x1 -> x0, matrix products: 2.95 us -> none  [per_device(): jnp.dot(teacher, low_weight, preferred_element_type=jnp.float32)]
    ppermute x33, starting transfers between devices: 30.7 us -> 32.3 us  [swapped(): lax.ppermute(value, axis, [(source, source ^ bit) for source in range(cou...]
    dynamic_slice x1, local copies, waits for them, and re-layouts: 0.08 us -> 1.36 us  [cut(): return lax.dynamic_slice_in_dim(teacher, start, part, 1)]
    gather x2 -> x0, local copies, waits for them, and re-layouts: 1.12 us -> none  [per_device(): sym = jnp.take(jnp.take(sym, order, 0), order, 1)]
    pallas_call x3 -> x5, Pallas kernels: 11.6 us -> 11.6 us  [the longest x2 5.86 us: pairs(): pl.pallas_call(functools.partial(pair_values_kernel, planes, lanes, rows,...]
  transfers between devices with their start and end apart: 33 -> 33, of which waited for: 15 -> 17; matrix products, arithmetic and copies ran while one was open for 4% -> 1% of each run, Pallas kernels for 2% -> 4%
where the time goes in v2:
time: 85.5 us; the launch traced here: 85.3 us
  waiting for transfers between devices  38.6 us (45%)
  starting transfers between devices  32.3 us (38%)
  Pallas kernels  11.6 us (14%)
  local copies, waits for them, and re-layouts  1.45 us (2%)
  other arithmetic  1.15 us (1%)
    ppermute x33, waiting for transfers between devices, swapped(): lax.ppermute(value, axis, [(source, source ^ bit) for source in range(cou...  38.6 us
    ppermute x33, starting transfers between devices, swapped(): lax.ppermute(value, axis, [(source, source ^ bit) for source in range(cou...  32.3 us
    pallas_call x2, Pallas kernels, pairs(): pl.pallas_call(functools.partial(pair_values_kernel, planes, lanes, rows,...  5.86 us
    pallas_call x1, Pallas kernels, per_device(): pl.pallas_call(functools.partial(student_kernel, steps), out_shape=jax.Sh...  4.15 us
  transfers between devices with their start and end apart: 33, of which 17 were waited for; matrix products, arithmetic and copies ran while one was open for 1% of the time, Pallas kernels for 4%

profile of v2, /device:TPU:0, one launch (start us, length us, event | category | flops | bytes accessed | tf_op | source)
XLA Modules:
  0.0 85.3 jit_solution(13349024709287632495)
XLA Ops:
  0.0 1.4 %constant_dynamic-slice_fusion.1 = (bf16[128,512]{1,0:T(8,128)(2,1)S(1)}, bf16[128,512]{1,0:T(8,128)(2,1)S(1)}, bf16[128,512]{1,0:T(8,128)(2,1)S(1)}, bf16[128,5...) fusion(bf16[128,4096]{1,0:T(8,128)(2,1)} %teacher, ...), kind=kLoop, calls=%fused_computation.10 | loop fusion | bytes 2097184 | tf_op jit(solution)/shard_map/dynamic_slice | solution.py:268
  1.4 4.2 %student.1 = bf16[144,256]{1,0:T(8,128)(2,1)} custom-call(bf16[128,4096]{1,0:T(8,128)(2,1)} %teacher, f32[4096,256]{1,0:T(8,128)} %weight.1, s32[1,128]{1,0:T(1,128)} %bitcast.3), custom_call_target="tpu_custom_call" | custom-call | flops 268435456 | bytes 5242880 | tf_op jit(solution)/shard_map/student/pallas_call | solution.py:282
  5.6 5.1 %collective-permute-start.18 = (bf16[144,256]{1,0:T(8,128)(2,1)}, bf16[144,256]{1,0:T(8,128)(2,1)S(1)}, u32[]{:S(2)}, u32[]{:S(2)}) collective-permute-start(bf16[144,256]{1,0:T(8,128)(2,1)} %student.1), channel_id=1, source_target_pairs={{0,12},{4,8},{8,4},{12,0},{1,13},{5,9},{9,5},{13,1},{2,14},{6,10},... | collective-permute-start | bytes 221192 | tf_op jit(solution)/shard_map/ppermute | solution.py:20
  11.3 1.6 %collective-permute-start.7 = (bf16[256,512]{1,0:T(8,128)(2,1)S(1)}, bf16[256,512]{1,0:T(8,128)(2,1)S(1)}, u32[]{:S(2)}, u32[]{:S(2)}) collective-permute-start(bf16[256,512]{1,0:T(8,128)(2,1)S(1)} %pad_maximum_fusion.2), channel_id=1, source_target_pairs={{0,2},{1,3},{2,0},{3,1},{4,6},{5,7},{6,4},{7,5},{8,10},{9,11},{10,... | collective-permute-start | bytes 786440 | tf_op jit(solution)/shard_map/ppermute | solution.py:20
  13.0 3.6 %collective-permute-start.2 = (bf16[128,512]{1,0:T(8,128)(2,1)S(1)}, bf16[128,512]{1,0:T(8,128)(2,1)S(1)}, u32[]{:S(2)}, u32[]{:S(2)}) collective-permute-start(bf16[128,512]{1,0:T(8,128)(2,1)S(1)} %get-tuple-element.22), channel_id=1, source_target_pairs={{0,12},{4,8},{8,4},{12,0},{1,13},{5,9},{9,5},{13,1},{2,14},{6,10},... | collective-permute-start | bytes 393224 | tf_op jit(solution)/shard_map/ppermute | solution.py:20
  16.6 1.3 %collective-permute-start.1 = (bf16[128,512]{1,0:T(8,128)(2,1)S(1)}, bf16[128,512]{1,0:T(8,128)(2,1)S(1)}, u32[]{:S(2)}, u32[]{:S(2)}) collective-permute-start(bf16[128,512]{1,0:T(8,128)(2,1)S(1)} %get-tuple-element.23), channel_id=1, source_target_pairs={{0,8},{4,12},{8,0},{12,4},{1,9},{5,13},{9,1},{13,5},{2,10},{6,14},... | collective-permute-start | bytes 393224 | tf_op jit(solution)/shard_map/ppermute | solution.py:20
  17.8 5.0 %collective-permute-done.17 = bf16[144,256]{1,0:T(8,128)(2,1)S(1)} collective-permute-done((bf16[144,256]{1,0:T(8,128)(2,1)}, bf16[144,256]{1,0:T(8,128)(2,1)S(1)}, u32[]{:S(2)}, u32[]{:S(2)}) %collective-permute-start.17) | collective-permute-done | bytes 73760 | tf_op jit(solution)/shard_map/ppermute | solution.py:20
  22.8 0.9 %pad_maximum_fusion.refs_16_ = bf16[576,256]{1,0:T(8,128)(2,1)S(1)} fusion(bf16[144,256]{1,0:T(8,128)(2,1)S(1)} %collective-permute-done.18, bf16[144,256]{1,0:T(8,128)(2,1)S(1)} %collective-permute-done.17, bf16[144,256]{1,0:T(8,128)(2,1)S(1)} %collective-permute-done.16, bf16[144,256]{1,0:T(8,128)(2,1)} %student.1), kind=kLoop, calls=%fused_computation.1 | loop fusion | flops 1179648 | bytes 589824 | tf_op jit(solution)/shard_map/concatenate | solution.py:298
  23.7 1.4 %collective-permute-start.20 = (bf16[576,256]{1,0:T(8,128)(2,1)S(1)}, bf16[576,256]{1,0:T(8,128)(2,1)S(1)}, u32[]{:S(2)}, u32[]{:S(2)}) collective-permute-start(bf16[576,256]{1,0:T(8,128)(2,1)S(1)} %pad_maximum_fusion.refs_16_), channel_id=1, source_target_pairs={{0,2},{1,3},{2,0},{3,1},{4,6},{5,7},{6,4},{7,5},{8,10},{9,11},{10,... | collective-permute-start | bytes 884744 | tf_op jit(solution)/shard_map/ppermute | solution.py:20
  25.9 2.5 %collective-permute-done.1.refs_2_ = bf16[128,512]{1,0:T(8,128)(2,1)S(1)} collective-permute-done((bf16[128,512]{1,0:T(8,128)(2,1)S(1)}, bf16[128,512]{1,0:T(8,128)(2,1)S(1)}, u32[]{:S(2)}, u32[]{:S(2)}) %collective-permute-start.1) | collective-permute-done | bytes 131104 | tf_op jit(solution)/shard_map/ppermute | solution.py:20
  28.4 1.3 %collective-permute-done.refs_1_ = bf16[128,512]{1,0:T(8,128)(2,1)S(1)} collective-permute-done((bf16[128,512]{1,0:T(8,128)(2,1)S(1)}, bf16[128,512]{1,0:T(8,128)(2,1)S(1)}, u32[]{:S(2)}, u32[]{:S(2)}) %collective-permute-start) | collective-permute-done | bytes 131104 | tf_op jit(solution)/shard_map/ppermute | solution.py:20
  31.1 2.4 %collective-permute-start.11 = (bf16[128,512]{1,0:T(8,128)(2,1)S(1)}, bf16[128,512]{1,0:T(8,128)(2,1)S(1)}, u32[]{:S(2)}, u32[]{:S(2)}) collective-permute-start(bf16[128,512]{1,0:T(8,128)(2,1)S(1)} %get-tuple-element.30), channel_id=1, source_target_pairs={{0,12},{4,8},{8,4},{12,0},{1,13},{5,9},{9,5},{13,1},{2,14},{6,10},... | collective-permute-start | bytes 393224 | tf_op jit(solution)/shard_map/ppermute | solution.py:20
  33.7 1.9 %collective-permute-start.9 = (bf16[128,512]{1,0:T(8,128)(2,1)S(1)}, bf16[128,512]{1,0:T(8,128)(2,1)S(1)}, u32[]{:S(2)}, u32[]{:S(2)}) collective-permute-start(bf16[128,512]{1,0:T(8,128)(2,1)S(1)} %get-tuple-element.32), channel_id=1, source_target_pairs={{0,4},{4,0},{8,12},{12,8},{1,5},{5,1},{9,13},{13,9},{2,6},{6,2},{1... | collective-permute-start | bytes 393224 | tf_op jit(solution)/shard_map/ppermute | solution.py:20
  35.6 3.7 %collective-permute-done.11.refs_11_ = bf16[128,512]{1,0:T(8,128)(2,1)S(1)} collective-permute-done((bf16[128,512]{1,0:T(8,128)(2,1)S(1)}, bf16[128,512]{1,0:T(8,128)(2,1)S(1)}, u32[]{:S(2)}, u32[]{:S(2)}) %collective-permute-start.11) | collective-permute-done | bytes 131104 | tf_op jit(solution)/shard_map/ppermute | solution.py:20
  39.3 4.7 %collective-permute-done.10.refs_10_ = bf16[128,512]{1,0:T(8,128)(2,1)S(1)} collective-permute-done((bf16[128,512]{1,0:T(8,128)(2,1)S(1)}, bf16[128,512]{1,0:T(8,128)(2,1)S(1)}, u32[]{:S(2)}, u32[]{:S(2)}) %collective-permute-start.10) | collective-permute-done | bytes 131104 | tf_op jit(solution)/shard_map/ppermute | solution.py:20
  45.9 2.8 %pairs_far.1 = bf16[512,256]{1,0:T(8,128)(2,1)S(1)} custom-call(s32[4,4]{1,0:T(4,128)S(1)} %copy-done, s32[2]{0:T(128)S(1)} %pad_add_fusion.place, bf16[128,512]{1,0:T(8,128)(2,1)S(1)} %get-tuple-element.25.refs_0_, bf16[128,512]{1,0:T(8,128)(2,1)S(1)} %collective-permute-done.refs_1_, bf16[128,512]{1,0:T(8,128)(2,1)S(1)} %collective-permute-done.1.refs_2_, ...), custom_call_target="tpu_custom_call" | custom-call | flops 1610612736 | bytes 3145728 | tf_op jit(solution)/shard_map/pairs_far/pallas_call | solution.py:311
  48.7 1.6 %collective-permute-start.22 = (bf16[512,256]{1,0:T(8,128)(2,1)S(1)}, bf16[512,256]{1,0:T(8,128)(2,1)S(1)}, u32[]{:S(2)}, u32[]{:S(2)}) collective-permute-start(bf16[512,256]{1,0:T(8,128)(2,1)S(1)} %pairs_far.1), channel_id=1, source_target_pairs={{0,2},{1,3},{2,0},{3,1},{4,6},{5,7},{6,4},{7,5},{8,10},{9,11},{10,... | collective-permute-start | bytes 786440 | tf_op jit(solution)/shard_map/ppermute | solution.py:20
  50.3 3.1 %pairs_own.1 = (f32[512,256]{1,0:T(8,128)S(1)}, bf16[2048,256]{1,0:T(8,128)(2,1)S(1)}) custom-call(s32[4,4]{1,0:T(4,128)S(1)} %copy-done, s32[2]{0:T(128)S(1)} %pad_add_fusion.place, bf16[128,512]{1,0:T(8,128)(2,1)S(1)} %get-tuple-element.25.refs_0_, bf16[128,512]{1,0:T(8,128)(2,1)S(1)} %collective-permute-done.refs_1_, ...), custom_call_target="tpu_custom_call" | custom-call | flops 1610612736 | bytes 3145728 | tf_op jit(solution)/shard_map/pairs_own/pallas_call | solution.py:311
  53.4 3.8 %collective-permute-done.22 = bf16[512,256]{1,0:T(8,128)(2,1)S(1)} collective-permute-done((bf16[512,256]{1,0:T(8,128)(2,1)S(1)}, bf16[512,256]{1,0:T(8,128)(2,1)S(1)}, u32[]{:S(2)}, u32[]{:S(2)}) %collective-permute-start.22) | collective-permute-done | bytes 262176 | tf_op jit(solution)/shard_map/ppermute | solution.py:20
  57.5 2.4 %collective-permute-start.25 = (bf16[128,256]{1,0:T(8,128)(2,1)S(1)}, bf16[128,256]{1,0:T(8,128)(2,1)S(1)}, u32[]{:S(2)}, u32[]{:S(2)}) collective-permute-start(bf16[128,256]{1,0:T(8,128)(2,1)S(1)} %get-tuple-element.28), channel_id=1, source_target_pairs={{0,12},{4,8},{8,4},{12,0},{1,13},{5,9},{9,5},{13,1},{2,14},{6,10},... | collective-permute-start | bytes 196616 | tf_op jit(solution)/shard_map/ppermute | solution.py:20
  59.9 0.9 %collective-permute-start.24 = (bf16[128,256]{1,0:T(8,128)(2,1)S(1)}, bf16[128,256]{1,0:T(8,128)(2,1)S(1)}, u32[]{:S(2)}, u32[]{:S(2)}) collective-permute-start(bf16[128,256]{1,0:T(8,128)(2,1)S(1)} %get-tuple-element.29), channel_id=1, source_target_pairs={{0,8},{4,12},{8,0},{12,4},{1,9},{5,13},{9,1},{13,5},{2,10},{6,14},... | collective-permute-start | bytes 196616 | tf_op jit(solution)/shard_map/ppermute | solution.py:20
  61.2 1.0 %collective-permute-done.23 = bf16[128,256]{1,0:T(8,128)(2,1)S(1)} collective-permute-done((bf16[128,256]{1,0:T(8,128)(2,1)S(1)}, bf16[128,256]{1,0:T(8,128)(2,1)S(1)}, u32[]{:S(2)}, u32[]{:S(2)}) %collective-permute-start.23) | collective-permute-done | bytes 65568 | tf_op jit(solution)/shard_map/ppermute | solution.py:20
  62.2 1.9 %collective-permute-done.25 = bf16[128,256]{1,0:T(8,128)(2,1)S(1)} collective-permute-done((bf16[128,256]{1,0:T(8,128)(2,1)S(1)}, bf16[128,256]{1,0:T(8,128)(2,1)S(1)}, u32[]{:S(2)}, u32[]{:S(2)}) %collective-permute-start.25) | collective-permute-done | bytes 65568 | tf_op jit(solution)/shard_map/ppermute | solution.py:20
  64.1 2.5 %collective-permute-done.24 = bf16[128,256]{1,0:T(8,128)(2,1)S(1)} collective-permute-done((bf16[128,256]{1,0:T(8,128)(2,1)S(1)}, bf16[128,256]{1,0:T(8,128)(2,1)S(1)}, u32[]{:S(2)}, u32[]{:S(2)}) %collective-permute-start.24) | collective-permute-done | bytes 65568 | tf_op jit(solution)/shard_map/ppermute | solution.py:20
  66.6 1.6 %collective-permute-start.26 = (bf16[128,256]{1,0:T(8,128)(2,1)S(1)}, bf16[128,256]{1,0:T(8,128)(2,1)S(1)}, u32[]{:S(2)}, u32[]{:S(2)}) collective-permute-start(bf16[128,256]{1,0:T(8,128)(2,1)S(1)} %multiply_convert_fusion), channel_id=1, source_target_pairs={{0,2},{1,3},{2,0},{3,1},{4,6},{5,7},{6,4},{7,5},{8,10},{9,11},{10,... | collective-permute-start | bytes 196616 | tf_op jit(solution)/shard_map/ppermute | solution.py:20
  68.2 2.2 %collective-permute-start.30 = (bf16[128,256]{1,0:T(8,128)(2,1)S(1)}, bf16[128,256]{1,0:T(8,128)(2,1)S(1)}, u32[]{:S(2)}, u32[]{:S(2)}) collective-permute-start(bf16[128,256]{1,0:T(8,128)(2,1)S(1)} %multiply_convert_fusion), channel_id=1, source_target_pairs={{0,12},{4,8},{8,4},{12,0},{1,13},{5,9},{9,5},{13,1},{2,14},{6,10},... | collective-permute-start | bytes 196616 | tf_op jit(solution)/shard_map/ppermute | solution.py:20
  70.4 2.2 %collective-permute-start.28 = (bf16[128,256]{1,0:T(8,128)(2,1)S(1)}, bf16[128,256]{1,0:T(8,128)(2,1)S(1)}, u32[]{:S(2)}, u32[]{:S(2)}) collective-permute-start(bf16[128,256]{1,0:T(8,128)(2,1)S(1)} %multiply_convert_fusion), channel_id=1, source_target_pairs={{0,4},{4,0},{8,12},{12,8},{1,5},{5,1},{9,13},{13,9},{2,6},{6,2},{1... | collective-permute-start | bytes 196616 | tf_op jit(solution)/shard_map/ppermute | solution.py:20
  72.6 2.3 %collective-permute-done.30 = bf16[128,256]{1,0:T(8,128)(2,1)S(1)} collective-permute-done((bf16[128,256]{1,0:T(8,128)(2,1)S(1)}, bf16[128,256]{1,0:T(8,128)(2,1)S(1)}, u32[]{:S(2)}, u32[]{:S(2)}) %collective-permute-start.30) | collective-permute-done | bytes 65568 | tf_op jit(solution)/shard_map/ppermute | solution.py:20
  74.9 1.4 %collective-permute-done.29 = bf16[128,256]{1,0:T(8,128)(2,1)S(1)} collective-permute-done((bf16[128,256]{1,0:T(8,128)(2,1)S(1)}, bf16[128,256]{1,0:T(8,128)(2,1)S(1)}, u32[]{:S(2)}, u32[]{:S(2)}) %collective-permute-start.29) | collective-permute-done | bytes 65568 | tf_op jit(solution)/shard_map/ppermute | solution.py:20
  76.8 5.3 %collective-permute-done.31 = bf16[384,256]{1,0:T(8,128)(2,1)S(1)} collective-permute-done((bf16[384,256]{1,0:T(8,128)(2,1)S(1)}, bf16[384,256]{1,0:T(8,128)(2,1)S(1)}, u32[]{:S(2)}, u32[]{:S(2)}) %collective-permute-start.31) | collective-permute-done | bytes 196640 | tf_op jit(solution)/shard_map/ppermute | solution.py:20
  82.6 1.4 %collective-permute-done.27.refs_1_ = bf16[256,256]{1,0:T(8,128)(2,1)S(1)} collective-permute-done((bf16[256,256]{1,0:T(8,128)(2,1)S(1)}, bf16[256,256]{1,0:T(8,128)(2,1)S(1)}, u32[]{:S(2)}, u32[]{:S(2)}) %collective-permute-start.27) | collective-permute-done | bytes 131104 | tf_op jit(solution)/shard_map/ppermute | solution.py:20
  84.0 1.3 %last.1 = f32[256,256]{1,0:T(8,128)} custom-call(bf16[256,2048]{1,0:T(8,128)(2,1)S(1)} %flip.1.t_keep, bf16[256,256]{1,0:T(8,128)(2,1)S(1)} %pad_maximum_fusion.4.refs_0_, bf16[256,256]{1,0:T(8,128)(2,1)S(1)} %collective-permute-done.27.refs_1_, bf16[768,256]{1,0:T(8,128)(2,1)S(1)} %constant_dynamic-update-slice_fusion.refs_2_, ...), custom_call_target="tpu_custom_call" | custom-call | flops 268435456 | bytes 2097152 | tf_op jit(solution)/shard_map/last/pallas_call | solution.py:366
  (56 shorter events, 6.6 us)
Async XLA Ops:
  5.6 11.0 %collective-permute-start.18 = (bf16[144,256]{1,0:T(8,128)(2,1)}, bf16[144,256]{1,0:T(8,128)(2,1)S(1)}, u32[]{:S(2)}, u32[]{:S(2)}) collective-permute-start(bf16[144,256]{1,0:T(8,128)(2,1)} %student.1), channel_id=1, source_target_pairs={{0,12},{4,8},{8,4},{12,0},{1,13},{5,9},{9,5},{13,1},{2,14},{6,10},... | collective-permute-start | bytes 221192 | tf_op jit(solution)/shard_map/ppermute | solution.py:20
  10.7 12.2 %collective-permute-start.17 = (bf16[144,256]{1,0:T(8,128)(2,1)}, bf16[144,256]{1,0:T(8,128)(2,1)S(1)}, u32[]{:S(2)}, u32[]{:S(2)}) collective-permute-start(bf16[144,256]{1,0:T(8,128)(2,1)} %student.1), channel_id=1, source_target_pairs={{0,8},{4,12},{8,0},{12,4},{1,9},{5,13},{9,1},{13,5},{2,10},{6,14},... | collective-permute-start | bytes 221192 | tf_op jit(solution)/shard_map/ppermute | solution.py:20
  10.7 12.2 %collective-permute-start.16 = (bf16[144,256]{1,0:T(8,128)(2,1)}, bf16[144,256]{1,0:T(8,128)(2,1)S(1)}, u32[]{:S(2)}, u32[]{:S(2)}) collective-permute-start(bf16[144,256]{1,0:T(8,128)(2,1)} %student.1), channel_id=1, source_target_pairs={{0,4},{4,0},{8,12},{12,8},{1,5},{5,1},{9,13},{13,9},{2,6},{6,2},{1... | collective-permute-start | bytes 221192 | tf_op jit(solution)/shard_map/ppermute | solution.py:20
  11.3 13.9 %collective-permute-start.7 = (bf16[256,512]{1,0:T(8,128)(2,1)S(1)}, bf16[256,512]{1,0:T(8,128)(2,1)S(1)}, u32[]{:S(2)}, u32[]{:S(2)}) collective-permute-start(bf16[256,512]{1,0:T(8,128)(2,1)S(1)} %pad_maximum_fusion.2), channel_id=1, source_target_pairs={{0,2},{1,3},{2,0},{3,1},{4,6},{5,7},{6,4},{7,5},{8,10},{9,11},{10,... | collective-permute-start | bytes 786440 | tf_op jit(solution)/shard_map/ppermute | solution.py:20
  13.0 13.0 %collective-permute-start.2 = (bf16[128,512]{1,0:T(8,128)(2,1)S(1)}, bf16[128,512]{1,0:T(8,128)(2,1)S(1)}, u32[]{:S(2)}, u32[]{:S(2)}) collective-permute-start(bf16[128,512]{1,0:T(8,128)(2,1)S(1)} %get-tuple-element.22), channel_id=1, source_target_pairs={{0,12},{4,8},{8,4},{12,0},{1,13},{5,9},{9,5},{13,1},{2,14},{6,10},... | collective-permute-start | bytes 393224 | tf_op jit(solution)/shard_map/ppermute | solution.py:20
  16.6 11.9 %collective-permute-start.1 = (bf16[128,512]{1,0:T(8,128)(2,1)S(1)}, bf16[128,512]{1,0:T(8,128)(2,1)S(1)}, u32[]{:S(2)}, u32[]{:S(2)}) collective-permute-start(bf16[128,512]{1,0:T(8,128)(2,1)S(1)} %get-tuple-element.23), channel_id=1, source_target_pairs={{0,8},{4,12},{8,0},{12,4},{1,9},{5,13},{9,1},{13,5},{2,10},{6,14},... | collective-permute-start | bytes 393224 | tf_op jit(solution)/shard_map/ppermute | solution.py:20
  22.8 6.9 %collective-permute-start = (bf16[128,512]{1,0:T(8,128)(2,1)S(1)}, bf16[128,512]{1,0:T(8,128)(2,1)S(1)}, u32[]{:S(2)}, u32[]{:S(2)}) collective-permute-start(bf16[128,512]{1,0:T(8,128)(2,1)S(1)} %get-tuple-element.24), channel_id=1, source_target_pairs={{0,4},{4,0},{8,12},{12,8},{1,5},{5,1},{9,13},{13,9},{2,6},{6,2},{1... | collective-permute-start | bytes 393224 | tf_op jit(solution)/shard_map/ppermute | solution.py:20
  23.7 9.8 %collective-permute-start.20 = (bf16[576,256]{1,0:T(8,128)(2,1)S(1)}, bf16[576,256]{1,0:T(8,128)(2,1)S(1)}, u32[]{:S(2)}, u32[]{:S(2)}) collective-permute-start(bf16[576,256]{1,0:T(8,128)(2,1)S(1)} %pad_maximum_fusion.refs_16_), channel_id=1, source_target_pairs={{0,2},{1,3},{2,0},{3,1},{4,6},{5,7},{6,4},{7,5},{8,10},{9,11},{10,... | collective-permute-start | bytes 884744 | tf_op jit(solution)/shard_map/ppermute | solution.py:20
  25.2 8.4 %collective-permute-start.8 = (bf16[256,512]{1,0:T(8,128)(2,1)S(1)}, bf16[256,512]{1,0:T(8,128)(2,1)S(1)}, u32[]{:S(2)}, u32[]{:S(2)}) collective-permute-start(bf16[256,512]{1,0:T(8,128)(2,1)S(1)} %pad_maximum_fusion.1), channel_id=1, source_target_pairs={{0,2},{1,3},{2,0},{3,1},{4,6},{5,7},{6,4},{7,5},{8,10},{9,11},{10,... | collective-permute-start | bytes 786440 | tf_op jit(solution)/shard_map/ppermute | solution.py:20
  25.9 3.8 %collective-permute-start.3 = (bf16[128,512]{1,0:T(8,128)(2,1)S(1)}, bf16[128,512]{1,0:T(8,128)(2,1)S(1)}, u32[]{:S(2)}, u32[]{:S(2)}) collective-permute-start(bf16[128,512]{1,0:T(8,128)(2,1)S(1)} %get-tuple-element.25.refs_0_), channel_id=1, source_target_pairs={{0,1},{1,0},{2,3},{3,2},{4,5},{5,4},{6,7},{7,6},{8,9},{9,8},{10,11... | collective-permute-start | bytes 393224 | tf_op jit(solution)/shard_map/ppermute | solution.py:20
  28.4 1.9 %collective-permute-start.6 = (bf16[128,512]{1,0:T(8,128)(2,1)S(1)}, bf16[128,512]{1,0:T(8,128)(2,1)S(1)}, u32[]{:S(2)}, u32[]{:S(2)}) collective-permute-start(bf16[128,512]{1,0:T(8,128)(2,1)S(1)} %collective-permute-done.2.refs_3_), channel_id=1, source_target_pairs={{0,1},{1,0},{2,3},{3,2},{4,5},{5,4},{6,7},{7,6},{8,9},{9,8},{10,11... | collective-permute-start | bytes 393224 | tf_op jit(solution)/shard_map/ppermute | solution.py:20
  29.7 1.3 %collective-permute-start.5 = (bf16[128,512]{1,0:T(8,128)(2,1)S(1)}, bf16[128,512]{1,0:T(8,128)(2,1)S(1)}, u32[]{:S(2)}, u32[]{:S(2)}) collective-permute-start(bf16[128,512]{1,0:T(8,128)(2,1)S(1)} %collective-permute-done.1.refs_2_), channel_id=1, source_target_pairs={{0,1},{1,0},{2,3},{3,2},{4,5},{5,4},{6,7},{7,6},{8,9},{9,8},{10,11... | collective-permute-start | bytes 393224 | tf_op jit(solution)/shard_map/ppermute | solution.py:20
  29.8 14.3 %collective-permute-start.19 = (bf16[576,256]{1,0:T(8,128)(2,1)S(1)}, bf16[576,256]{1,0:T(8,128)(2,1)S(1)}, u32[]{:S(2)}, u32[]{:S(2)}) collective-permute-start(bf16[576,256]{1,0:T(8,128)(2,1)S(1)} %pad_maximum_fusion.refs_16_), channel_id=1, source_target_pairs={{0,1},{1,0},{2,3},{3,2},{4,5},{5,4},{6,7},{7,6},{8,9},{9,8},{10,11... | collective-permute-start | bytes 884744 | tf_op jit(solution)/shard_map/ppermute | solution.py:20
  30.4 3.3 %collective-permute-start.4 = (bf16[128,512]{1,0:T(8,128)(2,1)S(1)}, bf16[128,512]{1,0:T(8,128)(2,1)S(1)}, u32[]{:S(2)}, u32[]{:S(2)}) collective-permute-start(bf16[128,512]{1,0:T(8,128)(2,1)S(1)} %collective-permute-done.refs_1_), channel_id=1, source_target_pairs={{0,1},{1,0},{2,3},{3,2},{4,5},{5,4},{6,7},{7,6},{8,9},{9,8},{10,11... | collective-permute-start | bytes 393224 | tf_op jit(solution)/shard_map/ppermute | solution.py:20
  31.1 8.2 %collective-permute-start.11 = (bf16[128,512]{1,0:T(8,128)(2,1)S(1)}, bf16[128,512]{1,0:T(8,128)(2,1)S(1)}, u32[]{:S(2)}, u32[]{:S(2)}) collective-permute-start(bf16[128,512]{1,0:T(8,128)(2,1)S(1)} %get-tuple-element.30), channel_id=1, source_target_pairs={{0,12},{4,8},{8,4},{12,0},{1,13},{5,9},{9,5},{13,1},{2,14},{6,10},... | collective-permute-start | bytes 393224 | tf_op jit(solution)/shard_map/ppermute | solution.py:20
  33.5 10.5 %collective-permute-start.10 = (bf16[128,512]{1,0:T(8,128)(2,1)S(1)}, bf16[128,512]{1,0:T(8,128)(2,1)S(1)}, u32[]{:S(2)}, u32[]{:S(2)}) collective-permute-start(bf16[128,512]{1,0:T(8,128)(2,1)S(1)} %get-tuple-element.31), channel_id=1, source_target_pairs={{0,8},{4,12},{8,0},{12,4},{1,9},{5,13},{9,1},{13,5},{2,10},{6,14},... | collective-permute-start | bytes 393224 | tf_op jit(solution)/shard_map/ppermute | solution.py:20
  33.7 11.9 %collective-permute-start.21 = (bf16[576,256]{1,0:T(8,128)(2,1)S(1)}, bf16[576,256]{1,0:T(8,128)(2,1)S(1)}, u32[]{:S(2)}, u32[]{:S(2)}) collective-permute-start(bf16[576,256]{1,0:T(8,128)(2,1)S(1)} %collective-permute-done.20.refs_18_), channel_id=1, source_target_pairs={{0,1},{1,0},{2,3},{3,2},{4,5},{5,4},{6,7},{7,6},{8,9},{9,8},{10,11... | collective-permute-start | bytes 884744 | tf_op jit(solution)/shard_map/ppermute | solution.py:20
  33.7 10.9 %collective-permute-start.9 = (bf16[128,512]{1,0:T(8,128)(2,1)S(1)}, bf16[128,512]{1,0:T(8,128)(2,1)S(1)}, u32[]{:S(2)}, u32[]{:S(2)}) collective-permute-start(bf16[128,512]{1,0:T(8,128)(2,1)S(1)} %get-tuple-element.32), channel_id=1, source_target_pairs={{0,4},{4,0},{8,12},{12,8},{1,5},{5,1},{9,13},{13,9},{2,6},{6,2},{1... | collective-permute-start | bytes 393224 | tf_op jit(solution)/shard_map/ppermute | solution.py:20
  39.3 5.4 %collective-permute-start.15 = (bf16[128,512]{1,0:T(8,128)(2,1)S(1)}, bf16[128,512]{1,0:T(8,128)(2,1)S(1)}, u32[]{:S(2)}, u32[]{:S(2)}) collective-permute-start(bf16[128,512]{1,0:T(8,128)(2,1)S(1)} %collective-permute-done.11.refs_11_), channel_id=1, source_target_pairs={{0,1},{1,0},{2,3},{3,2},{4,5},{5,4},{6,7},{7,6},{8,9},{9,8},{10,11... | collective-permute-start | bytes 393224 | tf_op jit(solution)/shard_map/ppermute | solution.py:20
  44.1 1.5 %collective-permute-start.12 = (bf16[128,512]{1,0:T(8,128)(2,1)S(1)}, bf16[128,512]{1,0:T(8,128)(2,1)S(1)}, u32[]{:S(2)}, u32[]{:S(2)}) collective-permute-start(bf16[128,512]{1,0:T(8,128)(2,1)S(1)} %get-tuple-element.33.refs_8_), channel_id=1, source_target_pairs={{0,1},{1,0},{2,3},{3,2},{4,5},{5,4},{6,7},{7,6},{8,9},{9,8},{10,11... | collective-permute-start | bytes 393224 | tf_op jit(solution)/shard_map/ppermute | solution.py:20
  44.6 1.3 %collective-permute-start.13 = (bf16[128,512]{1,0:T(8,128)(2,1)S(1)}, bf16[128,512]{1,0:T(8,128)(2,1)S(1)}, u32[]{:S(2)}, u32[]{:S(2)}) collective-permute-start(bf16[128,512]{1,0:T(8,128)(2,1)S(1)} %collective-permute-done.9.refs_9_), channel_id=1, source_target_pairs={{0,1},{1,0},{2,3},{3,2},{4,5},{5,4},{6,7},{7,6},{8,9},{9,8},{10,11... | collective-permute-start | bytes 393224 | tf_op jit(solution)/shard_map/ppermute | solution.py:20
  48.7 8.5 %collective-permute-start.22 = (bf16[512,256]{1,0:T(8,128)(2,1)S(1)}, bf16[512,256]{1,0:T(8,128)(2,1)S(1)}, u32[]{:S(2)}, u32[]{:S(2)}) collective-permute-start(bf16[512,256]{1,0:T(8,128)(2,1)S(1)} %pairs_far.1), channel_id=1, source_target_pairs={{0,2},{1,3},{2,0},{3,1},{4,6},{5,7},{6,4},{7,5},{8,10},{9,11},{10,... | collective-permute-start | bytes 786440 | tf_op jit(solution)/shard_map/ppermute | solution.py:20
  57.3 4.9 %collective-permute-start.23 = (bf16[128,256]{1,0:T(8,128)(2,1)S(1)}, bf16[128,256]{1,0:T(8,128)(2,1)S(1)}, u32[]{:S(2)}, u32[]{:S(2)}) collective-permute-start(bf16[128,256]{1,0:T(8,128)(2,1)S(1)} %get-tuple-element.27), channel_id=1, source_target_pairs={{0,4},{4,0},{8,12},{12,8},{1,5},{5,1},{9,13},{13,9},{2,6},{6,2},{1... | collective-permute-start | bytes 196616 | tf_op jit(solution)/shard_map/ppermute | solution.py:20
  57.5 6.6 %collective-permute-start.25 = (bf16[128,256]{1,0:T(8,128)(2,1)S(1)}, bf16[128,256]{1,0:T(8,128)(2,1)S(1)}, u32[]{:S(2)}, u32[]{:S(2)}) collective-permute-start(bf16[128,256]{1,0:T(8,128)(2,1)S(1)} %get-tuple-element.28), channel_id=1, source_target_pairs={{0,12},{4,8},{8,4},{12,0},{1,13},{5,9},{9,5},{13,1},{2,14},{6,10},... | collective-permute-start | bytes 196616 | tf_op jit(solution)/shard_map/ppermute | solution.py:20
  59.9 6.7 %collective-permute-start.24 = (bf16[128,256]{1,0:T(8,128)(2,1)S(1)}, bf16[128,256]{1,0:T(8,128)(2,1)S(1)}, u32[]{:S(2)}, u32[]{:S(2)}) collective-permute-start(bf16[128,256]{1,0:T(8,128)(2,1)S(1)} %get-tuple-element.29), channel_id=1, source_target_pairs={{0,8},{4,12},{8,0},{12,4},{1,9},{5,13},{9,1},{13,5},{2,10},{6,14},... | collective-permute-start | bytes 196616 | tf_op jit(solution)/shard_map/ppermute | solution.py:20
  66.6 6.0 %collective-permute-start.26 = (bf16[128,256]{1,0:T(8,128)(2,1)S(1)}, bf16[128,256]{1,0:T(8,128)(2,1)S(1)}, u32[]{:S(2)}, u32[]{:S(2)}) collective-permute-start(bf16[128,256]{1,0:T(8,128)(2,1)S(1)} %multiply_convert_fusion), channel_id=1, source_target_pairs={{0,2},{1,3},{2,0},{3,1},{4,6},{5,7},{6,4},{7,5},{8,10},{9,11},{10,... | collective-permute-start | bytes 196616 | tf_op jit(solution)/shard_map/ppermute | solution.py:20
  68.2 6.7 %collective-permute-start.30 = (bf16[128,256]{1,0:T(8,128)(2,1)S(1)}, bf16[128,256]{1,0:T(8,128)(2,1)S(1)}, u32[]{:S(2)}, u32[]{:S(2)}) collective-permute-start(bf16[128,256]{1,0:T(8,128)(2,1)S(1)} %multiply_convert_fusion), channel_id=1, source_target_pairs={{0,12},{4,8},{8,4},{12,0},{1,13},{5,9},{9,5},{13,1},{2,14},{6,10},... | collective-permute-start | bytes 196616 | tf_op jit(solution)/shard_map/ppermute | solution.py:20
  70.4 5.9 %collective-permute-start.29 = (bf16[128,256]{1,0:T(8,128)(2,1)S(1)}, bf16[128,256]{1,0:T(8,128)(2,1)S(1)}, u32[]{:S(2)}, u32[]{:S(2)}) collective-permute-start(bf16[128,256]{1,0:T(8,128)(2,1)S(1)} %multiply_convert_fusion), channel_id=1, source_target_pairs={{0,8},{4,12},{8,0},{12,4},{1,9},{5,13},{9,1},{13,5},{2,10},{6,14},... | collective-permute-start | bytes 196616 | tf_op jit(solution)/shard_map/ppermute | solution.py:20
  70.4 5.9 %collective-permute-start.28 = (bf16[128,256]{1,0:T(8,128)(2,1)S(1)}, bf16[128,256]{1,0:T(8,128)(2,1)S(1)}, u32[]{:S(2)}, u32[]{:S(2)}) collective-permute-start(bf16[128,256]{1,0:T(8,128)(2,1)S(1)} %multiply_convert_fusion), channel_id=1, source_target_pairs={{0,4},{4,0},{8,12},{12,8},{1,5},{5,1},{9,13},{13,9},{2,6},{6,2},{1... | collective-permute-start | bytes 196616 | tf_op jit(solution)/shard_map/ppermute | solution.py:20
  76.3 5.7 %collective-permute-start.31 = (bf16[384,256]{1,0:T(8,128)(2,1)S(1)}, bf16[384,256]{1,0:T(8,128)(2,1)S(1)}, u32[]{:S(2)}, u32[]{:S(2)}) collective-permute-start(bf16[384,256]{1,0:T(8,128)(2,1)S(1)} %pad_maximum_fusion.3), channel_id=1, source_target_pairs={{0,2},{1,3},{2,0},{3,1},{4,6},{5,7},{6,4},{7,5},{8,10},{9,11},{10,... | collective-permute-start | bytes 589832 | tf_op jit(solution)/shard_map/ppermute | solution.py:20
  82.1 2.0 %collective-permute-start.32 = (bf16[768,256]{1,0:T(8,128)(2,1)S(1)}, bf16[768,256]{1,0:T(8,128)(2,1)S(1)}, u32[]{:S(2)}, u32[]{:S(2)}) collective-permute-start(bf16[768,256]{1,0:T(8,128)(2,1)S(1)} %constant_dynamic-update-slice_fusion.refs_2_), channel_id=1, source_target_pairs={{0,1},{1,0},{2,3},{3,2},{4,5},{5,4},{6,7},{7,6},{8,9},{9,8},{10,11... | collective-permute-start | bytes 1179656 | tf_op jit(solution)/shard_map/ppermute | solution.py:20
  82.1 1.9 %collective-permute-start.27 = (bf16[256,256]{1,0:T(8,128)(2,1)S(1)}, bf16[256,256]{1,0:T(8,128)(2,1)S(1)}, u32[]{:S(2)}, u32[]{:S(2)}) collective-permute-start(bf16[256,256]{1,0:T(8,128)(2,1)S(1)} %pad_maximum_fusion.4.refs_0_), channel_id=1, source_target_pairs={{0,1},{1,0},{2,3},{3,2},{4,5},{5,4},{6,7},{7,6},{8,9},{9,8},{10,11... | collective-permute-start | bytes 393224 | tf_op jit(solution)/shard_map/ppermute | solution.py:20
  (2 other events, 45.9 us)

commit v3 on v2

--- a/solution.py
+++ b/solution.py
@@ -13,6 +13,8 @@
 MIB = 1024 * 1024
 EXTRA = 16
 FAR, CORE = 2, 1
+HELD = 72_000_000
+NEAR = 2
 
 
 def swapped(value, axis, bit):
@@ -78,9 +80,9 @@
     pieces = planes * lanes
     panel = planes * rows
     prow = rows + EXTRA
-    t_in, s_in = refs[:pieces], refs[pieces : pieces + lanes]
-    result = refs[pieces + lanes]
-    rest = list(refs[pieces + lanes + 1 :])
+    t_in, s_in = refs[:pieces], refs[pieces : pieces + 2 * lanes]
+    result = refs[pieces + 2 * lanes]
+    rest = list(refs[pieces + 2 * lanes + 1 :])
     t_keep = rest.pop(0) if own else None
     t_all, s_all, g_raw, g_row, g_col, total, t_sem, s_sem, g_sem = rest
     here = place[0]
@@ -90,16 +92,20 @@
         at = m * planes + k
         return pltpu.make_async_copy(t_in[at], t_all.at[pl.ds(at * rows, rows)], t_sem.at[at])
 
+    def s_part(m, k, first, count):
+        late = k >= NEAR
+        return s_in[2 * m + late].at[pl.ds((k - late * NEAR) * prow + first, count)]
+
     def s_copy(m, k):
         at = m * planes + k
         return pltpu.make_async_copy(
-            s_in[m].at[pl.ds(k * prow, rows)], s_all.at[pl.ds(at * rows, rows)], s_sem.at[at]
+            s_part(m, k, 0, rows), s_all.at[pl.ds(at * rows, rows)], s_sem.at[at]
         )
 
     def g_copy(m, k):
         at = m * planes + k
         return pltpu.make_async_copy(
-            s_in[m].at[pl.ds(k * prow + rows, EXTRA)],
+            s_part(m, k, rows, EXTRA),
             g_raw.at[pl.ds(at * EXTRA, EXTRA)],
             g_sem.at[at],
         )
@@ -176,8 +182,8 @@
 def pair_values_kernel(planes, lanes, rows, out, width, own, mask, place, *refs):
     pieces = planes * lanes
     prow = rows + EXTRA
-    t_in, s_in = refs[:pieces], refs[pieces : pieces + lanes]
-    result = refs[pieces + lanes]
+    t_in, s_in = refs[:pieces], refs[pieces : pieces + 2 * lanes]
+    result = refs[pieces + 2 * lanes]
     here = place[0]
     lead = 0 if own else FAR
 
@@ -187,12 +193,16 @@
     def panel_of(m):
         return joined(t_in[m * planes + k][...] for k in range(planes))
 
+    def s_part(m, k, first, count):
+        late = k >= NEAR
+        at = (k - late * NEAR) * prow + first
+        return s_in[2 * m + late][at : at + count, :]
+
     def students_of(m):
-        return joined(s_in[m][k * prow : k * prow + rows, :] for k in range(planes))
+        return joined(s_part(m, k, 0, rows) for k in range(planes))
 
     def groups_of(m, k):
-        at = k * prow + rows
-        return s_in[m][at : at + EXTRA, :rows].astype(jnp.float32)[:1]
+        return s_part(m, k, rows, EXTRA)[:, :rows].astype(jnp.float32)[:1]
 
     weights = []
     for k in range(planes):
@@ -217,7 +227,7 @@
         total = total + jnp.dot(joined(terms), students, preferred_element_type=jnp.float32)
     result[...] = total.astype(result.dtype)
     if own:
-        t_keep = refs[pieces + lanes + 1]
+        t_keep = refs[pieces + 2 * lanes + 1]
         keep = t_keep.shape[1]
         for c in range(2):
 
@@ -225,6 +235,12 @@
             def _(c=c):
                 for at in range(pieces):
                     t_keep[at * rows : (at + 1) * rows, :] = t_in[at][:, c * keep : (c + 1) * keep]
+
+
+def hold_kernel(*refs):
+    half = len(refs) // 2
+    for source, target in zip(refs[:half], refs[half:]):
+        target[...] = source[...]
 
 
 def flip_kernel(value, result):
@@ -268,13 +284,10 @@
         return lax.dynamic_slice_in_dim(teacher, start, part, 1)
 
     mine = [cut(k, 0) for k in range(planes)]
-    theirs_far = jnp.concatenate([cut(k, 1) for k in range(half, planes)], 0)
-    theirs_near = jnp.concatenate([cut(k, 1) for k in range(half)], 0)
-    got_far = swapped(theirs_far, "narrow", FAR)
-    got_near = swapped(after(theirs_near, got_far), "narrow", FAR)
-    got = [
-        (got_near, got_far)[k >= half][k % half * rows : (k % half + 1) * rows] for k in range(planes)
-    ]
+    theirs = jnp.concatenate([cut(k, 1) for k in range(planes)], 0)
+    got = swapped(theirs, "narrow", FAR)
+    got = [got[k * rows : (k + 1) * rows] for k in range(planes)]
+    own_core = swapped(mine[0], "narrow", CORE)
     first = [mine[0]] + [swapped(mine[k], "wide", k) for k in range(1, planes)]
     second = [got[0]] + [swapped(got[k], "wide", k) for k in range(1, planes)]
 
@@ -293,14 +306,34 @@
         compiler_params=pltpu.CompilerParams(vmem_limit_bytes=56 * MIB),
         cost_estimate=cost(2 * rows * width * out, width * (2 * rows + 4 * out)),
         name="student",
-    )(after(teacher, theirs_far), weight, item_group.reshape(1, rows))
-    s_own = [packed] + [swapped(packed, "wide", k) for k in range(1, planes)]
-    s_own = jnp.concatenate(s_own, 0)
-    s_far = swapped(s_own, "narrow", FAR)
-    s_all = [s_own, swapped(s_own, "narrow", CORE), s_far, swapped(s_far, "narrow", CORE)]
-
-    t_all = [*first, *(swapped(t, "narrow", CORE) for t in first)]
+    )(after(teacher, own_core), weight, item_group.reshape(1, rows))
+    s_of = {0: packed}
+    bit = half
+    while bit:
+        for k in sorted(s_of):
+            s_of[k ^ bit] = swapped(s_of[k], "wide", bit)
+        bit //= 2
+    s_all = [None] * lanes * 2
+    for part_at, odd in enumerate((0, 1)):
+        own = jnp.concatenate([s_of[k] for k in range(planes) if (k >= NEAR) == odd], 0)
+        far = swapped(own, "narrow", FAR)
+        for m, value in ((0, own), (FAR, far)):
+            s_all[2 * m + part_at] = value
+            s_all[2 * (m ^ CORE) + part_at] = swapped(value, "narrow", CORE)
+
+    t_all = [*first, own_core, *(swapped(t, "narrow", CORE) for t in first[1:])]
     t_all += [*second, *(swapped(t, "narrow", CORE) for t in second)]
+
+    late = 2 * planes
+    t_all[late:] = pl.pallas_call(
+        hold_kernel,
+        out_shape=[jax.ShapeDtypeStruct((rows, part), jnp.bfloat16)] * late,
+        in_specs=[VMEM] * late,
+        out_specs=[VMEM] * late,
+        compiler_params=pltpu.CompilerParams(vmem_limit_bytes=vmem_room(8 * late * rows * part)),
+        cost_estimate=cost(0, HELD),
+        name="hold",
+    )(*t_all[late:])
 
     def pairs(own):
         shapes = [jax.ShapeDtypeStruct((panel, out), jnp.float32 if own else jnp.bfloat16)]
@@ -311,7 +344,7 @@
             return pl.pallas_call(
                 functools.partial(pair_values_kernel, planes, lanes, rows, out, width, own),
                 out_shape=shapes,
-                in_specs=[SMEM, SMEM] + [VMEM] * (pieces + lanes),
+                in_specs=[SMEM, SMEM] + [VMEM] * (pieces + 2 * lanes),
                 out_specs=[VMEM] * len(shapes),
                 compiler_params=pltpu.CompilerParams(vmem_limit_bytes=vmem_room(held)),
                 cost_estimate=cost(2 * panel * items * (part + out), 2 * items * (part + out)),
@@ -320,7 +353,7 @@
         return pl.pallas_call(
             functools.partial(pair_kernel, planes, lanes, rows, out, width, own),
             out_shape=shapes,
-            in_specs=[SMEM, SMEM] + [ANY] * (pieces + lanes),
+            in_specs=[SMEM, SMEM] + [ANY] * (pieces + 2 * lanes),
             out_specs=[VMEM] * len(shapes),
             scratch_shapes=[
                 pltpu.VMEM((items, part), jnp.bfloat16),

time: 85.5 us -> 80.7 us (0.944)
  waiting for transfers between devices: 38.6 us -> 31 us
  starting transfers between devices: 32.3 us -> 35 us
    ppermute x33 -> x35, waiting for transfers between devices: 38.6 us -> 31 us  [swapped(): lax.ppermute(value, axis, [(source, source ^ bit) for source in range(cou...]
    ppermute x33 -> x35, starting transfers between devices: 32.3 us -> 35 us  [swapped(): lax.ppermute(value, axis, [(source, source ^ bit) for source in range(cou...]
  transfers between devices with their start and end apart: 33 -> 35, of which waited for: 17 -> 15; matrix products, arithmetic and copies ran while one was open for 1% -> 1% of each run, Pallas kernels for 4% -> 10%
where the time goes in v3:
time: 80.7 us; the launch traced here: 80.5 us
  starting transfers between devices  35 us (43%)
  waiting for transfers between devices  31 us (38%)
  Pallas kernels  11.8 us (15%)
  local copies, waits for them, and re-layouts  1.46 us (2%)
  other arithmetic  1.15 us (1%)
    ppermute x35, starting transfers between devices, swapped(): lax.ppermute(value, axis, [(source, source ^ bit) for source in range(cou...  35 us
    ppermute x35, waiting for transfers between devices, swapped(): lax.ppermute(value, axis, [(source, source ^ bit) for source in range(cou...  31 us
    pallas_call x2, Pallas kernels, pairs(): pl.pallas_call(functools.partial(pair_values_kernel, planes, lanes, rows,...  5.95 us
    pallas_call x1, Pallas kernels, per_device(): pl.pallas_call(functools.partial(student_kernel, steps), out_shape=jax.Sh...  4.15 us
  transfers between devices with their start and end apart: 35, of which 15 were waited for; matrix products, arithmetic and copies ran while one was open for 1% of the time, Pallas kernels for 10%

profile of v3, /device:TPU:0, one launch (start us, length us, event | category | flops | bytes accessed | tf_op | source)
XLA Modules:
  0.0 80.5 jit_solution(14945243824622966352)
XLA Ops:
  0.0 1.4 %constant_dynamic-slice_fusion.3 = (bf16[128,512]{1,0:T(8,128)(2,1)S(1)}, bf16[128,512]{1,0:T(8,128)(2,1)S(1)}, bf16[128,512]{1,0:T(8,128)(2,1)S(1)}, bf16[128,5...) fusion(bf16[128,4096]{1,0:T(8,128)(2,1)} %teacher, ...), kind=kLoop, calls=%fused_computation.13 | loop fusion | bytes 2097184 | tf_op jit(solution)/shard_map/dynamic_slice | solution.py:284
  1.4 3.0 %collective-permute-start.7 = (bf16[512,512]{1,0:T(8,128)(2,1)S(1)}, bf16[512,512]{1,0:T(8,128)(2,1)S(1)}, u32[]{:S(2)}, u32[]{:S(2)}) collective-permute-start(bf16[512,512]{1,0:T(8,128)(2,1)S(1)} %pad_maximum_fusion), channel_id=1, source_target_pairs={{0,2},{1,3},{2,0},{3,1},{4,6},{5,7},{6,4},{7,5},{8,10},{9,11},{10,... | collective-permute-start | bytes 1572872 | tf_op jit(solution)/shard_map/ppermute | solution.py:22
  4.4 3.6 %collective-permute-start.2 = (bf16[128,512]{1,0:T(8,128)(2,1)S(1)}, bf16[128,512]{1,0:T(8,128)(2,1)S(1)}, u32[]{:S(2)}, u32[]{:S(2)}) collective-permute-start(bf16[128,512]{1,0:T(8,128)(2,1)S(1)} %get-tuple-element.36), channel_id=1, source_target_pairs={{0,12},{4,8},{8,4},{12,0},{1,13},{5,9},{9,5},{13,1},{2,14},{6,10},... | collective-permute-start | bytes 393224 | tf_op jit(solution)/shard_map/ppermute | solution.py:22
  8.0 4.1 %student.1 = bf16[144,256]{1,0:T(8,128)(2,1)} custom-call(bf16[128,4096]{1,0:T(8,128)(2,1)} %teacher, f32[4096,256]{1,0:T(8,128)} %weight.1, s32[1,128]{1,0:T(1,128)} %bitcast.3), custom_call_target="tpu_custom_call" | custom-call | flops 268435456 | bytes 5242880 | tf_op jit(solution)/shard_map/student/pallas_call | solution.py:295
  13.0 1.2 %collective-permute-start = (bf16[128,512]{1,0:T(8,128)(2,1)S(1)}, bf16[128,512]{1,0:T(8,128)(2,1)S(1)}, u32[]{:S(2)}, u32[]{:S(2)}) collective-permute-start(bf16[128,512]{1,0:T(8,128)(2,1)S(1)} %get-tuple-element.38), channel_id=1, source_target_pairs={{0,4},{4,0},{8,12},{12,8},{1,5},{5,1},{9,13},{13,9},{2,6},{6,2},{1... | collective-permute-start | bytes 393224 | tf_op jit(solution)/shard_map/ppermute | solution.py:22
  14.3 4.6 %collective-permute-start.16 = (bf16[144,256]{1,0:T(8,128)(2,1)}, bf16[144,256]{1,0:T(8,128)(2,1)S(1)}, u32[]{:S(2)}, u32[]{:S(2)}) collective-permute-start(bf16[144,256]{1,0:T(8,128)(2,1)} %student.1), channel_id=1, source_target_pairs={{0,8},{4,12},{8,0},{12,4},{1,9},{5,13},{9,1},{13,5},{2,10},{6,14},... | collective-permute-start | bytes 221192 | tf_op jit(solution)/shard_map/ppermute | solution.py:22
  18.9 1.3 %collective-permute-done.1.refs_2_ = bf16[128,512]{1,0:T(8,128)(2,1)S(1)} collective-permute-done((bf16[128,512]{1,0:T(8,128)(2,1)S(1)}, bf16[128,512]{1,0:T(8,128)(2,1)S(1)}, u32[]{:S(2)}, u32[]{:S(2)}) %collective-permute-start.1) | collective-permute-done | bytes 131104 | tf_op jit(solution)/shard_map/ppermute | solution.py:22
  20.3 1.4 %collective-permute-done.15 = bf16[144,256]{1,0:T(8,128)(2,1)S(1)} collective-permute-done((bf16[144,256]{1,0:T(8,128)(2,1)}, bf16[144,256]{1,0:T(8,128)(2,1)S(1)}, u32[]{:S(2)}, u32[]{:S(2)}) %collective-permute-start.15) | collective-permute-done | bytes 73760 | tf_op jit(solution)/shard_map/ppermute | solution.py:22
  23.2 1.2 %collective-permute-start.17 = (bf16[144,256]{1,0:T(8,128)(2,1)S(1)}, bf16[144,256]{1,0:T(8,128)(2,1)S(1)}, u32[]{:S(2)}, u32[]{:S(2)}) collective-permute-start(bf16[144,256]{1,0:T(8,128)(2,1)S(1)} %collective-permute-done.16), channel_id=1, source_target_pairs={{0,4},{4,0},{8,12},{12,8},{1,5},{5,1},{9,13},{13,9},{2,6},{6,2},{1... | collective-permute-start | bytes 221192 | tf_op jit(solution)/shard_map/ppermute | solution.py:22
  24.5 2.1 %collective-permute-start.10 = (bf16[128,512]{1,0:T(8,128)(2,1)S(1)}, bf16[128,512]{1,0:T(8,128)(2,1)S(1)}, u32[]{:S(2)}, u32[]{:S(2)}) collective-permute-start(bf16[128,512]{1,0:T(8,128)(2,1)S(1)} %get-tuple-element.41), channel_id=1, source_target_pairs={{0,12},{4,8},{8,4},{12,0},{1,13},{5,9},{9,5},{13,1},{2,14},{6,10},... | collective-permute-start | bytes 393224 | tf_op jit(solution)/shard_map/ppermute | solution.py:22
  27.6 1.4 %collective-permute-start.8 = (bf16[128,512]{1,0:T(8,128)(2,1)S(1)}, bf16[128,512]{1,0:T(8,128)(2,1)S(1)}, u32[]{:S(2)}, u32[]{:S(2)}) collective-permute-start(bf16[128,512]{1,0:T(8,128)(2,1)S(1)} %get-tuple-element.43), channel_id=1, source_target_pairs={{0,4},{4,0},{8,12},{12,8},{1,5},{5,1},{9,13},{13,9},{2,6},{6,2},{1... | collective-permute-start | bytes 393224 | tf_op jit(solution)/shard_map/ppermute | solution.py:22
  29.0 2.1 %collective-permute-start.21 = (bf16[288,256]{1,0:T(8,128)(2,1)S(1)}, bf16[288,256]{1,0:T(8,128)(2,1)S(1)}, u32[]{:S(2)}, u32[]{:S(2)}) collective-permute-start(bf16[288,256]{1,0:T(8,128)(2,1)S(1)} %constant_dynamic-update-slice_fusion.refs_17_), channel_id=1, source_target_pairs={{0,2},{1,3},{2,0},{3,1},{4,6},{5,7},{6,4},{7,5},{8,10},{9,11},{10,... | collective-permute-start | bytes 442376 | tf_op jit(solution)/shard_map/ppermute | solution.py:22
  31.2 1.7 %collective-permute-done.10.refs_3_ = bf16[128,512]{1,0:T(8,128)(2,1)S(1)} collective-permute-done((bf16[128,512]{1,0:T(8,128)(2,1)S(1)}, bf16[128,512]{1,0:T(8,128)(2,1)S(1)}, u32[]{:S(2)}, u32[]{:S(2)}) %collective-permute-start.10) | collective-permute-done | bytes 131104 | tf_op jit(solution)/shard_map/ppermute | solution.py:22
  32.8 5.7 %collective-permute-done.9.refs_2_ = bf16[128,512]{1,0:T(8,128)(2,1)S(1)} collective-permute-done((bf16[128,512]{1,0:T(8,128)(2,1)S(1)}, bf16[128,512]{1,0:T(8,128)(2,1)S(1)}, u32[]{:S(2)}, u32[]{:S(2)}) %collective-permute-start.9) | collective-permute-done | bytes 131104 | tf_op jit(solution)/shard_map/ppermute | solution.py:22
  40.6 0.9 %collective-permute-done.4.refs_5_ = bf16[128,512]{1,0:T(8,128)(2,1)S(1)} collective-permute-done((bf16[128,512]{1,0:T(8,128)(2,1)S(1)}, bf16[128,512]{1,0:T(8,128)(2,1)S(1)}, u32[]{:S(2)}, u32[]{:S(2)}) %collective-permute-start.4) | collective-permute-done | bytes 131104 | tf_op jit(solution)/shard_map/ppermute | solution.py:22
  41.5 2.8 %pairs_far.1 = bf16[512,256]{1,0:T(8,128)(2,1)S(1)} custom-call(s32[4,4]{1,0:T(4,128)S(1)} %copy-done, s32[2]{0:T(128)S(1)} %pad_add_fusion.place, bf16[128,512]{1,0:T(8,128)(2,1)S(1)} %get-tuple-element.39.refs_0_, bf16[128,512]{1,0:T(8,128)(2,1)S(1)} %collective-permute-done.refs_1_, bf16[128,512]{1,0:T(8,128)(2,1)S(1)} %collective-permute-done.1.refs_2_, ...), custom_call_target="tpu_custom_call" | custom-call | flops 1610612736 | bytes 3145728 | tf_op jit(solution)/shard_map/pairs_far/pallas_call | solution.py:344
  44.4 1.6 %collective-permute-start.24 = (bf16[512,256]{1,0:T(8,128)(2,1)S(1)}, bf16[512,256]{1,0:T(8,128)(2,1)S(1)}, u32[]{:S(2)}, u32[]{:S(2)}) collective-permute-start(bf16[512,256]{1,0:T(8,128)(2,1)S(1)} %pairs_far.1), channel_id=1, source_target_pairs={{0,2},{1,3},{2,0},{3,1},{4,6},{5,7},{6,4},{7,5},{8,10},{9,11},{10,... | collective-permute-start | bytes 786440 | tf_op jit(solution)/shard_map/ppermute | solution.py:22
  45.9 3.1 %pairs_own.1 = (f32[512,256]{1,0:T(8,128)S(1)}, bf16[2048,256]{1,0:T(8,128)(2,1)S(1)}) custom-call(s32[4,4]{1,0:T(4,128)S(1)} %copy-done, s32[2]{0:T(128)S(1)} %pad_add_fusion.place, bf16[128,512]{1,0:T(8,128)(2,1)S(1)} %get-tuple-element.39.refs_0_, bf16[128,512]{1,0:T(8,128)(2,1)S(1)} %collective-permute-done.refs_1_, ...), custom_call_target="tpu_custom_call" | custom-call | flops 1610612736 | bytes 3145728 | tf_op jit(solution)/shard_map/pairs_own/pallas_call | solution.py:344
  49.0 3.9 %collective-permute-done.24 = bf16[512,256]{1,0:T(8,128)(2,1)S(1)} collective-permute-done((bf16[512,256]{1,0:T(8,128)(2,1)S(1)}, bf16[512,256]{1,0:T(8,128)(2,1)S(1)}, u32[]{:S(2)}, u32[]{:S(2)}) %collective-permute-start.24) | collective-permute-done | bytes 262176 | tf_op jit(solution)/shard_map/ppermute | solution.py:22
  53.1 1.9 %collective-permute-start.27 = (bf16[128,256]{1,0:T(8,128)(2,1)S(1)}, bf16[128,256]{1,0:T(8,128)(2,1)S(1)}, u32[]{:S(2)}, u32[]{:S(2)}) collective-permute-start(bf16[128,256]{1,0:T(8,128)(2,1)S(1)} %get-tuple-element.46), channel_id=1, source_target_pairs={{0,12},{4,8},{8,4},{12,0},{1,13},{5,9},{9,5},{13,1},{2,14},{6,10},... | collective-permute-start | bytes 196616 | tf_op jit(solution)/shard_map/ppermute | solution.py:22
  55.0 1.6 %collective-permute-start.26 = (bf16[128,256]{1,0:T(8,128)(2,1)S(1)}, bf16[128,256]{1,0:T(8,128)(2,1)S(1)}, u32[]{:S(2)}, u32[]{:S(2)}) collective-permute-start(bf16[128,256]{1,0:T(8,128)(2,1)S(1)} %get-tuple-element.47), channel_id=1, source_target_pairs={{0,8},{4,12},{8,0},{12,4},{1,9},{5,13},{9,1},{13,5},{2,10},{6,14},... | collective-permute-start | bytes 196616 | tf_op jit(solution)/shard_map/ppermute | solution.py:22
  57.0 1.2 %collective-permute-done.25 = bf16[128,256]{1,0:T(8,128)(2,1)S(1)} collective-permute-done((bf16[128,256]{1,0:T(8,128)(2,1)S(1)}, bf16[128,256]{1,0:T(8,128)(2,1)S(1)}, u32[]{:S(2)}, u32[]{:S(2)}) %collective-permute-start.25) | collective-permute-done | bytes 65568 | tf_op jit(solution)/shard_map/ppermute | solution.py:22
  58.1 1.2 %collective-permute-done.27 = bf16[128,256]{1,0:T(8,128)(2,1)S(1)} collective-permute-done((bf16[128,256]{1,0:T(8,128)(2,1)S(1)}, bf16[128,256]{1,0:T(8,128)(2,1)S(1)}, u32[]{:S(2)}, u32[]{:S(2)}) %collective-permute-start.27) | collective-permute-done | bytes 65568 | tf_op jit(solution)/shard_map/ppermute | solution.py:22
  59.4 2.7 %collective-permute-done.26 = bf16[128,256]{1,0:T(8,128)(2,1)S(1)} collective-permute-done((bf16[128,256]{1,0:T(8,128)(2,1)S(1)}, bf16[128,256]{1,0:T(8,128)(2,1)S(1)}, u32[]{:S(2)}, u32[]{:S(2)}) %collective-permute-start.26) | collective-permute-done | bytes 65568 | tf_op jit(solution)/shard_map/ppermute | solution.py:22
  62.1 1.5 %collective-permute-start.28 = (bf16[128,256]{1,0:T(8,128)(2,1)S(1)}, bf16[128,256]{1,0:T(8,128)(2,1)S(1)}, u32[]{:S(2)}, u32[]{:S(2)}) collective-permute-start(bf16[128,256]{1,0:T(8,128)(2,1)S(1)} %multiply_convert_fusion), channel_id=1, source_target_pairs={{0,2},{1,3},{2,0},{3,1},{4,6},{5,7},{6,4},{7,5},{8,10},{9,11},{10,... | collective-permute-start | bytes 196616 | tf_op jit(solution)/shard_map/ppermute | solution.py:22
  63.6 2.0 %collective-permute-start.32 = (bf16[128,256]{1,0:T(8,128)(2,1)S(1)}, bf16[128,256]{1,0:T(8,128)(2,1)S(1)}, u32[]{:S(2)}, u32[]{:S(2)}) collective-permute-start(bf16[128,256]{1,0:T(8,128)(2,1)S(1)} %multiply_convert_fusion), channel_id=1, source_target_pairs={{0,12},{4,8},{8,4},{12,0},{1,13},{5,9},{9,5},{13,1},{2,14},{6,10},... | collective-permute-start | bytes 196616 | tf_op jit(solution)/shard_map/ppermute | solution.py:22
  65.6 2.3 %collective-permute-start.30 = (bf16[128,256]{1,0:T(8,128)(2,1)S(1)}, bf16[128,256]{1,0:T(8,128)(2,1)S(1)}, u32[]{:S(2)}, u32[]{:S(2)}) collective-permute-start(bf16[128,256]{1,0:T(8,128)(2,1)S(1)} %multiply_convert_fusion), channel_id=1, source_target_pairs={{0,4},{4,0},{8,12},{12,8},{1,5},{5,1},{9,13},{13,9},{2,6},{6,2},{1... | collective-permute-start | bytes 196616 | tf_op jit(solution)/shard_map/ppermute | solution.py:22
  68.0 2.1 %collective-permute-done.32 = bf16[128,256]{1,0:T(8,128)(2,1)S(1)} collective-permute-done((bf16[128,256]{1,0:T(8,128)(2,1)S(1)}, bf16[128,256]{1,0:T(8,128)(2,1)S(1)}, u32[]{:S(2)}, u32[]{:S(2)}) %collective-permute-start.32) | collective-permute-done | bytes 65568 | tf_op jit(solution)/shard_map/ppermute | solution.py:22
  70.1 1.4 %collective-permute-done.31 = bf16[128,256]{1,0:T(8,128)(2,1)S(1)} collective-permute-done((bf16[128,256]{1,0:T(8,128)(2,1)S(1)}, bf16[128,256]{1,0:T(8,128)(2,1)S(1)}, u32[]{:S(2)}, u32[]{:S(2)}) %collective-permute-start.31) | collective-permute-done | bytes 65568 | tf_op jit(solution)/shard_map/ppermute | solution.py:22
  72.3 4.9 %collective-permute-done.33 = bf16[384,256]{1,0:T(8,128)(2,1)S(1)} collective-permute-done((bf16[384,256]{1,0:T(8,128)(2,1)S(1)}, bf16[384,256]{1,0:T(8,128)(2,1)S(1)}, u32[]{:S(2)}, u32[]{:S(2)}) %collective-permute-start.33) | collective-permute-done | bytes 196640 | tf_op jit(solution)/shard_map/ppermute | solution.py:22
  77.9 1.4 %collective-permute-done.29.refs_1_ = bf16[256,256]{1,0:T(8,128)(2,1)S(1)} collective-permute-done((bf16[256,256]{1,0:T(8,128)(2,1)S(1)}, bf16[256,256]{1,0:T(8,128)(2,1)S(1)}, u32[]{:S(2)}, u32[]{:S(2)}) %collective-permute-start.29) | collective-permute-done | bytes 131104 | tf_op jit(solution)/shard_map/ppermute | solution.py:22
  79.3 1.3 %last.1 = f32[256,256]{1,0:T(8,128)} custom-call(bf16[256,2048]{1,0:T(8,128)(2,1)S(1)} %flip.1.t_keep, bf16[256,256]{1,0:T(8,128)(2,1)S(1)} %pad_maximum_fusion.3.refs_0_, bf16[256,256]{1,0:T(8,128)(2,1)S(1)} %collective-permute-done.29.refs_1_, bf16[768,256]{1,0:T(8,128)(2,1)S(1)} %constant_dynamic-update-slice_fusion.2.refs_2_, ...), custom_call_target="tpu_custom_call" | custom-call | flops 268435456 | bytes 2097152 | tf_op jit(solution)/shard_map/last/pallas_call | solution.py:399
  (61 shorter events, 7.5 us)
Async XLA Ops:
  1.4 21.8 %collective-permute-start.7 = (bf16[512,512]{1,0:T(8,128)(2,1)S(1)}, bf16[512,512]{1,0:T(8,128)(2,1)S(1)}, u32[]{:S(2)}, u32[]{:S(2)}) collective-permute-start(bf16[512,512]{1,0:T(8,128)(2,1)S(1)} %pad_maximum_fusion), channel_id=1, source_target_pairs={{0,2},{1,3},{2,0},{3,1},{4,6},{5,7},{6,4},{7,5},{8,10},{9,11},{10,... | collective-permute-start | bytes 1572872 | tf_op jit(solution)/shard_map/ppermute | solution.py:22
  4.4 3.6 %collective-permute-start.3 = (bf16[128,512]{1,0:T(8,128)(2,1)S(1)}, bf16[128,512]{1,0:T(8,128)(2,1)S(1)}, u32[]{:S(2)}, u32[]{:S(2)}) collective-permute-start(bf16[128,512]{1,0:T(8,128)(2,1)S(1)} %get-tuple-element.39.refs_0_), channel_id=1, source_target_pairs={{0,1},{1,0},{2,3},{3,2},{4,5},{5,4},{6,7},{7,6},{8,9},{9,8},{10,11... | collective-permute-start | bytes 393224 | tf_op jit(solution)/shard_map/ppermute | solution.py:22
  4.4 9.9 %collective-permute-start.2 = (bf16[128,512]{1,0:T(8,128)(2,1)S(1)}, bf16[128,512]{1,0:T(8,128)(2,1)S(1)}, u32[]{:S(2)}, u32[]{:S(2)}) collective-permute-start(bf16[128,512]{1,0:T(8,128)(2,1)S(1)} %get-tuple-element.36), channel_id=1, source_target_pairs={{0,12},{4,8},{8,4},{12,0},{1,13},{5,9},{9,5},{13,1},{2,14},{6,10},... | collective-permute-start | bytes 393224 | tf_op jit(solution)/shard_map/ppermute | solution.py:22
  8.0 12.2 %collective-permute-start.1 = (bf16[128,512]{1,0:T(8,128)(2,1)S(1)}, bf16[128,512]{1,0:T(8,128)(2,1)S(1)}, u32[]{:S(2)}, u32[]{:S(2)}) collective-permute-start(bf16[128,512]{1,0:T(8,128)(2,1)S(1)} %get-tuple-element.37), channel_id=1, source_target_pairs={{0,8},{4,12},{8,0},{12,4},{1,9},{5,13},{9,1},{13,5},{2,10},{6,14},... | collective-permute-start | bytes 393224 | tf_op jit(solution)/shard_map/ppermute | solution.py:22
  12.2 9.5 %collective-permute-start.15 = (bf16[144,256]{1,0:T(8,128)(2,1)}, bf16[144,256]{1,0:T(8,128)(2,1)S(1)}, u32[]{:S(2)}, u32[]{:S(2)}) collective-permute-start(bf16[144,256]{1,0:T(8,128)(2,1)} %student.1), channel_id=1, source_target_pairs={{0,4},{4,0},{8,12},{12,8},{1,5},{5,1},{9,13},{13,9},{2,6},{6,2},{1... | collective-permute-start | bytes 221192 | tf_op jit(solution)/shard_map/ppermute | solution.py:22
  13.0 11.4 %collective-permute-start = (bf16[128,512]{1,0:T(8,128)(2,1)S(1)}, bf16[128,512]{1,0:T(8,128)(2,1)S(1)}, u32[]{:S(2)}, u32[]{:S(2)}) collective-permute-start(bf16[128,512]{1,0:T(8,128)(2,1)S(1)} %get-tuple-element.38), channel_id=1, source_target_pairs={{0,4},{4,0},{8,12},{12,8},{1,5},{5,1},{9,13},{13,9},{2,6},{6,2},{1... | collective-permute-start | bytes 393224 | tf_op jit(solution)/shard_map/ppermute | solution.py:22
  14.3 8.3 %collective-permute-start.16 = (bf16[144,256]{1,0:T(8,128)(2,1)}, bf16[144,256]{1,0:T(8,128)(2,1)S(1)}, u32[]{:S(2)}, u32[]{:S(2)}) collective-permute-start(bf16[144,256]{1,0:T(8,128)(2,1)} %student.1), channel_id=1, source_target_pairs={{0,8},{4,12},{8,0},{12,4},{1,9},{5,13},{9,1},{13,5},{2,10},{6,14},... | collective-permute-start | bytes 221192 | tf_op jit(solution)/shard_map/ppermute | solution.py:22
  20.3 6.4 %collective-permute-start.6 = (bf16[128,512]{1,0:T(8,128)(2,1)S(1)}, bf16[128,512]{1,0:T(8,128)(2,1)S(1)}, u32[]{:S(2)}, u32[]{:S(2)}) collective-permute-start(bf16[128,512]{1,0:T(8,128)(2,1)S(1)} %collective-permute-done.2.refs_3_), channel_id=1, source_target_pairs={{0,1},{1,0},{2,3},{3,2},{4,5},{5,4},{6,7},{7,6},{8,9},{9,8},{10,11... | collective-permute-start | bytes 393224 | tf_op jit(solution)/shard_map/ppermute | solution.py:22
  21.7 7.3 %collective-permute-start.5 = (bf16[128,512]{1,0:T(8,128)(2,1)S(1)}, bf16[128,512]{1,0:T(8,128)(2,1)S(1)}, u32[]{:S(2)}, u32[]{:S(2)}) collective-permute-start(bf16[128,512]{1,0:T(8,128)(2,1)S(1)} %collective-permute-done.1.refs_2_), channel_id=1, source_target_pairs={{0,1},{1,0},{2,3},{3,2},{4,5},{5,4},{6,7},{7,6},{8,9},{9,8},{10,11... | collective-permute-start | bytes 393224 | tf_op jit(solution)/shard_map/ppermute | solution.py:22
  22.6 8.5 %collective-permute-start.20 = (bf16[288,256]{1,0:T(8,128)(2,1)S(1)}, bf16[288,256]{1,0:T(8,128)(2,1)S(1)}, u32[]{:S(2)}, u32[]{:S(2)}) collective-permute-start(bf16[288,256]{1,0:T(8,128)(2,1)S(1)} %pad_maximum_fusion.2.refs_16_), channel_id=1, source_target_pairs={{0,2},{1,3},{2,0},{3,1},{4,6},{5,7},{6,4},{7,5},{8,10},{9,11},{10,... | collective-permute-start | bytes 442376 | tf_op jit(solution)/shard_map/ppermute | solution.py:22
  23.2 4.4 %collective-permute-start.17 = (bf16[144,256]{1,0:T(8,128)(2,1)S(1)}, bf16[144,256]{1,0:T(8,128)(2,1)S(1)}, u32[]{:S(2)}, u32[]{:S(2)}) collective-permute-start(bf16[144,256]{1,0:T(8,128)(2,1)S(1)} %collective-permute-done.16), channel_id=1, source_target_pairs={{0,4},{4,0},{8,12},{12,8},{1,5},{5,1},{9,13},{13,9},{2,6},{6,2},{1... | collective-permute-start | bytes 221192 | tf_op jit(solution)/shard_map/ppermute | solution.py:22
  24.5 8.3 %collective-permute-start.10 = (bf16[128,512]{1,0:T(8,128)(2,1)S(1)}, bf16[128,512]{1,0:T(8,128)(2,1)S(1)}, u32[]{:S(2)}, u32[]{:S(2)}) collective-permute-start(bf16[128,512]{1,0:T(8,128)(2,1)S(1)} %get-tuple-element.41), channel_id=1, source_target_pairs={{0,12},{4,8},{8,4},{12,0},{1,13},{5,9},{9,5},{13,1},{2,14},{6,10},... | collective-permute-start | bytes 393224 | tf_op jit(solution)/shard_map/ppermute | solution.py:22
  26.6 12.0 %collective-permute-start.9 = (bf16[128,512]{1,0:T(8,128)(2,1)S(1)}, bf16[128,512]{1,0:T(8,128)(2,1)S(1)}, u32[]{:S(2)}, u32[]{:S(2)}) collective-permute-start(bf16[128,512]{1,0:T(8,128)(2,1)S(1)} %get-tuple-element.42), channel_id=1, source_target_pairs={{0,8},{4,12},{8,0},{12,4},{1,9},{5,13},{9,1},{13,5},{2,10},{6,14},... | collective-permute-start | bytes 393224 | tf_op jit(solution)/shard_map/ppermute | solution.py:22
  27.6 11.0 %collective-permute-start.8 = (bf16[128,512]{1,0:T(8,128)(2,1)S(1)}, bf16[128,512]{1,0:T(8,128)(2,1)S(1)}, u32[]{:S(2)}, u32[]{:S(2)}) collective-permute-start(bf16[128,512]{1,0:T(8,128)(2,1)S(1)} %get-tuple-element.43), channel_id=1, source_target_pairs={{0,4},{4,0},{8,12},{12,8},{1,5},{5,1},{9,13},{13,9},{2,6},{6,2},{1... | collective-permute-start | bytes 393224 | tf_op jit(solution)/shard_map/ppermute | solution.py:22
  29.0 10.1 %collective-permute-start.21 = (bf16[288,256]{1,0:T(8,128)(2,1)S(1)}, bf16[288,256]{1,0:T(8,128)(2,1)S(1)}, u32[]{:S(2)}, u32[]{:S(2)}) collective-permute-start(bf16[288,256]{1,0:T(8,128)(2,1)S(1)} %constant_dynamic-update-slice_fusion.refs_17_), channel_id=1, source_target_pairs={{0,2},{1,3},{2,0},{3,1},{4,6},{5,7},{6,4},{7,5},{8,10},{9,11},{10,... | collective-permute-start | bytes 442376 | tf_op jit(solution)/shard_map/ppermute | solution.py:22
  31.2 8.0 %collective-permute-start.11 = (bf16[128,512]{1,0:T(8,128)(2,1)S(1)}, bf16[128,512]{1,0:T(8,128)(2,1)S(1)}, u32[]{:S(2)}, u32[]{:S(2)}) collective-permute-start(bf16[128,512]{1,0:T(8,128)(2,1)S(1)} %get-tuple-element.44.refs_0_), channel_id=1, source_target_pairs={{0,1},{1,0},{2,3},{3,2},{4,5},{5,4},{6,7},{7,6},{8,9},{9,8},{10,11... | collective-permute-start | bytes 393224 | tf_op jit(solution)/shard_map/ppermute | solution.py:22
  32.8 6.8 %collective-permute-start.14 = (bf16[128,512]{1,0:T(8,128)(2,1)S(1)}, bf16[128,512]{1,0:T(8,128)(2,1)S(1)}, u32[]{:S(2)}, u32[]{:S(2)}) collective-permute-start(bf16[128,512]{1,0:T(8,128)(2,1)S(1)} %collective-permute-done.10.refs_3_), channel_id=1, source_target_pairs={{0,1},{1,0},{2,3},{3,2},{4,5},{5,4},{6,7},{7,6},{8,9},{9,8},{10,11... | collective-permute-start | bytes 393224 | tf_op jit(solution)/shard_map/ppermute | solution.py:22
  39.1 2.4 %collective-permute-start.18 = (bf16[288,256]{1,0:T(8,128)(2,1)S(1)}, bf16[288,256]{1,0:T(8,128)(2,1)S(1)}, u32[]{:S(2)}, u32[]{:S(2)}) collective-permute-start(bf16[288,256]{1,0:T(8,128)(2,1)S(1)} %pad_maximum_fusion.2.refs_16_), channel_id=1, source_target_pairs={{0,1},{1,0},{2,3},{3,2},{4,5},{5,4},{6,7},{7,6},{8,9},{9,8},{10,11... | collective-permute-start | bytes 442376 | tf_op jit(solution)/shard_map/ppermute | solution.py:22
  39.2 2.3 %collective-permute-start.19 = (bf16[288,256]{1,0:T(8,128)(2,1)S(1)}, bf16[288,256]{1,0:T(8,128)(2,1)S(1)}, u32[]{:S(2)}, u32[]{:S(2)}) collective-permute-start(bf16[288,256]{1,0:T(8,128)(2,1)S(1)} %constant_dynamic-update-slice_fusion.refs_17_), channel_id=1, source_target_pairs={{0,1},{1,0},{2,3},{3,2},{4,5},{5,4},{6,7},{7,6},{8,9},{9,8},{10,11... | collective-permute-start | bytes 442376 | tf_op jit(solution)/shard_map/ppermute | solution.py:22
  39.6 1.9 %collective-permute-start.22 = (bf16[288,256]{1,0:T(8,128)(2,1)S(1)}, bf16[288,256]{1,0:T(8,128)(2,1)S(1)}, u32[]{:S(2)}, u32[]{:S(2)}) collective-permute-start(bf16[288,256]{1,0:T(8,128)(2,1)S(1)} %collective-permute-done.20.refs_20_), channel_id=1, source_target_pairs={{0,1},{1,0},{2,3},{3,2},{4,5},{5,4},{6,7},{7,6},{8,9},{9,8},{10,11... | collective-permute-start | bytes 442376 | tf_op jit(solution)/shard_map/ppermute | solution.py:22
  39.9 1.6 %collective-permute-start.23 = (bf16[288,256]{1,0:T(8,128)(2,1)S(1)}, bf16[288,256]{1,0:T(8,128)(2,1)S(1)}, u32[]{:S(2)}, u32[]{:S(2)}) collective-permute-start(bf16[288,256]{1,0:T(8,128)(2,1)S(1)} %collective-permute-done.21.refs_21_), channel_id=1, source_target_pairs={{0,1},{1,0},{2,3},{3,2},{4,5},{5,4},{6,7},{7,6},{8,9},{9,8},{10,11... | collective-permute-start | bytes 442376 | tf_op jit(solution)/shard_map/ppermute | solution.py:22
  44.4 8.6 %collective-permute-start.24 = (bf16[512,256]{1,0:T(8,128)(2,1)S(1)}, bf16[512,256]{1,0:T(8,128)(2,1)S(1)}, u32[]{:S(2)}, u32[]{:S(2)}) collective-permute-start(bf16[512,256]{1,0:T(8,128)(2,1)S(1)} %pairs_far.1), channel_id=1, source_target_pairs={{0,2},{1,3},{2,0},{3,1},{4,6},{5,7},{6,4},{7,5},{8,10},{9,11},{10,... | collective-permute-start | bytes 786440 | tf_op jit(solution)/shard_map/ppermute | solution.py:22
  53.0 5.1 %collective-permute-start.25 = (bf16[128,256]{1,0:T(8,128)(2,1)S(1)}, bf16[128,256]{1,0:T(8,128)(2,1)S(1)}, u32[]{:S(2)}, u32[]{:S(2)}) collective-permute-start(bf16[128,256]{1,0:T(8,128)(2,1)S(1)} %get-tuple-element.45), channel_id=1, source_target_pairs={{0,4},{4,0},{8,12},{12,8},{1,5},{5,1},{9,13},{13,9},{2,6},{6,2},{1... | collective-permute-start | bytes 196616 | tf_op jit(solution)/shard_map/ppermute | solution.py:22
  53.1 6.2 %collective-permute-start.27 = (bf16[128,256]{1,0:T(8,128)(2,1)S(1)}, bf16[128,256]{1,0:T(8,128)(2,1)S(1)}, u32[]{:S(2)}, u32[]{:S(2)}) collective-permute-start(bf16[128,256]{1,0:T(8,128)(2,1)S(1)} %get-tuple-element.46), channel_id=1, source_target_pairs={{0,12},{4,8},{8,4},{12,0},{1,13},{5,9},{9,5},{13,1},{2,14},{6,10},... | collective-permute-start | bytes 196616 | tf_op jit(solution)/shard_map/ppermute | solution.py:22
  55.0 7.1 %collective-permute-start.26 = (bf16[128,256]{1,0:T(8,128)(2,1)S(1)}, bf16[128,256]{1,0:T(8,128)(2,1)S(1)}, u32[]{:S(2)}, u32[]{:S(2)}) collective-permute-start(bf16[128,256]{1,0:T(8,128)(2,1)S(1)} %get-tuple-element.47), channel_id=1, source_target_pairs={{0,8},{4,12},{8,0},{12,4},{1,9},{5,13},{9,1},{13,5},{2,10},{6,14},... | collective-permute-start | bytes 196616 | tf_op jit(solution)/shard_map/ppermute | solution.py:22
  62.1 5.9 %collective-permute-start.28 = (bf16[128,256]{1,0:T(8,128)(2,1)S(1)}, bf16[128,256]{1,0:T(8,128)(2,1)S(1)}, u32[]{:S(2)}, u32[]{:S(2)}) collective-permute-start(bf16[128,256]{1,0:T(8,128)(2,1)S(1)} %multiply_convert_fusion), channel_id=1, source_target_pairs={{0,2},{1,3},{2,0},{3,1},{4,6},{5,7},{6,4},{7,5},{8,10},{9,11},{10,... | collective-permute-start | bytes 196616 | tf_op jit(solution)/shard_map/ppermute | solution.py:22
  63.6 6.5 %collective-permute-start.32 = (bf16[128,256]{1,0:T(8,128)(2,1)S(1)}, bf16[128,256]{1,0:T(8,128)(2,1)S(1)}, u32[]{:S(2)}, u32[]{:S(2)}) collective-permute-start(bf16[128,256]{1,0:T(8,128)(2,1)S(1)} %multiply_convert_fusion), channel_id=1, source_target_pairs={{0,12},{4,8},{8,4},{12,0},{1,13},{5,9},{9,5},{13,1},{2,14},{6,10},... | collective-permute-start | bytes 196616 | tf_op jit(solution)/shard_map/ppermute | solution.py:22
  65.6 5.9 %collective-permute-start.31 = (bf16[128,256]{1,0:T(8,128)(2,1)S(1)}, bf16[128,256]{1,0:T(8,128)(2,1)S(1)}, u32[]{:S(2)}, u32[]{:S(2)}) collective-permute-start(bf16[128,256]{1,0:T(8,128)(2,1)S(1)} %multiply_convert_fusion), channel_id=1, source_target_pairs={{0,8},{4,12},{8,0},{12,4},{1,9},{5,13},{9,1},{13,5},{2,10},{6,14},... | collective-permute-start | bytes 196616 | tf_op jit(solution)/shard_map/ppermute | solution.py:22
  65.6 5.9 %collective-permute-start.30 = (bf16[128,256]{1,0:T(8,128)(2,1)S(1)}, bf16[128,256]{1,0:T(8,128)(2,1)S(1)}, u32[]{:S(2)}, u32[]{:S(2)}) collective-permute-start(bf16[128,256]{1,0:T(8,128)(2,1)S(1)} %multiply_convert_fusion), channel_id=1, source_target_pairs={{0,4},{4,0},{8,12},{12,8},{1,5},{5,1},{9,13},{13,9},{2,6},{6,2},{1... | collective-permute-start | bytes 196616 | tf_op jit(solution)/shard_map/ppermute | solution.py:22
  71.5 5.7 %collective-permute-start.33 = (bf16[384,256]{1,0:T(8,128)(2,1)S(1)}, bf16[384,256]{1,0:T(8,128)(2,1)S(1)}, u32[]{:S(2)}, u32[]{:S(2)}) collective-permute-start(bf16[384,256]{1,0:T(8,128)(2,1)S(1)} %pad_maximum_fusion.1), channel_id=1, source_target_pairs={{0,2},{1,3},{2,0},{3,1},{4,6},{5,7},{6,4},{7,5},{8,10},{9,11},{10,... | collective-permute-start | bytes 589832 | tf_op jit(solution)/shard_map/ppermute | solution.py:22
  77.3 2.0 %collective-permute-start.34 = (bf16[768,256]{1,0:T(8,128)(2,1)S(1)}, bf16[768,256]{1,0:T(8,128)(2,1)S(1)}, u32[]{:S(2)}, u32[]{:S(2)}) collective-permute-start(bf16[768,256]{1,0:T(8,128)(2,1)S(1)} %constant_dynamic-update-slice_fusion.2.refs_2_), channel_id=1, source_target_pairs={{0,1},{1,0},{2,3},{3,2},{4,5},{5,4},{6,7},{7,6},{8,9},{9,8},{10,11... | collective-permute-start | bytes 1179656 | tf_op jit(solution)/shard_map/ppermute | solution.py:22
  77.4 1.9 %collective-permute-start.29 = (bf16[256,256]{1,0:T(8,128)(2,1)S(1)}, bf16[256,256]{1,0:T(8,128)(2,1)S(1)}, u32[]{:S(2)}, u32[]{:S(2)}) collective-permute-start(bf16[256,256]{1,0:T(8,128)(2,1)S(1)} %pad_maximum_fusion.3.refs_0_), channel_id=1, source_target_pairs={{0,1},{1,0},{2,3},{3,2},{4,5},{5,4},{6,7},{7,6},{8,9},{9,8},{10,11... | collective-permute-start | bytes 393224 | tf_op jit(solution)/shard_map/ppermute | solution.py:22
  (4 other events, 44.4 us)

commit v4 on v3

--- a/solution.py
+++ b/solution.py
@@ -179,7 +179,7 @@
                 t_keep[...] = t_all[:, c * keep : (c + 1) * keep]
 
 
-def pair_values_kernel(planes, lanes, rows, out, width, own, mask, place, *refs):
+def pair_values_kernel(planes, lanes, rows, out, width, own, chosen, mask, place, *refs):
     pieces = planes * lanes
     prow = rows + EXTRA
     t_in, s_in = refs[:pieces], refs[pieces : pieces + 2 * lanes]
@@ -190,8 +190,8 @@
     def joined(parts, axis=0):
         return jnp.concatenate(list(parts), axis)
 
-    def panel_of(m):
-        return joined(t_in[m * planes + k][...] for k in range(planes))
+    def panel_of(m, some=range(planes)):
+        return joined(t_in[m * planes + k][...] for k in some)
 
     def s_part(m, k, first, count):
         late = k >= NEAR
@@ -205,24 +205,26 @@
         return s_part(m, k, rows, EXTRA)[:, :rows].astype(jnp.float32)[:1]
 
     weights = []
-    for k in range(planes):
+    for k in chosen:
         scalars = [mask[here ^ k, here ^ j] + mask[here ^ j, here ^ k] for j in range(planes)]
         line = [jnp.full((1, rows), one.astype(jnp.float32) * (-1.0 / width)) for one in scalars]
         weights.append(joined(line, 1))
-    column = joined(jnp.broadcast_to(groups_of(lead, k), (128, rows)).T for k in range(planes))
+    column = joined(jnp.broadcast_to(groups_of(lead, k), (128, rows)).T for k in chosen)
     column = joined([column] * (planes * rows // 128), 1)
-    lead_t = panel_of(lead)
-    total = jnp.zeros((planes * rows, out), jnp.float32)
+    lead_t = panel_of(lead, chosen)
+    total = jnp.zeros((len(chosen) * rows, out), jnp.float32)
     for m in [lead] + [m for m in range(lanes) if m != lead]:
         students = students_of(m)
         teach = nt(lead_t, panel_of(m))
         same = column == joined((groups_of(m, k) for k in range(planes)), 1)
         terms = []
-        for k in range(planes):
-            error = teach[k * rows : (k + 1) * rows]
+        for place_at, k in enumerate(chosen):
+            span = slice(place_at * rows, (place_at + 1) * rows)
+            weight = weights[place_at]
+            error = teach[span]
             if own and k == 0:
                 error = error - nt(s_in[0][:rows, :], students) * (width / out)
-            factor = jnp.where(same[k * rows : (k + 1) * rows], 2.0 * weights[k], weights[k])
+            factor = jnp.where(same[span], 2.0 * weight, weight)
             terms.append((factor * error).astype(jnp.bfloat16))
         total = total + jnp.dot(joined(terms), students, preferred_element_type=jnp.float32)
     result[...] = total.astype(result.dtype)
@@ -335,19 +337,23 @@
         name="hold",
     )(*t_all[late:])
 
-    def pairs(own):
-        shapes = [jax.ShapeDtypeStruct((panel, out), jnp.float32 if own else jnp.bfloat16)]
+    whole_tiles = pieces <= 16 and panel <= 512
+
+    def pairs(own, chosen):
+        chosen = tuple(chosen)
+        some = len(chosen) * rows
+        shapes = [jax.ShapeDtypeStruct((some, out), jnp.float32 if own else jnp.bfloat16)]
         if own:
             shapes.append(jax.ShapeDtypeStruct((items, keep), jnp.bfloat16))
         held = items * (2 * part + 2 * out) + 4 * panel * out
-        if pieces <= 16 and panel <= 512:
+        if whole_tiles:
             return pl.pallas_call(
-                functools.partial(pair_values_kernel, planes, lanes, rows, out, width, own),
+                functools.partial(pair_values_kernel, planes, lanes, rows, out, width, own, chosen),
                 out_shape=shapes,
                 in_specs=[SMEM, SMEM] + [VMEM] * (pieces + 2 * lanes),
                 out_specs=[VMEM] * len(shapes),
                 compiler_params=pltpu.CompilerParams(vmem_limit_bytes=vmem_room(held)),
-                cost_estimate=cost(2 * panel * items * (part + out), 2 * items * (part + out)),
+                cost_estimate=cost(2 * some * items * (part + out), 2 * items * (part + out)),
                 name="pairs_own" if own else "pairs_far",
             )(block_mask, here, *t_all, *s_all)
         return pl.pallas_call(
@@ -371,10 +377,18 @@
             name="pairs_own" if own else "pairs_far",
         )(block_mask, here, *t_all, *s_all)
 
-    (far_sum,) = pairs(False)
-    far_sum = swapped(far_sum, "narrow", FAR)
-    own_sum, t_keep = pairs(True)
-    sums = own_sum + far_sum.astype(jnp.float32)
+    if whole_tiles:
+        (far_high,) = pairs(False, range(half, planes))
+        far_high = swapped(far_high, "narrow", FAR)
+        (far_low,) = pairs(False, range(half))
+        far_low = swapped(far_low, "narrow", FAR)
+    else:
+        (far_all,) = pairs(False, range(planes))
+        far_high = swapped(far_all[half * rows :], "narrow", FAR)
+        far_low = swapped(far_all[: half * rows], "narrow", FAR)
+    own_sum, t_keep = pairs(True, range(planes))
+    sums_high = own_sum[half * rows :] + far_high.astype(jnp.float32)
+    sums_low = own_sum[: half * rows] + far_low.astype(jnp.float32)
     t_keep = pl.pallas_call(
         flip_kernel,
         out_shape=jax.ShapeDtypeStruct((keep, items), jnp.bfloat16),
@@ -385,9 +399,10 @@
         name="flip",
     )(t_keep)
 
-    grad = after(sums[:rows], t_keep)
+    grad = after(sums_low[:rows], t_keep)
     for k in range(1, planes):
-        piece = sums[k * rows : (k + 1) * rows].astype(jnp.bfloat16)
+        at = k % half * rows
+        piece = (sums_low, sums_high)[k >= half][at : at + rows].astype(jnp.bfloat16)
         grad = grad + swapped(piece, "wide", k).astype(jnp.float32)
     coef = 2.0 * width / (items * out)
     grad = (grad * coef).astype(jnp.bfloat16)

time: 80.7 us -> 78.7 us (0.975)
  waiting for transfers between devices: 31 us -> 26.7 us
  starting transfers between devices: 35 us -> 36.4 us
    ppermute x35 -> x36, waiting for transfers between devices: 31 us -> 26.7 us  [swapped(): lax.ppermute(value, axis, [(source, source ^ bit) for source in range(cou...]
    ppermute x35 -> x36, starting transfers between devices: 35 us -> 36.4 us  [swapped(): lax.ppermute(value, axis, [(source, source ^ bit) for source in range(cou...]
    pallas_call x2 -> x3, Pallas kernels: 5.95 us -> 6.82 us  [pairs(): pl.pallas_call(functools.partial(pair_values_kernel, planes, lanes, rows,...]
  transfers between devices with their start and end apart: 35 -> 36, of which waited for: 15 -> 14; matrix products, arithmetic and copies ran while one was open for 1% -> 1% of each run, Pallas kernels for 10% -> 12%
where the time goes in v4:
time: 78.7 us; the launch traced here: 78.5 us
  starting transfers between devices  36.4 us (46%)
  waiting for transfers between devices  26.7 us (34%)
  Pallas kernels  12.6 us (16%)
  local copies, waits for them, and re-layouts  1.47 us (2%)
  other arithmetic  1.12 us (1%)
    ppermute x36, starting transfers between devices, swapped(): lax.ppermute(value, axis, [(source, source ^ bit) for source in range(cou...  36.4 us
    ppermute x36, waiting for transfers between devices, swapped(): lax.ppermute(value, axis, [(source, source ^ bit) for source in range(cou...  26.7 us
    pallas_call x3, Pallas kernels, pairs(): pl.pallas_call(functools.partial(pair_values_kernel, planes, lanes, rows,...  6.82 us
    pallas_call x1, Pallas kernels, per_device(): pl.pallas_call(functools.partial(student_kernel, steps), out_shape=jax.Sh...  4.15 us
  transfers between devices with their start and end apart: 36, of which 14 were waited for; matrix products, arithmetic and copies ran while one was open for 1% of the time, Pallas kernels for 12%

profile of v4, /device:TPU:0, one launch (start us, length us, event | category | flops | bytes accessed | tf_op | source)
XLA Modules:
  0.0 78.5 jit_solution(14489305925833523268)
XLA Ops:
  0.0 1.4 %constant_dynamic-slice_fusion.3 = (bf16[128,512]{1,0:T(8,128)(2,1)S(1)}, bf16[128,512]{1,0:T(8,128)(2,1)S(1)}, bf16[128,512]{1,0:T(8,128)(2,1)S(1)}, bf16[128,5...) fusion(bf16[128,4096]{1,0:T(8,128)(2,1)} %teacher, ...), kind=kLoop, calls=%fused_computation.15 | loop fusion | bytes 2097184 | tf_op jit(solution)/shard_map/dynamic_slice | solution.py:286
  1.4 3.0 %collective-permute-start.7 = (bf16[512,512]{1,0:T(8,128)(2,1)S(1)}, bf16[512,512]{1,0:T(8,128)(2,1)S(1)}, u32[]{:S(2)}, u32[]{:S(2)}) collective-permute-start(bf16[512,512]{1,0:T(8,128)(2,1)S(1)} %pad_maximum_fusion), channel_id=1, source_target_pairs={{0,2},{1,3},{2,0},{3,1},{4,6},{5,7},{6,4},{7,5},{8,10},{9,11},{10,... | collective-permute-start | bytes 1572872 | tf_op jit(solution)/shard_map/ppermute | solution.py:22
  4.4 3.6 %collective-permute-start.2 = (bf16[128,512]{1,0:T(8,128)(2,1)S(1)}, bf16[128,512]{1,0:T(8,128)(2,1)S(1)}, u32[]{:S(2)}, u32[]{:S(2)}) collective-permute-start(bf16[128,512]{1,0:T(8,128)(2,1)S(1)} %get-tuple-element.34), channel_id=1, source_target_pairs={{0,12},{4,8},{8,4},{12,0},{1,13},{5,9},{9,5},{13,1},{2,14},{6,10},... | collective-permute-start | bytes 393224 | tf_op jit(solution)/shard_map/ppermute | solution.py:22
  8.0 4.1 %student.1 = bf16[144,256]{1,0:T(8,128)(2,1)} custom-call(bf16[128,4096]{1,0:T(8,128)(2,1)} %teacher, f32[4096,256]{1,0:T(8,128)} %weight.1, s32[1,128]{1,0:T(1,128)} %bitcast.3), custom_call_target="tpu_custom_call" | custom-call | flops 268435456 | bytes 5242880 | tf_op jit(solution)/shard_map/student/pallas_call | solution.py:297
  13.0 1.2 %collective-permute-start = (bf16[128,512]{1,0:T(8,128)(2,1)S(1)}, bf16[128,512]{1,0:T(8,128)(2,1)S(1)}, u32[]{:S(2)}, u32[]{:S(2)}) collective-permute-start(bf16[128,512]{1,0:T(8,128)(2,1)S(1)} %get-tuple-element.36), channel_id=1, source_target_pairs={{0,4},{4,0},{8,12},{12,8},{1,5},{5,1},{9,13},{13,9},{2,6},{6,2},{1... | collective-permute-start | bytes 393224 | tf_op jit(solution)/shard_map/ppermute | solution.py:22
  14.3 4.6 %collective-permute-start.16 = (bf16[144,256]{1,0:T(8,128)(2,1)}, bf16[144,256]{1,0:T(8,128)(2,1)S(1)}, u32[]{:S(2)}, u32[]{:S(2)}) collective-permute-start(bf16[144,256]{1,0:T(8,128)(2,1)} %student.1), channel_id=1, source_target_pairs={{0,8},{4,12},{8,0},{12,4},{1,9},{5,13},{9,1},{13,5},{2,10},{6,14},... | collective-permute-start | bytes 221192 | tf_op jit(solution)/shard_map/ppermute | solution.py:22
  18.9 1.3 %collective-permute-done.1.refs_2_ = bf16[128,512]{1,0:T(8,128)(2,1)S(1)} collective-permute-done((bf16[128,512]{1,0:T(8,128)(2,1)S(1)}, bf16[128,512]{1,0:T(8,128)(2,1)S(1)}, u32[]{:S(2)}, u32[]{:S(2)}) %collective-permute-start.1) | collective-permute-done | bytes 131104 | tf_op jit(solution)/shard_map/ppermute | solution.py:22
  20.3 1.4 %collective-permute-done.15 = bf16[144,256]{1,0:T(8,128)(2,1)S(1)} collective-permute-done((bf16[144,256]{1,0:T(8,128)(2,1)}, bf16[144,256]{1,0:T(8,128)(2,1)S(1)}, u32[]{:S(2)}, u32[]{:S(2)}) %collective-permute-start.15) | collective-permute-done | bytes 73760 | tf_op jit(solution)/shard_map/ppermute | solution.py:22
  23.2 1.2 %collective-permute-start.17 = (bf16[144,256]{1,0:T(8,128)(2,1)S(1)}, bf16[144,256]{1,0:T(8,128)(2,1)S(1)}, u32[]{:S(2)}, u32[]{:S(2)}) collective-permute-start(bf16[144,256]{1,0:T(8,128)(2,1)S(1)} %collective-permute-done.16), channel_id=1, source_target_pairs={{0,4},{4,0},{8,12},{12,8},{1,5},{5,1},{9,13},{13,9},{2,6},{6,2},{1... | collective-permute-start | bytes 221192 | tf_op jit(solution)/shard_map/ppermute | solution.py:22
  24.5 2.1 %collective-permute-start.10 = (bf16[128,512]{1,0:T(8,128)(2,1)S(1)}, bf16[128,512]{1,0:T(8,128)(2,1)S(1)}, u32[]{:S(2)}, u32[]{:S(2)}) collective-permute-start(bf16[128,512]{1,0:T(8,128)(2,1)S(1)} %get-tuple-element.41), channel_id=1, source_target_pairs={{0,12},{4,8},{8,4},{12,0},{1,13},{5,9},{9,5},{13,1},{2,14},{6,10},... | collective-permute-start | bytes 393224 | tf_op jit(solution)/shard_map/ppermute | solution.py:22
  27.6 1.4 %collective-permute-start.8 = (bf16[128,512]{1,0:T(8,128)(2,1)S(1)}, bf16[128,512]{1,0:T(8,128)(2,1)S(1)}, u32[]{:S(2)}, u32[]{:S(2)}) collective-permute-start(bf16[128,512]{1,0:T(8,128)(2,1)S(1)} %get-tuple-element.43), channel_id=1, source_target_pairs={{0,4},{4,0},{8,12},{12,8},{1,5},{5,1},{9,13},{13,9},{2,6},{6,2},{1... | collective-permute-start | bytes 393224 | tf_op jit(solution)/shard_map/ppermute | solution.py:22
  29.0 2.1 %collective-permute-start.21 = (bf16[288,256]{1,0:T(8,128)(2,1)S(1)}, bf16[288,256]{1,0:T(8,128)(2,1)S(1)}, u32[]{:S(2)}, u32[]{:S(2)}) collective-permute-start(bf16[288,256]{1,0:T(8,128)(2,1)S(1)} %constant_dynamic-update-slice_fusion.refs_17_), channel_id=1, source_target_pairs={{0,2},{1,3},{2,0},{3,1},{4,6},{5,7},{6,4},{7,5},{8,10},{9,11},{10,... | collective-permute-start | bytes 442376 | tf_op jit(solution)/shard_map/ppermute | solution.py:22
  31.2 1.7 %collective-permute-done.10.refs_3_ = bf16[128,512]{1,0:T(8,128)(2,1)S(1)} collective-permute-done((bf16[128,512]{1,0:T(8,128)(2,1)S(1)}, bf16[128,512]{1,0:T(8,128)(2,1)S(1)}, u32[]{:S(2)}, u32[]{:S(2)}) %collective-permute-start.10) | collective-permute-done | bytes 131104 | tf_op jit(solution)/shard_map/ppermute | solution.py:22
  32.8 5.7 %collective-permute-done.9.refs_2_ = bf16[128,512]{1,0:T(8,128)(2,1)S(1)} collective-permute-done((bf16[128,512]{1,0:T(8,128)(2,1)S(1)}, bf16[128,512]{1,0:T(8,128)(2,1)S(1)}, u32[]{:S(2)}, u32[]{:S(2)}) %collective-permute-start.9) | collective-permute-done | bytes 131104 | tf_op jit(solution)/shard_map/ppermute | solution.py:22
  41.5 1.9 %pairs_far.2 = bf16[256,256]{1,0:T(8,128)(2,1)S(1)} custom-call(s32[4,4]{1,0:T(4,128)S(1)} %copy-done, s32[2]{0:T(128)S(1)} %pad_add_fusion.place, bf16[128,512]{1,0:T(8,128)(2,1)S(1)} %get-tuple-element.37.refs_0_, bf16[128,512]{1,0:T(8,128)(2,1)S(1)} %collective-permute-done.refs_1_, bf16[128,512]{1,0:T(8,128)(2,1)S(1)} %collective-permute-done.1.refs_2_, ...), custom_call_target="tpu_custom_call" | custom-call | flops 805306368 | bytes 3145728 | tf_op jit(solution)/shard_map/pairs_far/pallas_call | solution.py:350
  43.4 1.6 %collective-permute-start.24 = (bf16[256,256]{1,0:T(8,128)(2,1)S(1)}, bf16[256,256]{1,0:T(8,128)(2,1)S(1)}, u32[]{:S(2)}, u32[]{:S(2)}) collective-permute-start(bf16[256,256]{1,0:T(8,128)(2,1)S(1)} %pairs_far.2), channel_id=1, source_target_pairs={{0,2},{1,3},{2,0},{3,1},{4,6},{5,7},{6,4},{7,5},{8,10},{9,11},{10,... | collective-permute-start | bytes 393224 | tf_op jit(solution)/shard_map/ppermute | solution.py:22
  44.9 1.8 %pairs_far.3 = bf16[256,256]{1,0:T(8,128)(2,1)S(1)} custom-call(s32[4,4]{1,0:T(4,128)S(1)} %copy-done, s32[2]{0:T(128)S(1)} %pad_add_fusion.place, bf16[128,512]{1,0:T(8,128)(2,1)S(1)} %get-tuple-element.37.refs_0_, bf16[128,512]{1,0:T(8,128)(2,1)S(1)} %collective-permute-done.refs_1_, bf16[128,512]{1,0:T(8,128)(2,1)S(1)} %collective-permute-done.1.refs_2_, ...), custom_call_target="tpu_custom_call" | custom-call | flops 805306368 | bytes 3145728 | tf_op jit(solution)/shard_map/pairs_far/pallas_call | solution.py:350
  47.4 3.1 %pairs_own.1 = (f32[512,256]{1,0:T(8,128)S(1)}, bf16[2048,256]{1,0:T(8,128)(2,1)S(1)}) custom-call(s32[4,4]{1,0:T(4,128)S(1)} %copy-done, s32[2]{0:T(128)S(1)} %pad_add_fusion.place, bf16[128,512]{1,0:T(8,128)(2,1)S(1)} %get-tuple-element.37.refs_0_, bf16[128,512]{1,0:T(8,128)(2,1)S(1)} %collective-permute-done.refs_1_, ...), custom_call_target="tpu_custom_call" | custom-call | flops 1610612736 | bytes 3145728 | tf_op jit(solution)/shard_map/pairs_own/pallas_call | solution.py:350
  50.5 1.8 %collective-permute-done.26 = bf16[256,256]{1,0:T(8,128)(2,1)S(1)} collective-permute-done((bf16[256,256]{1,0:T(8,128)(2,1)S(1)}, bf16[256,256]{1,0:T(8,128)(2,1)S(1)}, u32[]{:S(2)}, u32[]{:S(2)}) %collective-permute-start.26) | collective-permute-done | bytes 131104 | tf_op jit(solution)/shard_map/ppermute | solution.py:22
  52.5 2.1 %collective-permute-start.27 = (bf16[128,256]{1,0:T(8,128)(2,1)S(1)}, bf16[128,256]{1,0:T(8,128)(2,1)S(1)}, u32[]{:S(2)}, u32[]{:S(2)}) collective-permute-start(bf16[128,256]{1,0:T(8,128)(2,1)S(1)} %get-tuple-element.45), channel_id=1, source_target_pairs={{0,8},{4,12},{8,0},{12,4},{1,9},{5,13},{9,1},{13,5},{2,10},{6,14},... | collective-permute-start | bytes 196616 | tf_op jit(solution)/shard_map/ppermute | solution.py:22
  54.5 2.3 %collective-permute-start.28 = (bf16[128,256]{1,0:T(8,128)(2,1)S(1)}, bf16[128,256]{1,0:T(8,128)(2,1)S(1)}, u32[]{:S(2)}, u32[]{:S(2)}) collective-permute-start(bf16[128,256]{1,0:T(8,128)(2,1)S(1)} %get-tuple-element.46), channel_id=1, source_target_pairs={{0,12},{4,8},{8,4},{12,0},{1,13},{5,9},{9,5},{13,1},{2,14},{6,10},... | collective-permute-start | bytes 196616 | tf_op jit(solution)/shard_map/ppermute | solution.py:22
  57.2 2.2 %collective-permute-done.27 = bf16[128,256]{1,0:T(8,128)(2,1)S(1)} collective-permute-done((bf16[128,256]{1,0:T(8,128)(2,1)S(1)}, bf16[128,256]{1,0:T(8,128)(2,1)S(1)}, u32[]{:S(2)}, u32[]{:S(2)}) %collective-permute-start.27) | collective-permute-done | bytes 65568 | tf_op jit(solution)/shard_map/ppermute | solution.py:22
  59.4 1.3 %collective-permute-done.28 = bf16[128,256]{1,0:T(8,128)(2,1)S(1)} collective-permute-done((bf16[128,256]{1,0:T(8,128)(2,1)S(1)}, bf16[128,256]{1,0:T(8,128)(2,1)S(1)}, u32[]{:S(2)}, u32[]{:S(2)}) %collective-permute-start.28) | collective-permute-done | bytes 65568 | tf_op jit(solution)/shard_map/ppermute | solution.py:22
  60.7 1.2 %collective-permute-start.29 = (bf16[128,256]{1,0:T(8,128)(2,1)S(1)}, bf16[128,256]{1,0:T(8,128)(2,1)S(1)}, u32[]{:S(2)}, u32[]{:S(2)}) collective-permute-start(bf16[128,256]{1,0:T(8,128)(2,1)S(1)} %multiply_convert_fusion), channel_id=1, source_target_pairs={{0,2},{1,3},{2,0},{3,1},{4,6},{5,7},{6,4},{7,5},{8,10},{9,11},{10,... | collective-permute-start | bytes 196616 | tf_op jit(solution)/shard_map/ppermute | solution.py:22
  62.0 2.3 %collective-permute-start.33 = (bf16[128,256]{1,0:T(8,128)(2,1)S(1)}, bf16[128,256]{1,0:T(8,128)(2,1)S(1)}, u32[]{:S(2)}, u32[]{:S(2)}) collective-permute-start(bf16[128,256]{1,0:T(8,128)(2,1)S(1)} %multiply_convert_fusion), channel_id=1, source_target_pairs={{0,12},{4,8},{8,4},{12,0},{1,13},{5,9},{9,5},{13,1},{2,14},{6,10},... | collective-permute-start | bytes 196616 | tf_op jit(solution)/shard_map/ppermute | solution.py:22
  64.4 1.9 %collective-permute-start.31 = (bf16[128,256]{1,0:T(8,128)(2,1)S(1)}, bf16[128,256]{1,0:T(8,128)(2,1)S(1)}, u32[]{:S(2)}, u32[]{:S(2)}) collective-permute-start(bf16[128,256]{1,0:T(8,128)(2,1)S(1)} %multiply_convert_fusion), channel_id=1, source_target_pairs={{0,4},{4,0},{8,12},{12,8},{1,5},{5,1},{9,13},{13,9},{2,6},{6,2},{1... | collective-permute-start | bytes 196616 | tf_op jit(solution)/shard_map/ppermute | solution.py:22
  66.4 1.7 %collective-permute-done.33 = bf16[128,256]{1,0:T(8,128)(2,1)S(1)} collective-permute-done((bf16[128,256]{1,0:T(8,128)(2,1)S(1)}, bf16[128,256]{1,0:T(8,128)(2,1)S(1)}, u32[]{:S(2)}, u32[]{:S(2)}) %collective-permute-start.33) | collective-permute-done | bytes 65568 | tf_op jit(solution)/shard_map/ppermute | solution.py:22
  68.0 1.4 %collective-permute-done.32 = bf16[128,256]{1,0:T(8,128)(2,1)S(1)} collective-permute-done((bf16[128,256]{1,0:T(8,128)(2,1)S(1)}, bf16[128,256]{1,0:T(8,128)(2,1)S(1)}, u32[]{:S(2)}, u32[]{:S(2)}) %collective-permute-start.32) | collective-permute-done | bytes 65568 | tf_op jit(solution)/shard_map/ppermute | solution.py:22
  69.5 0.9 %collective-permute-start.34 = (bf16[384,256]{1,0:T(8,128)(2,1)S(1)}, bf16[384,256]{1,0:T(8,128)(2,1)S(1)}, u32[]{:S(2)}, u32[]{:S(2)}) collective-permute-start(bf16[384,256]{1,0:T(8,128)(2,1)S(1)} %pad_maximum_fusion.1), channel_id=1, source_target_pairs={{0,2},{1,3},{2,0},{3,1},{4,6},{5,7},{6,4},{7,5},{8,10},{9,11},{10,... | collective-permute-start | bytes 589832 | tf_op jit(solution)/shard_map/ppermute | solution.py:22
  70.4 4.8 %collective-permute-done.34 = bf16[384,256]{1,0:T(8,128)(2,1)S(1)} collective-permute-done((bf16[384,256]{1,0:T(8,128)(2,1)S(1)}, bf16[384,256]{1,0:T(8,128)(2,1)S(1)}, u32[]{:S(2)}, u32[]{:S(2)}) %collective-permute-start.34) | collective-permute-done | bytes 196640 | tf_op jit(solution)/shard_map/ppermute | solution.py:22
  75.8 1.4 %collective-permute-done.30.refs_1_ = bf16[256,256]{1,0:T(8,128)(2,1)S(1)} collective-permute-done((bf16[256,256]{1,0:T(8,128)(2,1)S(1)}, bf16[256,256]{1,0:T(8,128)(2,1)S(1)}, u32[]{:S(2)}, u32[]{:S(2)}) %collective-permute-start.30) | collective-permute-done | bytes 131104 | tf_op jit(solution)/shard_map/ppermute | solution.py:22
  77.2 1.3 %last.1 = f32[256,256]{1,0:T(8,128)} custom-call(bf16[256,2048]{1,0:T(8,128)(2,1)S(1)} %flip.1.t_keep, bf16[256,256]{1,0:T(8,128)(2,1)S(1)} %pad_maximum_fusion.3.refs_0_, bf16[256,256]{1,0:T(8,128)(2,1)S(1)} %collective-permute-done.30.refs_1_, bf16[768,256]{1,0:T(8,128)(2,1)S(1)} %constant_dynamic-update-slice_fusion.2.refs_2_, ...), custom_call_target="tpu_custom_call" | custom-call | flops 268435456 | bytes 2097152 | tf_op jit(solution)/shard_map/last/pallas_call | solution.py:414
  (65 shorter events, 8.3 us)
Async XLA Ops:
  1.4 21.8 %collective-permute-start.7 = (bf16[512,512]{1,0:T(8,128)(2,1)S(1)}, bf16[512,512]{1,0:T(8,128)(2,1)S(1)}, u32[]{:S(2)}, u32[]{:S(2)}) collective-permute-start(bf16[512,512]{1,0:T(8,128)(2,1)S(1)} %pad_maximum_fusion), channel_id=1, source_target_pairs={{0,2},{1,3},{2,0},{3,1},{4,6},{5,7},{6,4},{7,5},{8,10},{9,11},{10,... | collective-permute-start | bytes 1572872 | tf_op jit(solution)/shard_map/ppermute | solution.py:22
  4.4 3.6 %collective-permute-start.3 = (bf16[128,512]{1,0:T(8,128)(2,1)S(1)}, bf16[128,512]{1,0:T(8,128)(2,1)S(1)}, u32[]{:S(2)}, u32[]{:S(2)}) collective-permute-start(bf16[128,512]{1,0:T(8,128)(2,1)S(1)} %get-tuple-element.37.refs_0_), channel_id=1, source_target_pairs={{0,1},{1,0},{2,3},{3,2},{4,5},{5,4},{6,7},{7,6},{8,9},{9,8},{10,11... | collective-permute-start | bytes 393224 | tf_op jit(solution)/shard_map/ppermute | solution.py:22
  4.4 9.9 %collective-permute-start.2 = (bf16[128,512]{1,0:T(8,128)(2,1)S(1)}, bf16[128,512]{1,0:T(8,128)(2,1)S(1)}, u32[]{:S(2)}, u32[]{:S(2)}) collective-permute-start(bf16[128,512]{1,0:T(8,128)(2,1)S(1)} %get-tuple-element.34), channel_id=1, source_target_pairs={{0,12},{4,8},{8,4},{12,0},{1,13},{5,9},{9,5},{13,1},{2,14},{6,10},... | collective-permute-start | bytes 393224 | tf_op jit(solution)/shard_map/ppermute | solution.py:22
  8.0 12.2 %collective-permute-start.1 = (bf16[128,512]{1,0:T(8,128)(2,1)S(1)}, bf16[128,512]{1,0:T(8,128)(2,1)S(1)}, u32[]{:S(2)}, u32[]{:S(2)}) collective-permute-start(bf16[128,512]{1,0:T(8,128)(2,1)S(1)} %get-tuple-element.35), channel_id=1, source_target_pairs={{0,8},{4,12},{8,0},{12,4},{1,9},{5,13},{9,1},{13,5},{2,10},{6,14},... | collective-permute-start | bytes 393224 | tf_op jit(solution)/shard_map/ppermute | solution.py:22
  12.2 9.5 %collective-permute-start.15 = (bf16[144,256]{1,0:T(8,128)(2,1)}, bf16[144,256]{1,0:T(8,128)(2,1)S(1)}, u32[]{:S(2)}, u32[]{:S(2)}) collective-permute-start(bf16[144,256]{1,0:T(8,128)(2,1)} %student.1), channel_id=1, source_target_pairs={{0,4},{4,0},{8,12},{12,8},{1,5},{5,1},{9,13},{13,9},{2,6},{6,2},{1... | collective-permute-start | bytes 221192 | tf_op jit(solution)/shard_map/ppermute | solution.py:22
  13.0 11.4 %collective-permute-start = (bf16[128,512]{1,0:T(8,128)(2,1)S(1)}, bf16[128,512]{1,0:T(8,128)(2,1)S(1)}, u32[]{:S(2)}, u32[]{:S(2)}) collective-permute-start(bf16[128,512]{1,0:T(8,128)(2,1)S(1)} %get-tuple-element.36), channel_id=1, source_target_pairs={{0,4},{4,0},{8,12},{12,8},{1,5},{5,1},{9,13},{13,9},{2,6},{6,2},{1... | collective-permute-start | bytes 393224 | tf_op jit(solution)/shard_map/ppermute | solution.py:22
  14.3 8.3 %collective-permute-start.16 = (bf16[144,256]{1,0:T(8,128)(2,1)}, bf16[144,256]{1,0:T(8,128)(2,1)S(1)}, u32[]{:S(2)}, u32[]{:S(2)}) collective-permute-start(bf16[144,256]{1,0:T(8,128)(2,1)} %student.1), channel_id=1, source_target_pairs={{0,8},{4,12},{8,0},{12,4},{1,9},{5,13},{9,1},{13,5},{2,10},{6,14},... | collective-permute-start | bytes 221192 | tf_op jit(solution)/shard_map/ppermute | solution.py:22
  20.3 6.4 %collective-permute-start.6 = (bf16[128,512]{1,0:T(8,128)(2,1)S(1)}, bf16[128,512]{1,0:T(8,128)(2,1)S(1)}, u32[]{:S(2)}, u32[]{:S(2)}) collective-permute-start(bf16[128,512]{1,0:T(8,128)(2,1)S(1)} %collective-permute-done.2.refs_3_), channel_id=1, source_target_pairs={{0,1},{1,0},{2,3},{3,2},{4,5},{5,4},{6,7},{7,6},{8,9},{9,8},{10,11... | collective-permute-start | bytes 393224 | tf_op jit(solution)/shard_map/ppermute | solution.py:22
  21.7 7.3 %collective-permute-start.5 = (bf16[128,512]{1,0:T(8,128)(2,1)S(1)}, bf16[128,512]{1,0:T(8,128)(2,1)S(1)}, u32[]{:S(2)}, u32[]{:S(2)}) collective-permute-start(bf16[128,512]{1,0:T(8,128)(2,1)S(1)} %collective-permute-done.1.refs_2_), channel_id=1, source_target_pairs={{0,1},{1,0},{2,3},{3,2},{4,5},{5,4},{6,7},{7,6},{8,9},{9,8},{10,11... | collective-permute-start | bytes 393224 | tf_op jit(solution)/shard_map/ppermute | solution.py:22
  22.6 8.5 %collective-permute-start.20 = (bf16[288,256]{1,0:T(8,128)(2,1)S(1)}, bf16[288,256]{1,0:T(8,128)(2,1)S(1)}, u32[]{:S(2)}, u32[]{:S(2)}) collective-permute-start(bf16[288,256]{1,0:T(8,128)(2,1)S(1)} %pad_maximum_fusion.2.refs_16_), channel_id=1, source_target_pairs={{0,2},{1,3},{2,0},{3,1},{4,6},{5,7},{6,4},{7,5},{8,10},{9,11},{10,... | collective-permute-start | bytes 442376 | tf_op jit(solution)/shard_map/ppermute | solution.py:22
  23.2 4.4 %collective-permute-start.17 = (bf16[144,256]{1,0:T(8,128)(2,1)S(1)}, bf16[144,256]{1,0:T(8,128)(2,1)S(1)}, u32[]{:S(2)}, u32[]{:S(2)}) collective-permute-start(bf16[144,256]{1,0:T(8,128)(2,1)S(1)} %collective-permute-done.16), channel_id=1, source_target_pairs={{0,4},{4,0},{8,12},{12,8},{1,5},{5,1},{9,13},{13,9},{2,6},{6,2},{1... | collective-permute-start | bytes 221192 | tf_op jit(solution)/shard_map/ppermute | solution.py:22
  24.5 8.3 %collective-permute-start.10 = (bf16[128,512]{1,0:T(8,128)(2,1)S(1)}, bf16[128,512]{1,0:T(8,128)(2,1)S(1)}, u32[]{:S(2)}, u32[]{:S(2)}) collective-permute-start(bf16[128,512]{1,0:T(8,128)(2,1)S(1)} %get-tuple-element.41), channel_id=1, source_target_pairs={{0,12},{4,8},{8,4},{12,0},{1,13},{5,9},{9,5},{13,1},{2,14},{6,10},... | collective-permute-start | bytes 393224 | tf_op jit(solution)/shard_map/ppermute | solution.py:22
  26.6 12.0 %collective-permute-start.9 = (bf16[128,512]{1,0:T(8,128)(2,1)S(1)}, bf16[128,512]{1,0:T(8,128)(2,1)S(1)}, u32[]{:S(2)}, u32[]{:S(2)}) collective-permute-start(bf16[128,512]{1,0:T(8,128)(2,1)S(1)} %get-tuple-element.42), channel_id=1, source_target_pairs={{0,8},{4,12},{8,0},{12,4},{1,9},{5,13},{9,1},{13,5},{2,10},{6,14},... | collective-permute-start | bytes 393224 | tf_op jit(solution)/shard_map/ppermute | solution.py:22
  27.6 11.0 %collective-permute-start.8 = (bf16[128,512]{1,0:T(8,128)(2,1)S(1)}, bf16[128,512]{1,0:T(8,128)(2,1)S(1)}, u32[]{:S(2)}, u32[]{:S(2)}) collective-permute-start(bf16[128,512]{1,0:T(8,128)(2,1)S(1)} %get-tuple-element.43), channel_id=1, source_target_pairs={{0,4},{4,0},{8,12},{12,8},{1,5},{5,1},{9,13},{13,9},{2,6},{6,2},{1... | collective-permute-start | bytes 393224 | tf_op jit(solution)/shard_map/ppermute | solution.py:22
  29.0 10.1 %collective-permute-start.21 = (bf16[288,256]{1,0:T(8,128)(2,1)S(1)}, bf16[288,256]{1,0:T(8,128)(2,1)S(1)}, u32[]{:S(2)}, u32[]{:S(2)}) collective-permute-start(bf16[288,256]{1,0:T(8,128)(2,1)S(1)} %constant_dynamic-update-slice_fusion.refs_17_), channel_id=1, source_target_pairs={{0,2},{1,3},{2,0},{3,1},{4,6},{5,7},{6,4},{7,5},{8,10},{9,11},{10,... | collective-permute-start | bytes 442376 | tf_op jit(solution)/shard_map/ppermute | solution.py:22
  31.2 8.0 %collective-permute-start.11 = (bf16[128,512]{1,0:T(8,128)(2,1)S(1)}, bf16[128,512]{1,0:T(8,128)(2,1)S(1)}, u32[]{:S(2)}, u32[]{:S(2)}) collective-permute-start(bf16[128,512]{1,0:T(8,128)(2,1)S(1)} %get-tuple-element.44.refs_0_), channel_id=1, source_target_pairs={{0,1},{1,0},{2,3},{3,2},{4,5},{5,4},{6,7},{7,6},{8,9},{9,8},{10,11... | collective-permute-start | bytes 393224 | tf_op jit(solution)/shard_map/ppermute | solution.py:22
  32.8 6.8 %collective-permute-start.14 = (bf16[128,512]{1,0:T(8,128)(2,1)S(1)}, bf16[128,512]{1,0:T(8,128)(2,1)S(1)}, u32[]{:S(2)}, u32[]{:S(2)}) collective-permute-start(bf16[128,512]{1,0:T(8,128)(2,1)S(1)} %collective-permute-done.10.refs_3_), channel_id=1, source_target_pairs={{0,1},{1,0},{2,3},{3,2},{4,5},{5,4},{6,7},{7,6},{8,9},{9,8},{10,11... | collective-permute-start | bytes 393224 | tf_op jit(solution)/shard_map/ppermute | solution.py:22
  39.1 2.4 %collective-permute-start.18 = (bf16[288,256]{1,0:T(8,128)(2,1)S(1)}, bf16[288,256]{1,0:T(8,128)(2,1)S(1)}, u32[]{:S(2)}, u32[]{:S(2)}) collective-permute-start(bf16[288,256]{1,0:T(8,128)(2,1)S(1)} %pad_maximum_fusion.2.refs_16_), channel_id=1, source_target_pairs={{0,1},{1,0},{2,3},{3,2},{4,5},{5,4},{6,7},{7,6},{8,9},{9,8},{10,11... | collective-permute-start | bytes 442376 | tf_op jit(solution)/shard_map/ppermute | solution.py:22
  39.2 2.3 %collective-permute-start.19 = (bf16[288,256]{1,0:T(8,128)(2,1)S(1)}, bf16[288,256]{1,0:T(8,128)(2,1)S(1)}, u32[]{:S(2)}, u32[]{:S(2)}) collective-permute-start(bf16[288,256]{1,0:T(8,128)(2,1)S(1)} %constant_dynamic-update-slice_fusion.refs_17_), channel_id=1, source_target_pairs={{0,1},{1,0},{2,3},{3,2},{4,5},{5,4},{6,7},{7,6},{8,9},{9,8},{10,11... | collective-permute-start | bytes 442376 | tf_op jit(solution)/shard_map/ppermute | solution.py:22
  39.6 1.9 %collective-permute-start.22 = (bf16[288,256]{1,0:T(8,128)(2,1)S(1)}, bf16[288,256]{1,0:T(8,128)(2,1)S(1)}, u32[]{:S(2)}, u32[]{:S(2)}) collective-permute-start(bf16[288,256]{1,0:T(8,128)(2,1)S(1)} %collective-permute-done.20.refs_20_), channel_id=1, source_target_pairs={{0,1},{1,0},{2,3},{3,2},{4,5},{5,4},{6,7},{7,6},{8,9},{9,8},{10,11... | collective-permute-start | bytes 442376 | tf_op jit(solution)/shard_map/ppermute | solution.py:22
  43.4 7.1 %collective-permute-start.24 = (bf16[256,256]{1,0:T(8,128)(2,1)S(1)}, bf16[256,256]{1,0:T(8,128)(2,1)S(1)}, u32[]{:S(2)}, u32[]{:S(2)}) collective-permute-start(bf16[256,256]{1,0:T(8,128)(2,1)S(1)} %pairs_far.2), channel_id=1, source_target_pairs={{0,2},{1,3},{2,0},{3,1},{4,6},{5,7},{6,4},{7,5},{8,10},{9,11},{10,... | collective-permute-start | bytes 393224 | tf_op jit(solution)/shard_map/ppermute | solution.py:22
  46.8 5.5 %collective-permute-start.26 = (bf16[256,256]{1,0:T(8,128)(2,1)S(1)}, bf16[256,256]{1,0:T(8,128)(2,1)S(1)}, u32[]{:S(2)}, u32[]{:S(2)}) collective-permute-start(bf16[256,256]{1,0:T(8,128)(2,1)S(1)} %pairs_far.3), channel_id=1, source_target_pairs={{0,2},{1,3},{2,0},{3,1},{4,6},{5,7},{6,4},{7,5},{8,10},{9,11},{10,... | collective-permute-start | bytes 393224 | tf_op jit(solution)/shard_map/ppermute | solution.py:22
  52.4 4.8 %collective-permute-start.25 = (bf16[128,256]{1,0:T(8,128)(2,1)S(1)}, bf16[128,256]{1,0:T(8,128)(2,1)S(1)}, u32[]{:S(2)}, u32[]{:S(2)}) collective-permute-start(bf16[128,256]{1,0:T(8,128)(2,1)S(1)} %slice.54), channel_id=1, source_target_pairs={{0,4},{4,0},{8,12},{12,8},{1,5},{5,1},{9,13},{13,9},{2,6},{6,2},{1... | collective-permute-start | bytes 196616 | tf_op jit(solution)/shard_map/ppermute | solution.py:22
  52.5 6.9 %collective-permute-start.27 = (bf16[128,256]{1,0:T(8,128)(2,1)S(1)}, bf16[128,256]{1,0:T(8,128)(2,1)S(1)}, u32[]{:S(2)}, u32[]{:S(2)}) collective-permute-start(bf16[128,256]{1,0:T(8,128)(2,1)S(1)} %get-tuple-element.45), channel_id=1, source_target_pairs={{0,8},{4,12},{8,0},{12,4},{1,9},{5,13},{9,1},{13,5},{2,10},{6,14},... | collective-permute-start | bytes 196616 | tf_op jit(solution)/shard_map/ppermute | solution.py:22
  54.5 6.2 %collective-permute-start.28 = (bf16[128,256]{1,0:T(8,128)(2,1)S(1)}, bf16[128,256]{1,0:T(8,128)(2,1)S(1)}, u32[]{:S(2)}, u32[]{:S(2)}) collective-permute-start(bf16[128,256]{1,0:T(8,128)(2,1)S(1)} %get-tuple-element.46), channel_id=1, source_target_pairs={{0,12},{4,8},{8,4},{12,0},{1,13},{5,9},{9,5},{13,1},{2,14},{6,10},... | collective-permute-start | bytes 196616 | tf_op jit(solution)/shard_map/ppermute | solution.py:22
  60.7 5.6 %collective-permute-start.29 = (bf16[128,256]{1,0:T(8,128)(2,1)S(1)}, bf16[128,256]{1,0:T(8,128)(2,1)S(1)}, u32[]{:S(2)}, u32[]{:S(2)}) collective-permute-start(bf16[128,256]{1,0:T(8,128)(2,1)S(1)} %multiply_convert_fusion), channel_id=1, source_target_pairs={{0,2},{1,3},{2,0},{3,1},{4,6},{5,7},{6,4},{7,5},{8,10},{9,11},{10,... | collective-permute-start | bytes 196616 | tf_op jit(solution)/shard_map/ppermute | solution.py:22
  62.0 6.1 %collective-permute-start.33 = (bf16[128,256]{1,0:T(8,128)(2,1)S(1)}, bf16[128,256]{1,0:T(8,128)(2,1)S(1)}, u32[]{:S(2)}, u32[]{:S(2)}) collective-permute-start(bf16[128,256]{1,0:T(8,128)(2,1)S(1)} %multiply_convert_fusion), channel_id=1, source_target_pairs={{0,12},{4,8},{8,4},{12,0},{1,13},{5,9},{9,5},{13,1},{2,14},{6,10},... | collective-permute-start | bytes 196616 | tf_op jit(solution)/shard_map/ppermute | solution.py:22
  64.3 5.2 %collective-permute-start.32 = (bf16[128,256]{1,0:T(8,128)(2,1)S(1)}, bf16[128,256]{1,0:T(8,128)(2,1)S(1)}, u32[]{:S(2)}, u32[]{:S(2)}) collective-permute-start(bf16[128,256]{1,0:T(8,128)(2,1)S(1)} %multiply_convert_fusion), channel_id=1, source_target_pairs={{0,8},{4,12},{8,0},{12,4},{1,9},{5,13},{9,1},{13,5},{2,10},{6,14},... | collective-permute-start | bytes 196616 | tf_op jit(solution)/shard_map/ppermute | solution.py:22
  64.4 5.0 %collective-permute-start.31 = (bf16[128,256]{1,0:T(8,128)(2,1)S(1)}, bf16[128,256]{1,0:T(8,128)(2,1)S(1)}, u32[]{:S(2)}, u32[]{:S(2)}) collective-permute-start(bf16[128,256]{1,0:T(8,128)(2,1)S(1)} %multiply_convert_fusion), channel_id=1, source_target_pairs={{0,4},{4,0},{8,12},{12,8},{1,5},{5,1},{9,13},{13,9},{2,6},{6,2},{1... | collective-permute-start | bytes 196616 | tf_op jit(solution)/shard_map/ppermute | solution.py:22
  69.5 5.7 %collective-permute-start.34 = (bf16[384,256]{1,0:T(8,128)(2,1)S(1)}, bf16[384,256]{1,0:T(8,128)(2,1)S(1)}, u32[]{:S(2)}, u32[]{:S(2)}) collective-permute-start(bf16[384,256]{1,0:T(8,128)(2,1)S(1)} %pad_maximum_fusion.1), channel_id=1, source_target_pairs={{0,2},{1,3},{2,0},{3,1},{4,6},{5,7},{6,4},{7,5},{8,10},{9,11},{10,... | collective-permute-start | bytes 589832 | tf_op jit(solution)/shard_map/ppermute | solution.py:22
  75.2 2.0 %collective-permute-start.35 = (bf16[768,256]{1,0:T(8,128)(2,1)S(1)}, bf16[768,256]{1,0:T(8,128)(2,1)S(1)}, u32[]{:S(2)}, u32[]{:S(2)}) collective-permute-start(bf16[768,256]{1,0:T(8,128)(2,1)S(1)} %constant_dynamic-update-slice_fusion.2.refs_2_), channel_id=1, source_target_pairs={{0,1},{1,0},{2,3},{3,2},{4,5},{5,4},{6,7},{7,6},{8,9},{9,8},{10,11... | collective-permute-start | bytes 1179656 | tf_op jit(solution)/shard_map/ppermute | solution.py:22
  75.3 1.9 %collective-permute-start.30 = (bf16[256,256]{1,0:T(8,128)(2,1)S(1)}, bf16[256,256]{1,0:T(8,128)(2,1)S(1)}, u32[]{:S(2)}, u32[]{:S(2)}) collective-permute-start(bf16[256,256]{1,0:T(8,128)(2,1)S(1)} %pad_maximum_fusion.3.refs_0_), channel_id=1, source_target_pairs={{0,1},{1,0},{2,3},{3,2},{4,5},{5,4},{6,7},{7,6},{8,9},{9,8},{10,11... | collective-permute-start | bytes 393224 | tf_op jit(solution)/shard_map/ppermute | solution.py:22
  (5 other events, 45.9 us)

commit v5 on v4

--- a/solution.py
+++ b/solution.py
@@ -253,9 +253,9 @@
     g_in, result = refs[:4], refs[4]
     total = None
     for at in range(4):
-        count = 1 if at < 2 else planes - 1
+        count = NEAR if at < 2 else planes - NEAR
         for far in range(lanes // 2):
-            first = (2 * far + at % 2) * planes + (at >= 2)
+            first = (2 * far + at % 2) * planes + (at >= 2) * NEAR
             one = jnp.dot(
                 t_keep[:, first * rows : (first + count) * rows],
                 g_in[at][far * count * rows : (far + 1) * count * rows, :],
@@ -407,8 +407,9 @@
     coef = 2.0 * width / (items * out)
     grad = (grad * coef).astype(jnp.bfloat16)
     g_parts = [swapped(grad, "wide", k) for k in range(1, planes)]
-    g_near = jnp.concatenate([grad, swapped(grad, "narrow", FAR)], 0)
-    g_rest = after(jnp.concatenate(g_parts, 0), g_near)
+    g_near = jnp.concatenate([grad, *g_parts[: NEAR - 1]], 0)
+    g_near = jnp.concatenate([g_near, swapped(g_near, "narrow", FAR)], 0)
+    g_rest = jnp.concatenate(g_parts[NEAR - 1 :], 0)
     g_rest = jnp.concatenate([g_rest, swapped(g_rest, "narrow", FAR)], 0)
     g_all = [g_near, swapped(g_near, "narrow", CORE), g_rest, swapped(g_rest, "narrow", CORE)]
     return pl.pallas_call(

time: 78.7 us -> 77.8 us (0.989)
  transfers between devices with their start and end apart: 36 -> 36, of which waited for: 14 -> 16; matrix products, arithmetic and copies ran while one was open for 1% -> 1% of each run, Pallas kernels for 12% -> 12%
where the time goes in v5:
time: 77.8 us; the launch traced here: 77.7 us
  starting transfers between devices  36 us (46%)
  waiting for transfers between devices  26.3 us (34%)
  Pallas kernels  12.5 us (16%)
  local copies, waits for them, and re-layouts  1.46 us (2%)
  other arithmetic  1.14 us (1%)
    ppermute x36, starting transfers between devices, swapped(): lax.ppermute(value, axis, [(source, source ^ bit) for source in range(cou...  36 us
    ppermute x36, waiting for transfers between devices, swapped(): lax.ppermute(value, axis, [(source, source ^ bit) for source in range(cou...  26.3 us
    pallas_call x3, Pallas kernels, pairs(): pl.pallas_call(functools.partial(pair_values_kernel, planes, lanes, rows,...  6.82 us
    pallas_call x1, Pallas kernels, per_device(): pl.pallas_call(functools.partial(student_kernel, steps), out_shape=jax.Sh...  4.15 us
  transfers between devices with their start and end apart: 36, of which 16 were waited for; matrix products, arithmetic and copies ran while one was open for 1% of the time, Pallas kernels for 12%

profile of v5, /device:TPU:0, one launch (start us, length us, event | category | flops | bytes accessed | tf_op | source)
XLA Modules:
  0.0 77.7 jit_solution(2336895669207604518)
XLA Ops:
  0.0 1.4 %constant_dynamic-slice_fusion.3 = (bf16[128,512]{1,0:T(8,128)(2,1)S(1)}, bf16[128,512]{1,0:T(8,128)(2,1)S(1)}, bf16[128,512]{1,0:T(8,128)(2,1)S(1)}, bf16[128,5...) fusion(bf16[128,4096]{1,0:T(8,128)(2,1)} %teacher, ...), kind=kLoop, calls=%fused_computation.17 | loop fusion | bytes 2097184 | tf_op jit(solution)/shard_map/dynamic_slice | solution.py:286
  1.4 3.0 %collective-permute-start.7 = (bf16[512,512]{1,0:T(8,128)(2,1)S(1)}, bf16[512,512]{1,0:T(8,128)(2,1)S(1)}, u32[]{:S(2)}, u32[]{:S(2)}) collective-permute-start(bf16[512,512]{1,0:T(8,128)(2,1)S(1)} %pad_maximum_fusion), channel_id=1, source_target_pairs={{0,2},{1,3},{2,0},{3,1},{4,6},{5,7},{6,4},{7,5},{8,10},{9,11},{10,... | collective-permute-start | bytes 1572872 | tf_op jit(solution)/shard_map/ppermute | solution.py:22
  4.4 3.6 %collective-permute-start.2 = (bf16[128,512]{1,0:T(8,128)(2,1)S(1)}, bf16[128,512]{1,0:T(8,128)(2,1)S(1)}, u32[]{:S(2)}, u32[]{:S(2)}) collective-permute-start(bf16[128,512]{1,0:T(8,128)(2,1)S(1)} %get-tuple-element.32), channel_id=1, source_target_pairs={{0,12},{4,8},{8,4},{12,0},{1,13},{5,9},{9,5},{13,1},{2,14},{6,10},... | collective-permute-start | bytes 393224 | tf_op jit(solution)/shard_map/ppermute | solution.py:22
  8.0 4.1 %student.1 = bf16[144,256]{1,0:T(8,128)(2,1)} custom-call(bf16[128,4096]{1,0:T(8,128)(2,1)} %teacher, f32[4096,256]{1,0:T(8,128)} %weight.1, s32[1,128]{1,0:T(1,128)} %bitcast.3), custom_call_target="tpu_custom_call" | custom-call | flops 268435456 | bytes 5242880 | tf_op jit(solution)/shard_map/student/pallas_call | solution.py:297
  13.0 1.2 %collective-permute-start = (bf16[128,512]{1,0:T(8,128)(2,1)S(1)}, bf16[128,512]{1,0:T(8,128)(2,1)S(1)}, u32[]{:S(2)}, u32[]{:S(2)}) collective-permute-start(bf16[128,512]{1,0:T(8,128)(2,1)S(1)} %get-tuple-element.34), channel_id=1, source_target_pairs={{0,4},{4,0},{8,12},{12,8},{1,5},{5,1},{9,13},{13,9},{2,6},{6,2},{1... | collective-permute-start | bytes 393224 | tf_op jit(solution)/shard_map/ppermute | solution.py:22
  14.3 4.6 %collective-permute-start.16 = (bf16[144,256]{1,0:T(8,128)(2,1)}, bf16[144,256]{1,0:T(8,128)(2,1)S(1)}, u32[]{:S(2)}, u32[]{:S(2)}) collective-permute-start(bf16[144,256]{1,0:T(8,128)(2,1)} %student.1), channel_id=1, source_target_pairs={{0,8},{4,12},{8,0},{12,4},{1,9},{5,13},{9,1},{13,5},{2,10},{6,14},... | collective-permute-start | bytes 221192 | tf_op jit(solution)/shard_map/ppermute | solution.py:22
  18.9 1.3 %collective-permute-done.1.refs_2_ = bf16[128,512]{1,0:T(8,128)(2,1)S(1)} collective-permute-done((bf16[128,512]{1,0:T(8,128)(2,1)S(1)}, bf16[128,512]{1,0:T(8,128)(2,1)S(1)}, u32[]{:S(2)}, u32[]{:S(2)}) %collective-permute-start.1) | collective-permute-done | bytes 131104 | tf_op jit(solution)/shard_map/ppermute | solution.py:22
  20.3 1.4 %collective-permute-done.15 = bf16[144,256]{1,0:T(8,128)(2,1)S(1)} collective-permute-done((bf16[144,256]{1,0:T(8,128)(2,1)}, bf16[144,256]{1,0:T(8,128)(2,1)S(1)}, u32[]{:S(2)}, u32[]{:S(2)}) %collective-permute-start.15) | collective-permute-done | bytes 73760 | tf_op jit(solution)/shard_map/ppermute | solution.py:22
  23.2 1.2 %collective-permute-start.17 = (bf16[144,256]{1,0:T(8,128)(2,1)S(1)}, bf16[144,256]{1,0:T(8,128)(2,1)S(1)}, u32[]{:S(2)}, u32[]{:S(2)}) collective-permute-start(bf16[144,256]{1,0:T(8,128)(2,1)S(1)} %collective-permute-done.16), channel_id=1, source_target_pairs={{0,4},{4,0},{8,12},{12,8},{1,5},{5,1},{9,13},{13,9},{2,6},{6,2},{1... | collective-permute-start | bytes 221192 | tf_op jit(solution)/shard_map/ppermute | solution.py:22
  24.5 2.1 %collective-permute-start.10 = (bf16[128,512]{1,0:T(8,128)(2,1)S(1)}, bf16[128,512]{1,0:T(8,128)(2,1)S(1)}, u32[]{:S(2)}, u32[]{:S(2)}) collective-permute-start(bf16[128,512]{1,0:T(8,128)(2,1)S(1)} %get-tuple-element.39), channel_id=1, source_target_pairs={{0,12},{4,8},{8,4},{12,0},{1,13},{5,9},{9,5},{13,1},{2,14},{6,10},... | collective-permute-start | bytes 393224 | tf_op jit(solution)/shard_map/ppermute | solution.py:22
  27.6 1.4 %collective-permute-start.8 = (bf16[128,512]{1,0:T(8,128)(2,1)S(1)}, bf16[128,512]{1,0:T(8,128)(2,1)S(1)}, u32[]{:S(2)}, u32[]{:S(2)}) collective-permute-start(bf16[128,512]{1,0:T(8,128)(2,1)S(1)} %get-tuple-element.41), channel_id=1, source_target_pairs={{0,4},{4,0},{8,12},{12,8},{1,5},{5,1},{9,13},{13,9},{2,6},{6,2},{1... | collective-permute-start | bytes 393224 | tf_op jit(solution)/shard_map/ppermute | solution.py:22
  29.0 2.1 %collective-permute-start.21 = (bf16[288,256]{1,0:T(8,128)(2,1)S(1)}, bf16[288,256]{1,0:T(8,128)(2,1)S(1)}, u32[]{:S(2)}, u32[]{:S(2)}) collective-permute-start(bf16[288,256]{1,0:T(8,128)(2,1)S(1)} %constant_dynamic-update-slice_fusion.refs_17_), channel_id=1, source_target_pairs={{0,2},{1,3},{2,0},{3,1},{4,6},{5,7},{6,4},{7,5},{8,10},{9,11},{10,... | collective-permute-start | bytes 442376 | tf_op jit(solution)/shard_map/ppermute | solution.py:22
  31.2 1.7 %collective-permute-done.10.refs_3_ = bf16[128,512]{1,0:T(8,128)(2,1)S(1)} collective-permute-done((bf16[128,512]{1,0:T(8,128)(2,1)S(1)}, bf16[128,512]{1,0:T(8,128)(2,1)S(1)}, u32[]{:S(2)}, u32[]{:S(2)}) %collective-permute-start.10) | collective-permute-done | bytes 131104 | tf_op jit(solution)/shard_map/ppermute | solution.py:22
  32.8 5.7 %collective-permute-done.9.refs_2_ = bf16[128,512]{1,0:T(8,128)(2,1)S(1)} collective-permute-done((bf16[128,512]{1,0:T(8,128)(2,1)S(1)}, bf16[128,512]{1,0:T(8,128)(2,1)S(1)}, u32[]{:S(2)}, u32[]{:S(2)}) %collective-permute-start.9) | collective-permute-done | bytes 131104 | tf_op jit(solution)/shard_map/ppermute | solution.py:22
  41.5 1.9 %pairs_far.2 = bf16[256,256]{1,0:T(8,128)(2,1)S(1)} custom-call(s32[4,4]{1,0:T(4,128)S(1)} %copy-done, s32[2]{0:T(128)S(1)} %pad_add_fusion.place, bf16[128,512]{1,0:T(8,128)(2,1)S(1)} %get-tuple-element.35.refs_0_, bf16[128,512]{1,0:T(8,128)(2,1)S(1)} %collective-permute-done.refs_1_, bf16[128,512]{1,0:T(8,128)(2,1)S(1)} %collective-permute-done.1.refs_2_, ...), custom_call_target="tpu_custom_call" | custom-call | flops 805306368 | bytes 3145728 | tf_op jit(solution)/shard_map/pairs_far/pallas_call | solution.py:350
  43.4 1.6 %collective-permute-start.24 = (bf16[256,256]{1,0:T(8,128)(2,1)S(1)}, bf16[256,256]{1,0:T(8,128)(2,1)S(1)}, u32[]{:S(2)}, u32[]{:S(2)}) collective-permute-start(bf16[256,256]{1,0:T(8,128)(2,1)S(1)} %pairs_far.2), channel_id=1, source_target_pairs={{0,2},{1,3},{2,0},{3,1},{4,6},{5,7},{6,4},{7,5},{8,10},{9,11},{10,... | collective-permute-start | bytes 393224 | tf_op jit(solution)/shard_map/ppermute | solution.py:22
  44.9 1.8 %pairs_far.3 = bf16[256,256]{1,0:T(8,128)(2,1)S(1)} custom-call(s32[4,4]{1,0:T(4,128)S(1)} %copy-done, s32[2]{0:T(128)S(1)} %pad_add_fusion.place, bf16[128,512]{1,0:T(8,128)(2,1)S(1)} %get-tuple-element.35.refs_0_, bf16[128,512]{1,0:T(8,128)(2,1)S(1)} %collective-permute-done.refs_1_, bf16[128,512]{1,0:T(8,128)(2,1)S(1)} %collective-permute-done.1.refs_2_, ...), custom_call_target="tpu_custom_call" | custom-call | flops 805306368 | bytes 3145728 | tf_op jit(solution)/shard_map/pairs_far/pallas_call | solution.py:350
  47.4 3.1 %pairs_own.1 = (f32[512,256]{1,0:T(8,128)S(1)}, bf16[2048,256]{1,0:T(8,128)(2,1)S(1)}) custom-call(s32[4,4]{1,0:T(4,128)S(1)} %copy-done, s32[2]{0:T(128)S(1)} %pad_add_fusion.place, bf16[128,512]{1,0:T(8,128)(2,1)S(1)} %get-tuple-element.35.refs_0_, bf16[128,512]{1,0:T(8,128)(2,1)S(1)} %collective-permute-done.refs_1_, ...), custom_call_target="tpu_custom_call" | custom-call | flops 1610612736 | bytes 3145728 | tf_op jit(solution)/shard_map/pairs_own/pallas_call | solution.py:350
  50.5 1.8 %collective-permute-done.26 = bf16[256,256]{1,0:T(8,128)(2,1)S(1)} collective-permute-done((bf16[256,256]{1,0:T(8,128)(2,1)S(1)}, bf16[256,256]{1,0:T(8,128)(2,1)S(1)}, u32[]{:S(2)}, u32[]{:S(2)}) %collective-permute-start.26) | collective-permute-done | bytes 131104 | tf_op jit(solution)/shard_map/ppermute | solution.py:22
  52.5 2.1 %collective-permute-start.27 = (bf16[128,256]{1,0:T(8,128)(2,1)S(1)}, bf16[128,256]{1,0:T(8,128)(2,1)S(1)}, u32[]{:S(2)}, u32[]{:S(2)}) collective-permute-start(bf16[128,256]{1,0:T(8,128)(2,1)S(1)} %get-tuple-element.43), channel_id=1, source_target_pairs={{0,8},{4,12},{8,0},{12,4},{1,9},{5,13},{9,1},{13,5},{2,10},{6,14},... | collective-permute-start | bytes 196616 | tf_op jit(solution)/shard_map/ppermute | solution.py:22
  54.5 2.3 %collective-permute-start.28 = (bf16[128,256]{1,0:T(8,128)(2,1)S(1)}, bf16[128,256]{1,0:T(8,128)(2,1)S(1)}, u32[]{:S(2)}, u32[]{:S(2)}) collective-permute-start(bf16[128,256]{1,0:T(8,128)(2,1)S(1)} %get-tuple-element.44), channel_id=1, source_target_pairs={{0,12},{4,8},{8,4},{12,0},{1,13},{5,9},{9,5},{13,1},{2,14},{6,10},... | collective-permute-start | bytes 196616 | tf_op jit(solution)/shard_map/ppermute | solution.py:22
  57.2 2.2 %collective-permute-done.27 = bf16[128,256]{1,0:T(8,128)(2,1)S(1)} collective-permute-done((bf16[128,256]{1,0:T(8,128)(2,1)S(1)}, bf16[128,256]{1,0:T(8,128)(2,1)S(1)}, u32[]{:S(2)}, u32[]{:S(2)}) %collective-permute-start.27) | collective-permute-done | bytes 65568 | tf_op jit(solution)/shard_map/ppermute | solution.py:22
  59.4 1.3 %collective-permute-done.28 = bf16[128,256]{1,0:T(8,128)(2,1)S(1)} collective-permute-done((bf16[128,256]{1,0:T(8,128)(2,1)S(1)}, bf16[128,256]{1,0:T(8,128)(2,1)S(1)}, u32[]{:S(2)}, u32[]{:S(2)}) %collective-permute-start.28) | collective-permute-done | bytes 65568 | tf_op jit(solution)/shard_map/ppermute | solution.py:22
  60.7 2.4 %collective-permute-start.33 = (bf16[128,256]{1,0:T(8,128)(2,1)S(1)}, bf16[128,256]{1,0:T(8,128)(2,1)S(1)}, u32[]{:S(2)}, u32[]{:S(2)}) collective-permute-start(bf16[128,256]{1,0:T(8,128)(2,1)S(1)} %multiply_convert_fusion), channel_id=1, source_target_pairs={{0,12},{4,8},{8,4},{12,0},{1,13},{5,9},{9,5},{13,1},{2,14},{6,10},... | collective-permute-start | bytes 196616 | tf_op jit(solution)/shard_map/ppermute | solution.py:22
  63.1 2.1 %collective-permute-start.29 = (bf16[128,256]{1,0:T(8,128)(2,1)S(1)}, bf16[128,256]{1,0:T(8,128)(2,1)S(1)}, u32[]{:S(2)}, u32[]{:S(2)}) collective-permute-start(bf16[128,256]{1,0:T(8,128)(2,1)S(1)} %multiply_convert_fusion), channel_id=1, source_target_pairs={{0,4},{4,0},{8,12},{12,8},{1,5},{5,1},{9,13},{13,9},{2,6},{6,2},{1... | collective-permute-start | bytes 196616 | tf_op jit(solution)/shard_map/ppermute | solution.py:22
  65.2 1.9 %collective-permute-done.33 = bf16[128,256]{1,0:T(8,128)(2,1)S(1)} collective-permute-done((bf16[128,256]{1,0:T(8,128)(2,1)S(1)}, bf16[128,256]{1,0:T(8,128)(2,1)S(1)}, u32[]{:S(2)}, u32[]{:S(2)}) %collective-permute-start.33) | collective-permute-done | bytes 65568 | tf_op jit(solution)/shard_map/ppermute | solution.py:22
  67.1 1.4 %collective-permute-done.32 = bf16[128,256]{1,0:T(8,128)(2,1)S(1)} collective-permute-done((bf16[128,256]{1,0:T(8,128)(2,1)S(1)}, bf16[128,256]{1,0:T(8,128)(2,1)S(1)}, u32[]{:S(2)}, u32[]{:S(2)}) %collective-permute-start.32) | collective-permute-done | bytes 65568 | tf_op jit(solution)/shard_map/ppermute | solution.py:22
  68.4 1.3 %collective-permute-start.34 = (bf16[256,256]{1,0:T(8,128)(2,1)S(1)}, bf16[256,256]{1,0:T(8,128)(2,1)S(1)}, u32[]{:S(2)}, u32[]{:S(2)}) collective-permute-start(bf16[256,256]{1,0:T(8,128)(2,1)S(1)} %pad_maximum_fusion.4), channel_id=1, source_target_pairs={{0,2},{1,3},{2,0},{3,1},{4,6},{5,7},{6,4},{7,5},{8,10},{9,11},{10,... | collective-permute-start | bytes 393224 | tf_op jit(solution)/shard_map/ppermute | solution.py:22
  70.6 2.8 %collective-permute-done.34 = bf16[256,256]{1,0:T(8,128)(2,1)S(1)} collective-permute-done((bf16[256,256]{1,0:T(8,128)(2,1)S(1)}, bf16[256,256]{1,0:T(8,128)(2,1)S(1)}, u32[]{:S(2)}, u32[]{:S(2)}) %collective-permute-start.34) | collective-permute-done | bytes 131104 | tf_op jit(solution)/shard_map/ppermute | solution.py:22
  73.6 1.3 %collective-permute-done.30 = bf16[256,256]{1,0:T(8,128)(2,1)S(1)} collective-permute-done((bf16[256,256]{1,0:T(8,128)(2,1)S(1)}, bf16[256,256]{1,0:T(8,128)(2,1)S(1)}, u32[]{:S(2)}, u32[]{:S(2)}) %collective-permute-start.30) | collective-permute-done | bytes 131104 | tf_op jit(solution)/shard_map/ppermute | solution.py:22
  75.1 1.4 %collective-permute-done.31.refs_1_ = bf16[512,256]{1,0:T(8,128)(2,1)S(1)} collective-permute-done((bf16[512,256]{1,0:T(8,128)(2,1)S(1)}, bf16[512,256]{1,0:T(8,128)(2,1)S(1)}, u32[]{:S(2)}, u32[]{:S(2)}) %collective-permute-start.31) | collective-permute-done | bytes 262176 | tf_op jit(solution)/shard_map/ppermute | solution.py:22
  76.5 1.1 %last.1 = f32[256,256]{1,0:T(8,128)} custom-call(bf16[256,2048]{1,0:T(8,128)(2,1)S(1)} %flip.1.t_keep, bf16[512,256]{1,0:T(8,128)(2,1)S(1)} %pad_maximum_fusion.1.refs_0_, bf16[512,256]{1,0:T(8,128)(2,1)S(1)} %collective-permute-done.31.refs_1_, bf16[512,256]{1,0:T(8,128)(2,1)S(1)} %constant_dynamic-update-slice_fusion.2.refs_2_, ...), custom_call_target="tpu_custom_call" | custom-call | flops 268435456 | bytes 2097152 | tf_op jit(solution)/shard_map/last/pallas_call | solution.py:415
  (67 shorter events, 8.7 us)
Async XLA Ops:
  1.4 21.8 %collective-permute-start.7 = (bf16[512,512]{1,0:T(8,128)(2,1)S(1)}, bf16[512,512]{1,0:T(8,128)(2,1)S(1)}, u32[]{:S(2)}, u32[]{:S(2)}) collective-permute-start(bf16[512,512]{1,0:T(8,128)(2,1)S(1)} %pad_maximum_fusion), channel_id=1, source_target_pairs={{0,2},{1,3},{2,0},{3,1},{4,6},{5,7},{6,4},{7,5},{8,10},{9,11},{10,... | collective-permute-start | bytes 1572872 | tf_op jit(solution)/shard_map/ppermute | solution.py:22
  4.4 3.6 %collective-permute-start.3 = (bf16[128,512]{1,0:T(8,128)(2,1)S(1)}, bf16[128,512]{1,0:T(8,128)(2,1)S(1)}, u32[]{:S(2)}, u32[]{:S(2)}) collective-permute-start(bf16[128,512]{1,0:T(8,128)(2,1)S(1)} %get-tuple-element.35.refs_0_), channel_id=1, source_target_pairs={{0,1},{1,0},{2,3},{3,2},{4,5},{5,4},{6,7},{7,6},{8,9},{9,8},{10,11... | collective-permute-start | bytes 393224 | tf_op jit(solution)/shard_map/ppermute | solution.py:22
  4.4 9.9 %collective-permute-start.2 = (bf16[128,512]{1,0:T(8,128)(2,1)S(1)}, bf16[128,512]{1,0:T(8,128)(2,1)S(1)}, u32[]{:S(2)}, u32[]{:S(2)}) collective-permute-start(bf16[128,512]{1,0:T(8,128)(2,1)S(1)} %get-tuple-element.32), channel_id=1, source_target_pairs={{0,12},{4,8},{8,4},{12,0},{1,13},{5,9},{9,5},{13,1},{2,14},{6,10},... | collective-permute-start | bytes 393224 | tf_op jit(solution)/shard_map/ppermute | solution.py:22
  8.0 12.2 %collective-permute-start.1 = (bf16[128,512]{1,0:T(8,128)(2,1)S(1)}, bf16[128,512]{1,0:T(8,128)(2,1)S(1)}, u32[]{:S(2)}, u32[]{:S(2)}) collective-permute-start(bf16[128,512]{1,0:T(8,128)(2,1)S(1)} %get-tuple-element.33), channel_id=1, source_target_pairs={{0,8},{4,12},{8,0},{12,4},{1,9},{5,13},{9,1},{13,5},{2,10},{6,14},... | collective-permute-start | bytes 393224 | tf_op jit(solution)/shard_map/ppermute | solution.py:22
  12.2 9.5 %collective-permute-start.15 = (bf16[144,256]{1,0:T(8,128)(2,1)}, bf16[144,256]{1,0:T(8,128)(2,1)S(1)}, u32[]{:S(2)}, u32[]{:S(2)}) collective-permute-start(bf16[144,256]{1,0:T(8,128)(2,1)} %student.1), channel_id=1, source_target_pairs={{0,4},{4,0},{8,12},{12,8},{1,5},{5,1},{9,13},{13,9},{2,6},{6,2},{1... | collective-permute-start | bytes 221192 | tf_op jit(solution)/shard_map/ppermute | solution.py:22
  13.0 11.4 %collective-permute-start = (bf16[128,512]{1,0:T(8,128)(2,1)S(1)}, bf16[128,512]{1,0:T(8,128)(2,1)S(1)}, u32[]{:S(2)}, u32[]{:S(2)}) collective-permute-start(bf16[128,512]{1,0:T(8,128)(2,1)S(1)} %get-tuple-element.34), channel_id=1, source_target_pairs={{0,4},{4,0},{8,12},{12,8},{1,5},{5,1},{9,13},{13,9},{2,6},{6,2},{1... | collective-permute-start | bytes 393224 | tf_op jit(solution)/shard_map/ppermute | solution.py:22
  14.3 8.3 %collective-permute-start.16 = (bf16[144,256]{1,0:T(8,128)(2,1)}, bf16[144,256]{1,0:T(8,128)(2,1)S(1)}, u32[]{:S(2)}, u32[]{:S(2)}) collective-permute-start(bf16[144,256]{1,0:T(8,128)(2,1)} %student.1), channel_id=1, source_target_pairs={{0,8},{4,12},{8,0},{12,4},{1,9},{5,13},{9,1},{13,5},{2,10},{6,14},... | collective-permute-start | bytes 221192 | tf_op jit(solution)/shard_map/ppermute | solution.py:22
  20.3 6.4 %collective-permute-start.6 = (bf16[128,512]{1,0:T(8,128)(2,1)S(1)}, bf16[128,512]{1,0:T(8,128)(2,1)S(1)}, u32[]{:S(2)}, u32[]{:S(2)}) collective-permute-start(bf16[128,512]{1,0:T(8,128)(2,1)S(1)} %collective-permute-done.2.refs_3_), channel_id=1, source_target_pairs={{0,1},{1,0},{2,3},{3,2},{4,5},{5,4},{6,7},{7,6},{8,9},{9,8},{10,11... | collective-permute-start | bytes 393224 | tf_op jit(solution)/shard_map/ppermute | solution.py:22
  21.7 7.3 %collective-permute-start.5 = (bf16[128,512]{1,0:T(8,128)(2,1)S(1)}, bf16[128,512]{1,0:T(8,128)(2,1)S(1)}, u32[]{:S(2)}, u32[]{:S(2)}) collective-permute-start(bf16[128,512]{1,0:T(8,128)(2,1)S(1)} %collective-permute-done.1.refs_2_), channel_id=1, source_target_pairs={{0,1},{1,0},{2,3},{3,2},{4,5},{5,4},{6,7},{7,6},{8,9},{9,8},{10,11... | collective-permute-start | bytes 393224 | tf_op jit(solution)/shard_map/ppermute | solution.py:22
  22.6 8.5 %collective-permute-start.20 = (bf16[288,256]{1,0:T(8,128)(2,1)S(1)}, bf16[288,256]{1,0:T(8,128)(2,1)S(1)}, u32[]{:S(2)}, u32[]{:S(2)}) collective-permute-start(bf16[288,256]{1,0:T(8,128)(2,1)S(1)} %pad_maximum_fusion.2.refs_16_), channel_id=1, source_target_pairs={{0,2},{1,3},{2,0},{3,1},{4,6},{5,7},{6,4},{7,5},{8,10},{9,11},{10,... | collective-permute-start | bytes 442376 | tf_op jit(solution)/shard_map/ppermute | solution.py:22
  23.2 4.4 %collective-permute-start.17 = (bf16[144,256]{1,0:T(8,128)(2,1)S(1)}, bf16[144,256]{1,0:T(8,128)(2,1)S(1)}, u32[]{:S(2)}, u32[]{:S(2)}) collective-permute-start(bf16[144,256]{1,0:T(8,128)(2,1)S(1)} %collective-permute-done.16), channel_id=1, source_target_pairs={{0,4},{4,0},{8,12},{12,8},{1,5},{5,1},{9,13},{13,9},{2,6},{6,2},{1... | collective-permute-start | bytes 221192 | tf_op jit(solution)/shard_map/ppermute | solution.py:22
  24.5 8.3 %collective-permute-start.10 = (bf16[128,512]{1,0:T(8,128)(2,1)S(1)}, bf16[128,512]{1,0:T(8,128)(2,1)S(1)}, u32[]{:S(2)}, u32[]{:S(2)}) collective-permute-start(bf16[128,512]{1,0:T(8,128)(2,1)S(1)} %get-tuple-element.39), channel_id=1, source_target_pairs={{0,12},{4,8},{8,4},{12,0},{1,13},{5,9},{9,5},{13,1},{2,14},{6,10},... | collective-permute-start | bytes 393224 | tf_op jit(solution)/shard_map/ppermute | solution.py:22
  26.6 12.0 %collective-permute-start.9 = (bf16[128,512]{1,0:T(8,128)(2,1)S(1)}, bf16[128,512]{1,0:T(8,128)(2,1)S(1)}, u32[]{:S(2)}, u32[]{:S(2)}) collective-permute-start(bf16[128,512]{1,0:T(8,128)(2,1)S(1)} %get-tuple-element.40), channel_id=1, source_target_pairs={{0,8},{4,12},{8,0},{12,4},{1,9},{5,13},{9,1},{13,5},{2,10},{6,14},... | collective-permute-start | bytes 393224 | tf_op jit(solution)/shard_map/ppermute | solution.py:22
  27.6 11.0 %collective-permute-start.8 = (bf16[128,512]{1,0:T(8,128)(2,1)S(1)}, bf16[128,512]{1,0:T(8,128)(2,1)S(1)}, u32[]{:S(2)}, u32[]{:S(2)}) collective-permute-start(bf16[128,512]{1,0:T(8,128)(2,1)S(1)} %get-tuple-element.41), channel_id=1, source_target_pairs={{0,4},{4,0},{8,12},{12,8},{1,5},{5,1},{9,13},{13,9},{2,6},{6,2},{1... | collective-permute-start | bytes 393224 | tf_op jit(solution)/shard_map/ppermute | solution.py:22
  29.0 10.1 %collective-permute-start.21 = (bf16[288,256]{1,0:T(8,128)(2,1)S(1)}, bf16[288,256]{1,0:T(8,128)(2,1)S(1)}, u32[]{:S(2)}, u32[]{:S(2)}) collective-permute-start(bf16[288,256]{1,0:T(8,128)(2,1)S(1)} %constant_dynamic-update-slice_fusion.refs_17_), channel_id=1, source_target_pairs={{0,2},{1,3},{2,0},{3,1},{4,6},{5,7},{6,4},{7,5},{8,10},{9,11},{10,... | collective-permute-start | bytes 442376 | tf_op jit(solution)/shard_map/ppermute | solution.py:22
  31.2 8.0 %collective-permute-start.11 = (bf16[128,512]{1,0:T(8,128)(2,1)S(1)}, bf16[128,512]{1,0:T(8,128)(2,1)S(1)}, u32[]{:S(2)}, u32[]{:S(2)}) collective-permute-start(bf16[128,512]{1,0:T(8,128)(2,1)S(1)} %get-tuple-element.42.refs_0_), channel_id=1, source_target_pairs={{0,1},{1,0},{2,3},{3,2},{4,5},{5,4},{6,7},{7,6},{8,9},{9,8},{10,11... | collective-permute-start | bytes 393224 | tf_op jit(solution)/shard_map/ppermute | solution.py:22
  32.8 6.8 %collective-permute-start.14 = (bf16[128,512]{1,0:T(8,128)(2,1)S(1)}, bf16[128,512]{1,0:T(8,128)(2,1)S(1)}, u32[]{:S(2)}, u32[]{:S(2)}) collective-permute-start(bf16[128,512]{1,0:T(8,128)(2,1)S(1)} %collective-permute-done.10.refs_3_), channel_id=1, source_target_pairs={{0,1},{1,0},{2,3},{3,2},{4,5},{5,4},{6,7},{7,6},{8,9},{9,8},{10,11... | collective-permute-start | bytes 393224 | tf_op jit(solution)/shard_map/ppermute | solution.py:22
  39.1 2.4 %collective-permute-start.18 = (bf16[288,256]{1,0:T(8,128)(2,1)S(1)}, bf16[288,256]{1,0:T(8,128)(2,1)S(1)}, u32[]{:S(2)}, u32[]{:S(2)}) collective-permute-start(bf16[288,256]{1,0:T(8,128)(2,1)S(1)} %pad_maximum_fusion.2.refs_16_), channel_id=1, source_target_pairs={{0,1},{1,0},{2,3},{3,2},{4,5},{5,4},{6,7},{7,6},{8,9},{9,8},{10,11... | collective-permute-start | bytes 442376 | tf_op jit(solution)/shard_map/ppermute | solution.py:22
  39.2 2.3 %collective-permute-start.19 = (bf16[288,256]{1,0:T(8,128)(2,1)S(1)}, bf16[288,256]{1,0:T(8,128)(2,1)S(1)}, u32[]{:S(2)}, u32[]{:S(2)}) collective-permute-start(bf16[288,256]{1,0:T(8,128)(2,1)S(1)} %constant_dynamic-update-slice_fusion.refs_17_), channel_id=1, source_target_pairs={{0,1},{1,0},{2,3},{3,2},{4,5},{5,4},{6,7},{7,6},{8,9},{9,8},{10,11... | collective-permute-start | bytes 442376 | tf_op jit(solution)/shard_map/ppermute | solution.py:22
  39.6 1.9 %collective-permute-start.22 = (bf16[288,256]{1,0:T(8,128)(2,1)S(1)}, bf16[288,256]{1,0:T(8,128)(2,1)S(1)}, u32[]{:S(2)}, u32[]{:S(2)}) collective-permute-start(bf16[288,256]{1,0:T(8,128)(2,1)S(1)} %collective-permute-done.20.refs_20_), channel_id=1, source_target_pairs={{0,1},{1,0},{2,3},{3,2},{4,5},{5,4},{6,7},{7,6},{8,9},{9,8},{10,11... | collective-permute-start | bytes 442376 | tf_op jit(solution)/shard_map/ppermute | solution.py:22
  43.4 7.1 %collective-permute-start.24 = (bf16[256,256]{1,0:T(8,128)(2,1)S(1)}, bf16[256,256]{1,0:T(8,128)(2,1)S(1)}, u32[]{:S(2)}, u32[]{:S(2)}) collective-permute-start(bf16[256,256]{1,0:T(8,128)(2,1)S(1)} %pairs_far.2), channel_id=1, source_target_pairs={{0,2},{1,3},{2,0},{3,1},{4,6},{5,7},{6,4},{7,5},{8,10},{9,11},{10,... | collective-permute-start | bytes 393224 | tf_op jit(solution)/shard_map/ppermute | solution.py:22
  46.8 5.5 %collective-permute-start.26 = (bf16[256,256]{1,0:T(8,128)(2,1)S(1)}, bf16[256,256]{1,0:T(8,128)(2,1)S(1)}, u32[]{:S(2)}, u32[]{:S(2)}) collective-permute-start(bf16[256,256]{1,0:T(8,128)(2,1)S(1)} %pairs_far.3), channel_id=1, source_target_pairs={{0,2},{1,3},{2,0},{3,1},{4,6},{5,7},{6,4},{7,5},{8,10},{9,11},{10,... | collective-permute-start | bytes 393224 | tf_op jit(solution)/shard_map/ppermute | solution.py:22
  52.4 4.8 %collective-permute-start.25 = (bf16[128,256]{1,0:T(8,128)(2,1)S(1)}, bf16[128,256]{1,0:T(8,128)(2,1)S(1)}, u32[]{:S(2)}, u32[]{:S(2)}) collective-permute-start(bf16[128,256]{1,0:T(8,128)(2,1)S(1)} %slice.54), channel_id=1, source_target_pairs={{0,4},{4,0},{8,12},{12,8},{1,5},{5,1},{9,13},{13,9},{2,6},{6,2},{1... | collective-permute-start | bytes 196616 | tf_op jit(solution)/shard_map/ppermute | solution.py:22
  52.5 6.9 %collective-permute-start.27 = (bf16[128,256]{1,0:T(8,128)(2,1)S(1)}, bf16[128,256]{1,0:T(8,128)(2,1)S(1)}, u32[]{:S(2)}, u32[]{:S(2)}) collective-permute-start(bf16[128,256]{1,0:T(8,128)(2,1)S(1)} %get-tuple-element.43), channel_id=1, source_target_pairs={{0,8},{4,12},{8,0},{12,4},{1,9},{5,13},{9,1},{13,5},{2,10},{6,14},... | collective-permute-start | bytes 196616 | tf_op jit(solution)/shard_map/ppermute | solution.py:22
  54.5 6.2 %collective-permute-start.28 = (bf16[128,256]{1,0:T(8,128)(2,1)S(1)}, bf16[128,256]{1,0:T(8,128)(2,1)S(1)}, u32[]{:S(2)}, u32[]{:S(2)}) collective-permute-start(bf16[128,256]{1,0:T(8,128)(2,1)S(1)} %get-tuple-element.44), channel_id=1, source_target_pairs={{0,12},{4,8},{8,4},{12,0},{1,13},{5,9},{9,5},{13,1},{2,14},{6,10},... | collective-permute-start | bytes 196616 | tf_op jit(solution)/shard_map/ppermute | solution.py:22
  60.7 6.3 %collective-permute-start.33 = (bf16[128,256]{1,0:T(8,128)(2,1)S(1)}, bf16[128,256]{1,0:T(8,128)(2,1)S(1)}, u32[]{:S(2)}, u32[]{:S(2)}) collective-permute-start(bf16[128,256]{1,0:T(8,128)(2,1)S(1)} %multiply_convert_fusion), channel_id=1, source_target_pairs={{0,12},{4,8},{8,4},{12,0},{1,13},{5,9},{9,5},{13,1},{2,14},{6,10},... | collective-permute-start | bytes 196616 | tf_op jit(solution)/shard_map/ppermute | solution.py:22
  63.1 5.3 %collective-permute-start.32 = (bf16[128,256]{1,0:T(8,128)(2,1)S(1)}, bf16[128,256]{1,0:T(8,128)(2,1)S(1)}, u32[]{:S(2)}, u32[]{:S(2)}) collective-permute-start(bf16[128,256]{1,0:T(8,128)(2,1)S(1)} %multiply_convert_fusion), channel_id=1, source_target_pairs={{0,8},{4,12},{8,0},{12,4},{1,9},{5,13},{9,1},{13,5},{2,10},{6,14},... | collective-permute-start | bytes 196616 | tf_op jit(solution)/shard_map/ppermute | solution.py:22
  63.1 6.7 %collective-permute-start.29 = (bf16[128,256]{1,0:T(8,128)(2,1)S(1)}, bf16[128,256]{1,0:T(8,128)(2,1)S(1)}, u32[]{:S(2)}, u32[]{:S(2)}) collective-permute-start(bf16[128,256]{1,0:T(8,128)(2,1)S(1)} %multiply_convert_fusion), channel_id=1, source_target_pairs={{0,4},{4,0},{8,12},{12,8},{1,5},{5,1},{9,13},{13,9},{2,6},{6,2},{1... | collective-permute-start | bytes 196616 | tf_op jit(solution)/shard_map/ppermute | solution.py:22
  68.4 5.0 %collective-permute-start.34 = (bf16[256,256]{1,0:T(8,128)(2,1)S(1)}, bf16[256,256]{1,0:T(8,128)(2,1)S(1)}, u32[]{:S(2)}, u32[]{:S(2)}) collective-permute-start(bf16[256,256]{1,0:T(8,128)(2,1)S(1)} %pad_maximum_fusion.4), channel_id=1, source_target_pairs={{0,2},{1,3},{2,0},{3,1},{4,6},{5,7},{6,4},{7,5},{8,10},{9,11},{10,... | collective-permute-start | bytes 393224 | tf_op jit(solution)/shard_map/ppermute | solution.py:22
  69.8 5.1 %collective-permute-start.30 = (bf16[256,256]{1,0:T(8,128)(2,1)S(1)}, bf16[256,256]{1,0:T(8,128)(2,1)S(1)}, u32[]{:S(2)}, u32[]{:S(2)}) collective-permute-start(bf16[256,256]{1,0:T(8,128)(2,1)S(1)} %pad_maximum_fusion.3), channel_id=1, source_target_pairs={{0,2},{1,3},{2,0},{3,1},{4,6},{5,7},{6,4},{7,5},{8,10},{9,11},{10,... | collective-permute-start | bytes 393224 | tf_op jit(solution)/shard_map/ppermute | solution.py:22
  73.5 1.6 %collective-permute-start.35 = (bf16[512,256]{1,0:T(8,128)(2,1)S(1)}, bf16[512,256]{1,0:T(8,128)(2,1)S(1)}, u32[]{:S(2)}, u32[]{:S(2)}) collective-permute-start(bf16[512,256]{1,0:T(8,128)(2,1)S(1)} %constant_dynamic-update-slice_fusion.2.refs_2_), channel_id=1, source_target_pairs={{0,1},{1,0},{2,3},{3,2},{4,5},{5,4},{6,7},{7,6},{8,9},{9,8},{10,11... | collective-permute-start | bytes 786440 | tf_op jit(solution)/shard_map/ppermute | solution.py:22
  74.9 1.6 %collective-permute-start.31 = (bf16[512,256]{1,0:T(8,128)(2,1)S(1)}, bf16[512,256]{1,0:T(8,128)(2,1)S(1)}, u32[]{:S(2)}, u32[]{:S(2)}) collective-permute-start(bf16[512,256]{1,0:T(8,128)(2,1)S(1)} %pad_maximum_fusion.1.refs_0_), channel_id=1, source_target_pairs={{0,1},{1,0},{2,3},{3,2},{4,5},{5,4},{6,7},{7,6},{8,9},{9,8},{10,11... | collective-permute-start | bytes 786440 | tf_op jit(solution)/shard_map/ppermute | solution.py:22
  (5 other events, 45.9 us)

commit v6 on v5

--- a/solution.py
+++ b/solution.py
@@ -44,36 +44,6 @@
             body(step)
     else:
         lax.fori_loop(0, count, lambda step, carry: (body(step), carry)[1], 0)
-
-
-def student_kernel(steps, teacher, weight, group, packed, t_all, w_all, t_sem, w_sem):
-    rows, width = teacher.shape
-    out = weight.shape[1]
-    depth = width // steps
-
-    def w_copy(step):
-        part = pl.ds(step * depth, depth)
-        return pltpu.make_async_copy(weight.at[part], w_all.at[part], w_sem.at[step])
-
-    def t_copy(step):
-        part = pl.ds(step * depth, depth)
-        return pltpu.make_async_copy(teacher.at[:, part], t_all.at[:, part], t_sem.at[step])
-
-    for step in range(steps):
-        t_copy(step).start()
-        w_copy(step).start()
-    line = jnp.broadcast_to(group[...].astype(jnp.float32), (EXTRA, rows))
-    packed[rows:, :rows] = line.astype(jnp.bfloat16)
-    total = jnp.zeros((rows, out), jnp.float32)
-    for step in range(steps):
-        t_copy(step).wait()
-        w_copy(step).wait()
-        total += jnp.dot(
-            t_all[:, step * depth : (step + 1) * depth],
-            w_all[step * depth : (step + 1) * depth, :].astype(jnp.bfloat16),
-            preferred_element_type=jnp.float32,
-        )
-    packed[:rows, :] = total.astype(jnp.bfloat16)
 
 
 def pair_kernel(planes, lanes, rows, out, width, own, mask, place, *refs):
@@ -293,22 +263,13 @@
     first = [mine[0]] + [swapped(mine[k], "wide", k) for k in range(1, planes)]
     second = [got[0]] + [swapped(got[k], "wide", k) for k in range(1, planes)]
 
-    steps = 8
-    packed = pl.pallas_call(
-        functools.partial(student_kernel, steps),
-        out_shape=jax.ShapeDtypeStruct((rows + EXTRA, out), jnp.bfloat16),
-        in_specs=[ANY, ANY, VMEM],
-        out_specs=VMEM,
-        scratch_shapes=[
-            pltpu.VMEM((rows, width), jnp.bfloat16),
-            pltpu.VMEM((width, out), jnp.float32),
-            pltpu.SemaphoreType.DMA((steps,)),
-            pltpu.SemaphoreType.DMA((steps,)),
-        ],
-        compiler_params=pltpu.CompilerParams(vmem_limit_bytes=56 * MIB),
-        cost_estimate=cost(2 * rows * width * out, width * (2 * rows + 4 * out)),
-        name="student",
-    )(after(teacher, own_core), weight, item_group.reshape(1, rows))
+    low_weight = weight.astype(jnp.bfloat16)
+    student = jnp.dot(
+        after(teacher, own_core), low_weight, preferred_element_type=jnp.float32
+    ).astype(jnp.bfloat16)
+    extra = jnp.zeros((EXTRA, out), jnp.bfloat16).at[0, :rows].set(item_group.astype(jnp.bfloat16))
+    packed = jnp.concatenate([student, extra], 0)
+
     s_of = {0: packed}
     bit = half
     while bit:
@@ -378,17 +339,17 @@
         )(block_mask, here, *t_all, *s_all)
 
     if whole_tiles:
-        (far_high,) = pairs(False, range(half, planes))
+        (far_high,) = pairs(False, range(1, planes))
         far_high = swapped(far_high, "narrow", FAR)
-        (far_low,) = pairs(False, range(half))
+        (far_low,) = pairs(False, range(1))
         far_low = swapped(far_low, "narrow", FAR)
     else:
         (far_all,) = pairs(False, range(planes))
-        far_high = swapped(far_all[half * rows :], "narrow", FAR)
-        far_low = swapped(far_all[: half * rows], "narrow", FAR)
+        far_high = swapped(far_all[rows:], "narrow", FAR)
+        far_low = swapped(far_all[:rows], "narrow", FAR)
     own_sum, t_keep = pairs(True, range(planes))
-    sums_high = own_sum[half * rows :] + far_high.astype(jnp.float32)
-    sums_low = own_sum[: half * rows] + far_low.astype(jnp.float32)
+    sums_high = own_sum[rows:] + far_high.astype(jnp.float32)
+    sums_low = own_sum[:rows] + far_low.astype(jnp.float32)
     t_keep = pl.pallas_call(
         flip_kernel,
         out_shape=jax.ShapeDtypeStruct((keep, items), jnp.bfloat16),
@@ -399,10 +360,9 @@
         name="flip",
     )(t_keep)
 
-    grad = after(sums_low[:rows], t_keep)
+    grad = after(sums_low, t_keep)
     for k in range(1, planes):
-        at = k % half * rows
-        piece = (sums_low, sums_high)[k >= half][at : at + rows].astype(jnp.bfloat16)
+        piece = sums_high[(k - 1) * rows : k * rows].astype(jnp.bfloat16)
         grad = grad + swapped(piece, "wide", k).astype(jnp.float32)
     coef = 2.0 * width / (items * out)
     grad = (grad * coef).astype(jnp.bfloat16)

time: 77.8 us -> 76.8 us (0.987)
  Pallas kernels: 12.5 us -> 8.58 us
  matrix products: 0 us -> 2.96 us
    pallas_call x1 -> x0, Pallas kernels: 4.15 us -> none  [per_device(): pl.pallas_call(functools.partial(student_kernel, steps), out_shape=jax.Sh...]
    dot_general x0 -> x1, matrix products: none -> 2.96 us  [per_device(): jnp.dot(after(teacher, own_core), low_weight, preferred_element_type=jnp....]
    concatenate x1, other arithmetic: 0.89 us -> 0.01 us  [per_device(): jnp.concatenate([s_of[k] for k in range(planes) if (k >= NEAR) == odd], 0)]
  transfers between devices with their start and end apart: 36 -> 36, of which waited for: 16 -> 17; matrix products, arithmetic and copies ran while one was open for 1% -> 5% of each run, Pallas kernels for 12% -> 7%
where the time goes in v6:
time: 76.8 us; the launch traced here: 76.6 us
  starting transfers between devices  36 us (47%)
  waiting for transfers between devices  26.5 us (35%)
  Pallas kernels  8.58 us (11%)
  matrix products  2.96 us (4%)
  local copies, waits for them, and re-layouts  1.46 us (2%)
  other arithmetic  0.92 us (1%)
    ppermute x36, starting transfers between devices, swapped(): lax.ppermute(value, axis, [(source, source ^ bit) for source in range(cou...  36 us
    ppermute x36, waiting for transfers between devices, swapped(): lax.ppermute(value, axis, [(source, source ^ bit) for source in range(cou...  26.5 us
    pallas_call x3, Pallas kernels, pairs(): pl.pallas_call(functools.partial(pair_values_kernel, planes, lanes, rows,...  7.04 us
    dot_general x1, matrix products, per_device(): jnp.dot(after(teacher, own_core), low_weight, preferred_element_type=jnp....  2.96 us
  transfers between devices with their start and end apart: 36, of which 17 were waited for; matrix products, arithmetic and copies ran while one was open for 5% of the time, Pallas kernels for 7%

profile of v6, /device:TPU:0, one launch (start us, length us, event | category | flops | bytes accessed | tf_op | source)
XLA Modules:
  0.0 76.6 jit_solution(3964635155499859944)
XLA Ops:
  0.0 1.4 %constant_dynamic-slice_fusion.3 = (bf16[128,512]{1,0:T(8,128)(2,1)S(1)}, bf16[128,512]{1,0:T(8,128)(2,1)S(1)}, bf16[128,512]{1,0:T(8,128)(2,1)S(1)}, bf16[128,5...) fusion(bf16[128,4096]{1,0:T(8,128)(2,1)} %param.6, ...), kind=kLoop, calls=%fused_computation.20 | loop fusion | bytes 2097184 | tf_op jit(solution)/shard_map/dynamic_slice | solution.py:256
  1.4 5.1 %collective-permute-start.2 = (bf16[128,512]{1,0:T(8,128)(2,1)S(1)}, bf16[128,512]{1,0:T(8,128)(2,1)S(1)}, u32[]{:S(2)}, u32[]{:S(2)}) collective-permute-start(bf16[128,512]{1,0:T(8,128)(2,1)S(1)} %get-tuple-element.44), channel_id=1, source_target_pairs={{0,12},{4,8},{8,4},{12,0},{1,13},{5,9},{9,5},{13,1},{2,14},{6,10},... | collective-permute-start | bytes 393224 | tf_op jit(solution)/shard_map/ppermute | solution.py:22
  6.5 1.6 %collective-permute-start.7 = (bf16[512,512]{1,0:T(8,128)(2,1)S(1)}, bf16[512,512]{1,0:T(8,128)(2,1)S(1)}, u32[]{:S(2)}, u32[]{:S(2)}) collective-permute-start(bf16[512,512]{1,0:T(8,128)(2,1)S(1)} %pad_maximum_fusion), channel_id=1, source_target_pairs={{0,2},{1,3},{2,0},{3,1},{4,6},{5,7},{6,4},{7,5},{8,10},{9,11},{10,... | collective-permute-start | bytes 1572872 | tf_op jit(solution)/shard_map/ppermute | solution.py:22
  8.8 3.0 %fusion.2 = bf16[128,256]{1,0:T(8,128)(2,1)S(1)} fusion(bf16[128,4096]{1,0:T(8,128)(2,1)} %param.6, f32[4096,256]{1,0:T(8,128)} %param.7), kind=kOutput, calls=%fused_computation.2 | convolution fusion | flops 269516800 | bytes 5308416 | tf_op jit(solution)/shard_map/dot_general | solution.py:267
  12.6 1.2 %collective-permute-start = (bf16[128,512]{1,0:T(8,128)(2,1)S(1)}, bf16[128,512]{1,0:T(8,128)(2,1)S(1)}, u32[]{:S(2)}, u32[]{:S(2)}) collective-permute-start(bf16[128,512]{1,0:T(8,128)(2,1)S(1)} %get-tuple-element.46), channel_id=1, source_target_pairs={{0,4},{4,0},{8,12},{12,8},{1,5},{5,1},{9,13},{13,9},{2,6},{6,2},{1... | collective-permute-start | bytes 393224 | tf_op jit(solution)/shard_map/ppermute | solution.py:22
  13.8 3.6 %collective-permute-start.16 = (bf16[144,256]{1,0:T(8,128)(2,1)S(1)}, bf16[144,256]{1,0:T(8,128)(2,1)S(1)}, u32[]{:S(2)}, u32[]{:S(2)}) collective-permute-start(bf16[144,256]{1,0:T(8,128)(2,1)S(1)} %pad_maximum_fusion.5), channel_id=1, source_target_pairs={{0,8},{4,12},{8,0},{12,4},{1,9},{5,13},{9,1},{13,5},{2,10},{6,14},... | collective-permute-start | bytes 221192 | tf_op jit(solution)/shard_map/ppermute | solution.py:22
  17.9 2.6 %collective-permute-done.15 = bf16[144,256]{1,0:T(8,128)(2,1)S(1)} collective-permute-done((bf16[144,256]{1,0:T(8,128)(2,1)S(1)}, bf16[144,256]{1,0:T(8,128)(2,1)S(1)}, u32[]{:S(2)}, u32[]{:S(2)}) %collective-permute-start.15) | collective-permute-done | bytes 73760 | tf_op jit(solution)/shard_map/ppermute | solution.py:22
  20.5 1.1 %collective-permute-start.20 = (bf16[288,256]{1,0:T(8,128)(2,1)S(1)}, bf16[288,256]{1,0:T(8,128)(2,1)S(1)}, u32[]{:S(2)}, u32[]{:S(2)}) collective-permute-start(bf16[288,256]{1,0:T(8,128)(2,1)S(1)} %pad_maximum_fusion.2.refs_16_), channel_id=1, source_target_pairs={{0,2},{1,3},{2,0},{3,1},{4,6},{5,7},{6,4},{7,5},{8,10},{9,11},{10,... | collective-permute-start | bytes 442376 | tf_op jit(solution)/shard_map/ppermute | solution.py:22
  21.6 2.4 %collective-permute-start.17 = (bf16[144,256]{1,0:T(8,128)(2,1)S(1)}, bf16[144,256]{1,0:T(8,128)(2,1)S(1)}, u32[]{:S(2)}, u32[]{:S(2)}) collective-permute-start(bf16[144,256]{1,0:T(8,128)(2,1)S(1)} %collective-permute-done.16), channel_id=1, source_target_pairs={{0,4},{4,0},{8,12},{12,8},{1,5},{5,1},{9,13},{13,9},{2,6},{6,2},{1... | collective-permute-start | bytes 221192 | tf_op jit(solution)/shard_map/ppermute | solution.py:22
  24.1 1.7 %collective-permute-start.10 = (bf16[128,512]{1,0:T(8,128)(2,1)S(1)}, bf16[128,512]{1,0:T(8,128)(2,1)S(1)}, u32[]{:S(2)}, u32[]{:S(2)}) collective-permute-start(bf16[128,512]{1,0:T(8,128)(2,1)S(1)} %get-tuple-element.49), channel_id=1, source_target_pairs={{0,12},{4,8},{8,4},{12,0},{1,13},{5,9},{9,5},{13,1},{2,14},{6,10},... | collective-permute-start | bytes 393224 | tf_op jit(solution)/shard_map/ppermute | solution.py:22
  26.4 2.5 %collective-permute-start.8 = (bf16[128,512]{1,0:T(8,128)(2,1)S(1)}, bf16[128,512]{1,0:T(8,128)(2,1)S(1)}, u32[]{:S(2)}, u32[]{:S(2)}) collective-permute-start(bf16[128,512]{1,0:T(8,128)(2,1)S(1)} %get-tuple-element.51), channel_id=1, source_target_pairs={{0,4},{4,0},{8,12},{12,8},{1,5},{5,1},{9,13},{13,9},{2,6},{6,2},{1... | collective-permute-start | bytes 393224 | tf_op jit(solution)/shard_map/ppermute | solution.py:22
  28.9 1.9 %collective-permute-start.21 = (bf16[288,256]{1,0:T(8,128)(2,1)S(1)}, bf16[288,256]{1,0:T(8,128)(2,1)S(1)}, u32[]{:S(2)}, u32[]{:S(2)}) collective-permute-start(bf16[288,256]{1,0:T(8,128)(2,1)S(1)} %constant_dynamic-update-slice_fusion.refs_17_), channel_id=1, source_target_pairs={{0,2},{1,3},{2,0},{3,1},{4,6},{5,7},{6,4},{7,5},{8,10},{9,11},{10,... | collective-permute-start | bytes 442376 | tf_op jit(solution)/shard_map/ppermute | solution.py:22
  30.8 1.7 %collective-permute-done.10.refs_3_ = bf16[128,512]{1,0:T(8,128)(2,1)S(1)} collective-permute-done((bf16[128,512]{1,0:T(8,128)(2,1)S(1)}, bf16[128,512]{1,0:T(8,128)(2,1)S(1)}, u32[]{:S(2)}, u32[]{:S(2)}) %collective-permute-start.10) | collective-permute-done | bytes 131104 | tf_op jit(solution)/shard_map/ppermute | solution.py:22
  32.5 4.5 %collective-permute-done.9.refs_2_ = bf16[128,512]{1,0:T(8,128)(2,1)S(1)} collective-permute-done((bf16[128,512]{1,0:T(8,128)(2,1)S(1)}, bf16[128,512]{1,0:T(8,128)(2,1)S(1)}, u32[]{:S(2)}, u32[]{:S(2)}) %collective-permute-start.9) | collective-permute-done | bytes 131104 | tf_op jit(solution)/shard_map/ppermute | solution.py:22
  40.0 2.3 %pairs_far.3 = bf16[384,256]{1,0:T(8,128)(2,1)S(1)} custom-call(s32[4,4]{1,0:T(4,128)S(1)} %copy-done, s32[2]{0:T(128)S(1)} %pad_add_fusion.place, bf16[128,512]{1,0:T(8,128)(2,1)S(1)} %get-tuple-element.47.refs_0_, bf16[128,512]{1,0:T(8,128)(2,1)S(1)} %collective-permute-done.refs_1_, bf16[128,512]{1,0:T(8,128)(2,1)S(1)} %collective-permute-done.1.refs_2_, ...), custom_call_target="tpu_custom_call" | custom-call | flops 1207959552 | bytes 3145728 | tf_op jit(solution)/shard_map/pairs_far/pallas_call | solution.py:311
  42.3 1.6 %collective-permute-start.25 = (bf16[384,256]{1,0:T(8,128)(2,1)S(1)}, bf16[384,256]{1,0:T(8,128)(2,1)S(1)}, u32[]{:S(2)}, u32[]{:S(2)}) collective-permute-start(bf16[384,256]{1,0:T(8,128)(2,1)S(1)} %pairs_far.3), channel_id=1, source_target_pairs={{0,2},{1,3},{2,0},{3,1},{4,6},{5,7},{6,4},{7,5},{8,10},{9,11},{10,... | collective-permute-start | bytes 589832 | tf_op jit(solution)/shard_map/ppermute | solution.py:22
  43.8 1.6 %pairs_far.2 = bf16[128,256]{1,0:T(8,128)(2,1)S(1)} custom-call(s32[4,4]{1,0:T(4,128)S(1)} %copy-done, s32[2]{0:T(128)S(1)} %pad_add_fusion.place, bf16[128,512]{1,0:T(8,128)(2,1)S(1)} %get-tuple-element.47.refs_0_, bf16[128,512]{1,0:T(8,128)(2,1)S(1)} %collective-permute-done.refs_1_, bf16[128,512]{1,0:T(8,128)(2,1)S(1)} %collective-permute-done.1.refs_2_, ...), custom_call_target="tpu_custom_call" | custom-call | flops 402653184 | bytes 3145728 | tf_op jit(solution)/shard_map/pairs_far/pallas_call | solution.py:311
  46.1 3.1 %pairs_own.1 = (f32[512,256]{1,0:T(8,128)S(1)}, bf16[2048,256]{1,0:T(8,128)(2,1)S(1)}) custom-call(s32[4,4]{1,0:T(4,128)S(1)} %copy-done, s32[2]{0:T(128)S(1)} %pad_add_fusion.place, bf16[128,512]{1,0:T(8,128)(2,1)S(1)} %get-tuple-element.47.refs_0_, bf16[128,512]{1,0:T(8,128)(2,1)S(1)} %collective-permute-done.refs_1_, ...), custom_call_target="tpu_custom_call" | custom-call | flops 1610612736 | bytes 3145728 | tf_op jit(solution)/shard_map/pairs_own/pallas_call | solution.py:311
  50.2 2.0 %collective-permute-start.28 = (bf16[128,256]{1,0:T(8,128)(2,1)S(1)}, bf16[128,256]{1,0:T(8,128)(2,1)S(1)}, u32[]{:S(2)}, u32[]{:S(2)}) collective-permute-start(bf16[128,256]{1,0:T(8,128)(2,1)S(1)} %get-tuple-element.54), channel_id=1, source_target_pairs={{0,12},{4,8},{8,4},{12,0},{1,13},{5,9},{9,5},{13,1},{2,14},{6,10},... | collective-permute-start | bytes 196616 | tf_op jit(solution)/shard_map/ppermute | solution.py:22
  52.3 1.4 %collective-permute-start.27 = (bf16[128,256]{1,0:T(8,128)(2,1)S(1)}, bf16[128,256]{1,0:T(8,128)(2,1)S(1)}, u32[]{:S(2)}, u32[]{:S(2)}) collective-permute-start(bf16[128,256]{1,0:T(8,128)(2,1)S(1)} %get-tuple-element.55), channel_id=1, source_target_pairs={{0,8},{4,12},{8,0},{12,4},{1,9},{5,13},{9,1},{13,5},{2,10},{6,14},... | collective-permute-start | bytes 196616 | tf_op jit(solution)/shard_map/ppermute | solution.py:22
  53.7 1.7 %collective-permute-done.26 = bf16[128,256]{1,0:T(8,128)(2,1)S(1)} collective-permute-done((bf16[128,256]{1,0:T(8,128)(2,1)S(1)}, bf16[128,256]{1,0:T(8,128)(2,1)S(1)}, u32[]{:S(2)}, u32[]{:S(2)}) %collective-permute-start.26) | collective-permute-done | bytes 65568 | tf_op jit(solution)/shard_map/ppermute | solution.py:22
  55.4 1.2 %collective-permute-done.28 = bf16[128,256]{1,0:T(8,128)(2,1)S(1)} collective-permute-done((bf16[128,256]{1,0:T(8,128)(2,1)S(1)}, bf16[128,256]{1,0:T(8,128)(2,1)S(1)}, u32[]{:S(2)}, u32[]{:S(2)}) %collective-permute-start.28) | collective-permute-done | bytes 65568 | tf_op jit(solution)/shard_map/ppermute | solution.py:22
  56.6 2.6 %collective-permute-done.27 = bf16[128,256]{1,0:T(8,128)(2,1)S(1)} collective-permute-done((bf16[128,256]{1,0:T(8,128)(2,1)S(1)}, bf16[128,256]{1,0:T(8,128)(2,1)S(1)}, u32[]{:S(2)}, u32[]{:S(2)}) %collective-permute-start.27) | collective-permute-done | bytes 65568 | tf_op jit(solution)/shard_map/ppermute | solution.py:22
  59.2 2.3 %collective-permute-start.33 = (bf16[128,256]{1,0:T(8,128)(2,1)S(1)}, bf16[128,256]{1,0:T(8,128)(2,1)S(1)}, u32[]{:S(2)}, u32[]{:S(2)}) collective-permute-start(bf16[128,256]{1,0:T(8,128)(2,1)S(1)} %multiply_convert_fusion), channel_id=1, source_target_pairs={{0,12},{4,8},{8,4},{12,0},{1,13},{5,9},{9,5},{13,1},{2,14},{6,10},... | collective-permute-start | bytes 196616 | tf_op jit(solution)/shard_map/ppermute | solution.py:22
  61.6 2.1 %collective-permute-start.29 = (bf16[128,256]{1,0:T(8,128)(2,1)S(1)}, bf16[128,256]{1,0:T(8,128)(2,1)S(1)}, u32[]{:S(2)}, u32[]{:S(2)}) collective-permute-start(bf16[128,256]{1,0:T(8,128)(2,1)S(1)} %multiply_convert_fusion), channel_id=1, source_target_pairs={{0,4},{4,0},{8,12},{12,8},{1,5},{5,1},{9,13},{13,9},{2,6},{6,2},{1... | collective-permute-start | bytes 196616 | tf_op jit(solution)/shard_map/ppermute | solution.py:22
  63.7 2.3 %collective-permute-done.33 = bf16[128,256]{1,0:T(8,128)(2,1)S(1)} collective-permute-done((bf16[128,256]{1,0:T(8,128)(2,1)S(1)}, bf16[128,256]{1,0:T(8,128)(2,1)S(1)}, u32[]{:S(2)}, u32[]{:S(2)}) %collective-permute-start.33) | collective-permute-done | bytes 65568 | tf_op jit(solution)/shard_map/ppermute | solution.py:22
  66.0 1.4 %collective-permute-done.32 = bf16[128,256]{1,0:T(8,128)(2,1)S(1)} collective-permute-done((bf16[128,256]{1,0:T(8,128)(2,1)S(1)}, bf16[128,256]{1,0:T(8,128)(2,1)S(1)}, u32[]{:S(2)}, u32[]{:S(2)}) %collective-permute-start.32) | collective-permute-done | bytes 65568 | tf_op jit(solution)/shard_map/ppermute | solution.py:22
  67.4 1.4 %collective-permute-start.34 = (bf16[256,256]{1,0:T(8,128)(2,1)S(1)}, bf16[256,256]{1,0:T(8,128)(2,1)S(1)}, u32[]{:S(2)}, u32[]{:S(2)}) collective-permute-start(bf16[256,256]{1,0:T(8,128)(2,1)S(1)} %pad_maximum_fusion.4), channel_id=1, source_target_pairs={{0,2},{1,3},{2,0},{3,1},{4,6},{5,7},{6,4},{7,5},{8,10},{9,11},{10,... | collective-permute-start | bytes 393224 | tf_op jit(solution)/shard_map/ppermute | solution.py:22
  69.6 2.8 %collective-permute-done.34 = bf16[256,256]{1,0:T(8,128)(2,1)S(1)} collective-permute-done((bf16[256,256]{1,0:T(8,128)(2,1)S(1)}, bf16[256,256]{1,0:T(8,128)(2,1)S(1)}, u32[]{:S(2)}, u32[]{:S(2)}) %collective-permute-start.34) | collective-permute-done | bytes 131104 | tf_op jit(solution)/shard_map/ppermute | solution.py:22
  72.5 1.4 %collective-permute-done.30 = bf16[256,256]{1,0:T(8,128)(2,1)S(1)} collective-permute-done((bf16[256,256]{1,0:T(8,128)(2,1)S(1)}, bf16[256,256]{1,0:T(8,128)(2,1)S(1)}, u32[]{:S(2)}, u32[]{:S(2)}) %collective-permute-start.30) | collective-permute-done | bytes 131104 | tf_op jit(solution)/shard_map/ppermute | solution.py:22
  74.0 1.5 %collective-permute-done.31.refs_1_ = bf16[512,256]{1,0:T(8,128)(2,1)S(1)} collective-permute-done((bf16[512,256]{1,0:T(8,128)(2,1)S(1)}, bf16[512,256]{1,0:T(8,128)(2,1)S(1)}, u32[]{:S(2)}, u32[]{:S(2)}) %collective-permute-start.31) | collective-permute-done | bytes 262176 | tf_op jit(solution)/shard_map/ppermute | solution.py:22
  75.5 1.1 %last.1 = f32[256,256]{1,0:T(8,128)} custom-call(bf16[256,2048]{1,0:T(8,128)(2,1)S(1)} %flip.1.t_keep, bf16[512,256]{1,0:T(8,128)(2,1)S(1)} %pad_maximum_fusion.1.refs_0_, bf16[512,256]{1,0:T(8,128)(2,1)S(1)} %collective-permute-done.31.refs_1_, bf16[512,256]{1,0:T(8,128)(2,1)S(1)} %constant_dynamic-update-slice_fusion.2.refs_2_, ...), custom_call_target="tpu_custom_call" | custom-call | flops 268435456 | bytes 2097152 | tf_op jit(solution)/shard_map/last/pallas_call | solution.py:375
  (69 shorter events, 8.3 us)
Async XLA Ops:
  1.4 12.5 %collective-permute-start.2 = (bf16[128,512]{1,0:T(8,128)(2,1)S(1)}, bf16[128,512]{1,0:T(8,128)(2,1)S(1)}, u32[]{:S(2)}, u32[]{:S(2)}) collective-permute-start(bf16[128,512]{1,0:T(8,128)(2,1)S(1)} %get-tuple-element.44), channel_id=1, source_target_pairs={{0,12},{4,8},{8,4},{12,0},{1,13},{5,9},{9,5},{13,1},{2,14},{6,10},... | collective-permute-start | bytes 393224 | tf_op jit(solution)/shard_map/ppermute | solution.py:22
  6.5 11.4 %collective-permute-start.1 = (bf16[128,512]{1,0:T(8,128)(2,1)S(1)}, bf16[128,512]{1,0:T(8,128)(2,1)S(1)}, u32[]{:S(2)}, u32[]{:S(2)}) collective-permute-start(bf16[128,512]{1,0:T(8,128)(2,1)S(1)} %get-tuple-element.45), channel_id=1, source_target_pairs={{0,8},{4,12},{8,0},{12,4},{1,9},{5,13},{9,1},{13,5},{2,10},{6,14},... | collective-permute-start | bytes 393224 | tf_op jit(solution)/shard_map/ppermute | solution.py:22
  6.5 2.3 %collective-permute-start.3 = (bf16[128,512]{1,0:T(8,128)(2,1)S(1)}, bf16[128,512]{1,0:T(8,128)(2,1)S(1)}, u32[]{:S(2)}, u32[]{:S(2)}) collective-permute-start(bf16[128,512]{1,0:T(8,128)(2,1)S(1)} %get-tuple-element.47.refs_0_), channel_id=1, source_target_pairs={{0,1},{1,0},{2,3},{3,2},{4,5},{5,4},{6,7},{7,6},{8,9},{9,8},{10,11... | collective-permute-start | bytes 393224 | tf_op jit(solution)/shard_map/ppermute | solution.py:22
  6.5 15.1 %collective-permute-start.7 = (bf16[512,512]{1,0:T(8,128)(2,1)S(1)}, bf16[512,512]{1,0:T(8,128)(2,1)S(1)}, u32[]{:S(2)}, u32[]{:S(2)}) collective-permute-start(bf16[512,512]{1,0:T(8,128)(2,1)S(1)} %pad_maximum_fusion), channel_id=1, source_target_pairs={{0,2},{1,3},{2,0},{3,1},{4,6},{5,7},{6,4},{7,5},{8,10},{9,11},{10,... | collective-permute-start | bytes 1572872 | tf_op jit(solution)/shard_map/ppermute | solution.py:22
  11.8 8.8 %collective-permute-start.15 = (bf16[144,256]{1,0:T(8,128)(2,1)S(1)}, bf16[144,256]{1,0:T(8,128)(2,1)S(1)}, u32[]{:S(2)}, u32[]{:S(2)}) collective-permute-start(bf16[144,256]{1,0:T(8,128)(2,1)S(1)} %pad_maximum_fusion.5), channel_id=1, source_target_pairs={{0,4},{4,0},{8,12},{12,8},{1,5},{5,1},{9,13},{13,9},{2,6},{6,2},{1... | collective-permute-start | bytes 221192 | tf_op jit(solution)/shard_map/ppermute | solution.py:22
  12.6 11.5 %collective-permute-start = (bf16[128,512]{1,0:T(8,128)(2,1)S(1)}, bf16[128,512]{1,0:T(8,128)(2,1)S(1)}, u32[]{:S(2)}, u32[]{:S(2)}) collective-permute-start(bf16[128,512]{1,0:T(8,128)(2,1)S(1)} %get-tuple-element.46), channel_id=1, source_target_pairs={{0,4},{4,0},{8,12},{12,8},{1,5},{5,1},{9,13},{13,9},{2,6},{6,2},{1... | collective-permute-start | bytes 393224 | tf_op jit(solution)/shard_map/ppermute | solution.py:22
  13.8 6.7 %collective-permute-start.16 = (bf16[144,256]{1,0:T(8,128)(2,1)S(1)}, bf16[144,256]{1,0:T(8,128)(2,1)S(1)}, u32[]{:S(2)}, u32[]{:S(2)}) collective-permute-start(bf16[144,256]{1,0:T(8,128)(2,1)S(1)} %pad_maximum_fusion.5), channel_id=1, source_target_pairs={{0,8},{4,12},{8,0},{12,4},{1,9},{5,13},{9,1},{13,5},{2,10},{6,14},... | collective-permute-start | bytes 221192 | tf_op jit(solution)/shard_map/ppermute | solution.py:22
  17.9 7.9 %collective-permute-start.6 = (bf16[128,512]{1,0:T(8,128)(2,1)S(1)}, bf16[128,512]{1,0:T(8,128)(2,1)S(1)}, u32[]{:S(2)}, u32[]{:S(2)}) collective-permute-start(bf16[128,512]{1,0:T(8,128)(2,1)S(1)} %collective-permute-done.2.refs_3_), channel_id=1, source_target_pairs={{0,1},{1,0},{2,3},{3,2},{4,5},{5,4},{6,7},{7,6},{8,9},{9,8},{10,11... | collective-permute-start | bytes 393224 | tf_op jit(solution)/shard_map/ppermute | solution.py:22
  20.5 8.4 %collective-permute-start.5 = (bf16[128,512]{1,0:T(8,128)(2,1)S(1)}, bf16[128,512]{1,0:T(8,128)(2,1)S(1)}, u32[]{:S(2)}, u32[]{:S(2)}) collective-permute-start(bf16[128,512]{1,0:T(8,128)(2,1)S(1)} %collective-permute-done.1.refs_2_), channel_id=1, source_target_pairs={{0,1},{1,0},{2,3},{3,2},{4,5},{5,4},{6,7},{7,6},{8,9},{9,8},{10,11... | collective-permute-start | bytes 393224 | tf_op jit(solution)/shard_map/ppermute | solution.py:22
  20.5 10.2 %collective-permute-start.20 = (bf16[288,256]{1,0:T(8,128)(2,1)S(1)}, bf16[288,256]{1,0:T(8,128)(2,1)S(1)}, u32[]{:S(2)}, u32[]{:S(2)}) collective-permute-start(bf16[288,256]{1,0:T(8,128)(2,1)S(1)} %pad_maximum_fusion.2.refs_16_), channel_id=1, source_target_pairs={{0,2},{1,3},{2,0},{3,1},{4,6},{5,7},{6,4},{7,5},{8,10},{9,11},{10,... | collective-permute-start | bytes 442376 | tf_op jit(solution)/shard_map/ppermute | solution.py:22
  21.6 4.8 %collective-permute-start.17 = (bf16[144,256]{1,0:T(8,128)(2,1)S(1)}, bf16[144,256]{1,0:T(8,128)(2,1)S(1)}, u32[]{:S(2)}, u32[]{:S(2)}) collective-permute-start(bf16[144,256]{1,0:T(8,128)(2,1)S(1)} %collective-permute-done.16), channel_id=1, source_target_pairs={{0,4},{4,0},{8,12},{12,8},{1,5},{5,1},{9,13},{13,9},{2,6},{6,2},{1... | collective-permute-start | bytes 221192 | tf_op jit(solution)/shard_map/ppermute | solution.py:22
  24.1 8.3 %collective-permute-start.10 = (bf16[128,512]{1,0:T(8,128)(2,1)S(1)}, bf16[128,512]{1,0:T(8,128)(2,1)S(1)}, u32[]{:S(2)}, u32[]{:S(2)}) collective-permute-start(bf16[128,512]{1,0:T(8,128)(2,1)S(1)} %get-tuple-element.49), channel_id=1, source_target_pairs={{0,12},{4,8},{8,4},{12,0},{1,13},{5,9},{9,5},{13,1},{2,14},{6,10},... | collective-permute-start | bytes 393224 | tf_op jit(solution)/shard_map/ppermute | solution.py:22
  25.8 11.2 %collective-permute-start.9 = (bf16[128,512]{1,0:T(8,128)(2,1)S(1)}, bf16[128,512]{1,0:T(8,128)(2,1)S(1)}, u32[]{:S(2)}, u32[]{:S(2)}) collective-permute-start(bf16[128,512]{1,0:T(8,128)(2,1)S(1)} %get-tuple-element.50), channel_id=1, source_target_pairs={{0,8},{4,12},{8,0},{12,4},{1,9},{5,13},{9,1},{13,5},{2,10},{6,14},... | collective-permute-start | bytes 393224 | tf_op jit(solution)/shard_map/ppermute | solution.py:22
  26.4 10.6 %collective-permute-start.8 = (bf16[128,512]{1,0:T(8,128)(2,1)S(1)}, bf16[128,512]{1,0:T(8,128)(2,1)S(1)}, u32[]{:S(2)}, u32[]{:S(2)}) collective-permute-start(bf16[128,512]{1,0:T(8,128)(2,1)S(1)} %get-tuple-element.51), channel_id=1, source_target_pairs={{0,4},{4,0},{8,12},{12,8},{1,5},{5,1},{9,13},{13,9},{2,6},{6,2},{1... | collective-permute-start | bytes 393224 | tf_op jit(solution)/shard_map/ppermute | solution.py:22
  28.9 8.6 %collective-permute-start.21 = (bf16[288,256]{1,0:T(8,128)(2,1)S(1)}, bf16[288,256]{1,0:T(8,128)(2,1)S(1)}, u32[]{:S(2)}, u32[]{:S(2)}) collective-permute-start(bf16[288,256]{1,0:T(8,128)(2,1)S(1)} %constant_dynamic-update-slice_fusion.refs_17_), channel_id=1, source_target_pairs={{0,2},{1,3},{2,0},{3,1},{4,6},{5,7},{6,4},{7,5},{8,10},{9,11},{10,... | collective-permute-start | bytes 442376 | tf_op jit(solution)/shard_map/ppermute | solution.py:22
  30.8 6.8 %collective-permute-start.11 = (bf16[128,512]{1,0:T(8,128)(2,1)S(1)}, bf16[128,512]{1,0:T(8,128)(2,1)S(1)}, u32[]{:S(2)}, u32[]{:S(2)}) collective-permute-start(bf16[128,512]{1,0:T(8,128)(2,1)S(1)} %get-tuple-element.52.refs_0_), channel_id=1, source_target_pairs={{0,1},{1,0},{2,3},{3,2},{4,5},{5,4},{6,7},{7,6},{8,9},{9,8},{10,11... | collective-permute-start | bytes 393224 | tf_op jit(solution)/shard_map/ppermute | solution.py:22
  32.5 5.6 %collective-permute-start.14 = (bf16[128,512]{1,0:T(8,128)(2,1)S(1)}, bf16[128,512]{1,0:T(8,128)(2,1)S(1)}, u32[]{:S(2)}, u32[]{:S(2)}) collective-permute-start(bf16[128,512]{1,0:T(8,128)(2,1)S(1)} %collective-permute-done.10.refs_3_), channel_id=1, source_target_pairs={{0,1},{1,0},{2,3},{3,2},{4,5},{5,4},{6,7},{7,6},{8,9},{9,8},{10,11... | collective-permute-start | bytes 393224 | tf_op jit(solution)/shard_map/ppermute | solution.py:22
  37.5 2.4 %collective-permute-start.18 = (bf16[288,256]{1,0:T(8,128)(2,1)S(1)}, bf16[288,256]{1,0:T(8,128)(2,1)S(1)}, u32[]{:S(2)}, u32[]{:S(2)}) collective-permute-start(bf16[288,256]{1,0:T(8,128)(2,1)S(1)} %pad_maximum_fusion.2.refs_16_), channel_id=1, source_target_pairs={{0,1},{1,0},{2,3},{3,2},{4,5},{5,4},{6,7},{7,6},{8,9},{9,8},{10,11... | collective-permute-start | bytes 442376 | tf_op jit(solution)/shard_map/ppermute | solution.py:22
  37.6 2.3 %collective-permute-start.19 = (bf16[288,256]{1,0:T(8,128)(2,1)S(1)}, bf16[288,256]{1,0:T(8,128)(2,1)S(1)}, u32[]{:S(2)}, u32[]{:S(2)}) collective-permute-start(bf16[288,256]{1,0:T(8,128)(2,1)S(1)} %constant_dynamic-update-slice_fusion.refs_17_), channel_id=1, source_target_pairs={{0,1},{1,0},{2,3},{3,2},{4,5},{5,4},{6,7},{7,6},{8,9},{9,8},{10,11... | collective-permute-start | bytes 442376 | tf_op jit(solution)/shard_map/ppermute | solution.py:22
  38.1 1.9 %collective-permute-start.22 = (bf16[288,256]{1,0:T(8,128)(2,1)S(1)}, bf16[288,256]{1,0:T(8,128)(2,1)S(1)}, u32[]{:S(2)}, u32[]{:S(2)}) collective-permute-start(bf16[288,256]{1,0:T(8,128)(2,1)S(1)} %collective-permute-done.20.refs_20_), channel_id=1, source_target_pairs={{0,1},{1,0},{2,3},{3,2},{4,5},{5,4},{6,7},{7,6},{8,9},{9,8},{10,11... | collective-permute-start | bytes 442376 | tf_op jit(solution)/shard_map/ppermute | solution.py:22
  42.3 7.8 %collective-permute-start.25 = (bf16[384,256]{1,0:T(8,128)(2,1)S(1)}, bf16[384,256]{1,0:T(8,128)(2,1)S(1)}, u32[]{:S(2)}, u32[]{:S(2)}) collective-permute-start(bf16[384,256]{1,0:T(8,128)(2,1)S(1)} %pairs_far.3), channel_id=1, source_target_pairs={{0,2},{1,3},{2,0},{3,1},{4,6},{5,7},{6,4},{7,5},{8,10},{9,11},{10,... | collective-permute-start | bytes 589832 | tf_op jit(solution)/shard_map/ppermute | solution.py:22
  45.5 8.2 %collective-permute-start.24 = (bf16[128,256]{1,0:T(8,128)(2,1)S(1)}, bf16[128,256]{1,0:T(8,128)(2,1)S(1)}, u32[]{:S(2)}, u32[]{:S(2)}) collective-permute-start(bf16[128,256]{1,0:T(8,128)(2,1)S(1)} %pairs_far.2), channel_id=1, source_target_pairs={{0,2},{1,3},{2,0},{3,1},{4,6},{5,7},{6,4},{7,5},{8,10},{9,11},{10,... | collective-permute-start | bytes 196616 | tf_op jit(solution)/shard_map/ppermute | solution.py:22
  50.2 5.3 %collective-permute-start.26 = (bf16[128,256]{1,0:T(8,128)(2,1)S(1)}, bf16[128,256]{1,0:T(8,128)(2,1)S(1)}, u32[]{:S(2)}, u32[]{:S(2)}) collective-permute-start(bf16[128,256]{1,0:T(8,128)(2,1)S(1)} %get-tuple-element.53), channel_id=1, source_target_pairs={{0,4},{4,0},{8,12},{12,8},{1,5},{5,1},{9,13},{13,9},{2,6},{6,2},{1... | collective-permute-start | bytes 196616 | tf_op jit(solution)/shard_map/ppermute | solution.py:22
  50.2 6.4 %collective-permute-start.28 = (bf16[128,256]{1,0:T(8,128)(2,1)S(1)}, bf16[128,256]{1,0:T(8,128)(2,1)S(1)}, u32[]{:S(2)}, u32[]{:S(2)}) collective-permute-start(bf16[128,256]{1,0:T(8,128)(2,1)S(1)} %get-tuple-element.54), channel_id=1, source_target_pairs={{0,12},{4,8},{8,4},{12,0},{1,13},{5,9},{9,5},{13,1},{2,14},{6,10},... | collective-permute-start | bytes 196616 | tf_op jit(solution)/shard_map/ppermute | solution.py:22
  52.3 6.9 %collective-permute-start.27 = (bf16[128,256]{1,0:T(8,128)(2,1)S(1)}, bf16[128,256]{1,0:T(8,128)(2,1)S(1)}, u32[]{:S(2)}, u32[]{:S(2)}) collective-permute-start(bf16[128,256]{1,0:T(8,128)(2,1)S(1)} %get-tuple-element.55), channel_id=1, source_target_pairs={{0,8},{4,12},{8,0},{12,4},{1,9},{5,13},{9,1},{13,5},{2,10},{6,14},... | collective-permute-start | bytes 196616 | tf_op jit(solution)/shard_map/ppermute | solution.py:22
  59.2 6.7 %collective-permute-start.33 = (bf16[128,256]{1,0:T(8,128)(2,1)S(1)}, bf16[128,256]{1,0:T(8,128)(2,1)S(1)}, u32[]{:S(2)}, u32[]{:S(2)}) collective-permute-start(bf16[128,256]{1,0:T(8,128)(2,1)S(1)} %multiply_convert_fusion), channel_id=1, source_target_pairs={{0,12},{4,8},{8,4},{12,0},{1,13},{5,9},{9,5},{13,1},{2,14},{6,10},... | collective-permute-start | bytes 196616 | tf_op jit(solution)/shard_map/ppermute | solution.py:22
  61.6 5.8 %collective-permute-start.32 = (bf16[128,256]{1,0:T(8,128)(2,1)S(1)}, bf16[128,256]{1,0:T(8,128)(2,1)S(1)}, u32[]{:S(2)}, u32[]{:S(2)}) collective-permute-start(bf16[128,256]{1,0:T(8,128)(2,1)S(1)} %multiply_convert_fusion), channel_id=1, source_target_pairs={{0,8},{4,12},{8,0},{12,4},{1,9},{5,13},{9,1},{13,5},{2,10},{6,14},... | collective-permute-start | bytes 196616 | tf_op jit(solution)/shard_map/ppermute | solution.py:22
  61.6 7.2 %collective-permute-start.29 = (bf16[128,256]{1,0:T(8,128)(2,1)S(1)}, bf16[128,256]{1,0:T(8,128)(2,1)S(1)}, u32[]{:S(2)}, u32[]{:S(2)}) collective-permute-start(bf16[128,256]{1,0:T(8,128)(2,1)S(1)} %multiply_convert_fusion), channel_id=1, source_target_pairs={{0,4},{4,0},{8,12},{12,8},{1,5},{5,1},{9,13},{13,9},{2,6},{6,2},{1... | collective-permute-start | bytes 196616 | tf_op jit(solution)/shard_map/ppermute | solution.py:22
  67.4 5.0 %collective-permute-start.34 = (bf16[256,256]{1,0:T(8,128)(2,1)S(1)}, bf16[256,256]{1,0:T(8,128)(2,1)S(1)}, u32[]{:S(2)}, u32[]{:S(2)}) collective-permute-start(bf16[256,256]{1,0:T(8,128)(2,1)S(1)} %pad_maximum_fusion.4), channel_id=1, source_target_pairs={{0,2},{1,3},{2,0},{3,1},{4,6},{5,7},{6,4},{7,5},{8,10},{9,11},{10,... | collective-permute-start | bytes 393224 | tf_op jit(solution)/shard_map/ppermute | solution.py:22
  68.8 5.0 %collective-permute-start.30 = (bf16[256,256]{1,0:T(8,128)(2,1)S(1)}, bf16[256,256]{1,0:T(8,128)(2,1)S(1)}, u32[]{:S(2)}, u32[]{:S(2)}) collective-permute-start(bf16[256,256]{1,0:T(8,128)(2,1)S(1)} %pad_maximum_fusion.3), channel_id=1, source_target_pairs={{0,2},{1,3},{2,0},{3,1},{4,6},{5,7},{6,4},{7,5},{8,10},{9,11},{10,... | collective-permute-start | bytes 393224 | tf_op jit(solution)/shard_map/ppermute | solution.py:22
  72.4 1.6 %collective-permute-start.35 = (bf16[512,256]{1,0:T(8,128)(2,1)S(1)}, bf16[512,256]{1,0:T(8,128)(2,1)S(1)}, u32[]{:S(2)}, u32[]{:S(2)}) collective-permute-start(bf16[512,256]{1,0:T(8,128)(2,1)S(1)} %constant_dynamic-update-slice_fusion.2.refs_2_), channel_id=1, source_target_pairs={{0,1},{1,0},{2,3},{3,2},{4,5},{5,4},{6,7},{7,6},{8,9},{9,8},{10,11... | collective-permute-start | bytes 786440 | tf_op jit(solution)/shard_map/ppermute | solution.py:22
  73.9 1.6 %collective-permute-start.31 = (bf16[512,256]{1,0:T(8,128)(2,1)S(1)}, bf16[512,256]{1,0:T(8,128)(2,1)S(1)}, u32[]{:S(2)}, u32[]{:S(2)}) collective-permute-start(bf16[512,256]{1,0:T(8,128)(2,1)S(1)} %pad_maximum_fusion.1.refs_0_), channel_id=1, source_target_pairs={{0,1},{1,0},{2,3},{3,2},{4,5},{5,4},{6,7},{7,6},{8,9},{9,8},{10,11... | collective-permute-start | bytes 786440 | tf_op jit(solution)/shard_map/ppermute | solution.py:22
  (5 other events, 39.2 us)

commit v7 on v6

--- a/solution.py
+++ b/solution.py
@@ -342,12 +342,12 @@
         (far_high,) = pairs(False, range(1, planes))
         far_high = swapped(far_high, "narrow", FAR)
         (far_low,) = pairs(False, range(1))
-        far_low = swapped(far_low, "narrow", FAR)
     else:
         (far_all,) = pairs(False, range(planes))
         far_high = swapped(far_all[rows:], "narrow", FAR)
-        far_low = swapped(far_all[:rows], "narrow", FAR)
+        far_low = far_all[:rows]
     own_sum, t_keep = pairs(True, range(planes))
+    far_low = swapped(after(far_low, own_sum), "narrow", FAR)
     sums_high = own_sum[rows:] + far_high.astype(jnp.float32)
     sums_low = own_sum[:rows] + far_low.astype(jnp.float32)
     t_keep = pl.pallas_call(

time: 76.8 us -> 76.5 us (level)
  transfers between devices with their start and end apart: 36 -> 36, of which waited for: 17 -> 16; matrix products, arithmetic and copies ran while one was open for 5% -> 5% of each run, Pallas kernels for 7% -> 7%
where the time goes in v7:
time: 76.5 us; the launch traced here: 76.3 us
  starting transfers between devices  36 us (47%)
  waiting for transfers between devices  26.1 us (34%)
  Pallas kernels  8.63 us (11%)
  matrix products  2.96 us (4%)
  local copies, waits for them, and re-layouts  1.49 us (2%)
  other arithmetic  0.92 us (1%)
    ppermute x36, starting transfers between devices, swapped(): lax.ppermute(value, axis, [(source, source ^ bit) for source in range(cou...  36 us
    ppermute x36, waiting for transfers between devices, swapped(): lax.ppermute(value, axis, [(source, source ^ bit) for source in range(cou...  26.1 us
    pallas_call x3, Pallas kernels, pairs(): pl.pallas_call(functools.partial(pair_values_kernel, planes, lanes, rows,...  7.06 us
    dot_general x1, matrix products, per_device(): jnp.dot(after(teacher, own_core), low_weight, preferred_element_type=jnp....  2.96 us
  transfers between devices with their start and end apart: 36, of which 16 were waited for; matrix products, arithmetic and copies ran while one was open for 5% of the time, Pallas kernels for 7%

profile of v7, /device:TPU:0, one launch (start us, length us, event | category | flops | bytes accessed | tf_op | source)
XLA Modules:
  0.0 76.3 jit_solution(5694264019611395817)
XLA Ops:
  0.0 1.4 %constant_dynamic-slice_fusion.3 = (bf16[128,512]{1,0:T(8,128)(2,1)S(1)}, bf16[128,512]{1,0:T(8,128)(2,1)S(1)}, bf16[128,512]{1,0:T(8,128)(2,1)S(1)}, bf16[128,5...) fusion(bf16[128,4096]{1,0:T(8,128)(2,1)} %param.6, ...), kind=kLoop, calls=%fused_computation.20 | loop fusion | bytes 2097184 | tf_op jit(solution)/shard_map/dynamic_slice | solution.py:256
  1.4 5.1 %collective-permute-start.2 = (bf16[128,512]{1,0:T(8,128)(2,1)S(1)}, bf16[128,512]{1,0:T(8,128)(2,1)S(1)}, u32[]{:S(2)}, u32[]{:S(2)}) collective-permute-start(bf16[128,512]{1,0:T(8,128)(2,1)S(1)} %get-tuple-element.46), channel_id=1, source_target_pairs={{0,12},{4,8},{8,4},{12,0},{1,13},{5,9},{9,5},{13,1},{2,14},{6,10},... | collective-permute-start | bytes 393224 | tf_op jit(solution)/shard_map/ppermute | solution.py:22
  6.6 1.6 %collective-permute-start.7 = (bf16[512,512]{1,0:T(8,128)(2,1)S(1)}, bf16[512,512]{1,0:T(8,128)(2,1)S(1)}, u32[]{:S(2)}, u32[]{:S(2)}) collective-permute-start(bf16[512,512]{1,0:T(8,128)(2,1)S(1)} %pad_maximum_fusion), channel_id=1, source_target_pairs={{0,2},{1,3},{2,0},{3,1},{4,6},{5,7},{6,4},{7,5},{8,10},{9,11},{10,... | collective-permute-start | bytes 1572872 | tf_op jit(solution)/shard_map/ppermute | solution.py:22
  8.8 3.0 %fusion.2 = bf16[128,256]{1,0:T(8,128)(2,1)S(1)} fusion(bf16[128,4096]{1,0:T(8,128)(2,1)} %param.6, f32[4096,256]{1,0:T(8,128)} %param.7), kind=kOutput, calls=%fused_computation.2 | convolution fusion | flops 269516800 | bytes 5308416 | tf_op jit(solution)/shard_map/dot_general | solution.py:267
  12.6 1.2 %collective-permute-start = (bf16[128,512]{1,0:T(8,128)(2,1)S(1)}, bf16[128,512]{1,0:T(8,128)(2,1)S(1)}, u32[]{:S(2)}, u32[]{:S(2)}) collective-permute-start(bf16[128,512]{1,0:T(8,128)(2,1)S(1)} %get-tuple-element.48), channel_id=1, source_target_pairs={{0,4},{4,0},{8,12},{12,8},{1,5},{5,1},{9,13},{13,9},{2,6},{6,2},{1... | collective-permute-start | bytes 393224 | tf_op jit(solution)/shard_map/ppermute | solution.py:22
  13.9 3.6 %collective-permute-start.16 = (bf16[144,256]{1,0:T(8,128)(2,1)S(1)}, bf16[144,256]{1,0:T(8,128)(2,1)S(1)}, u32[]{:S(2)}, u32[]{:S(2)}) collective-permute-start(bf16[144,256]{1,0:T(8,128)(2,1)S(1)} %pad_maximum_fusion.5), channel_id=1, source_target_pairs={{0,8},{4,12},{8,0},{12,4},{1,9},{5,13},{9,1},{13,5},{2,10},{6,14},... | collective-permute-start | bytes 221192 | tf_op jit(solution)/shard_map/ppermute | solution.py:22
  17.9 2.6 %collective-permute-done.15 = bf16[144,256]{1,0:T(8,128)(2,1)S(1)} collective-permute-done((bf16[144,256]{1,0:T(8,128)(2,1)S(1)}, bf16[144,256]{1,0:T(8,128)(2,1)S(1)}, u32[]{:S(2)}, u32[]{:S(2)}) %collective-permute-start.15) | collective-permute-done | bytes 73760 | tf_op jit(solution)/shard_map/ppermute | solution.py:22
  20.6 1.1 %collective-permute-start.20 = (bf16[288,256]{1,0:T(8,128)(2,1)S(1)}, bf16[288,256]{1,0:T(8,128)(2,1)S(1)}, u32[]{:S(2)}, u32[]{:S(2)}) collective-permute-start(bf16[288,256]{1,0:T(8,128)(2,1)S(1)} %pad_maximum_fusion.2.refs_16_), channel_id=1, source_target_pairs={{0,2},{1,3},{2,0},{3,1},{4,6},{5,7},{6,4},{7,5},{8,10},{9,11},{10,... | collective-permute-start | bytes 442376 | tf_op jit(solution)/shard_map/ppermute | solution.py:22
  21.7 2.4 %collective-permute-start.17 = (bf16[144,256]{1,0:T(8,128)(2,1)S(1)}, bf16[144,256]{1,0:T(8,128)(2,1)S(1)}, u32[]{:S(2)}, u32[]{:S(2)}) collective-permute-start(bf16[144,256]{1,0:T(8,128)(2,1)S(1)} %collective-permute-done.16), channel_id=1, source_target_pairs={{0,4},{4,0},{8,12},{12,8},{1,5},{5,1},{9,13},{13,9},{2,6},{6,2},{1... | collective-permute-start | bytes 221192 | tf_op jit(solution)/shard_map/ppermute | solution.py:22
  24.1 1.7 %collective-permute-start.10 = (bf16[128,512]{1,0:T(8,128)(2,1)S(1)}, bf16[128,512]{1,0:T(8,128)(2,1)S(1)}, u32[]{:S(2)}, u32[]{:S(2)}) collective-permute-start(bf16[128,512]{1,0:T(8,128)(2,1)S(1)} %get-tuple-element.51), channel_id=1, source_target_pairs={{0,12},{4,8},{8,4},{12,0},{1,13},{5,9},{9,5},{13,1},{2,14},{6,10},... | collective-permute-start | bytes 393224 | tf_op jit(solution)/shard_map/ppermute | solution.py:22
  26.4 2.5 %collective-permute-start.8 = (bf16[128,512]{1,0:T(8,128)(2,1)S(1)}, bf16[128,512]{1,0:T(8,128)(2,1)S(1)}, u32[]{:S(2)}, u32[]{:S(2)}) collective-permute-start(bf16[128,512]{1,0:T(8,128)(2,1)S(1)} %get-tuple-element.53), channel_id=1, source_target_pairs={{0,4},{4,0},{8,12},{12,8},{1,5},{5,1},{9,13},{13,9},{2,6},{6,2},{1... | collective-permute-start | bytes 393224 | tf_op jit(solution)/shard_map/ppermute | solution.py:22
  28.9 1.9 %collective-permute-start.21 = (bf16[288,256]{1,0:T(8,128)(2,1)S(1)}, bf16[288,256]{1,0:T(8,128)(2,1)S(1)}, u32[]{:S(2)}, u32[]{:S(2)}) collective-permute-start(bf16[288,256]{1,0:T(8,128)(2,1)S(1)} %constant_dynamic-update-slice_fusion.refs_17_), channel_id=1, source_target_pairs={{0,2},{1,3},{2,0},{3,1},{4,6},{5,7},{6,4},{7,5},{8,10},{9,11},{10,... | collective-permute-start | bytes 442376 | tf_op jit(solution)/shard_map/ppermute | solution.py:22
  30.8 1.7 %collective-permute-done.10.refs_3_ = bf16[128,512]{1,0:T(8,128)(2,1)S(1)} collective-permute-done((bf16[128,512]{1,0:T(8,128)(2,1)S(1)}, bf16[128,512]{1,0:T(8,128)(2,1)S(1)}, u32[]{:S(2)}, u32[]{:S(2)}) %collective-permute-start.10) | collective-permute-done | bytes 131104 | tf_op jit(solution)/shard_map/ppermute | solution.py:22
  32.5 4.5 %collective-permute-done.9.refs_2_ = bf16[128,512]{1,0:T(8,128)(2,1)S(1)} collective-permute-done((bf16[128,512]{1,0:T(8,128)(2,1)S(1)}, bf16[128,512]{1,0:T(8,128)(2,1)S(1)}, u32[]{:S(2)}, u32[]{:S(2)}) %collective-permute-start.9) | collective-permute-done | bytes 131104 | tf_op jit(solution)/shard_map/ppermute | solution.py:22
  39.0 0.9 %collective-permute-done.4.refs_5_ = bf16[128,512]{1,0:T(8,128)(2,1)S(1)} collective-permute-done((bf16[128,512]{1,0:T(8,128)(2,1)S(1)}, bf16[128,512]{1,0:T(8,128)(2,1)S(1)}, u32[]{:S(2)}, u32[]{:S(2)}) %collective-permute-start.4) | collective-permute-done | bytes 131104 | tf_op jit(solution)/shard_map/ppermute | solution.py:22
  40.0 2.3 %pairs_far.3 = bf16[384,256]{1,0:T(8,128)(2,1)S(1)} custom-call(s32[4,4]{1,0:T(4,128)S(1)} %copy-done, s32[2]{0:T(128)S(1)} %pad_add_fusion.place, bf16[128,512]{1,0:T(8,128)(2,1)S(1)} %get-tuple-element.49.refs_0_, bf16[128,512]{1,0:T(8,128)(2,1)S(1)} %collective-permute-done.refs_1_, bf16[128,512]{1,0:T(8,128)(2,1)S(1)} %collective-permute-done.1.refs_2_, ...), custom_call_target="tpu_custom_call" | custom-call | flops 1207959552 | bytes 3145728 | tf_op jit(solution)/shard_map/pairs_far/pallas_call | solution.py:311
  42.3 1.6 %collective-permute-start.25 = (bf16[384,256]{1,0:T(8,128)(2,1)S(1)}, bf16[384,256]{1,0:T(8,128)(2,1)S(1)}, u32[]{:S(2)}, u32[]{:S(2)}) collective-permute-start(bf16[384,256]{1,0:T(8,128)(2,1)S(1)} %pairs_far.3), channel_id=1, source_target_pairs={{0,2},{1,3},{2,0},{3,1},{4,6},{5,7},{6,4},{7,5},{8,10},{9,11},{10,... | collective-permute-start | bytes 589832 | tf_op jit(solution)/shard_map/ppermute | solution.py:22
  43.9 3.1 %pairs_own.1 = (f32[512,256]{1,0:T(8,128)S(1)}, bf16[2048,256]{1,0:T(8,128)(2,1)S(1)}) custom-call(s32[4,4]{1,0:T(4,128)S(1)} %copy-done, s32[2]{0:T(128)S(1)} %pad_add_fusion.place, bf16[128,512]{1,0:T(8,128)(2,1)S(1)} %get-tuple-element.49.refs_0_, bf16[128,512]{1,0:T(8,128)(2,1)S(1)} %collective-permute-done.refs_1_, ...), custom_call_target="tpu_custom_call" | custom-call | flops 1610612736 | bytes 3145728 | tf_op jit(solution)/shard_map/pairs_own/pallas_call | solution.py:311
  47.3 1.6 %pairs_far.2 = bf16[128,256]{1,0:T(8,128)(2,1)S(1)} custom-call(s32[4,4]{1,0:T(4,128)S(1)} %copy-done, s32[2]{0:T(128)S(1)} %pad_add_fusion.place, bf16[128,512]{1,0:T(8,128)(2,1)S(1)} %get-tuple-element.49.refs_0_, bf16[128,512]{1,0:T(8,128)(2,1)S(1)} %collective-permute-done.refs_1_, bf16[128,512]{1,0:T(8,128)(2,1)S(1)} %collective-permute-done.1.refs_2_, ...), custom_call_target="tpu_custom_call" | custom-call | flops 402653184 | bytes 3145728 | tf_op jit(solution)/shard_map/pairs_far/pallas_call | solution.py:311
  49.7 2.0 %collective-permute-start.28 = (bf16[128,256]{1,0:T(8,128)(2,1)S(1)}, bf16[128,256]{1,0:T(8,128)(2,1)S(1)}, u32[]{:S(2)}, u32[]{:S(2)}) collective-permute-start(bf16[128,256]{1,0:T(8,128)(2,1)S(1)} %get-tuple-element.56), channel_id=1, source_target_pairs={{0,12},{4,8},{8,4},{12,0},{1,13},{5,9},{9,5},{13,1},{2,14},{6,10},... | collective-permute-start | bytes 196616 | tf_op jit(solution)/shard_map/ppermute | solution.py:22
  51.8 1.4 %collective-permute-start.27 = (bf16[128,256]{1,0:T(8,128)(2,1)S(1)}, bf16[128,256]{1,0:T(8,128)(2,1)S(1)}, u32[]{:S(2)}, u32[]{:S(2)}) collective-permute-start(bf16[128,256]{1,0:T(8,128)(2,1)S(1)} %get-tuple-element.57), channel_id=1, source_target_pairs={{0,8},{4,12},{8,0},{12,4},{1,9},{5,13},{9,1},{13,5},{2,10},{6,14},... | collective-permute-start | bytes 196616 | tf_op jit(solution)/shard_map/ppermute | solution.py:22
  54.0 2.4 %collective-permute-done.28 = bf16[128,256]{1,0:T(8,128)(2,1)S(1)} collective-permute-done((bf16[128,256]{1,0:T(8,128)(2,1)S(1)}, bf16[128,256]{1,0:T(8,128)(2,1)S(1)}, u32[]{:S(2)}, u32[]{:S(2)}) %collective-permute-start.28) | collective-permute-done | bytes 65568 | tf_op jit(solution)/shard_map/ppermute | solution.py:22
  56.3 2.6 %collective-permute-done.27 = bf16[128,256]{1,0:T(8,128)(2,1)S(1)} collective-permute-done((bf16[128,256]{1,0:T(8,128)(2,1)S(1)}, bf16[128,256]{1,0:T(8,128)(2,1)S(1)}, u32[]{:S(2)}, u32[]{:S(2)}) %collective-permute-start.27) | collective-permute-done | bytes 65568 | tf_op jit(solution)/shard_map/ppermute | solution.py:22
  59.0 2.0 %collective-permute-start.33 = (bf16[128,256]{1,0:T(8,128)(2,1)S(1)}, bf16[128,256]{1,0:T(8,128)(2,1)S(1)}, u32[]{:S(2)}, u32[]{:S(2)}) collective-permute-start(bf16[128,256]{1,0:T(8,128)(2,1)S(1)} %multiply_convert_fusion), channel_id=1, source_target_pairs={{0,12},{4,8},{8,4},{12,0},{1,13},{5,9},{9,5},{13,1},{2,14},{6,10},... | collective-permute-start | bytes 196616 | tf_op jit(solution)/shard_map/ppermute | solution.py:22
  60.9 2.5 %collective-permute-start.29 = (bf16[128,256]{1,0:T(8,128)(2,1)S(1)}, bf16[128,256]{1,0:T(8,128)(2,1)S(1)}, u32[]{:S(2)}, u32[]{:S(2)}) collective-permute-start(bf16[128,256]{1,0:T(8,128)(2,1)S(1)} %multiply_convert_fusion), channel_id=1, source_target_pairs={{0,4},{4,0},{8,12},{12,8},{1,5},{5,1},{9,13},{13,9},{2,6},{6,2},{1... | collective-permute-start | bytes 196616 | tf_op jit(solution)/shard_map/ppermute | solution.py:22
  63.4 2.4 %collective-permute-done.33 = bf16[128,256]{1,0:T(8,128)(2,1)S(1)} collective-permute-done((bf16[128,256]{1,0:T(8,128)(2,1)S(1)}, bf16[128,256]{1,0:T(8,128)(2,1)S(1)}, u32[]{:S(2)}, u32[]{:S(2)}) %collective-permute-start.33) | collective-permute-done | bytes 65568 | tf_op jit(solution)/shard_map/ppermute | solution.py:22
  65.8 1.2 %collective-permute-done.32 = bf16[128,256]{1,0:T(8,128)(2,1)S(1)} collective-permute-done((bf16[128,256]{1,0:T(8,128)(2,1)S(1)}, bf16[128,256]{1,0:T(8,128)(2,1)S(1)}, u32[]{:S(2)}, u32[]{:S(2)}) %collective-permute-start.32) | collective-permute-done | bytes 65568 | tf_op jit(solution)/shard_map/ppermute | solution.py:22
  67.0 1.5 %collective-permute-start.34 = (bf16[256,256]{1,0:T(8,128)(2,1)S(1)}, bf16[256,256]{1,0:T(8,128)(2,1)S(1)}, u32[]{:S(2)}, u32[]{:S(2)}) collective-permute-start(bf16[256,256]{1,0:T(8,128)(2,1)S(1)} %pad_maximum_fusion.4), channel_id=1, source_target_pairs={{0,2},{1,3},{2,0},{3,1},{4,6},{5,7},{6,4},{7,5},{8,10},{9,11},{10,... | collective-permute-start | bytes 393224 | tf_op jit(solution)/shard_map/ppermute | solution.py:22
  69.2 2.8 %collective-permute-done.34 = bf16[256,256]{1,0:T(8,128)(2,1)S(1)} collective-permute-done((bf16[256,256]{1,0:T(8,128)(2,1)S(1)}, bf16[256,256]{1,0:T(8,128)(2,1)S(1)}, u32[]{:S(2)}, u32[]{:S(2)}) %collective-permute-start.34) | collective-permute-done | bytes 131104 | tf_op jit(solution)/shard_map/ppermute | solution.py:22
  72.2 1.4 %collective-permute-done.30 = bf16[256,256]{1,0:T(8,128)(2,1)S(1)} collective-permute-done((bf16[256,256]{1,0:T(8,128)(2,1)S(1)}, bf16[256,256]{1,0:T(8,128)(2,1)S(1)}, u32[]{:S(2)}, u32[]{:S(2)}) %collective-permute-start.30) | collective-permute-done | bytes 131104 | tf_op jit(solution)/shard_map/ppermute | solution.py:22
  73.7 1.5 %collective-permute-done.31.refs_1_ = bf16[512,256]{1,0:T(8,128)(2,1)S(1)} collective-permute-done((bf16[512,256]{1,0:T(8,128)(2,1)S(1)}, bf16[512,256]{1,0:T(8,128)(2,1)S(1)}, u32[]{:S(2)}, u32[]{:S(2)}) %collective-permute-start.31) | collective-permute-done | bytes 262176 | tf_op jit(solution)/shard_map/ppermute | solution.py:22
  75.2 1.2 %last.1 = f32[256,256]{1,0:T(8,128)} custom-call(bf16[256,2048]{1,0:T(8,128)(2,1)S(1)} %flip.1.t_keep, bf16[512,256]{1,0:T(8,128)(2,1)S(1)} %pad_maximum_fusion.1.refs_0_, bf16[512,256]{1,0:T(8,128)(2,1)S(1)} %collective-permute-done.31.refs_1_, bf16[512,256]{1,0:T(8,128)(2,1)S(1)} %constant_dynamic-update-slice_fusion.2.refs_2_, ...), custom_call_target="tpu_custom_call" | custom-call | flops 268435456 | bytes 2097152 | tf_op jit(solution)/shard_map/last/pallas_call | solution.py:375
  (69 shorter events, 7.6 us)
Async XLA Ops:
  1.4 12.5 %collective-permute-start.2 = (bf16[128,512]{1,0:T(8,128)(2,1)S(1)}, bf16[128,512]{1,0:T(8,128)(2,1)S(1)}, u32[]{:S(2)}, u32[]{:S(2)}) collective-permute-start(bf16[128,512]{1,0:T(8,128)(2,1)S(1)} %get-tuple-element.46), channel_id=1, source_target_pairs={{0,12},{4,8},{8,4},{12,0},{1,13},{5,9},{9,5},{13,1},{2,14},{6,10},... | collective-permute-start | bytes 393224 | tf_op jit(solution)/shard_map/ppermute | solution.py:22
  6.5 11.4 %collective-permute-start.1 = (bf16[128,512]{1,0:T(8,128)(2,1)S(1)}, bf16[128,512]{1,0:T(8,128)(2,1)S(1)}, u32[]{:S(2)}, u32[]{:S(2)}) collective-permute-start(bf16[128,512]{1,0:T(8,128)(2,1)S(1)} %get-tuple-element.47), channel_id=1, source_target_pairs={{0,8},{4,12},{8,0},{12,4},{1,9},{5,13},{9,1},{13,5},{2,10},{6,14},... | collective-permute-start | bytes 393224 | tf_op jit(solution)/shard_map/ppermute | solution.py:22
  6.5 2.3 %collective-permute-start.3 = (bf16[128,512]{1,0:T(8,128)(2,1)S(1)}, bf16[128,512]{1,0:T(8,128)(2,1)S(1)}, u32[]{:S(2)}, u32[]{:S(2)}) collective-permute-start(bf16[128,512]{1,0:T(8,128)(2,1)S(1)} %get-tuple-element.49.refs_0_), channel_id=1, source_target_pairs={{0,1},{1,0},{2,3},{3,2},{4,5},{5,4},{6,7},{7,6},{8,9},{9,8},{10,11... | collective-permute-start | bytes 393224 | tf_op jit(solution)/shard_map/ppermute | solution.py:22
  6.6 15.1 %collective-permute-start.7 = (bf16[512,512]{1,0:T(8,128)(2,1)S(1)}, bf16[512,512]{1,0:T(8,128)(2,1)S(1)}, u32[]{:S(2)}, u32[]{:S(2)}) collective-permute-start(bf16[512,512]{1,0:T(8,128)(2,1)S(1)} %pad_maximum_fusion), channel_id=1, source_target_pairs={{0,2},{1,3},{2,0},{3,1},{4,6},{5,7},{6,4},{7,5},{8,10},{9,11},{10,... | collective-permute-start | bytes 1572872 | tf_op jit(solution)/shard_map/ppermute | solution.py:22
  11.8 8.8 %collective-permute-start.15 = (bf16[144,256]{1,0:T(8,128)(2,1)S(1)}, bf16[144,256]{1,0:T(8,128)(2,1)S(1)}, u32[]{:S(2)}, u32[]{:S(2)}) collective-permute-start(bf16[144,256]{1,0:T(8,128)(2,1)S(1)} %pad_maximum_fusion.5), channel_id=1, source_target_pairs={{0,4},{4,0},{8,12},{12,8},{1,5},{5,1},{9,13},{13,9},{2,6},{6,2},{1... | collective-permute-start | bytes 221192 | tf_op jit(solution)/shard_map/ppermute | solution.py:22
  12.6 11.5 %collective-permute-start = (bf16[128,512]{1,0:T(8,128)(2,1)S(1)}, bf16[128,512]{1,0:T(8,128)(2,1)S(1)}, u32[]{:S(2)}, u32[]{:S(2)}) collective-permute-start(bf16[128,512]{1,0:T(8,128)(2,1)S(1)} %get-tuple-element.48), channel_id=1, source_target_pairs={{0,4},{4,0},{8,12},{12,8},{1,5},{5,1},{9,13},{13,9},{2,6},{6,2},{1... | collective-permute-start | bytes 393224 | tf_op jit(solution)/shard_map/ppermute | solution.py:22
  13.9 6.7 %collective-permute-start.16 = (bf16[144,256]{1,0:T(8,128)(2,1)S(1)}, bf16[144,256]{1,0:T(8,128)(2,1)S(1)}, u32[]{:S(2)}, u32[]{:S(2)}) collective-permute-start(bf16[144,256]{1,0:T(8,128)(2,1)S(1)} %pad_maximum_fusion.5), channel_id=1, source_target_pairs={{0,8},{4,12},{8,0},{12,4},{1,9},{5,13},{9,1},{13,5},{2,10},{6,14},... | collective-permute-start | bytes 221192 | tf_op jit(solution)/shard_map/ppermute | solution.py:22
  17.9 7.9 %collective-permute-start.6 = (bf16[128,512]{1,0:T(8,128)(2,1)S(1)}, bf16[128,512]{1,0:T(8,128)(2,1)S(1)}, u32[]{:S(2)}, u32[]{:S(2)}) collective-permute-start(bf16[128,512]{1,0:T(8,128)(2,1)S(1)} %collective-permute-done.2.refs_3_), channel_id=1, source_target_pairs={{0,1},{1,0},{2,3},{3,2},{4,5},{5,4},{6,7},{7,6},{8,9},{9,8},{10,11... | collective-permute-start | bytes 393224 | tf_op jit(solution)/shard_map/ppermute | solution.py:22
  20.5 8.4 %collective-permute-start.5 = (bf16[128,512]{1,0:T(8,128)(2,1)S(1)}, bf16[128,512]{1,0:T(8,128)(2,1)S(1)}, u32[]{:S(2)}, u32[]{:S(2)}) collective-permute-start(bf16[128,512]{1,0:T(8,128)(2,1)S(1)} %collective-permute-done.1.refs_2_), channel_id=1, source_target_pairs={{0,1},{1,0},{2,3},{3,2},{4,5},{5,4},{6,7},{7,6},{8,9},{9,8},{10,11... | collective-permute-start | bytes 393224 | tf_op jit(solution)/shard_map/ppermute | solution.py:22
  20.6 10.2 %collective-permute-start.20 = (bf16[288,256]{1,0:T(8,128)(2,1)S(1)}, bf16[288,256]{1,0:T(8,128)(2,1)S(1)}, u32[]{:S(2)}, u32[]{:S(2)}) collective-permute-start(bf16[288,256]{1,0:T(8,128)(2,1)S(1)} %pad_maximum_fusion.2.refs_16_), channel_id=1, source_target_pairs={{0,2},{1,3},{2,0},{3,1},{4,6},{5,7},{6,4},{7,5},{8,10},{9,11},{10,... | collective-permute-start | bytes 442376 | tf_op jit(solution)/shard_map/ppermute | solution.py:22
  21.7 4.8 %collective-permute-start.17 = (bf16[144,256]{1,0:T(8,128)(2,1)S(1)}, bf16[144,256]{1,0:T(8,128)(2,1)S(1)}, u32[]{:S(2)}, u32[]{:S(2)}) collective-permute-start(bf16[144,256]{1,0:T(8,128)(2,1)S(1)} %collective-permute-done.16), channel_id=1, source_target_pairs={{0,4},{4,0},{8,12},{12,8},{1,5},{5,1},{9,13},{13,9},{2,6},{6,2},{1... | collective-permute-start | bytes 221192 | tf_op jit(solution)/shard_map/ppermute | solution.py:22
  24.1 8.4 %collective-permute-start.10 = (bf16[128,512]{1,0:T(8,128)(2,1)S(1)}, bf16[128,512]{1,0:T(8,128)(2,1)S(1)}, u32[]{:S(2)}, u32[]{:S(2)}) collective-permute-start(bf16[128,512]{1,0:T(8,128)(2,1)S(1)} %get-tuple-element.51), channel_id=1, source_target_pairs={{0,12},{4,8},{8,4},{12,0},{1,13},{5,9},{9,5},{13,1},{2,14},{6,10},... | collective-permute-start | bytes 393224 | tf_op jit(solution)/shard_map/ppermute | solution.py:22
  25.8 11.2 %collective-permute-start.9 = (bf16[128,512]{1,0:T(8,128)(2,1)S(1)}, bf16[128,512]{1,0:T(8,128)(2,1)S(1)}, u32[]{:S(2)}, u32[]{:S(2)}) collective-permute-start(bf16[128,512]{1,0:T(8,128)(2,1)S(1)} %get-tuple-element.52), channel_id=1, source_target_pairs={{0,8},{4,12},{8,0},{12,4},{1,9},{5,13},{9,1},{13,5},{2,10},{6,14},... | collective-permute-start | bytes 393224 | tf_op jit(solution)/shard_map/ppermute | solution.py:22
  26.4 10.6 %collective-permute-start.8 = (bf16[128,512]{1,0:T(8,128)(2,1)S(1)}, bf16[128,512]{1,0:T(8,128)(2,1)S(1)}, u32[]{:S(2)}, u32[]{:S(2)}) collective-permute-start(bf16[128,512]{1,0:T(8,128)(2,1)S(1)} %get-tuple-element.53), channel_id=1, source_target_pairs={{0,4},{4,0},{8,12},{12,8},{1,5},{5,1},{9,13},{13,9},{2,6},{6,2},{1... | collective-permute-start | bytes 393224 | tf_op jit(solution)/shard_map/ppermute | solution.py:22
  28.9 8.6 %collective-permute-start.21 = (bf16[288,256]{1,0:T(8,128)(2,1)S(1)}, bf16[288,256]{1,0:T(8,128)(2,1)S(1)}, u32[]{:S(2)}, u32[]{:S(2)}) collective-permute-start(bf16[288,256]{1,0:T(8,128)(2,1)S(1)} %constant_dynamic-update-slice_fusion.refs_17_), channel_id=1, source_target_pairs={{0,2},{1,3},{2,0},{3,1},{4,6},{5,7},{6,4},{7,5},{8,10},{9,11},{10,... | collective-permute-start | bytes 442376 | tf_op jit(solution)/shard_map/ppermute | solution.py:22
  30.8 6.8 %collective-permute-start.11 = (bf16[128,512]{1,0:T(8,128)(2,1)S(1)}, bf16[128,512]{1,0:T(8,128)(2,1)S(1)}, u32[]{:S(2)}, u32[]{:S(2)}) collective-permute-start(bf16[128,512]{1,0:T(8,128)(2,1)S(1)} %get-tuple-element.54.refs_0_), channel_id=1, source_target_pairs={{0,1},{1,0},{2,3},{3,2},{4,5},{5,4},{6,7},{7,6},{8,9},{9,8},{10,11... | collective-permute-start | bytes 393224 | tf_op jit(solution)/shard_map/ppermute | solution.py:22
  32.5 5.6 %collective-permute-start.14 = (bf16[128,512]{1,0:T(8,128)(2,1)S(1)}, bf16[128,512]{1,0:T(8,128)(2,1)S(1)}, u32[]{:S(2)}, u32[]{:S(2)}) collective-permute-start(bf16[128,512]{1,0:T(8,128)(2,1)S(1)} %collective-permute-done.10.refs_3_), channel_id=1, source_target_pairs={{0,1},{1,0},{2,3},{3,2},{4,5},{5,4},{6,7},{7,6},{8,9},{9,8},{10,11... | collective-permute-start | bytes 393224 | tf_op jit(solution)/shard_map/ppermute | solution.py:22
  37.6 2.4 %collective-permute-start.18 = (bf16[288,256]{1,0:T(8,128)(2,1)S(1)}, bf16[288,256]{1,0:T(8,128)(2,1)S(1)}, u32[]{:S(2)}, u32[]{:S(2)}) collective-permute-start(bf16[288,256]{1,0:T(8,128)(2,1)S(1)} %pad_maximum_fusion.2.refs_16_), channel_id=1, source_target_pairs={{0,1},{1,0},{2,3},{3,2},{4,5},{5,4},{6,7},{7,6},{8,9},{9,8},{10,11... | collective-permute-start | bytes 442376 | tf_op jit(solution)/shard_map/ppermute | solution.py:22
  37.6 2.3 %collective-permute-start.19 = (bf16[288,256]{1,0:T(8,128)(2,1)S(1)}, bf16[288,256]{1,0:T(8,128)(2,1)S(1)}, u32[]{:S(2)}, u32[]{:S(2)}) collective-permute-start(bf16[288,256]{1,0:T(8,128)(2,1)S(1)} %constant_dynamic-update-slice_fusion.refs_17_), channel_id=1, source_target_pairs={{0,1},{1,0},{2,3},{3,2},{4,5},{5,4},{6,7},{7,6},{8,9},{9,8},{10,11... | collective-permute-start | bytes 442376 | tf_op jit(solution)/shard_map/ppermute | solution.py:22
  38.1 1.9 %collective-permute-start.22 = (bf16[288,256]{1,0:T(8,128)(2,1)S(1)}, bf16[288,256]{1,0:T(8,128)(2,1)S(1)}, u32[]{:S(2)}, u32[]{:S(2)}) collective-permute-start(bf16[288,256]{1,0:T(8,128)(2,1)S(1)} %collective-permute-done.20.refs_20_), channel_id=1, source_target_pairs={{0,1},{1,0},{2,3},{3,2},{4,5},{5,4},{6,7},{7,6},{8,9},{9,8},{10,11... | collective-permute-start | bytes 442376 | tf_op jit(solution)/shard_map/ppermute | solution.py:22
  42.3 7.3 %collective-permute-start.25 = (bf16[384,256]{1,0:T(8,128)(2,1)S(1)}, bf16[384,256]{1,0:T(8,128)(2,1)S(1)}, u32[]{:S(2)}, u32[]{:S(2)}) collective-permute-start(bf16[384,256]{1,0:T(8,128)(2,1)S(1)} %pairs_far.3), channel_id=1, source_target_pairs={{0,2},{1,3},{2,0},{3,1},{4,6},{5,7},{6,4},{7,5},{8,10},{9,11},{10,... | collective-permute-start | bytes 589832 | tf_op jit(solution)/shard_map/ppermute | solution.py:22
  49.0 4.3 %collective-permute-start.24 = (bf16[128,256]{1,0:T(8,128)(2,1)S(1)}, bf16[128,256]{1,0:T(8,128)(2,1)S(1)}, u32[]{:S(2)}, u32[]{:S(2)}) collective-permute-start(bf16[128,256]{1,0:T(8,128)(2,1)S(1)} %pairs_far.2), channel_id=1, source_target_pairs={{0,2},{1,3},{2,0},{3,1},{4,6},{5,7},{6,4},{7,5},{8,10},{9,11},{10,... | collective-permute-start | bytes 196616 | tf_op jit(solution)/shard_map/ppermute | solution.py:22
  49.6 4.3 %collective-permute-start.26 = (bf16[128,256]{1,0:T(8,128)(2,1)S(1)}, bf16[128,256]{1,0:T(8,128)(2,1)S(1)}, u32[]{:S(2)}, u32[]{:S(2)}) collective-permute-start(bf16[128,256]{1,0:T(8,128)(2,1)S(1)} %get-tuple-element.55), channel_id=1, source_target_pairs={{0,4},{4,0},{8,12},{12,8},{1,5},{5,1},{9,13},{13,9},{2,6},{6,2},{1... | collective-permute-start | bytes 196616 | tf_op jit(solution)/shard_map/ppermute | solution.py:22
  49.7 6.6 %collective-permute-start.28 = (bf16[128,256]{1,0:T(8,128)(2,1)S(1)}, bf16[128,256]{1,0:T(8,128)(2,1)S(1)}, u32[]{:S(2)}, u32[]{:S(2)}) collective-permute-start(bf16[128,256]{1,0:T(8,128)(2,1)S(1)} %get-tuple-element.56), channel_id=1, source_target_pairs={{0,12},{4,8},{8,4},{12,0},{1,13},{5,9},{9,5},{13,1},{2,14},{6,10},... | collective-permute-start | bytes 196616 | tf_op jit(solution)/shard_map/ppermute | solution.py:22
  51.8 7.2 %collective-permute-start.27 = (bf16[128,256]{1,0:T(8,128)(2,1)S(1)}, bf16[128,256]{1,0:T(8,128)(2,1)S(1)}, u32[]{:S(2)}, u32[]{:S(2)}) collective-permute-start(bf16[128,256]{1,0:T(8,128)(2,1)S(1)} %get-tuple-element.57), channel_id=1, source_target_pairs={{0,8},{4,12},{8,0},{12,4},{1,9},{5,13},{9,1},{13,5},{2,10},{6,14},... | collective-permute-start | bytes 196616 | tf_op jit(solution)/shard_map/ppermute | solution.py:22
  59.0 6.8 %collective-permute-start.33 = (bf16[128,256]{1,0:T(8,128)(2,1)S(1)}, bf16[128,256]{1,0:T(8,128)(2,1)S(1)}, u32[]{:S(2)}, u32[]{:S(2)}) collective-permute-start(bf16[128,256]{1,0:T(8,128)(2,1)S(1)} %multiply_convert_fusion), channel_id=1, source_target_pairs={{0,12},{4,8},{8,4},{12,0},{1,13},{5,9},{9,5},{13,1},{2,14},{6,10},... | collective-permute-start | bytes 196616 | tf_op jit(solution)/shard_map/ppermute | solution.py:22
  60.9 6.1 %collective-permute-start.32 = (bf16[128,256]{1,0:T(8,128)(2,1)S(1)}, bf16[128,256]{1,0:T(8,128)(2,1)S(1)}, u32[]{:S(2)}, u32[]{:S(2)}) collective-permute-start(bf16[128,256]{1,0:T(8,128)(2,1)S(1)} %multiply_convert_fusion), channel_id=1, source_target_pairs={{0,8},{4,12},{8,0},{12,4},{1,9},{5,13},{9,1},{13,5},{2,10},{6,14},... | collective-permute-start | bytes 196616 | tf_op jit(solution)/shard_map/ppermute | solution.py:22
  60.9 7.5 %collective-permute-start.29 = (bf16[128,256]{1,0:T(8,128)(2,1)S(1)}, bf16[128,256]{1,0:T(8,128)(2,1)S(1)}, u32[]{:S(2)}, u32[]{:S(2)}) collective-permute-start(bf16[128,256]{1,0:T(8,128)(2,1)S(1)} %multiply_convert_fusion), channel_id=1, source_target_pairs={{0,4},{4,0},{8,12},{12,8},{1,5},{5,1},{9,13},{13,9},{2,6},{6,2},{1... | collective-permute-start | bytes 196616 | tf_op jit(solution)/shard_map/ppermute | solution.py:22
  67.0 5.0 %collective-permute-start.34 = (bf16[256,256]{1,0:T(8,128)(2,1)S(1)}, bf16[256,256]{1,0:T(8,128)(2,1)S(1)}, u32[]{:S(2)}, u32[]{:S(2)}) collective-permute-start(bf16[256,256]{1,0:T(8,128)(2,1)S(1)} %pad_maximum_fusion.4), channel_id=1, source_target_pairs={{0,2},{1,3},{2,0},{3,1},{4,6},{5,7},{6,4},{7,5},{8,10},{9,11},{10,... | collective-permute-start | bytes 393224 | tf_op jit(solution)/shard_map/ppermute | solution.py:22
  68.5 5.0 %collective-permute-start.30 = (bf16[256,256]{1,0:T(8,128)(2,1)S(1)}, bf16[256,256]{1,0:T(8,128)(2,1)S(1)}, u32[]{:S(2)}, u32[]{:S(2)}) collective-permute-start(bf16[256,256]{1,0:T(8,128)(2,1)S(1)} %pad_maximum_fusion.3), channel_id=1, source_target_pairs={{0,2},{1,3},{2,0},{3,1},{4,6},{5,7},{6,4},{7,5},{8,10},{9,11},{10,... | collective-permute-start | bytes 393224 | tf_op jit(solution)/shard_map/ppermute | solution.py:22
  72.1 1.6 %collective-permute-start.35 = (bf16[512,256]{1,0:T(8,128)(2,1)S(1)}, bf16[512,256]{1,0:T(8,128)(2,1)S(1)}, u32[]{:S(2)}, u32[]{:S(2)}) collective-permute-start(bf16[512,256]{1,0:T(8,128)(2,1)S(1)} %constant_dynamic-update-slice_fusion.2.refs_2_), channel_id=1, source_target_pairs={{0,1},{1,0},{2,3},{3,2},{4,5},{5,4},{6,7},{7,6},{8,9},{9,8},{10,11... | collective-permute-start | bytes 786440 | tf_op jit(solution)/shard_map/ppermute | solution.py:22
  73.6 1.6 %collective-permute-start.31 = (bf16[512,256]{1,0:T(8,128)(2,1)S(1)}, bf16[512,256]{1,0:T(8,128)(2,1)S(1)}, u32[]{:S(2)}, u32[]{:S(2)}) collective-permute-start(bf16[512,256]{1,0:T(8,128)(2,1)S(1)} %pad_maximum_fusion.1.refs_0_), channel_id=1, source_target_pairs={{0,1},{1,0},{2,3},{3,2},{4,5},{5,4},{6,7},{7,6},{8,9},{9,8},{10,11... | collective-permute-start | bytes 786440 | tf_op jit(solution)/shard_map/ppermute | solution.py:22
  (5 other events, 39.2 us)

commit v8 on v7

--- a/solution.py
+++ b/solution.py
@@ -219,13 +219,12 @@
     result[...] = value[...].T
 
 
-def last_kernel(planes, lanes, rows, t_keep, *refs):
-    g_in, result = refs[:4], refs[4]
-    total = None
-    for at in range(4):
-        count = NEAR if at < 2 else planes - NEAR
+def last_kernel(planes, lanes, rows, start, count, t_keep, *refs):
+    g_in, result = refs[:2], refs[-1]
+    total = refs[2][...] if len(refs) == 4 else None
+    for at in range(2):
         for far in range(lanes // 2):
-            first = (2 * far + at % 2) * planes + (at >= 2) * NEAR
+            first = (2 * far + at) * planes + start
             one = jnp.dot(
                 t_keep[:, first * rows : (first + count) * rows],
                 g_in[at][far * count * rows : (far + 1) * count * rows, :],
@@ -372,15 +371,21 @@
     g_rest = jnp.concatenate(g_parts[NEAR - 1 :], 0)
     g_rest = jnp.concatenate([g_rest, swapped(g_rest, "narrow", FAR)], 0)
     g_all = [g_near, swapped(g_near, "narrow", CORE), g_rest, swapped(g_rest, "narrow", CORE)]
-    return pl.pallas_call(
-        functools.partial(last_kernel, planes, lanes, rows),
-        out_shape=jax.ShapeDtypeStruct((keep, out), jnp.float32),
-        in_specs=[VMEM] * 5,
-        out_specs=VMEM,
-        compiler_params=pltpu.CompilerParams(vmem_limit_bytes=vmem_room(4 * items * (out + keep))),
-        cost_estimate=cost(2 * items * keep * out, 2 * items * (keep + out)),
-        name="last",
-    )(t_keep, *g_all)
+    def product(name, start, count, *operands):
+        return pl.pallas_call(
+            functools.partial(last_kernel, planes, lanes, rows, start, count),
+            out_shape=jax.ShapeDtypeStruct((keep, out), jnp.float32),
+            in_specs=[VMEM] * (1 + len(operands)),
+            out_specs=VMEM,
+            compiler_params=pltpu.CompilerParams(
+                vmem_limit_bytes=vmem_room(4 * items * (out + keep))
+            ),
+            cost_estimate=cost(2 * lanes * count * rows * keep * out, 2 * items * (keep + out)),
+            name=name,
+        )(t_keep, *operands)
+
+    rest = product("rest", NEAR, planes - NEAR, *g_all[2:])
+    return product("last", 0, NEAR, *g_all[:2], rest)
 
 
 def solution(mesh):

time: 76.5 us -> 76.3 us (level)
  no operation moved by 1% of the time
where the time goes in v8:
time: 76.3 us; the launch traced here: 76.2 us
  starting transfers between devices  36 us (47%)
  waiting for transfers between devices  25.8 us (34%)
  Pallas kernels  8.78 us (12%)
  matrix products  2.96 us (4%)
  local copies, waits for them, and re-layouts  1.49 us (2%)
  other arithmetic  0.92 us (1%)
    ppermute x36, starting transfers between devices, swapped(): lax.ppermute(value, axis, [(source, source ^ bit) for source in range(cou...  36 us
    ppermute x36, waiting for transfers between devices, swapped(): lax.ppermute(value, axis, [(source, source ^ bit) for source in range(cou...  25.8 us
    pallas_call x3, Pallas kernels, pairs(): pl.pallas_call(functools.partial(pair_values_kernel, planes, lanes, rows,...  7.06 us
    dot_general x1, matrix products, per_device(): jnp.dot(after(teacher, own_core), low_weight, preferred_element_type=jnp....  2.96 us
  transfers between devices with their start and end apart: 36, of which 16 were waited for; matrix products, arithmetic and copies ran while one was open for 5% of the time, Pallas kernels for 7%

profile of v8, /device:TPU:0, one launch (start us, length us, event | category | flops | bytes accessed | tf_op | source)
XLA Modules:
  0.0 76.2 jit_solution(16431449650364775862)
XLA Ops:
  0.0 1.4 %constant_dynamic-slice_fusion.3 = (bf16[128,512]{1,0:T(8,128)(2,1)S(1)}, bf16[128,512]{1,0:T(8,128)(2,1)S(1)}, bf16[128,512]{1,0:T(8,128)(2,1)S(1)}, bf16[128,5...) fusion(bf16[128,4096]{1,0:T(8,128)(2,1)} %param.6, ...), kind=kLoop, calls=%fused_computation.20 | loop fusion | bytes 2097184 | tf_op jit(solution)/shard_map/dynamic_slice | solution.py:255
  1.4 5.1 %collective-permute-start.2 = (bf16[128,512]{1,0:T(8,128)(2,1)S(1)}, bf16[128,512]{1,0:T(8,128)(2,1)S(1)}, u32[]{:S(2)}, u32[]{:S(2)}) collective-permute-start(bf16[128,512]{1,0:T(8,128)(2,1)S(1)} %get-tuple-element.46), channel_id=1, source_target_pairs={{0,12},{4,8},{8,4},{12,0},{1,13},{5,9},{9,5},{13,1},{2,14},{6,10},... | collective-permute-start | bytes 393224 | tf_op jit(solution)/shard_map/ppermute | solution.py:22
  6.6 1.6 %collective-permute-start.7 = (bf16[512,512]{1,0:T(8,128)(2,1)S(1)}, bf16[512,512]{1,0:T(8,128)(2,1)S(1)}, u32[]{:S(2)}, u32[]{:S(2)}) collective-permute-start(bf16[512,512]{1,0:T(8,128)(2,1)S(1)} %pad_maximum_fusion), channel_id=1, source_target_pairs={{0,2},{1,3},{2,0},{3,1},{4,6},{5,7},{6,4},{7,5},{8,10},{9,11},{10,... | collective-permute-start | bytes 1572872 | tf_op jit(solution)/shard_map/ppermute | solution.py:22
  8.8 3.0 %fusion.2 = bf16[128,256]{1,0:T(8,128)(2,1)S(1)} fusion(bf16[128,4096]{1,0:T(8,128)(2,1)} %param.6, f32[4096,256]{1,0:T(8,128)} %param.7), kind=kOutput, calls=%fused_computation.2 | convolution fusion | flops 269516800 | bytes 5308416 | tf_op jit(solution)/shard_map/dot_general | solution.py:266
  12.6 1.2 %collective-permute-start = (bf16[128,512]{1,0:T(8,128)(2,1)S(1)}, bf16[128,512]{1,0:T(8,128)(2,1)S(1)}, u32[]{:S(2)}, u32[]{:S(2)}) collective-permute-start(bf16[128,512]{1,0:T(8,128)(2,1)S(1)} %get-tuple-element.48), channel_id=1, source_target_pairs={{0,4},{4,0},{8,12},{12,8},{1,5},{5,1},{9,13},{13,9},{2,6},{6,2},{1... | collective-permute-start | bytes 393224 | tf_op jit(solution)/shard_map/ppermute | solution.py:22
  13.9 3.6 %collective-permute-start.16 = (bf16[144,256]{1,0:T(8,128)(2,1)S(1)}, bf16[144,256]{1,0:T(8,128)(2,1)S(1)}, u32[]{:S(2)}, u32[]{:S(2)}) collective-permute-start(bf16[144,256]{1,0:T(8,128)(2,1)S(1)} %pad_maximum_fusion.5), channel_id=1, source_target_pairs={{0,8},{4,12},{8,0},{12,4},{1,9},{5,13},{9,1},{13,5},{2,10},{6,14},... | collective-permute-start | bytes 221192 | tf_op jit(solution)/shard_map/ppermute | solution.py:22
  17.9 2.6 %collective-permute-done.15 = bf16[144,256]{1,0:T(8,128)(2,1)S(1)} collective-permute-done((bf16[144,256]{1,0:T(8,128)(2,1)S(1)}, bf16[144,256]{1,0:T(8,128)(2,1)S(1)}, u32[]{:S(2)}, u32[]{:S(2)}) %collective-permute-start.15) | collective-permute-done | bytes 73760 | tf_op jit(solution)/shard_map/ppermute | solution.py:22
  20.6 1.1 %collective-permute-start.20 = (bf16[288,256]{1,0:T(8,128)(2,1)S(1)}, bf16[288,256]{1,0:T(8,128)(2,1)S(1)}, u32[]{:S(2)}, u32[]{:S(2)}) collective-permute-start(bf16[288,256]{1,0:T(8,128)(2,1)S(1)} %pad_maximum_fusion.2.refs_16_), channel_id=1, source_target_pairs={{0,2},{1,3},{2,0},{3,1},{4,6},{5,7},{6,4},{7,5},{8,10},{9,11},{10,... | collective-permute-start | bytes 442376 | tf_op jit(solution)/shard_map/ppermute | solution.py:22
  21.7 2.4 %collective-permute-start.17 = (bf16[144,256]{1,0:T(8,128)(2,1)S(1)}, bf16[144,256]{1,0:T(8,128)(2,1)S(1)}, u32[]{:S(2)}, u32[]{:S(2)}) collective-permute-start(bf16[144,256]{1,0:T(8,128)(2,1)S(1)} %collective-permute-done.16), channel_id=1, source_target_pairs={{0,4},{4,0},{8,12},{12,8},{1,5},{5,1},{9,13},{13,9},{2,6},{6,2},{1... | collective-permute-start | bytes 221192 | tf_op jit(solution)/shard_map/ppermute | solution.py:22
  24.1 1.7 %collective-permute-start.10 = (bf16[128,512]{1,0:T(8,128)(2,1)S(1)}, bf16[128,512]{1,0:T(8,128)(2,1)S(1)}, u32[]{:S(2)}, u32[]{:S(2)}) collective-permute-start(bf16[128,512]{1,0:T(8,128)(2,1)S(1)} %get-tuple-element.51), channel_id=1, source_target_pairs={{0,12},{4,8},{8,4},{12,0},{1,13},{5,9},{9,5},{13,1},{2,14},{6,10},... | collective-permute-start | bytes 393224 | tf_op jit(solution)/shard_map/ppermute | solution.py:22
  26.4 2.5 %collective-permute-start.8 = (bf16[128,512]{1,0:T(8,128)(2,1)S(1)}, bf16[128,512]{1,0:T(8,128)(2,1)S(1)}, u32[]{:S(2)}, u32[]{:S(2)}) collective-permute-start(bf16[128,512]{1,0:T(8,128)(2,1)S(1)} %get-tuple-element.53), channel_id=1, source_target_pairs={{0,4},{4,0},{8,12},{12,8},{1,5},{5,1},{9,13},{13,9},{2,6},{6,2},{1... | collective-permute-start | bytes 393224 | tf_op jit(solution)/shard_map/ppermute | solution.py:22
  28.9 1.9 %collective-permute-start.21 = (bf16[288,256]{1,0:T(8,128)(2,1)S(1)}, bf16[288,256]{1,0:T(8,128)(2,1)S(1)}, u32[]{:S(2)}, u32[]{:S(2)}) collective-permute-start(bf16[288,256]{1,0:T(8,128)(2,1)S(1)} %constant_dynamic-update-slice_fusion.refs_17_), channel_id=1, source_target_pairs={{0,2},{1,3},{2,0},{3,1},{4,6},{5,7},{6,4},{7,5},{8,10},{9,11},{10,... | collective-permute-start | bytes 442376 | tf_op jit(solution)/shard_map/ppermute | solution.py:22
  30.8 1.7 %collective-permute-done.10.refs_3_ = bf16[128,512]{1,0:T(8,128)(2,1)S(1)} collective-permute-done((bf16[128,512]{1,0:T(8,128)(2,1)S(1)}, bf16[128,512]{1,0:T(8,128)(2,1)S(1)}, u32[]{:S(2)}, u32[]{:S(2)}) %collective-permute-start.10) | collective-permute-done | bytes 131104 | tf_op jit(solution)/shard_map/ppermute | solution.py:22
  32.5 4.5 %collective-permute-done.9.refs_2_ = bf16[128,512]{1,0:T(8,128)(2,1)S(1)} collective-permute-done((bf16[128,512]{1,0:T(8,128)(2,1)S(1)}, bf16[128,512]{1,0:T(8,128)(2,1)S(1)}, u32[]{:S(2)}, u32[]{:S(2)}) %collective-permute-start.9) | collective-permute-done | bytes 131104 | tf_op jit(solution)/shard_map/ppermute | solution.py:22
  39.0 0.9 %collective-permute-done.4.refs_5_ = bf16[128,512]{1,0:T(8,128)(2,1)S(1)} collective-permute-done((bf16[128,512]{1,0:T(8,128)(2,1)S(1)}, bf16[128,512]{1,0:T(8,128)(2,1)S(1)}, u32[]{:S(2)}, u32[]{:S(2)}) %collective-permute-start.4) | collective-permute-done | bytes 131104 | tf_op jit(solution)/shard_map/ppermute | solution.py:22
  40.0 2.3 %pairs_far.3 = bf16[384,256]{1,0:T(8,128)(2,1)S(1)} custom-call(s32[4,4]{1,0:T(4,128)S(1)} %copy-done, s32[2]{0:T(128)S(1)} %pad_add_fusion.place, bf16[128,512]{1,0:T(8,128)(2,1)S(1)} %get-tuple-element.49.refs_0_, bf16[128,512]{1,0:T(8,128)(2,1)S(1)} %collective-permute-done.refs_1_, bf16[128,512]{1,0:T(8,128)(2,1)S(1)} %collective-permute-done.1.refs_2_, ...), custom_call_target="tpu_custom_call" | custom-call | flops 1207959552 | bytes 3145728 | tf_op jit(solution)/shard_map/pairs_far/pallas_call | solution.py:310
  42.3 1.6 %collective-permute-start.25 = (bf16[384,256]{1,0:T(8,128)(2,1)S(1)}, bf16[384,256]{1,0:T(8,128)(2,1)S(1)}, u32[]{:S(2)}, u32[]{:S(2)}) collective-permute-start(bf16[384,256]{1,0:T(8,128)(2,1)S(1)} %pairs_far.3), channel_id=1, source_target_pairs={{0,2},{1,3},{2,0},{3,1},{4,6},{5,7},{6,4},{7,5},{8,10},{9,11},{10,... | collective-permute-start | bytes 589832 | tf_op jit(solution)/shard_map/ppermute | solution.py:22
  43.9 3.1 %pairs_own.1 = (f32[512,256]{1,0:T(8,128)S(1)}, bf16[2048,256]{1,0:T(8,128)(2,1)S(1)}) custom-call(s32[4,4]{1,0:T(4,128)S(1)} %copy-done, s32[2]{0:T(128)S(1)} %pad_add_fusion.place, bf16[128,512]{1,0:T(8,128)(2,1)S(1)} %get-tuple-element.49.refs_0_, bf16[128,512]{1,0:T(8,128)(2,1)S(1)} %collective-permute-done.refs_1_, ...), custom_call_target="tpu_custom_call" | custom-call | flops 1610612736 | bytes 3145728 | tf_op jit(solution)/shard_map/pairs_own/pallas_call | solution.py:310
  47.3 1.6 %pairs_far.2 = bf16[128,256]{1,0:T(8,128)(2,1)S(1)} custom-call(s32[4,4]{1,0:T(4,128)S(1)} %copy-done, s32[2]{0:T(128)S(1)} %pad_add_fusion.place, bf16[128,512]{1,0:T(8,128)(2,1)S(1)} %get-tuple-element.49.refs_0_, bf16[128,512]{1,0:T(8,128)(2,1)S(1)} %collective-permute-done.refs_1_, bf16[128,512]{1,0:T(8,128)(2,1)S(1)} %collective-permute-done.1.refs_2_, ...), custom_call_target="tpu_custom_call" | custom-call | flops 402653184 | bytes 3145728 | tf_op jit(solution)/shard_map/pairs_far/pallas_call | solution.py:310
  49.7 2.0 %collective-permute-start.28 = (bf16[128,256]{1,0:T(8,128)(2,1)S(1)}, bf16[128,256]{1,0:T(8,128)(2,1)S(1)}, u32[]{:S(2)}, u32[]{:S(2)}) collective-permute-start(bf16[128,256]{1,0:T(8,128)(2,1)S(1)} %get-tuple-element.56), channel_id=1, source_target_pairs={{0,12},{4,8},{8,4},{12,0},{1,13},{5,9},{9,5},{13,1},{2,14},{6,10},... | collective-permute-start | bytes 196616 | tf_op jit(solution)/shard_map/ppermute | solution.py:22
  51.8 1.4 %collective-permute-start.27 = (bf16[128,256]{1,0:T(8,128)(2,1)S(1)}, bf16[128,256]{1,0:T(8,128)(2,1)S(1)}, u32[]{:S(2)}, u32[]{:S(2)}) collective-permute-start(bf16[128,256]{1,0:T(8,128)(2,1)S(1)} %get-tuple-element.57), channel_id=1, source_target_pairs={{0,8},{4,12},{8,0},{12,4},{1,9},{5,13},{9,1},{13,5},{2,10},{6,14},... | collective-permute-start | bytes 196616 | tf_op jit(solution)/shard_map/ppermute | solution.py:22
  54.0 2.4 %collective-permute-done.28 = bf16[128,256]{1,0:T(8,128)(2,1)S(1)} collective-permute-done((bf16[128,256]{1,0:T(8,128)(2,1)S(1)}, bf16[128,256]{1,0:T(8,128)(2,1)S(1)}, u32[]{:S(2)}, u32[]{:S(2)}) %collective-permute-start.28) | collective-permute-done | bytes 65568 | tf_op jit(solution)/shard_map/ppermute | solution.py:22
  56.3 2.6 %collective-permute-done.27 = bf16[128,256]{1,0:T(8,128)(2,1)S(1)} collective-permute-done((bf16[128,256]{1,0:T(8,128)(2,1)S(1)}, bf16[128,256]{1,0:T(8,128)(2,1)S(1)}, u32[]{:S(2)}, u32[]{:S(2)}) %collective-permute-start.27) | collective-permute-done | bytes 65568 | tf_op jit(solution)/shard_map/ppermute | solution.py:22
  59.0 2.0 %collective-permute-start.33 = (bf16[128,256]{1,0:T(8,128)(2,1)S(1)}, bf16[128,256]{1,0:T(8,128)(2,1)S(1)}, u32[]{:S(2)}, u32[]{:S(2)}) collective-permute-start(bf16[128,256]{1,0:T(8,128)(2,1)S(1)} %multiply_convert_fusion), channel_id=1, source_target_pairs={{0,12},{4,8},{8,4},{12,0},{1,13},{5,9},{9,5},{13,1},{2,14},{6,10},... | collective-permute-start | bytes 196616 | tf_op jit(solution)/shard_map/ppermute | solution.py:22
  60.9 2.5 %collective-permute-start.29 = (bf16[128,256]{1,0:T(8,128)(2,1)S(1)}, bf16[128,256]{1,0:T(8,128)(2,1)S(1)}, u32[]{:S(2)}, u32[]{:S(2)}) collective-permute-start(bf16[128,256]{1,0:T(8,128)(2,1)S(1)} %multiply_convert_fusion), channel_id=1, source_target_pairs={{0,4},{4,0},{8,12},{12,8},{1,5},{5,1},{9,13},{13,9},{2,6},{6,2},{1... | collective-permute-start | bytes 196616 | tf_op jit(solution)/shard_map/ppermute | solution.py:22
  63.4 2.4 %collective-permute-done.33 = bf16[128,256]{1,0:T(8,128)(2,1)S(1)} collective-permute-done((bf16[128,256]{1,0:T(8,128)(2,1)S(1)}, bf16[128,256]{1,0:T(8,128)(2,1)S(1)}, u32[]{:S(2)}, u32[]{:S(2)}) %collective-permute-start.33) | collective-permute-done | bytes 65568 | tf_op jit(solution)/shard_map/ppermute | solution.py:22
  65.8 1.2 %collective-permute-done.32 = bf16[128,256]{1,0:T(8,128)(2,1)S(1)} collective-permute-done((bf16[128,256]{1,0:T(8,128)(2,1)S(1)}, bf16[128,256]{1,0:T(8,128)(2,1)S(1)}, u32[]{:S(2)}, u32[]{:S(2)}) %collective-permute-start.32) | collective-permute-done | bytes 65568 | tf_op jit(solution)/shard_map/ppermute | solution.py:22
  67.0 1.5 %collective-permute-start.34 = (bf16[256,256]{1,0:T(8,128)(2,1)S(1)}, bf16[256,256]{1,0:T(8,128)(2,1)S(1)}, u32[]{:S(2)}, u32[]{:S(2)}) collective-permute-start(bf16[256,256]{1,0:T(8,128)(2,1)S(1)} %pad_maximum_fusion.4), channel_id=1, source_target_pairs={{0,2},{1,3},{2,0},{3,1},{4,6},{5,7},{6,4},{7,5},{8,10},{9,11},{10,... | collective-permute-start | bytes 393224 | tf_op jit(solution)/shard_map/ppermute | solution.py:22
  69.2 2.8 %collective-permute-done.34 = bf16[256,256]{1,0:T(8,128)(2,1)S(1)} collective-permute-done((bf16[256,256]{1,0:T(8,128)(2,1)S(1)}, bf16[256,256]{1,0:T(8,128)(2,1)S(1)}, u32[]{:S(2)}, u32[]{:S(2)}) %collective-permute-start.34) | collective-permute-done | bytes 131104 | tf_op jit(solution)/shard_map/ppermute | solution.py:22
  72.2 1.4 %collective-permute-done.30 = bf16[256,256]{1,0:T(8,128)(2,1)S(1)} collective-permute-done((bf16[256,256]{1,0:T(8,128)(2,1)S(1)}, bf16[256,256]{1,0:T(8,128)(2,1)S(1)}, u32[]{:S(2)}, u32[]{:S(2)}) %collective-permute-start.30) | collective-permute-done | bytes 131104 | tf_op jit(solution)/shard_map/ppermute | solution.py:22
  74.0 1.2 %collective-permute-done.31.refs_1_ = bf16[512,256]{1,0:T(8,128)(2,1)S(1)} collective-permute-done((bf16[512,256]{1,0:T(8,128)(2,1)S(1)}, bf16[512,256]{1,0:T(8,128)(2,1)S(1)}, u32[]{:S(2)}, u32[]{:S(2)}) %collective-permute-start.31) | collective-permute-done | bytes 262176 | tf_op jit(solution)/shard_map/ppermute | solution.py:22
  75.2 1.0 %last.1 = f32[256,256]{1,0:T(8,128)} custom-call(bf16[256,2048]{1,0:T(8,128)(2,1)S(1)} %flip.1.t_keep, bf16[512,256]{1,0:T(8,128)(2,1)S(1)} %pad_maximum_fusion.1.refs_0_, bf16[512,256]{1,0:T(8,128)(2,1)S(1)} %collective-permute-done.31.refs_1_, f32[256,256]{1,0:T(8,128)S(1)} %rest.1.refs_2_), custom_call_target="tpu_custom_call" | custom-call | flops 134217728 | bytes 2097152 | tf_op jit(solution)/shard_map/last/pallas_call | solution.py:375
  (70 shorter events, 7.9 us)
Async XLA Ops:
  1.4 12.5 %collective-permute-start.2 = (bf16[128,512]{1,0:T(8,128)(2,1)S(1)}, bf16[128,512]{1,0:T(8,128)(2,1)S(1)}, u32[]{:S(2)}, u32[]{:S(2)}) collective-permute-start(bf16[128,512]{1,0:T(8,128)(2,1)S(1)} %get-tuple-element.46), channel_id=1, source_target_pairs={{0,12},{4,8},{8,4},{12,0},{1,13},{5,9},{9,5},{13,1},{2,14},{6,10},... | collective-permute-start | bytes 393224 | tf_op jit(solution)/shard_map/ppermute | solution.py:22
  6.5 11.4 %collective-permute-start.1 = (bf16[128,512]{1,0:T(8,128)(2,1)S(1)}, bf16[128,512]{1,0:T(8,128)(2,1)S(1)}, u32[]{:S(2)}, u32[]{:S(2)}) collective-permute-start(bf16[128,512]{1,0:T(8,128)(2,1)S(1)} %get-tuple-element.47), channel_id=1, source_target_pairs={{0,8},{4,12},{8,0},{12,4},{1,9},{5,13},{9,1},{13,5},{2,10},{6,14},... | collective-permute-start | bytes 393224 | tf_op jit(solution)/shard_map/ppermute | solution.py:22
  6.5 2.3 %collective-permute-start.3 = (bf16[128,512]{1,0:T(8,128)(2,1)S(1)}, bf16[128,512]{1,0:T(8,128)(2,1)S(1)}, u32[]{:S(2)}, u32[]{:S(2)}) collective-permute-start(bf16[128,512]{1,0:T(8,128)(2,1)S(1)} %get-tuple-element.49.refs_0_), channel_id=1, source_target_pairs={{0,1},{1,0},{2,3},{3,2},{4,5},{5,4},{6,7},{7,6},{8,9},{9,8},{10,11... | collective-permute-start | bytes 393224 | tf_op jit(solution)/shard_map/ppermute | solution.py:22
  6.6 15.1 %collective-permute-start.7 = (bf16[512,512]{1,0:T(8,128)(2,1)S(1)}, bf16[512,512]{1,0:T(8,128)(2,1)S(1)}, u32[]{:S(2)}, u32[]{:S(2)}) collective-permute-start(bf16[512,512]{1,0:T(8,128)(2,1)S(1)} %pad_maximum_fusion), channel_id=1, source_target_pairs={{0,2},{1,3},{2,0},{3,1},{4,6},{5,7},{6,4},{7,5},{8,10},{9,11},{10,... | collective-permute-start | bytes 1572872 | tf_op jit(solution)/shard_map/ppermute | solution.py:22
  11.8 8.8 %collective-permute-start.15 = (bf16[144,256]{1,0:T(8,128)(2,1)S(1)}, bf16[144,256]{1,0:T(8,128)(2,1)S(1)}, u32[]{:S(2)}, u32[]{:S(2)}) collective-permute-start(bf16[144,256]{1,0:T(8,128)(2,1)S(1)} %pad_maximum_fusion.5), channel_id=1, source_target_pairs={{0,4},{4,0},{8,12},{12,8},{1,5},{5,1},{9,13},{13,9},{2,6},{6,2},{1... | collective-permute-start | bytes 221192 | tf_op jit(solution)/shard_map/ppermute | solution.py:22
  12.6 11.5 %collective-permute-start = (bf16[128,512]{1,0:T(8,128)(2,1)S(1)}, bf16[128,512]{1,0:T(8,128)(2,1)S(1)}, u32[]{:S(2)}, u32[]{:S(2)}) collective-permute-start(bf16[128,512]{1,0:T(8,128)(2,1)S(1)} %get-tuple-element.48), channel_id=1, source_target_pairs={{0,4},{4,0},{8,12},{12,8},{1,5},{5,1},{9,13},{13,9},{2,6},{6,2},{1... | collective-permute-start | bytes 393224 | tf_op jit(solution)/shard_map/ppermute | solution.py:22
  13.9 6.7 %collective-permute-start.16 = (bf16[144,256]{1,0:T(8,128)(2,1)S(1)}, bf16[144,256]{1,0:T(8,128)(2,1)S(1)}, u32[]{:S(2)}, u32[]{:S(2)}) collective-permute-start(bf16[144,256]{1,0:T(8,128)(2,1)S(1)} %pad_maximum_fusion.5), channel_id=1, source_target_pairs={{0,8},{4,12},{8,0},{12,4},{1,9},{5,13},{9,1},{13,5},{2,10},{6,14},... | collective-permute-start | bytes 221192 | tf_op jit(solution)/shard_map/ppermute | solution.py:22
  17.9 7.9 %collective-permute-start.6 = (bf16[128,512]{1,0:T(8,128)(2,1)S(1)}, bf16[128,512]{1,0:T(8,128)(2,1)S(1)}, u32[]{:S(2)}, u32[]{:S(2)}) collective-permute-start(bf16[128,512]{1,0:T(8,128)(2,1)S(1)} %collective-permute-done.2.refs_3_), channel_id=1, source_target_pairs={{0,1},{1,0},{2,3},{3,2},{4,5},{5,4},{6,7},{7,6},{8,9},{9,8},{10,11... | collective-permute-start | bytes 393224 | tf_op jit(solution)/shard_map/ppermute | solution.py:22
  20.5 8.4 %collective-permute-start.5 = (bf16[128,512]{1,0:T(8,128)(2,1)S(1)}, bf16[128,512]{1,0:T(8,128)(2,1)S(1)}, u32[]{:S(2)}, u32[]{:S(2)}) collective-permute-start(bf16[128,512]{1,0:T(8,128)(2,1)S(1)} %collective-permute-done.1.refs_2_), channel_id=1, source_target_pairs={{0,1},{1,0},{2,3},{3,2},{4,5},{5,4},{6,7},{7,6},{8,9},{9,8},{10,11... | collective-permute-start | bytes 393224 | tf_op jit(solution)/shard_map/ppermute | solution.py:22
  20.6 10.2 %collective-permute-start.20 = (bf16[288,256]{1,0:T(8,128)(2,1)S(1)}, bf16[288,256]{1,0:T(8,128)(2,1)S(1)}, u32[]{:S(2)}, u32[]{:S(2)}) collective-permute-start(bf16[288,256]{1,0:T(8,128)(2,1)S(1)} %pad_maximum_fusion.2.refs_16_), channel_id=1, source_target_pairs={{0,2},{1,3},{2,0},{3,1},{4,6},{5,7},{6,4},{7,5},{8,10},{9,11},{10,... | collective-permute-start | bytes 442376 | tf_op jit(solution)/shard_map/ppermute | solution.py:22
  21.7 4.8 %collective-permute-start.17 = (bf16[144,256]{1,0:T(8,128)(2,1)S(1)}, bf16[144,256]{1,0:T(8,128)(2,1)S(1)}, u32[]{:S(2)}, u32[]{:S(2)}) collective-permute-start(bf16[144,256]{1,0:T(8,128)(2,1)S(1)} %collective-permute-done.16), channel_id=1, source_target_pairs={{0,4},{4,0},{8,12},{12,8},{1,5},{5,1},{9,13},{13,9},{2,6},{6,2},{1... | collective-permute-start | bytes 221192 | tf_op jit(solution)/shard_map/ppermute | solution.py:22
  24.1 8.4 %collective-permute-start.10 = (bf16[128,512]{1,0:T(8,128)(2,1)S(1)}, bf16[128,512]{1,0:T(8,128)(2,1)S(1)}, u32[]{:S(2)}, u32[]{:S(2)}) collective-permute-start(bf16[128,512]{1,0:T(8,128)(2,1)S(1)} %get-tuple-element.51), channel_id=1, source_target_pairs={{0,12},{4,8},{8,4},{12,0},{1,13},{5,9},{9,5},{13,1},{2,14},{6,10},... | collective-permute-start | bytes 393224 | tf_op jit(solution)/shard_map/ppermute | solution.py:22
  25.8 11.2 %collective-permute-start.9 = (bf16[128,512]{1,0:T(8,128)(2,1)S(1)}, bf16[128,512]{1,0:T(8,128)(2,1)S(1)}, u32[]{:S(2)}, u32[]{:S(2)}) collective-permute-start(bf16[128,512]{1,0:T(8,128)(2,1)S(1)} %get-tuple-element.52), channel_id=1, source_target_pairs={{0,8},{4,12},{8,0},{12,4},{1,9},{5,13},{9,1},{13,5},{2,10},{6,14},... | collective-permute-start | bytes 393224 | tf_op jit(solution)/shard_map/ppermute | solution.py:22
  26.4 10.6 %collective-permute-start.8 = (bf16[128,512]{1,0:T(8,128)(2,1)S(1)}, bf16[128,512]{1,0:T(8,128)(2,1)S(1)}, u32[]{:S(2)}, u32[]{:S(2)}) collective-permute-start(bf16[128,512]{1,0:T(8,128)(2,1)S(1)} %get-tuple-element.53), channel_id=1, source_target_pairs={{0,4},{4,0},{8,12},{12,8},{1,5},{5,1},{9,13},{13,9},{2,6},{6,2},{1... | collective-permute-start | bytes 393224 | tf_op jit(solution)/shard_map/ppermute | solution.py:22
  28.9 8.6 %collective-permute-start.21 = (bf16[288,256]{1,0:T(8,128)(2,1)S(1)}, bf16[288,256]{1,0:T(8,128)(2,1)S(1)}, u32[]{:S(2)}, u32[]{:S(2)}) collective-permute-start(bf16[288,256]{1,0:T(8,128)(2,1)S(1)} %constant_dynamic-update-slice_fusion.refs_17_), channel_id=1, source_target_pairs={{0,2},{1,3},{2,0},{3,1},{4,6},{5,7},{6,4},{7,5},{8,10},{9,11},{10,... | collective-permute-start | bytes 442376 | tf_op jit(solution)/shard_map/ppermute | solution.py:22
  30.8 6.8 %collective-permute-start.11 = (bf16[128,512]{1,0:T(8,128)(2,1)S(1)}, bf16[128,512]{1,0:T(8,128)(2,1)S(1)}, u32[]{:S(2)}, u32[]{:S(2)}) collective-permute-start(bf16[128,512]{1,0:T(8,128)(2,1)S(1)} %get-tuple-element.54.refs_0_), channel_id=1, source_target_pairs={{0,1},{1,0},{2,3},{3,2},{4,5},{5,4},{6,7},{7,6},{8,9},{9,8},{10,11... | collective-permute-start | bytes 393224 | tf_op jit(solution)/shard_map/ppermute | solution.py:22
  32.5 5.6 %collective-permute-start.14 = (bf16[128,512]{1,0:T(8,128)(2,1)S(1)}, bf16[128,512]{1,0:T(8,128)(2,1)S(1)}, u32[]{:S(2)}, u32[]{:S(2)}) collective-permute-start(bf16[128,512]{1,0:T(8,128)(2,1)S(1)} %collective-permute-done.10.refs_3_), channel_id=1, source_target_pairs={{0,1},{1,0},{2,3},{3,2},{4,5},{5,4},{6,7},{7,6},{8,9},{9,8},{10,11... | collective-permute-start | bytes 393224 | tf_op jit(solution)/shard_map/ppermute | solution.py:22
  37.6 2.4 %collective-permute-start.18 = (bf16[288,256]{1,0:T(8,128)(2,1)S(1)}, bf16[288,256]{1,0:T(8,128)(2,1)S(1)}, u32[]{:S(2)}, u32[]{:S(2)}) collective-permute-start(bf16[288,256]{1,0:T(8,128)(2,1)S(1)} %pad_maximum_fusion.2.refs_16_), channel_id=1, source_target_pairs={{0,1},{1,0},{2,3},{3,2},{4,5},{5,4},{6,7},{7,6},{8,9},{9,8},{10,11... | collective-permute-start | bytes 442376 | tf_op jit(solution)/shard_map/ppermute | solution.py:22
  37.6 2.3 %collective-permute-start.19 = (bf16[288,256]{1,0:T(8,128)(2,1)S(1)}, bf16[288,256]{1,0:T(8,128)(2,1)S(1)}, u32[]{:S(2)}, u32[]{:S(2)}) collective-permute-start(bf16[288,256]{1,0:T(8,128)(2,1)S(1)} %constant_dynamic-update-slice_fusion.refs_17_), channel_id=1, source_target_pairs={{0,1},{1,0},{2,3},{3,2},{4,5},{5,4},{6,7},{7,6},{8,9},{9,8},{10,11... | collective-permute-start | bytes 442376 | tf_op jit(solution)/shard_map/ppermute | solution.py:22
  38.1 1.9 %collective-permute-start.22 = (bf16[288,256]{1,0:T(8,128)(2,1)S(1)}, bf16[288,256]{1,0:T(8,128)(2,1)S(1)}, u32[]{:S(2)}, u32[]{:S(2)}) collective-permute-start(bf16[288,256]{1,0:T(8,128)(2,1)S(1)} %collective-permute-done.20.refs_20_), channel_id=1, source_target_pairs={{0,1},{1,0},{2,3},{3,2},{4,5},{5,4},{6,7},{7,6},{8,9},{9,8},{10,11... | collective-permute-start | bytes 442376 | tf_op jit(solution)/shard_map/ppermute | solution.py:22
  42.3 7.3 %collective-permute-start.25 = (bf16[384,256]{1,0:T(8,128)(2,1)S(1)}, bf16[384,256]{1,0:T(8,128)(2,1)S(1)}, u32[]{:S(2)}, u32[]{:S(2)}) collective-permute-start(bf16[384,256]{1,0:T(8,128)(2,1)S(1)} %pairs_far.3), channel_id=1, source_target_pairs={{0,2},{1,3},{2,0},{3,1},{4,6},{5,7},{6,4},{7,5},{8,10},{9,11},{10,... | collective-permute-start | bytes 589832 | tf_op jit(solution)/shard_map/ppermute | solution.py:22
  49.0 4.3 %collective-permute-start.24 = (bf16[128,256]{1,0:T(8,128)(2,1)S(1)}, bf16[128,256]{1,0:T(8,128)(2,1)S(1)}, u32[]{:S(2)}, u32[]{:S(2)}) collective-permute-start(bf16[128,256]{1,0:T(8,128)(2,1)S(1)} %pairs_far.2), channel_id=1, source_target_pairs={{0,2},{1,3},{2,0},{3,1},{4,6},{5,7},{6,4},{7,5},{8,10},{9,11},{10,... | collective-permute-start | bytes 196616 | tf_op jit(solution)/shard_map/ppermute | solution.py:22
  49.6 4.3 %collective-permute-start.26 = (bf16[128,256]{1,0:T(8,128)(2,1)S(1)}, bf16[128,256]{1,0:T(8,128)(2,1)S(1)}, u32[]{:S(2)}, u32[]{:S(2)}) collective-permute-start(bf16[128,256]{1,0:T(8,128)(2,1)S(1)} %get-tuple-element.55), channel_id=1, source_target_pairs={{0,4},{4,0},{8,12},{12,8},{1,5},{5,1},{9,13},{13,9},{2,6},{6,2},{1... | collective-permute-start | bytes 196616 | tf_op jit(solution)/shard_map/ppermute | solution.py:22
  49.7 6.6 %collective-permute-start.28 = (bf16[128,256]{1,0:T(8,128)(2,1)S(1)}, bf16[128,256]{1,0:T(8,128)(2,1)S(1)}, u32[]{:S(2)}, u32[]{:S(2)}) collective-permute-start(bf16[128,256]{1,0:T(8,128)(2,1)S(1)} %get-tuple-element.56), channel_id=1, source_target_pairs={{0,12},{4,8},{8,4},{12,0},{1,13},{5,9},{9,5},{13,1},{2,14},{6,10},... | collective-permute-start | bytes 196616 | tf_op jit(solution)/shard_map/ppermute | solution.py:22
  51.8 7.2 %collective-permute-start.27 = (bf16[128,256]{1,0:T(8,128)(2,1)S(1)}, bf16[128,256]{1,0:T(8,128)(2,1)S(1)}, u32[]{:S(2)}, u32[]{:S(2)}) collective-permute-start(bf16[128,256]{1,0:T(8,128)(2,1)S(1)} %get-tuple-element.57), channel_id=1, source_target_pairs={{0,8},{4,12},{8,0},{12,4},{1,9},{5,13},{9,1},{13,5},{2,10},{6,14},... | collective-permute-start | bytes 196616 | tf_op jit(solution)/shard_map/ppermute | solution.py:22
  59.0 6.8 %collective-permute-start.33 = (bf16[128,256]{1,0:T(8,128)(2,1)S(1)}, bf16[128,256]{1,0:T(8,128)(2,1)S(1)}, u32[]{:S(2)}, u32[]{:S(2)}) collective-permute-start(bf16[128,256]{1,0:T(8,128)(2,1)S(1)} %multiply_convert_fusion), channel_id=1, source_target_pairs={{0,12},{4,8},{8,4},{12,0},{1,13},{5,9},{9,5},{13,1},{2,14},{6,10},... | collective-permute-start | bytes 196616 | tf_op jit(solution)/shard_map/ppermute | solution.py:22
  60.9 6.1 %collective-permute-start.32 = (bf16[128,256]{1,0:T(8,128)(2,1)S(1)}, bf16[128,256]{1,0:T(8,128)(2,1)S(1)}, u32[]{:S(2)}, u32[]{:S(2)}) collective-permute-start(bf16[128,256]{1,0:T(8,128)(2,1)S(1)} %multiply_convert_fusion), channel_id=1, source_target_pairs={{0,8},{4,12},{8,0},{12,4},{1,9},{5,13},{9,1},{13,5},{2,10},{6,14},... | collective-permute-start | bytes 196616 | tf_op jit(solution)/shard_map/ppermute | solution.py:22
  60.9 7.5 %collective-permute-start.29 = (bf16[128,256]{1,0:T(8,128)(2,1)S(1)}, bf16[128,256]{1,0:T(8,128)(2,1)S(1)}, u32[]{:S(2)}, u32[]{:S(2)}) collective-permute-start(bf16[128,256]{1,0:T(8,128)(2,1)S(1)} %multiply_convert_fusion), channel_id=1, source_target_pairs={{0,4},{4,0},{8,12},{12,8},{1,5},{5,1},{9,13},{13,9},{2,6},{6,2},{1... | collective-permute-start | bytes 196616 | tf_op jit(solution)/shard_map/ppermute | solution.py:22
  67.0 5.0 %collective-permute-start.34 = (bf16[256,256]{1,0:T(8,128)(2,1)S(1)}, bf16[256,256]{1,0:T(8,128)(2,1)S(1)}, u32[]{:S(2)}, u32[]{:S(2)}) collective-permute-start(bf16[256,256]{1,0:T(8,128)(2,1)S(1)} %pad_maximum_fusion.4), channel_id=1, source_target_pairs={{0,2},{1,3},{2,0},{3,1},{4,6},{5,7},{6,4},{7,5},{8,10},{9,11},{10,... | collective-permute-start | bytes 393224 | tf_op jit(solution)/shard_map/ppermute | solution.py:22
  68.5 5.0 %collective-permute-start.30 = (bf16[256,256]{1,0:T(8,128)(2,1)S(1)}, bf16[256,256]{1,0:T(8,128)(2,1)S(1)}, u32[]{:S(2)}, u32[]{:S(2)}) collective-permute-start(bf16[256,256]{1,0:T(8,128)(2,1)S(1)} %pad_maximum_fusion.3), channel_id=1, source_target_pairs={{0,2},{1,3},{2,0},{3,1},{4,6},{5,7},{6,4},{7,5},{8,10},{9,11},{10,... | collective-permute-start | bytes 393224 | tf_op jit(solution)/shard_map/ppermute | solution.py:22
  72.1 1.6 %collective-permute-start.35 = (bf16[512,256]{1,0:T(8,128)(2,1)S(1)}, bf16[512,256]{1,0:T(8,128)(2,1)S(1)}, u32[]{:S(2)}, u32[]{:S(2)}) collective-permute-start(bf16[512,256]{1,0:T(8,128)(2,1)S(1)} %constant_dynamic-update-slice_fusion.2.refs_0_), channel_id=1, source_target_pairs={{0,1},{1,0},{2,3},{3,2},{4,5},{5,4},{6,7},{7,6},{8,9},{9,8},{10,11... | collective-permute-start | bytes 786440 | tf_op jit(solution)/shard_map/ppermute | solution.py:22
  73.6 1.6 %collective-permute-start.31 = (bf16[512,256]{1,0:T(8,128)(2,1)S(1)}, bf16[512,256]{1,0:T(8,128)(2,1)S(1)}, u32[]{:S(2)}, u32[]{:S(2)}) collective-permute-start(bf16[512,256]{1,0:T(8,128)(2,1)S(1)} %pad_maximum_fusion.1.refs_0_), channel_id=1, source_target_pairs={{0,1},{1,0},{2,3},{3,2},{4,5},{5,4},{6,7},{7,6},{8,9},{9,8},{10,11... | collective-permute-start | bytes 786440 | tf_op jit(solution)/shard_map/ppermute | solution.py:22
  (5 other events, 39.2 us)
